TPU v7x, 32 devices: a whole 2x2x4 slice. The times are simulated.
32 devices in a mesh: group: 2 (over x), dp: 16 (over z, y, core).
Axes of the slice: x: 2, y: 2, z: 4, core: 2. Of those that a mesh axis runs over, the one named last changes fastest.
Arguments:
- tokens: bfloat16 [512, 4096], P(('group', 'dp')), parts along dimension 0, may hold values from -6 to 6
- cotangent: bfloat16 [512, 8192], P('group', 'dp'), parts along dimension 0, may hold values from -0.75 to 0.75
- token_weight: float32 [512], P('group'), parts along dimension 0, may hold values from 0.5 to 1.5
- weight: bfloat16 [4096, 8192], P(None, 'dp'), may hold values from -0.09375 to 0.09375
- moment_one: bfloat16 [4096, 8192], P(None, 'dp'), may hold values from -6 to 6
- moment_two: bfloat16 [4096, 8192], P(None, 'dp'), may hold values from 0.003 to 10
- adjoint: float32 [4096, 8192], P(None, 'dp'), may hold values from -5 to 5
Outputs:
- theta_bar: float32 [8192, 8192], P('group', 'dp'), parts along dimension 0
- token_scores: float32 [512], P(('group', 'dp')), parts along dimension 0
There are 2 independent parts, one for each index of `group`. A program takes and returns all parts, laid end to end along the dimension named above; an argument that names none is the same for every part. Nothing has to cross between parts.
All inputs are finite; a program needn't handle non-finite values.
Results may differ from a plain program's by a relative error of at most 0.0038.
Values may be sent and summed in bfloat16 or wider, within the bound.
No kernel may reach another device: no remote copies, remote signals or barrier semaphores. Data moves between devices by JAX's collectives and lax.ppermute only.
A program may use at most 128 MiB of HBM per device.

v0:
```python
import jax
import jax.numpy as jnp
from jax import lax
from jax.sharding import PartitionSpec as P

D = 4096
FW = 8192


def slopes(gate):
    sig = jax.nn.sigmoid(gate)
    slope = sig * (1.0 + gate * (1.0 - sig))
    curve = sig * (1.0 - sig) * (2.0 + gate * (1.0 - 2.0 * sig))
    return (slope, curve)


def contract_rows(rows, other):
    return lax.dot_general(
        rows, other, (((0,), (0,)), ((), ())), preferred_element_type=jnp.float32
    )


def forward_rows(rows, weight, cot_rows, weight_rows):
    gate = jnp.dot(rows, weight, preferred_element_type=jnp.float32)
    slope, curve = slopes(gate)
    scaled = (weight_rows[:, None] * cot_rows.astype(jnp.float32) * slope).astype(jnp.bfloat16)
    return (gate, scaled)


def backward_rows(rows, grad_adj, gate, cot_rows, weight_rows):
    probe = jnp.dot(rows, grad_adj, preferred_element_type=jnp.float32)
    slope, curve = slopes(gate)
    cot_f = cot_rows.astype(jnp.float32)
    bent = (weight_rows[:, None] * cot_f * curve * probe).astype(jnp.bfloat16)
    score = jnp.sum(cot_f * slope * probe, axis=1)
    return (bent, score)


def adjoint_step(grad, moment_one, moment_two, adjoint):
    first = 0.9 * moment_one.astype(jnp.float32) + 0.1 * grad
    second = 0.95 * moment_two.astype(jnp.float32) + 0.05 * grad * grad
    root = jnp.sqrt(second)
    den = root + 1e-08
    upd = first / den
    sq, cross = lax.psum((jnp.sum(upd * upd), jnp.sum(adjoint * upd)), "dp")
    count = D * FW
    rms = jnp.sqrt(sq / count)
    scale = 1.0 / jnp.maximum(1.0, rms)
    bind = jnp.where(rms > 1.0, 1.0 / (rms * rms * rms), 0.0)
    ubar = -0.01 * scale * adjoint + 0.01 * cross * bind / count * upd
    mbar = ubar / den
    vbar = -ubar * first / (den * den) / (2.0 * root)
    return (0.1 * mbar + 0.1 * grad * vbar).astype(jnp.bfloat16)


def shards(tokens, cotangent, token_weight, weight, moment_one, moment_two, adjoint):
    kept_rows = lax.all_gather(tokens, "dp", axis=0, tiled=True)
    gate, scaled = forward_rows(kept_rows, weight, cotangent, token_weight)
    grad = contract_rows(kept_rows, scaled)
    grad_adj = adjoint_step(grad, moment_one, moment_two, adjoint)
    bent, scores = backward_rows(kept_rows, grad_adj, gate, cotangent, token_weight)
    curvature = contract_rows(kept_rows, bent)
    theta_bar = 0.999 * adjoint + curvature
    token_scores = lax.psum_scatter(scores, "dp", scatter_dimension=0, tiled=True)
    return (theta_bar, token_scores)


def solution(mesh):
    in_specs = (
        P(("group", "dp"), None),
        P("group", "dp"),
        P("group"),
        P(None, "dp"),
        P(None, "dp"),
        P(None, "dp"),
        P(None, "dp"),
    )
    out_specs = (P("group", "dp"), P(("group", "dp")))
    return jax.shard_map(shards, mesh=mesh, in_specs=in_specs, out_specs=out_specs, check_vma=False)
```

profile of v0, /device:TPU:0, one launch (start us, length us, event | category | flops | bytes accessed | tf_op | source)
XLA Modules:
  0.0 176.0 jit_solution(10430388128339516694)
XLA Ops:
  7.2 0.0 all-gather.2.cloned.1.call-start
  7.2 0.7 all-gather.2.cloned.1.call-update
  7.9 8.9 %copy.16 = f32[4096,512]{0,1:T(8,128)} copy(f32[4096,512]{1,0:T(8,128)} %param.13) | data formatting | bytes 16777216 | tf_op args[6]
  16.8 0.0 copy-start.3
  16.8 6.4 %copy.17 = bf16[4096,512]{0,1:T(8,128)(2,1)} copy(bf16[4096,512]{1,0:T(8,128)(2,1)} %param.11) | data formatting | bytes 8388608 | tf_op args[4]
  23.2 0.0 copy-start.1
  23.2 0.0 copy-start.2
  23.2 6.5 %copy.18 = bf16[4096,512]{0,1:T(8,128)(2,1)} copy(bf16[4096,512]{1,0:T(8,128)(2,1)} %param.12) | data formatting | bytes 8388608 | tf_op args[5]
  29.7 0.0 copy-done.3
  29.7 0.6 dynamic-slice
  30.9 23.3 %all-gather.2.cloned.1.call-done = bf16[256,4096]{1,0:T(8,128)(2,1)} async-done(((bf16[16,4096]{1,0:T(8,128)(2,1)}), bf16[256,4096]{1,0:T(8,128)(2,1)}) %all-gather.2.cloned.1.call-update) | async-done | bytes 2097168 | tf_op jit(solution)/shard_map/all_gather | solution.py:57
  54.3 4.1 %fusion.30 = f32[256,512]{1,0:T(8,128)S(1)} fusion(bf16[256,4096]{1,0:T(8,128)(2,1)} %all-gather.2.cloned.1.call-done, bf16[4096,512]{1,0:T(8,128)(2,1)} %param.10), kind=kOutput, calls=%fused_computation.40 | convolution fusion | flops 1073741824 | bytes 6815744 | tf_op jit(solution)/shard_map/dot_general | solution.py:24
  58.4 0.0 copy-done.1
  58.4 0.0 copy-done.2
  58.4 0.0 copy-start
  58.4 15.1 %multiply_reduce_fusion.1 = (f32[]{:T(128)}, f32[]{:T(128)}, f32[512,4096]{1,0:T(8,128)}) fusion(bf16[4096,512]{0,1:T(8,128)(2,1)} %copy.18, bf16[4096,512]{0,1:T(8,128)(2,1)} %copy.17, f32[4096,512]{0,1:T(8,128)} %copy.16, bf16[256,4096]{1,0:T(8,128)(2,1)} %all-gather.2.cloned.1.call-done, bf16[256,512]{1,0:T(8,128)(2,1)S(1)} %copy-done.1, ...), kind=kOutput, calls=%fused_computation.8 | convolution fusion | flops 1106640896 | bytes 28050440 | tf_op jit(solution)/shard_map/dot_general | solution.py:18
  73.5 32.2 %all-reduce.1 = (f32[]{:T(128)}, f32[]{:T(128)}) all-reduce(f32[]{:T(128)} %get-tuple-element.7, f32[]{:T(128)} %get-tuple-element.6), channel_id=1, replica_groups=mesh['group'=2,'dp'=16] {'dp'}, use_global_device_ids=true, to_apply=%region_3.0 | all-reduce | flops 2 | bytes 16 | tf_op jit(solution)/shard_map/psum | solution.py:45
  107.1 0.0 copy-done
  107.1 14.8 %fusion.10 = (f32[256]{0:T(256)S(1)}, f32[256,512]{1,0:T(8,128)S(1)}) fusion(bf16[256,512]{1,0:T(8,128)(2,1)S(1)} %copy-done.1, f32[256,512]{1,0:T(8,128)S(1)} %fusion.30, bf16[256,4096]{1,0:T(8,128)(2,1)S(1)} %copy-done, f32[4096,512]{0,1:T(8,128)} %copy.16, bf16[4096,512]{0,1:T(8,128)(2,1)} %copy.17, f32[512,4096]{1,0:T(8,128)} %get-tuple-element.10, ...), kind=kOutput, calls=%fused_computation.22 | convolution fusion | flops 1127612160 | bytes 28574728 | tf_op jit(solution)/shard_map/dot_general | solution.py:31
  121.9 8.2 %bitcast_add_fusion = f32[4096,512]{0,1:T(8,128)} fusion(f32[4096,512]{0,1:T(8,128)} %copy.16, bf16[256,4096]{1,0:T(8,128)(2,1)S(1)} %copy-done, f32[256,512]{1,0:T(8,128)S(1)} %get-tuple-element.12, bf16[256,512]{1,0:T(8,128)(2,1)S(1)} %copy-done.1, f32[256,512]{1,0:T(8,128)S(1)} %fusion.30, f32[256]{0:T(256)S(1)} %copy-done.2), kind=kOutput, calls=%fused_computation.3 | convolution fusion | flops 1079902208 | bytes 20186112 | tf_op jit(solution)/shard_map/dot_general | solution.py:18
  130.1 8.9 %copy.22 = f32[4096,512]{1,0:T(8,128)} copy(f32[4096,512]{0,1:T(8,128)} %bitcast_add_fusion) | data formatting | bytes 16777216
  139.1 29.5 %all-reduce = f32[256]{0:T(256)S(1)} all-reduce(f32[256]{0:T(256)S(1)} %get-tuple-element.11), channel_id=2, replica_groups=mesh['group'=2,'dp'=16] {'dp'}, use_global_device_ids=true, to_apply=%region_5.6.clone | all-reduce | flops 256 | bytes 2048
  168.6 0.6 dynamic-slice.1
Async XLA Ops:
  7.2 47.1 %all-gather.2.cloned.1.call-start = ((), (), s32[]{:S(2)}) async-start(), calls=%async_computation | async-start | bytes 2228224 | tf_op jit(solution)/shard_map/all_gather | solution.py:57
  16.8 12.9 %copy-start.3 = (u32[32]{0:T(128)S(1)}, u32[32]{0:T(128)}, u32[]{:S(2)}) copy-start(u32[32]{0:T(128)} %constant.31) | copy-start | bytes 388
  23.2 35.1 %copy-start.1 = (bf16[256,512]{1,0:T(8,128)(2,1)S(1)}, bf16[256,512]{1,0:T(8,128)(2,1)}, u32[]{:S(2)}) copy-start(bf16[256,512]{1,0:T(8,128)(2,1)} %param.8) | copy-start | bytes 786436
  23.2 35.1 %copy-start.2 = (f32[256]{0:T(256)S(1)}, f32[256]{0:T(256)}, u32[]{:S(2)}) copy-start(f32[256]{0:T(256)} %param.9) | copy-start | bytes 3076
  58.4 48.7 %copy-start = (bf16[256,4096]{1,0:T(8,128)(2,1)S(1)}, bf16[256,4096]{1,0:T(8,128)(2,1)}, u32[]{:S(2)}) copy-start(bf16[256,4096]{1,0:T(8,128)(2,1)} %all-gather.2.cloned.1.call-done) | copy-start | bytes 6291460
Sparse Core Ops, SparseCore 0:
  10.2 44.0 all-gather.1
where the time goes:
time: 177 us; the launch traced here: 176 us
  blocking collectives  61.7 us (35%)
  matrix products  42.2 us (24%)
  local copies, waits for them, and re-layouts  31.9 us (18%)
  waiting for transfers between devices  24 us (14%)
  between operations  16.1 us (9%)
    psum x1, blocking collectives, adjoint_step(): sq, cross = lax.psum((jnp.sum(upd * upd), jnp.sum(adjoint * upd)), 'dp')  32.2 us
    unnamed x14, local copies, waits for them, and re-layouts  31.9 us
    unnamed x1, blocking collectives  29.5 us
    all_gather x1, waiting for transfers between devices, shards(): kept_rows = lax.all_gather(tokens, 'dp', axis=0, tiled=True)  23.3 us
    dot_general x2, matrix products, contract_rows(): lax.dot_general(rows, other, (((0,), (0,)), ((), ())), preferred_element_...  23.3 us
    dot_general x1, matrix products, backward_rows(): probe = jnp.dot(rows, grad_adj, preferred_element_type=jnp.float32)  14.8 us
    dot_general x1, matrix products, forward_rows(): gate = jnp.dot(rows, weight, preferred_element_type=jnp.float32)  4.06 us
  transfers between devices with their start and end apart: 1, of which 1 were waited for; matrix products, arithmetic and copies ran while one was open for 13% of the time, Pallas kernels for 0%

commit v1 on v0

v1 whole, which is shorter than its diff:
```python
import functools

import jax
import jax.numpy as jnp
from jax import lax
from jax.experimental import pallas as pl
from jax.experimental.pallas import tpu as pltpu
from jax.sharding import PartitionSpec as P

TILE = 512
ROWS = 16
VMEM_BYTES = 56 << 20
TN = (((0,), (0,)), ((), ()))


def params():
    return pltpu.CompilerParams(vmem_limit_bytes=VMEM_BYTES, dimension_semantics=("arbitrary",))


def f32dot(a, b):
    return jnp.dot(a, b, preferred_element_type=jnp.float32)


def digits(n):
    return (n // 4, 2, 2)


def shift(value, n, slow, mid, core):
    z, y, c = digits(n)
    pairs = []
    for d in range(n):
        dz, dy, dc = d // (y * c), d // c % y, d % c
        source = ((dz + slow) % z * y + (dy + mid) % y) * c + (dc + core) % c
        pairs.append((source, d))
    return lax.ppermute(value, "dp", pairs)


def gather(tokens, n):
    z, y, c = digits(n)
    parts = {(0, 0, 0): tokens}
    for slow in range(1, z):
        parts[slow, 0, 0] = shift(tokens, n, slow, 0, 0)
    for slow in range(z):
        parts[slow, 1, 0] = shift(parts[slow, 0, 0], n, 0, 1, 0)
    for slow in range(z):
        for mid in range(y):
            parts[slow, mid, 1] = shift(parts[slow, mid, 0], n, 0, 0, 1)
    me = lax.axis_index("dp")
    mz, my, mc = me // (y * c), me // c % y, me % c
    places = [((mz + a) % z * y + (my + b) % y) * c + (mc + d) % c for a, b, d in parts]
    return list(parts.values()), jnp.stack(places).astype(jnp.int32)


def all_sum(value, n):
    z, y, c = digits(n)
    total = value
    for slow in range(1, z):
        total = total + shift(value, n, slow, 0, 0)
    return [total] + [shift(total, n, 0, a, b) for a, b in ((0, 1), (1, 0), (1, 1))]


def gate_kernel(n, places, *refs):
    parts = refs[:n]
    weight, cot, token_weight, tokens, turned, scaled, bend, score, rows, total = refs[n:]
    step = pl.program_id(0)
    height = parts[0].shape[0]
    for part, ref in enumerate(parts):
        at = pl.multiple_of(places[part] * height, height)
        rows[pl.ds(at, height), :] = ref[...]
    here = rows[...]
    tokens[...] = here
    turned[...] = here.T

    @pl.when(step == 0)
    def _():
        total[...] = jnp.zeros_like(total)

    total[...] += f32dot(here, weight[...])

    @pl.when(step == pl.num_programs(0) - 1)
    def _():
        gate = total[...]
        tw = jnp.transpose(jnp.broadcast_to(token_weight[...], (8, token_weight.shape[1])))[:, :1]
        cot_f = cot[...].astype(jnp.float32)
        sig = 1.0 / (1.0 + jnp.exp(-gate))
        slope = sig * (1.0 + gate * (1.0 - sig))
        curve = sig * (1.0 - sig) * (2.0 + gate * (1.0 - 2.0 * sig))
        scaled[...] = (tw * cot_f * slope).astype(jnp.bfloat16)
        bend[...] = tw * cot_f * curve
        score[...] = cot_f * slope


def gate_call(parts, places, weight, cot, token_weight):
    n = len(parts)
    height, depth = parts[0].shape
    count, width = cot.shape
    whole = lambda shape: pl.BlockSpec(shape, lambda i, s: (0, 0))
    return pl.pallas_call(
        functools.partial(gate_kernel, n),
        grid_spec=pltpu.PrefetchScalarGridSpec(
            num_scalar_prefetch=1,
            grid=(depth // TILE,),
            in_specs=[pl.BlockSpec((height, TILE), lambda i, s: (0, i))] * n
            + [
                pl.BlockSpec((TILE, width), lambda i, s: (i, 0)),
                whole((count, width)),
                whole((1, count)),
            ],
            out_specs=[
                pl.BlockSpec((count, TILE), lambda i, s: (0, i)),
                pl.BlockSpec((TILE, count), lambda i, s: (i, 0)),
                whole((count, width)),
                whole((count, width)),
                whole((count, width)),
            ],
            scratch_shapes=[pltpu.VMEM((count, TILE), jnp.bfloat16), pltpu.VMEM((count, width), jnp.float32)],
        ),
        out_shape=[
            jax.ShapeDtypeStruct((count, depth), jnp.bfloat16),
            jax.ShapeDtypeStruct((depth, count), jnp.bfloat16),
            jax.ShapeDtypeStruct((count, width), jnp.bfloat16),
            jax.ShapeDtypeStruct((count, width), jnp.float32),
            jax.ShapeDtypeStruct((count, width), jnp.float32),
        ],
        compiler_params=params(),
        name="gate",
    )(places, *parts, weight, cot, token_weight)


def update(grad, one, two):
    first = 0.9 * one.astype(jnp.float32) + 0.1 * grad
    second = 0.95 * two.astype(jnp.float32) + 0.05 * (grad * grad)
    over = lax.rsqrt(second)
    inv = pltpu.reciprocal(second * over + 1e-08, approx=True)
    return over, inv, first * inv


def fold(x):
    return jnp.sum(x.reshape(x.shape[0] // 8, 8, x.shape[1]), axis=0)


def step_kernel(tokens, turned, scaled, one, two, adjoint, score, along, across, stats, grad, va, vb, sums, lean):
    step = pl.program_id(0)
    tall, width = one.shape

    grad[...] = f32dot(turned[...], scaled[...])

    @pl.when(step == 0)
    def _():
        sums[...] = jnp.zeros_like(sums)
        along[...] = jnp.zeros_like(along)
        across[...] = jnp.zeros_like(across)
        sq = jnp.zeros((8, width), jnp.float32)
        cross = jnp.zeros((8, width), jnp.float32)
        for r in range(0, 256, ROWS):
            at = pl.ds(r, ROWS)
            _, _, upd = update(grad[at, :], one[at, :], two[at, :])
            sq += fold(upd * upd)
            cross += fold(adjoint[at, :] * upd)
        sq = jnp.sum(sq, keepdims=True)
        lean[...] = jnp.broadcast_to(
            jnp.where(sq > 256.0 * width, jnp.sum(cross, keepdims=True) / jnp.maximum(sq, 1.0), 0.0), lean.shape
        )

    guess = lean[0:1, 0:1]
    sq = sums[0]
    cross = sums[1]
    for r in range(0, tall, ROWS):
        at = pl.ds(r, ROWS)
        g, adj = grad[at, :], adjoint[at, :]
        over, inv, upd = update(g, one[at, :], two[at, :])
        sq += fold(upd * upd)
        cross += fold(adj * upd)
        pull = inv * (0.1 - 0.05 * (g * (upd * over)))
        va[at, :] = ((adj - guess * upd) * pull).astype(jnp.bfloat16)
        vb[at, :] = (upd * pull).astype(jnp.bfloat16)
    sums[0] = sq
    sums[1] = cross
    along[...] += f32dot(tokens[...], va[...])
    across[...] += f32dot(tokens[...], vb[...])

    @pl.when(step == pl.num_programs(0) - 1)
    def _():
        b = score[...] * across[...]
        a = score[...] * along[...] + guess * b

        def lanes(x):
            x = sum(x[:, i : i + 128] for i in range(0, width, 128))
            return jnp.sum(jnp.transpose(x), axis=0, keepdims=True)

        count = a.shape[0]
        one_row = lambda x: jnp.broadcast_to(jnp.sum(x, keepdims=True), (1, count))
        stats[0:1, :] = lanes(a)
        stats[1:2, :] = lanes(b)
        stats[2:3, :] = one_row(sums[0])
        stats[3:4, :] = one_row(sums[1])
        stats[4:8, :] = jnp.broadcast_to(guess, (4, count))


def step_call(tokens, turned, scaled, one, two, adjoint, score):
    count, depth = tokens.shape
    width = one.shape[1]
    whole = lambda shape: pl.BlockSpec(shape, lambda i: (0, 0))
    tile = pl.BlockSpec((TILE, width), lambda i: (i, 0))
    return pl.pallas_call(
        step_kernel,
        grid=(depth // TILE,),
        in_specs=[
            pl.BlockSpec((count, TILE), lambda i: (0, i)),
            pl.BlockSpec((TILE, count), lambda i: (i, 0)),
            whole((count, width)),
            tile,
            tile,
            tile,
            whole((count, width)),
        ],
        out_specs=[whole((count, width)), whole((count, width)), whole((8, count))],
        out_shape=[
            jax.ShapeDtypeStruct((count, width), jnp.float32),
            jax.ShapeDtypeStruct((count, width), jnp.float32),
            jax.ShapeDtypeStruct((8, count), jnp.float32),
        ],
        scratch_shapes=[
            pltpu.VMEM((TILE, width), jnp.float32),
            pltpu.VMEM((TILE, width), jnp.bfloat16),
            pltpu.VMEM((TILE, width), jnp.bfloat16),
            pltpu.VMEM((2, 8, width), jnp.float32),
            pltpu.VMEM((8, 128), jnp.float32),
        ],
        compiler_params=params(),
        name="step",
    )(tokens, turned, scaled, one, two, adjoint, score)


def theta_kernel(entries, s0, s1, s2, s3, own, along, across, bend, turned, adjoint, theta, scores, bent):
    @pl.when(pl.program_id(0) == 0)
    def _():
        total = s0[...] + s1[...] + (s2[...] + s3[...])
        sq, cross = total[2:3, 0:1], total[3:4, 0:1]
        rms = jnp.sqrt(sq / entries)
        scale = 1.0 / jnp.maximum(1.0, rms)
        bind = jnp.where(rms > 1.0, 1.0 / (rms * rms * rms), 0.0)
        lead = -0.01 * scale
        rest = 0.01 * cross * bind / entries
        scores[...] = lead * total[0:1, :] + rest * total[1:2, :]
        mixed = rest + lead * own[4:5, 0:1]
        bent[...] = (bend[...] * (lead * along[...] + mixed * across[...])).astype(jnp.bfloat16)

    theta[...] = 0.999 * adjoint[...] + f32dot(turned[...], bent[...])


def theta_call(entries, sums, own, along, across, bend, turned, adjoint):
    depth, width = adjoint.shape
    count = turned.shape[1]
    whole = lambda shape: pl.BlockSpec(shape, lambda i: (0, 0))
    tile = pl.BlockSpec((TILE, width), lambda i: (i, 0))
    return pl.pallas_call(
        functools.partial(theta_kernel, entries),
        grid=(depth // TILE,),
        in_specs=[whole((8, count))] * 5
        + [whole((count, width))] * 3
        + [pl.BlockSpec((TILE, count), lambda i: (i, 0)), tile],
        out_specs=[tile, whole((1, count))],
        out_shape=[
            jax.ShapeDtypeStruct((depth, width), jnp.float32),
            jax.ShapeDtypeStruct((1, count), jnp.float32),
        ],
        scratch_shapes=[pltpu.VMEM((count, width), jnp.bfloat16)],
        compiler_params=params(),
        name="theta",
    )(*sums, own, along, across, bend, turned, adjoint)


def shards(n, tokens, cotangent, token_weight, weight, moment_one, moment_two, adjoint):
    entries = float(adjoint.shape[0] * adjoint.shape[1] * n)
    parts, places = gather(tokens, n)
    rows, turned, scaled, bend, score = gate_call(
        parts, places, weight, cotangent, token_weight.reshape(1, -1)
    )
    along, across, stats = step_call(rows, turned, scaled, moment_one, moment_two, adjoint, score)
    sums = all_sum(stats, n)
    theta_bar, scores = theta_call(entries, sums, stats, along, across, bend, turned, adjoint)
    height = tokens.shape[0]
    token_scores = lax.dynamic_slice(scores[0], (lax.axis_index("dp") * height,), (height,))
    return (theta_bar, token_scores)


def solution(mesh):
    in_specs = (
        P(("group", "dp"), None),
        P("group", "dp"),
        P("group"),
        P(None, "dp"),
        P(None, "dp"),
        P(None, "dp"),
        P(None, "dp"),
    )
    out_specs = (P("group", "dp"), P(("group", "dp")))
    body = functools.partial(shards, mesh.shape["dp"])
    return jax.shard_map(body, mesh=mesh, in_specs=in_specs, out_specs=out_specs, check_vma=False)
```

time: 177 us -> 82.1 us (0.46)
  blocking collectives: 61.7 us -> 0 us
  matrix products: 42.2 us -> 0 us
  Pallas kernels: 0 us -> 38.5 us
  local copies, waits for them, and re-layouts: 31.9 us -> 3.15 us
  starting transfers between devices: 0.04 us -> 19.4 us
  between operations: 16.1 us -> 0.82 us
  waiting for transfers between devices: 24 us -> 18.7 us
    dot_general x4 -> x0, matrix products: 42.2 us -> none  [the longest x2 23.3 us: contract_rows(): lax.dot_general(rows, other, (((0,), (0,)), ((), ())), preferred_element_...]
    pallas_call x0 -> x3, Pallas kernels: none -> 38.5 us  [the longest x1 17 us: step_call(): pl.pallas_call(step_kernel, grid=(depth // TILE,), in_specs=[pl.BlockSpec...]
    psum x1 -> x0, blocking collectives: 32.2 us -> none  [adjoint_step(): sq, cross = lax.psum((jnp.sum(upd * upd), jnp.sum(adjoint * upd)), 'dp')]
    unnamed x14 -> x38, local copies, waits for them, and re-layouts: 31.9 us -> 1.2 us
    unnamed x1 -> x0, blocking collectives: 29.5 us -> none
    all_gather x1 -> x0, waiting for transfers between devices: 23.3 us -> none  [shards(): kept_rows = lax.all_gather(tokens, 'dp', axis=0, tiled=True)]
    ppermute x0 -> x21, starting transfers between devices: none -> 19.4 us  [shift(): return lax.ppermute(value, 'dp', pairs)]
    ppermute x0 -> x21, waiting for transfers between devices: none -> 18.7 us  [shift(): return lax.ppermute(value, 'dp', pairs)]
  transfers between devices with their start and end apart: 1 -> 21, of which waited for: 1 -> 11; matrix products, arithmetic and copies ran while one was open for 13% -> 1% of each run, Pallas kernels for 0% -> 0%
where the time goes in v1:
time: 82.1 us; the launch traced here: 81.3 us
  Pallas kernels  38.5 us (47%)
  starting transfers between devices  19.4 us (24%)
  waiting for transfers between devices  18.7 us (23%)
  local copies, waits for them, and re-layouts  3.15 us (4%)
    ppermute x21, starting transfers between devices, shift(): return lax.ppermute(value, 'dp', pairs)  19.4 us
    ppermute x21, waiting for transfers between devices, shift(): return lax.ppermute(value, 'dp', pairs)  18.7 us
    pallas_call x1, Pallas kernels, step_call(): pl.pallas_call(step_kernel, grid=(depth // TILE,), in_specs=[pl.BlockSpec...  17 us
    pallas_call x1, Pallas kernels, theta_call(): pl.pallas_call(functools.partial(theta_kernel, entries), grid=(depth // T...  10.9 us
    pallas_call x1, Pallas kernels, gate_call(): pl.pallas_call(functools.partial(gate_kernel, n), grid_spec=pltpu.Prefetc...  10.6 us
  transfers between devices with their start and end apart: 21, of which 11 were waited for; matrix products, arithmetic and copies ran while one was open for 1% of the time, Pallas kernels for 0%

profile of v1, /device:TPU:0, one launch (start us, length us, event | category | flops | bytes accessed | tf_op | source)
XLA Modules:
  0.0 81.3 jit_solution(4364585516936630428)
XLA Ops:
  0.6 3.0 %collective-permute-start.3 = (bf16[16,4096]{1,0:T(8,128)(2,1)}, bf16[16,4096]{1,0:T(8,128)(2,1)S(1)}, u32[]{:S(2)}, u32[]{:S(2)}) collective-permute-start(bf16[16,4096]{1,0:T(8,128)(2,1)} %refs_0_.1), channel_id=1, source_target_pairs={{2,0},{3,1},{0,2},{1,3},{6,4},{7,5},{4,6},{5,7},{10,8},{11,9},{8,1... | collective-permute-start | bytes 393224 | tf_op jit(solution)/shard_map/ppermute | solution.py:35
  3.7 1.6 %collective-permute-start.2 = (bf16[16,4096]{1,0:T(8,128)(2,1)}, bf16[16,4096]{1,0:T(8,128)(2,1)S(1)}, u32[]{:S(2)}, u32[]{:S(2)}) collective-permute-start(bf16[16,4096]{1,0:T(8,128)(2,1)} %refs_0_.1), channel_id=1, source_target_pairs={{12,0},{13,1},{14,2},{15,3},{0,4},{1,5},{2,6},{3,7},{4,8},{5,9},{6... | collective-permute-start | bytes 393224 | tf_op jit(solution)/shard_map/ppermute | solution.py:35
  5.2 2.6 %collective-permute-start.1 = (bf16[16,4096]{1,0:T(8,128)(2,1)}, bf16[16,4096]{1,0:T(8,128)(2,1)S(1)}, u32[]{:S(2)}, u32[]{:S(2)}) collective-permute-start(bf16[16,4096]{1,0:T(8,128)(2,1)} %refs_0_.1), channel_id=1, source_target_pairs={{8,0},{9,1},{10,2},{11,3},{12,4},{13,5},{14,6},{15,7},{0,8},{1,9},... | collective-permute-start | bytes 393224 | tf_op jit(solution)/shard_map/ppermute | solution.py:35
  7.8 1.3 %collective-permute-start = (bf16[16,4096]{1,0:T(8,128)(2,1)}, bf16[16,4096]{1,0:T(8,128)(2,1)S(1)}, u32[]{:S(2)}, u32[]{:S(2)}) collective-permute-start(bf16[16,4096]{1,0:T(8,128)(2,1)} %refs_0_.1), channel_id=1, source_target_pairs={{4,0},{5,1},{6,2},{7,3},{8,4},{9,5},{10,6},{11,7},{12,8},{13,9},{1... | collective-permute-start | bytes 393224 | tf_op jit(solution)/shard_map/ppermute | solution.py:35
  9.2 0.0 collective-permute-start.7
  9.2 0.0 collective-permute-done.3.refs_4_
  9.2 0.5 collective-permute-start.8
  9.7 2.5 %collective-permute-done.2.refs_3_ = bf16[16,4096]{1,0:T(8,128)(2,1)S(1)} collective-permute-done((bf16[16,4096]{1,0:T(8,128)(2,1)}, bf16[16,4096]{1,0:T(8,128)(2,1)S(1)}, u32[]{:S(2)}, u32[]{:S(2)}) %collective-permute-start.2) | collective-permute-done | bytes 131104 | tf_op jit(solution)/shard_map/ppermute | solution.py:35
  12.2 0.0 collective-permute-start.13
  12.2 4.3 %collective-permute-done.1.refs_2_ = bf16[16,4096]{1,0:T(8,128)(2,1)S(1)} collective-permute-done((bf16[16,4096]{1,0:T(8,128)(2,1)}, bf16[16,4096]{1,0:T(8,128)(2,1)S(1)}, u32[]{:S(2)}, u32[]{:S(2)}) %collective-permute-start.1) | collective-permute-done | bytes 131104 | tf_op jit(solution)/shard_map/ppermute | solution.py:35
  16.5 0.5 collective-permute-start.6
  16.9 0.0 collective-permute-done.refs_1_
  16.9 1.6 %collective-permute-start.5 = (bf16[16,4096]{1,0:T(8,128)(2,1)S(1)}, bf16[16,4096]{1,0:T(8,128)(2,1)S(1)}, u32[]{:S(2)}, u32[]{:S(2)}) collective-permute-start(bf16[16,4096]{1,0:T(8,128)(2,1)S(1)} %collective-permute-done.1.refs_2_), channel_id=1, source_target_pairs={{2,0},{3,1},{0,2},{1,3},{6,4},{7,5},{4,6},{5,7},{10,8},{11,9},{8,1... | collective-permute-start | bytes 393224 | tf_op jit(solution)/shard_map/ppermute | solution.py:35
  18.5 0.0 collective-permute-done.7.refs_8_
  18.5 0.5 collective-permute-start.4
  19.0 0.0 collective-permute-done.8.refs_9_
  19.0 0.0 collective-permute-start.11
  19.0 0.5 collective-permute-start.9
  19.5 3.3 %collective-permute-done.6.refs_7_ = bf16[16,4096]{1,0:T(8,128)(2,1)S(1)} collective-permute-done((bf16[16,4096]{1,0:T(8,128)(2,1)S(1)}, bf16[16,4096]{1,0:T(8,128)(2,1)S(1)}, u32[]{:S(2)}, u32[]{:S(2)}) %collective-permute-start.6) | collective-permute-done | bytes 131104 | tf_op jit(solution)/shard_map/ppermute | solution.py:35
  22.8 2.8 %collective-permute-done.5.refs_6_ = bf16[16,4096]{1,0:T(8,128)(2,1)S(1)} collective-permute-done((bf16[16,4096]{1,0:T(8,128)(2,1)S(1)}, bf16[16,4096]{1,0:T(8,128)(2,1)S(1)}, u32[]{:S(2)}, u32[]{:S(2)}) %collective-permute-start.5) | collective-permute-done | bytes 131104 | tf_op jit(solution)/shard_map/ppermute | solution.py:35
  25.6 0.0 collective-permute-start.12
  25.7 1.8 %collective-permute-done.4.refs_5_ = bf16[16,4096]{1,0:T(8,128)(2,1)S(1)} collective-permute-done((bf16[16,4096]{1,0:T(8,128)(2,1)S(1)}, bf16[16,4096]{1,0:T(8,128)(2,1)S(1)}, u32[]{:S(2)}, u32[]{:S(2)}) %collective-permute-start.4) | collective-permute-done | bytes 131104 | tf_op jit(solution)/shard_map/ppermute | solution.py:35
  27.4 0.7 stack.67.places
  28.1 0.0 collective-permute-done.11.refs_12_
  28.1 0.0 collective-permute-done.9.refs_10_
  28.1 0.0 collective-permute-done.12.refs_13_
  28.2 0.6 collective-permute-done.10.refs_11_
  28.9 0.0 copy-done.12
  28.9 0.0 copy-done.13
  28.9 0.5 copy-done.14
  29.4 10.6 %gate.1 = (bf16[256,4096]{1,0:T(8,128)(2,1)}, bf16[4096,256]{1,0:T(8,128)(2,1)}, bf16[256,512]{1,0:T(8,128)(2,1)}, f32[256,512]{1,0:T(8,128)}, f32[256,512]{1,0:T(8,128)}) custom-call(s32[16]{0:T(128)} %stack.67.places, bf16[16,4096]{1,0:T(8,128)(2,1)} %refs_0_.1, bf16[16,4096]{1,0:T(8,128)(2,1)} %copy-done.3, bf16[16,4096]{1,0:T(8,128)(2,1)} %copy-done.2, ...), custom_call_target="tpu_custom_call" | custom-call | tf_op jit(solution)/shard_map/gate/pallas_call | solution.py:98
  40.0 17.0 %step.1 = (f32[256,512]{1,0:T(8,128)}, f32[256,512]{1,0:T(8,128)}, f32[8,256]{1,0:T(8,128)}) custom-call(bf16[256,4096]{1,0:T(8,128)(2,1)} %get-tuple-element.12.tokens, bf16[4096,256]{1,0:T(8,128)(2,1)} %get-tuple-element.13.turned, bf16[256,512]{1,0:T(8,128)(2,1)} %get-tuple-element.14.scaled, bf16[4096,512]{1,0:T(8,128)(2,1)} %one.1, ...), custom_call_target="tpu_custom_call" | custom-call | tf_op jit(solution)/shard_map/step/pallas_call | solution.py:205
  57.0 1.2 %collective-permute-start.17 = (f32[8,256]{1,0:T(8,128)}, f32[8,256]{1,0:T(8,128)S(1)}, u32[]{:S(2)}, u32[]{:S(2)}) collective-permute-start(f32[8,256]{1,0:T(8,128)} %get-tuple-element.16.own), channel_id=1, source_target_pairs={{12,0},{13,1},{14,2},{15,3},{0,4},{1,5},{2,6},{3,7},{4,8},{5,9},{6... | collective-permute-start | bytes 24584 | tf_op jit(solution)/shard_map/ppermute | solution.py:35
  58.2 2.0 %collective-permute-start.16 = (f32[8,256]{1,0:T(8,128)}, f32[8,256]{1,0:T(8,128)S(1)}, u32[]{:S(2)}, u32[]{:S(2)}) collective-permute-start(f32[8,256]{1,0:T(8,128)} %get-tuple-element.16.own), channel_id=1, source_target_pairs={{8,0},{9,1},{10,2},{11,3},{12,4},{13,5},{14,6},{15,7},{0,8},{1,9},... | collective-permute-start | bytes 24584 | tf_op jit(solution)/shard_map/ppermute | solution.py:35
  60.2 2.2 %collective-permute-start.15 = (f32[8,256]{1,0:T(8,128)}, f32[8,256]{1,0:T(8,128)S(1)}, u32[]{:S(2)}, u32[]{:S(2)}) collective-permute-start(f32[8,256]{1,0:T(8,128)} %get-tuple-element.16.own), channel_id=1, source_target_pairs={{4,0},{5,1},{6,2},{7,3},{8,4},{9,5},{10,6},{11,7},{12,8},{13,9},{1... | collective-permute-start | bytes 24584 | tf_op jit(solution)/shard_map/ppermute | solution.py:35
  62.5 0.2 collective-permute-done.17
  62.6 0.3 collective-permute-done.16
  63.0 1.1 %collective-permute-done.15 = f32[8,256]{1,0:T(8,128)S(1)} collective-permute-done((f32[8,256]{1,0:T(8,128)}, f32[8,256]{1,0:T(8,128)S(1)}, u32[]{:S(2)}, u32[]{:S(2)}) %collective-permute-start.15) | collective-permute-done | bytes 8224 | tf_op jit(solution)/shard_map/ppermute | solution.py:35
  64.1 0.7 add_add_fusion.s0
  64.8 0.6 collective-permute-start.19
  65.4 1.3 %collective-permute-start.18 = (f32[8,256]{1,0:T(8,128)S(1)}, f32[8,256]{1,0:T(8,128)S(1)}, u32[]{:S(2)}, u32[]{:S(2)}) collective-permute-start(f32[8,256]{1,0:T(8,128)S(1)} %add_add_fusion.s0), channel_id=1, source_target_pairs={{1,0},{0,1},{3,2},{2,3},{5,4},{4,5},{7,6},{6,7},{9,8},{8,9},{11,10... | collective-permute-start | bytes 24584 | tf_op jit(solution)/shard_map/ppermute | solution.py:35
  66.7 1.2 %collective-permute-done.20.s3 = f32[8,256]{1,0:T(8,128)S(1)} collective-permute-done((f32[8,256]{1,0:T(8,128)S(1)}, f32[8,256]{1,0:T(8,128)S(1)}, u32[]{:S(2)}, u32[]{:S(2)}) %collective-permute-start.20) | collective-permute-done | bytes 8224 | tf_op jit(solution)/shard_map/ppermute | solution.py:35
  67.9 0.6 collective-permute-done.19.s2
  68.5 0.0 collective-permute-done.18.s1
  68.6 0.6 copy-done.17
  69.1 0.0 copy-done.18
  69.1 10.9 %theta.1 = (f32[4096,512]{1,0:T(8,128)}, f32[1,256]{1,0:T(1,128)}) custom-call(f32[8,256]{1,0:T(8,128)} %copy-done.15, f32[8,256]{1,0:T(8,128)} %copy-done.18, f32[8,256]{1,0:T(8,128)} %copy-done.17, f32[8,256]{1,0:T(8,128)} %copy-done.16, f32[8,256]{1,0:T(8,128)} %get-tuple-element.16.own, f32[256,512]{1,0:T(8,128)} %get-tuple-element.17.along, ...), custom_call_target="tpu_custom_call" | custom-call | tf_op jit(solution)/shard_map/theta/pallas_call | solution.py:257
  80.1 1.2 %dynamic-slice_bitcast_fusion = f32[16]{0:T(128)} fusion(f32[1,256]{1,0:T(1,128)} %get-tuple-element.21, s32[]{:T(128)S(6)} %select_n.145), kind=kLoop, calls=%fused_computation.1 | loop fusion | bytes 132 | tf_op jit(solution)/shard_map/dynamic_slice | solution.py:284
  (38 shorter events, 0.1 us)
Async XLA Ops:
  0.6 8.6 %collective-permute-start.3 = (bf16[16,4096]{1,0:T(8,128)(2,1)}, bf16[16,4096]{1,0:T(8,128)(2,1)S(1)}, u32[]{:S(2)}, u32[]{:S(2)}) collective-permute-start(bf16[16,4096]{1,0:T(8,128)(2,1)} %refs_0_.1), channel_id=1, source_target_pairs={{2,0},{3,1},{0,2},{1,3},{6,4},{7,5},{4,6},{5,7},{10,8},{11,9},{8,1... | collective-permute-start | bytes 393224 | tf_op jit(solution)/shard_map/ppermute | solution.py:35
  3.7 8.5 %collective-permute-start.2 = (bf16[16,4096]{1,0:T(8,128)(2,1)}, bf16[16,4096]{1,0:T(8,128)(2,1)S(1)}, u32[]{:S(2)}, u32[]{:S(2)}) collective-permute-start(bf16[16,4096]{1,0:T(8,128)(2,1)} %refs_0_.1), channel_id=1, source_target_pairs={{12,0},{13,1},{14,2},{15,3},{0,4},{1,5},{2,6},{3,7},{4,8},{5,9},{6... | collective-permute-start | bytes 393224 | tf_op jit(solution)/shard_map/ppermute | solution.py:35
  5.2 11.2 %collective-permute-start.1 = (bf16[16,4096]{1,0:T(8,128)(2,1)}, bf16[16,4096]{1,0:T(8,128)(2,1)S(1)}, u32[]{:S(2)}, u32[]{:S(2)}) collective-permute-start(bf16[16,4096]{1,0:T(8,128)(2,1)} %refs_0_.1), channel_id=1, source_target_pairs={{8,0},{9,1},{10,2},{11,3},{12,4},{13,5},{14,6},{15,7},{0,8},{1,9},... | collective-permute-start | bytes 393224 | tf_op jit(solution)/shard_map/ppermute | solution.py:35
  7.8 9.1 %collective-permute-start = (bf16[16,4096]{1,0:T(8,128)(2,1)}, bf16[16,4096]{1,0:T(8,128)(2,1)S(1)}, u32[]{:S(2)}, u32[]{:S(2)}) collective-permute-start(bf16[16,4096]{1,0:T(8,128)(2,1)} %refs_0_.1), channel_id=1, source_target_pairs={{4,0},{5,1},{6,2},{7,3},{8,4},{9,5},{10,6},{11,7},{12,8},{13,9},{1... | collective-permute-start | bytes 393224 | tf_op jit(solution)/shard_map/ppermute | solution.py:35
  9.2 9.3 %collective-permute-start.7 = (bf16[16,4096]{1,0:T(8,128)(2,1)}, bf16[16,4096]{1,0:T(8,128)(2,1)S(1)}, u32[]{:S(2)}, u32[]{:S(2)}) collective-permute-start(bf16[16,4096]{1,0:T(8,128)(2,1)} %refs_0_.1), channel_id=1, source_target_pairs={{1,0},{0,1},{3,2},{2,3},{5,4},{4,5},{7,6},{6,7},{9,8},{8,9},{11,10... | collective-permute-start | bytes 393224 | tf_op jit(solution)/shard_map/ppermute | solution.py:35
  9.2 19.6 %copy-start = (bf16[16,4096]{1,0:T(8,128)(2,1)}, bf16[16,4096]{1,0:T(8,128)(2,1)S(1)}, u32[]{:S(2)}) copy-start(bf16[16,4096]{1,0:T(8,128)(2,1)S(1)} %collective-permute-done.3.refs_4_) | copy-start | bytes 393220
  9.2 9.8 %collective-permute-start.8 = (bf16[16,4096]{1,0:T(8,128)(2,1)S(1)}, bf16[16,4096]{1,0:T(8,128)(2,1)S(1)}, u32[]{:S(2)}, u32[]{:S(2)}) collective-permute-start(bf16[16,4096]{1,0:T(8,128)(2,1)S(1)} %collective-permute-done.3.refs_4_), channel_id=1, source_target_pairs={{1,0},{0,1},{3,2},{2,3},{5,4},{4,5},{7,6},{6,7},{9,8},{8,9},{11,10... | collective-permute-start | bytes 393224 | tf_op jit(solution)/shard_map/ppermute | solution.py:35
  12.2 16.6 %copy-start.1 = (bf16[16,4096]{1,0:T(8,128)(2,1)}, bf16[16,4096]{1,0:T(8,128)(2,1)S(1)}, u32[]{:S(2)}) copy-start(bf16[16,4096]{1,0:T(8,128)(2,1)S(1)} %collective-permute-done.2.refs_3_) | copy-start | bytes 393220
  12.2 6.8 %collective-permute-start.13 = (bf16[16,4096]{1,0:T(8,128)(2,1)S(1)}, bf16[16,4096]{1,0:T(8,128)(2,1)S(1)}, u32[]{:S(2)}, u32[]{:S(2)}) collective-permute-start(bf16[16,4096]{1,0:T(8,128)(2,1)S(1)} %collective-permute-done.2.refs_3_), channel_id=1, source_target_pairs={{1,0},{0,1},{3,2},{2,3},{5,4},{4,5},{7,6},{6,7},{9,8},{8,9},{11,10... | collective-permute-start | bytes 393224 | tf_op jit(solution)/shard_map/ppermute | solution.py:35
  16.5 12.3 %copy-start.2 = (bf16[16,4096]{1,0:T(8,128)(2,1)}, bf16[16,4096]{1,0:T(8,128)(2,1)S(1)}, u32[]{:S(2)}) copy-start(bf16[16,4096]{1,0:T(8,128)(2,1)S(1)} %collective-permute-done.1.refs_2_) | copy-start | bytes 393220
  16.5 6.4 %collective-permute-start.6 = (bf16[16,4096]{1,0:T(8,128)(2,1)S(1)}, bf16[16,4096]{1,0:T(8,128)(2,1)S(1)}, u32[]{:S(2)}, u32[]{:S(2)}) collective-permute-start(bf16[16,4096]{1,0:T(8,128)(2,1)S(1)} %collective-permute-done.2.refs_3_), channel_id=1, source_target_pairs={{2,0},{3,1},{0,2},{1,3},{6,4},{7,5},{4,6},{5,7},{10,8},{11,9},{8,1... | collective-permute-start | bytes 393224 | tf_op jit(solution)/shard_map/ppermute | solution.py:35
  16.9 11.8 %copy-start.3 = (bf16[16,4096]{1,0:T(8,128)(2,1)}, bf16[16,4096]{1,0:T(8,128)(2,1)S(1)}, u32[]{:S(2)}) copy-start(bf16[16,4096]{1,0:T(8,128)(2,1)S(1)} %collective-permute-done.refs_1_) | copy-start | bytes 393220
  16.9 8.7 %collective-permute-start.5 = (bf16[16,4096]{1,0:T(8,128)(2,1)S(1)}, bf16[16,4096]{1,0:T(8,128)(2,1)S(1)}, u32[]{:S(2)}, u32[]{:S(2)}) collective-permute-start(bf16[16,4096]{1,0:T(8,128)(2,1)S(1)} %collective-permute-done.1.refs_2_), channel_id=1, source_target_pairs={{2,0},{3,1},{0,2},{1,3},{6,4},{7,5},{4,6},{5,7},{10,8},{11,9},{8,1... | collective-permute-start | bytes 393224 | tf_op jit(solution)/shard_map/ppermute | solution.py:35
  18.5 10.3 %copy-start.4 = (bf16[16,4096]{1,0:T(8,128)(2,1)}, bf16[16,4096]{1,0:T(8,128)(2,1)S(1)}, u32[]{:S(2)}) copy-start(bf16[16,4096]{1,0:T(8,128)(2,1)S(1)} %collective-permute-done.7.refs_8_) | copy-start | bytes 393220
  18.5 8.9 %collective-permute-start.4 = (bf16[16,4096]{1,0:T(8,128)(2,1)S(1)}, bf16[16,4096]{1,0:T(8,128)(2,1)S(1)}, u32[]{:S(2)}, u32[]{:S(2)}) collective-permute-start(bf16[16,4096]{1,0:T(8,128)(2,1)S(1)} %collective-permute-done.refs_1_), channel_id=1, source_target_pairs={{2,0},{3,1},{0,2},{1,3},{6,4},{7,5},{4,6},{5,7},{10,8},{11,9},{8,1... | collective-permute-start | bytes 393224 | tf_op jit(solution)/shard_map/ppermute | solution.py:35
  19.0 9.8 %copy-start.5 = (bf16[16,4096]{1,0:T(8,128)(2,1)}, bf16[16,4096]{1,0:T(8,128)(2,1)S(1)}, u32[]{:S(2)}) copy-start(bf16[16,4096]{1,0:T(8,128)(2,1)S(1)} %collective-permute-done.8.refs_9_) | copy-start | bytes 393220
  19.0 9.1 %collective-permute-start.11 = (bf16[16,4096]{1,0:T(8,128)(2,1)S(1)}, bf16[16,4096]{1,0:T(8,128)(2,1)S(1)}, u32[]{:S(2)}, u32[]{:S(2)}) collective-permute-start(bf16[16,4096]{1,0:T(8,128)(2,1)S(1)} %collective-permute-done.1.refs_2_), channel_id=1, source_target_pairs={{1,0},{0,1},{3,2},{2,3},{5,4},{4,5},{7,6},{6,7},{9,8},{8,9},{11,10... | collective-permute-start | bytes 393224 | tf_op jit(solution)/shard_map/ppermute | solution.py:35
  19.0 9.8 %copy-start.6 = (bf16[16,4096]{1,0:T(8,128)(2,1)}, bf16[16,4096]{1,0:T(8,128)(2,1)S(1)}, u32[]{:S(2)}) copy-start(bf16[16,4096]{1,0:T(8,128)(2,1)S(1)} %collective-permute-done.13.refs_14_) | copy-start | bytes 393220
  19.0 9.1 %collective-permute-start.9 = (bf16[16,4096]{1,0:T(8,128)(2,1)S(1)}, bf16[16,4096]{1,0:T(8,128)(2,1)S(1)}, u32[]{:S(2)}, u32[]{:S(2)}) collective-permute-start(bf16[16,4096]{1,0:T(8,128)(2,1)S(1)} %collective-permute-done.refs_1_), channel_id=1, source_target_pairs={{1,0},{0,1},{3,2},{2,3},{5,4},{4,5},{7,6},{6,7},{9,8},{8,9},{11,10... | collective-permute-start | bytes 393224 | tf_op jit(solution)/shard_map/ppermute | solution.py:35
  22.8 6.0 %copy-start.7 = (bf16[16,4096]{1,0:T(8,128)(2,1)}, bf16[16,4096]{1,0:T(8,128)(2,1)S(1)}, u32[]{:S(2)}) copy-start(bf16[16,4096]{1,0:T(8,128)(2,1)S(1)} %collective-permute-done.6.refs_7_) | copy-start | bytes 393220
  22.8 5.3 %collective-permute-start.14 = (bf16[16,4096]{1,0:T(8,128)(2,1)S(1)}, bf16[16,4096]{1,0:T(8,128)(2,1)S(1)}, u32[]{:S(2)}, u32[]{:S(2)}) collective-permute-start(bf16[16,4096]{1,0:T(8,128)(2,1)S(1)} %collective-permute-done.6.refs_7_), channel_id=1, source_target_pairs={{1,0},{0,1},{3,2},{2,3},{5,4},{4,5},{7,6},{6,7},{9,8},{8,9},{11,10... | collective-permute-start | bytes 393224 | tf_op jit(solution)/shard_map/ppermute | solution.py:35
  25.6 3.2 %copy-start.8 = (bf16[16,4096]{1,0:T(8,128)(2,1)}, bf16[16,4096]{1,0:T(8,128)(2,1)S(1)}, u32[]{:S(2)}) copy-start(bf16[16,4096]{1,0:T(8,128)(2,1)S(1)} %collective-permute-done.5.refs_6_) | copy-start | bytes 393220
  25.6 2.5 %collective-permute-start.12 = (bf16[16,4096]{1,0:T(8,128)(2,1)S(1)}, bf16[16,4096]{1,0:T(8,128)(2,1)S(1)}, u32[]{:S(2)}, u32[]{:S(2)}) collective-permute-start(bf16[16,4096]{1,0:T(8,128)(2,1)S(1)} %collective-permute-done.5.refs_6_), channel_id=1, source_target_pairs={{1,0},{0,1},{3,2},{2,3},{5,4},{4,5},{7,6},{6,7},{9,8},{8,9},{11,10... | collective-permute-start | bytes 393224 | tf_op jit(solution)/shard_map/ppermute | solution.py:35
  27.4 1.4 %copy-start.9 = (bf16[16,4096]{1,0:T(8,128)(2,1)}, bf16[16,4096]{1,0:T(8,128)(2,1)S(1)}, u32[]{:S(2)}) copy-start(bf16[16,4096]{1,0:T(8,128)(2,1)S(1)} %collective-permute-done.4.refs_5_) | copy-start | bytes 393220
  27.4 1.3 %collective-permute-start.10 = (bf16[16,4096]{1,0:T(8,128)(2,1)S(1)}, bf16[16,4096]{1,0:T(8,128)(2,1)S(1)}, u32[]{:S(2)}, u32[]{:S(2)}) collective-permute-start(bf16[16,4096]{1,0:T(8,128)(2,1)S(1)} %collective-permute-done.4.refs_5_), channel_id=1, source_target_pairs={{1,0},{0,1},{3,2},{2,3},{5,4},{4,5},{7,6},{6,7},{9,8},{8,9},{11,10... | collective-permute-start | bytes 393224 | tf_op jit(solution)/shard_map/ppermute | solution.py:35
  28.1 0.7 copy-start.10
  28.1 0.7 copy-start.11
  28.1 0.7 copy-start.12
  28.2 0.7 copy-start.13
  28.8 0.7 copy-start.14
  57.0 5.7 %collective-permute-start.17 = (f32[8,256]{1,0:T(8,128)}, f32[8,256]{1,0:T(8,128)S(1)}, u32[]{:S(2)}, u32[]{:S(2)}) collective-permute-start(f32[8,256]{1,0:T(8,128)} %get-tuple-element.16.own), channel_id=1, source_target_pairs={{12,0},{13,1},{14,2},{15,3},{0,4},{1,5},{2,6},{3,7},{4,8},{5,9},{6... | collective-permute-start | bytes 24584 | tf_op jit(solution)/shard_map/ppermute | solution.py:35
  58.2 4.8 %collective-permute-start.16 = (f32[8,256]{1,0:T(8,128)}, f32[8,256]{1,0:T(8,128)S(1)}, u32[]{:S(2)}, u32[]{:S(2)}) collective-permute-start(f32[8,256]{1,0:T(8,128)} %get-tuple-element.16.own), channel_id=1, source_target_pairs={{8,0},{9,1},{10,2},{11,3},{12,4},{13,5},{14,6},{15,7},{0,8},{1,9},... | collective-permute-start | bytes 24584 | tf_op jit(solution)/shard_map/ppermute | solution.py:35
  60.2 3.9 %collective-permute-start.15 = (f32[8,256]{1,0:T(8,128)}, f32[8,256]{1,0:T(8,128)S(1)}, u32[]{:S(2)}, u32[]{:S(2)}) collective-permute-start(f32[8,256]{1,0:T(8,128)} %get-tuple-element.16.own), channel_id=1, source_target_pairs={{4,0},{5,1},{6,2},{7,3},{8,4},{9,5},{10,6},{11,7},{12,8},{13,9},{1... | collective-permute-start | bytes 24584 | tf_op jit(solution)/shard_map/ppermute | solution.py:35
  64.8 3.7 %copy-start.15 = (f32[8,256]{1,0:T(8,128)}, f32[8,256]{1,0:T(8,128)S(1)}, u32[]{:S(2)}) copy-start(f32[8,256]{1,0:T(8,128)S(1)} %add_add_fusion.s0) | copy-start | bytes 24580
  64.8 3.1 %collective-permute-start.20 = (f32[8,256]{1,0:T(8,128)S(1)}, f32[8,256]{1,0:T(8,128)S(1)}, u32[]{:S(2)}, u32[]{:S(2)}) collective-permute-start(f32[8,256]{1,0:T(8,128)S(1)} %add_add_fusion.s0), channel_id=1, source_target_pairs={{3,0},{2,1},{1,2},{0,3},{7,4},{6,5},{5,6},{4,7},{11,8},{10,9},{9,1... | collective-permute-start | bytes 24584 | tf_op jit(solution)/shard_map/ppermute | solution.py:35
  64.8 3.7 %collective-permute-start.19 = (f32[8,256]{1,0:T(8,128)S(1)}, f32[8,256]{1,0:T(8,128)S(1)}, u32[]{:S(2)}, u32[]{:S(2)}) collective-permute-start(f32[8,256]{1,0:T(8,128)S(1)} %add_add_fusion.s0), channel_id=1, source_target_pairs={{2,0},{3,1},{0,2},{1,3},{6,4},{7,5},{4,6},{5,7},{10,8},{11,9},{8,1... | collective-permute-start | bytes 24584 | tf_op jit(solution)/shard_map/ppermute | solution.py:35
  65.4 3.1 %collective-permute-start.18 = (f32[8,256]{1,0:T(8,128)S(1)}, f32[8,256]{1,0:T(8,128)S(1)}, u32[]{:S(2)}, u32[]{:S(2)}) collective-permute-start(f32[8,256]{1,0:T(8,128)S(1)} %add_add_fusion.s0), channel_id=1, source_target_pairs={{1,0},{0,1},{3,2},{2,3},{5,4},{4,5},{7,6},{6,7},{9,8},{8,9},{11,10... | collective-permute-start | bytes 24584 | tf_op jit(solution)/shard_map/ppermute | solution.py:35
  67.9 0.7 copy-start.16
  68.5 0.6 copy-start.17
  68.5 0.6 copy-start.18

commit v2 on v0

v2 whole, which is shorter than its diff:
```python
import functools

import jax
import jax.numpy as jnp
from jax import lax
from jax.experimental import pallas as pl
from jax.experimental.pallas import tpu as pltpu
from jax.sharding import PartitionSpec as P

TILE = 512
ROWS = 16
SAMPLE = 256
VMEM_BYTES = 18 << 20
RATIO = 0.1 / 0.05**0.5


def f32dot(a, b):
    return jnp.dot(a, b, preferred_element_type=jnp.float32)


def digits(n):
    return (n // 4, 2, 2)


def shift(value, n, slow, mid, core):
    z, y, c = digits(n)
    pairs = []
    for d in range(n):
        dz, dy, dc = d // (y * c), d // c % y, d % c
        source = ((dz + slow) % z * y + (dy + mid) % y) * c + (dc + core) % c
        pairs.append((source, d))
    return lax.ppermute(value, "dp", pairs)


def gather(tokens, n):
    z, y, c = digits(n)
    parts = {(0, 0, 0): tokens}
    for slow in range(1, z):
        parts[slow, 0, 0] = shift(tokens, n, slow, 0, 0)
    for slow in range(z):
        parts[slow, 1, 0] = shift(parts[slow, 0, 0], n, 0, 1, 0)
    for slow in range(z):
        for mid in range(y):
            parts[slow, mid, 1] = shift(parts[slow, mid, 0], n, 0, 0, 1)
    me = lax.axis_index("dp")
    mz, my, mc = me // (y * c), me // c % y, me % c
    places = [((mz + a) % z * y + (my + b) % y) * c + (mc + d) % c for a, b, d in parts]
    return list(parts.values()), jnp.stack(places).astype(jnp.int32)


def all_sum(value, n):
    z, y, c = digits(n)
    total = value
    for slow in range(1, z):
        total = total + shift(value, n, slow, 0, 0)
    return [total] + [shift(total, n, 0, a, b) for a, b in ((0, 1), (1, 0), (1, 1))]


def over_columns(row):
    return jnp.transpose(jnp.broadcast_to(row, (8, row.shape[1])))[:, :1]


def over_lanes(x):
    x = sum(x[:, i : i + 128] for i in range(0, x.shape[1], 128))
    return jnp.sum(jnp.transpose(x), axis=0, keepdims=True)


def fold(x):
    return jnp.sum(x.reshape(x.shape[0] // 8, 8, x.shape[1]), axis=0)


def update(grad, one, two):
    first = 9.0 * one.astype(jnp.float32) + grad
    second = 19.0 * two.astype(jnp.float32) + grad * grad
    over = lax.rsqrt(second)
    inv = pltpu.reciprocal(second * over + 1e-08 / 0.05**0.5, approx=True)
    return over, inv, first * inv


def replay_kernel(n, *refs):
    places, parts = refs[0], refs[1 : n + 1]
    (weight, cot, token_weight, one, two, adjoint) = refs[n + 1 : n + 7]
    (turned, along, across, bend, stats) = refs[n + 7 : n + 12]
    (tokens, scaled, score, g0, g1, a0, a1, b0, b1, sums) = refs[n + 12 :]
    grads, firsts, seconds = (g0, g1), (a0, a1), (b0, b1)
    height, depth = parts[0].shape
    count, width = cot.shape
    tiles = depth // TILE

    for part, ref in enumerate(parts):
        at = pl.multiple_of(places[part] * height, height)
        tokens[pl.ds(at, height), :] = ref[...]

    def span(i):
        return pl.ds(pl.multiple_of(i * TILE, TILE), TILE)

    along[...] = jnp.zeros_like(along)
    across[...] = jnp.zeros_like(across)

    def gate_step(i, _):
        here = tokens[:, span(i)]
        along[...] += f32dot(here, weight[span(i), :])
        turned[span(i), :] = here.T
        return 0

    lax.fori_loop(0, tiles, gate_step, 0)

    gate = along[...]
    weights = over_columns(token_weight[...])
    cot_f = cot[...].astype(jnp.float32)
    sig = 1.0 / (1.0 + jnp.exp(-gate))
    slope = sig * (1.0 + gate * (1.0 - sig))
    curve = sig * (1.0 - sig) * (2.0 + gate * (1.0 - 2.0 * sig))
    scaled[...] = (weights * cot_f * slope).astype(jnp.bfloat16)
    bend[...] = weights * cot_f * curve
    score[...] = cot_f * slope
    along[...] = jnp.zeros_like(along)

    def grad_tile(i, slot):
        grads[slot][...] = f32dot(turned[span(i), :], scaled[...])

    def probe_tile(i, slot):
        here = tokens[:, span(i)]
        along[...] += f32dot(here, firsts[slot][...])
        across[...] += f32dot(here, seconds[slot][...])

    def rows_of(i, slot, r):
        at = pl.ds(pl.multiple_of(i * TILE + r, ROWS), ROWS)
        return grads[slot][r : r + ROWS, :], one[at, :], two[at, :], adjoint[at, :]

    grad_tile(0, 0)
    sq = jnp.zeros((8, width), jnp.float32)
    cross = jnp.zeros((8, width), jnp.float32)
    for r in range(0, SAMPLE, ROWS):
        g, m1, m2, adj = rows_of(0, 0, r)
        _, _, upd = update(g, m1, m2)
        sq += fold(upd * upd)
        cross += fold(adj * upd)
    sq = jnp.sum(sq, keepdims=True)
    clipped = sq * RATIO**2 > float(SAMPLE * width)
    guess = jnp.where(clipped, jnp.sum(cross, keepdims=True) / jnp.maximum(sq, 1.0), 0.0)

    sums[...] = jnp.zeros_like(sums)

    def update_tile(i, slot):
        sq, cross = sums[0], sums[1]
        for r in range(0, TILE, ROWS):
            g, m1, m2, adj = rows_of(i, slot, r)
            over, inv, upd = update(g, m1, m2)
            sq += fold(upd * upd)
            cross += fold(adj * upd)
            pull = inv * (1.0 - g * (upd * over))
            firsts[slot][r : r + ROWS, :] = ((adj - guess * upd) * pull).astype(jnp.bfloat16)
            seconds[slot][r : r + ROWS, :] = (upd * pull).astype(jnp.bfloat16)
        sums[0] = sq
        sums[1] = cross

    grad_tile(1, 1)
    update_tile(0, 0)

    def pair(k, _):
        i = 2 * k + 1
        for j, slot in ((0, 1), (1, 0)):
            grad_tile(i + j + 1, 1 - slot)
            update_tile(i + j, slot)
            probe_tile(i + j - 1, 1 - slot)
        return 0

    lax.fori_loop(0, tiles // 2 - 1, pair, 0)
    update_tile(tiles - 1, 1)
    probe_tile(tiles - 2, 0)
    probe_tile(tiles - 1, 1)

    b = score[...] * across[...]
    a = score[...] * along[...] + guess * b
    whole = lambda x: jnp.broadcast_to(jnp.sum(x, keepdims=True), (1, count))
    stats[0:1, :] = RATIO * over_lanes(a)
    stats[1:2, :] = RATIO**2 * over_lanes(b)
    stats[2:3, :] = RATIO**2 * whole(sums[0])
    stats[3:4, :] = RATIO * whole(sums[1])
    stats[4:8, :] = jnp.broadcast_to(guess, (4, count))


def replay_call(places, parts, weight, cot, token_weight, one, two, adjoint):
    n = len(parts)
    depth = parts[0].shape[1]
    count, width = cot.shape
    vmem = pl.BlockSpec(memory_space=pltpu.VMEM)
    block = lambda dtype: pltpu.VMEM((TILE, width), dtype)
    return pl.pallas_call(
        functools.partial(replay_kernel, n),
        in_specs=[pl.BlockSpec(memory_space=pltpu.SMEM)] + [vmem] * (n + 6),
        out_specs=[vmem] * 5,
        out_shape=[
            pltpu.VMEM((depth, count), jnp.bfloat16),
            pltpu.VMEM((count, width), jnp.float32),
            pltpu.VMEM((count, width), jnp.float32),
            pltpu.VMEM((count, width), jnp.float32),
            pltpu.VMEM((8, count), jnp.float32),
        ],
        scratch_shapes=[
            pltpu.VMEM((count, depth), jnp.bfloat16),
            pltpu.VMEM((count, width), jnp.bfloat16),
            pltpu.VMEM((count, width), jnp.float32),
            block(jnp.float32),
            block(jnp.float32),
            block(jnp.bfloat16),
            block(jnp.bfloat16),
            block(jnp.bfloat16),
            block(jnp.bfloat16),
            pltpu.VMEM((2, 8, width), jnp.float32),
        ],
        compiler_params=pltpu.CompilerParams(vmem_limit_bytes=VMEM_BYTES),
        name="replay",
    )(places, *[resident(x) for x in (*parts, weight, cot, token_weight, one, two, adjoint)])


def resident(x):
    return pltpu.with_memory_space_constraint(x, pltpu.VMEM)


def theta_kernel(entries, s0, s1, s2, s3, own, along, across, bend, turned, adjoint, theta, scores, ready, sent):
    total = s0[...] + s1[...] + (s2[...] + s3[...])
    sq, cross = total[2:3, 0:1], total[3:4, 0:1]
    rms = jnp.sqrt(sq / entries)
    scale = 1.0 / jnp.maximum(1.0, rms)
    bind = jnp.where(rms > 1.0, 1.0 / (rms * rms * rms), 0.0)
    lead = -0.01 * scale
    rest = 0.01 * cross * bind / entries
    scores[...] = lead * total[0:1, :] + rest * total[1:2, :]
    lead_here = RATIO * lead
    rest_here = RATIO**2 * rest + lead_here * own[4:5, 0:1]
    bent = (bend[...] * (lead_here * along[...] + rest_here * across[...])).astype(jnp.bfloat16)

    def copy(i):
        at = pl.ds(i * TILE, TILE)
        return pltpu.make_async_copy(ready.at[at, :], theta.at[at, :], sent.at[i])

    tiles = theta.shape[0] // TILE
    for i in range(tiles):
        at = pl.ds(i * TILE, TILE)
        ready[at, :] = 0.999 * adjoint[at, :] + f32dot(turned[at, :], bent)
        copy(i).start()
    for i in range(tiles):
        copy(i).wait()


def theta_call(entries, sums, own, along, across, bend, turned, adjoint):
    depth, width = adjoint.shape
    count = turned.shape[1]
    vmem = pl.BlockSpec(memory_space=pltpu.VMEM)
    return pl.pallas_call(
        functools.partial(theta_kernel, entries),
        in_specs=[vmem] * 10,
        out_specs=[pl.BlockSpec(memory_space=pl.ANY), vmem],
        out_shape=[
            jax.ShapeDtypeStruct((depth, width), jnp.float32),
            jax.ShapeDtypeStruct((1, count), jnp.float32),
        ],
        scratch_shapes=[pltpu.VMEM((depth, width), jnp.float32), pltpu.SemaphoreType.DMA((depth // TILE,))],
        compiler_params=pltpu.CompilerParams(vmem_limit_bytes=VMEM_BYTES),
        name="theta",
    )(*[resident(x) for x in (*sums, own, along, across, bend, turned, adjoint)])


def shards(n, tokens, cotangent, token_weight, weight, moment_one, moment_two, adjoint):
    entries = float(adjoint.shape[0] * adjoint.shape[1] * n)
    parts, places = gather(tokens, n)
    turned, along, across, bend, stats = replay_call(
        places, parts, weight, cotangent, token_weight.reshape(1, -1), moment_one, moment_two, adjoint
    )
    sums = all_sum(stats, n)
    theta_bar, scores = theta_call(entries, sums, stats, along, across, bend, turned, adjoint)
    height = tokens.shape[0]
    token_scores = lax.dynamic_slice(scores[0], (lax.axis_index("dp") * height,), (height,))
    return (theta_bar, token_scores)


def solution(mesh):
    in_specs = (
        P(("group", "dp"), None),
        P("group", "dp"),
        P("group"),
        P(None, "dp"),
        P(None, "dp"),
        P(None, "dp"),
        P(None, "dp"),
    )
    out_specs = (P("group", "dp"), P(("group", "dp")))
    body = functools.partial(shards, mesh.shape["dp"])
    return jax.shard_map(body, mesh=mesh, in_specs=in_specs, out_specs=out_specs, check_vma=False)
```

time: 177 us -> 89.3 us (0.50)
  blocking collectives: 61.7 us -> 0 us
  matrix products: 42.2 us -> 0 us
  starting transfers between devices: 0.04 us -> 19.4 us
  Pallas kernels: 0 us -> 17.4 us
  between operations: 16.1 us -> 0.73 us
  waiting for transfers between devices: 24 us -> 15.4 us
  local copies, waits for them, and re-layouts: 31.9 us -> 35.8 us
    dot_general x4 -> x0, matrix products: 42.2 us -> none  [the longest x2 23.3 us: contract_rows(): lax.dot_general(rows, other, (((0,), (0,)), ((), ())), preferred_element_...]
    psum x1 -> x0, blocking collectives: 32.2 us -> none  [adjoint_step(): sq, cross = lax.psum((jnp.sum(upd * upd), jnp.sum(adjoint * upd)), 'dp')]
    unnamed x1 -> x0, blocking collectives: 29.5 us -> none
    all_gather x1 -> x0, waiting for transfers between devices: 23.3 us -> none  [shards(): kept_rows = lax.all_gather(tokens, 'dp', axis=0, tiled=True)]
    ppermute x0 -> x21, starting transfers between devices: none -> 19.4 us  [shift(): return lax.ppermute(value, 'dp', pairs)]
    pallas_call x0 -> x2, Pallas kernels: none -> 17.4 us  [the longest x1 13.6 us: replay_call(): pl.pallas_call(functools.partial(replay_kernel, n), in_specs=[pl.BlockSpe...]
    ppermute x0 -> x21, waiting for transfers between devices: none -> 15.4 us  [shift(): return lax.ppermute(value, 'dp', pairs)]
    unnamed x14 -> x68, local copies, waits for them, and re-layouts: 31.9 us -> 35.1 us
  transfers between devices with their start and end apart: 1 -> 21, of which waited for: 1 -> 9; matrix products, arithmetic and copies ran while one was open for 13% -> 0% of each run, Pallas kernels for 0% -> 0%
where the time goes in v2:
time: 89.3 us; the launch traced here: 88.7 us
  local copies, waits for them, and re-layouts  35.8 us (40%)
  starting transfers between devices  19.4 us (22%)
  Pallas kernels  17.4 us (19%)
  waiting for transfers between devices  15.4 us (17%)
    unnamed x68, local copies, waits for them, and re-layouts  35.1 us
    ppermute x21, starting transfers between devices, shift(): return lax.ppermute(value, 'dp', pairs)  19.4 us
    ppermute x21, waiting for transfers between devices, shift(): return lax.ppermute(value, 'dp', pairs)  15.4 us
    pallas_call x1, Pallas kernels, replay_call(): pl.pallas_call(functools.partial(replay_kernel, n), in_specs=[pl.BlockSpe...  13.6 us
    pallas_call x1, Pallas kernels, theta_call(): pl.pallas_call(functools.partial(theta_kernel, entries), in_specs=[vmem]...  3.78 us
  transfers between devices with their start and end apart: 21, of which 9 were waited for; matrix products, arithmetic and copies ran while one was open for 0% of the time, Pallas kernels for 0%

profile of v2, /device:TPU:0, one launch (start us, length us, event | category | flops | bytes accessed | tf_op | source)
XLA Modules:
  0.0 88.7 jit_solution(15052451241490964303)
XLA Ops:
  0.6 3.0 %collective-permute-start.3 = (bf16[16,4096]{1,0:T(8,128)(2,1)}, bf16[16,4096]{1,0:T(8,128)(2,1)S(1)}, u32[]{:S(2)}, u32[]{:S(2)}) collective-permute-start(bf16[16,4096]{1,0:T(8,128)(2,1)} %refs_1_.1), channel_id=1, source_target_pairs={{2,0},{3,1},{0,2},{1,3},{6,4},{7,5},{4,6},{5,7},{10,8},{11,9},{8,1... | collective-permute-start | bytes 393224 | tf_op jit(solution)/shard_map/ppermute | solution.py:32
  3.7 1.6 %collective-permute-start.2 = (bf16[16,4096]{1,0:T(8,128)(2,1)}, bf16[16,4096]{1,0:T(8,128)(2,1)S(1)}, u32[]{:S(2)}, u32[]{:S(2)}) collective-permute-start(bf16[16,4096]{1,0:T(8,128)(2,1)} %refs_1_.1), channel_id=1, source_target_pairs={{12,0},{13,1},{14,2},{15,3},{0,4},{1,5},{2,6},{3,7},{4,8},{5,9},{6... | collective-permute-start | bytes 393224 | tf_op jit(solution)/shard_map/ppermute | solution.py:32
  5.2 2.6 %collective-permute-start.1 = (bf16[16,4096]{1,0:T(8,128)(2,1)}, bf16[16,4096]{1,0:T(8,128)(2,1)S(1)}, u32[]{:S(2)}, u32[]{:S(2)}) collective-permute-start(bf16[16,4096]{1,0:T(8,128)(2,1)} %refs_1_.1), channel_id=1, source_target_pairs={{8,0},{9,1},{10,2},{11,3},{12,4},{13,5},{14,6},{15,7},{0,8},{1,9},... | collective-permute-start | bytes 393224 | tf_op jit(solution)/shard_map/ppermute | solution.py:32
  7.8 1.3 %collective-permute-start = (bf16[16,4096]{1,0:T(8,128)(2,1)}, bf16[16,4096]{1,0:T(8,128)(2,1)S(1)}, u32[]{:S(2)}, u32[]{:S(2)}) collective-permute-start(bf16[16,4096]{1,0:T(8,128)(2,1)} %refs_1_.1), channel_id=1, source_target_pairs={{4,0},{5,1},{6,2},{7,3},{8,4},{9,5},{10,6},{11,7},{12,8},{13,9},{1... | collective-permute-start | bytes 393224 | tf_op jit(solution)/shard_map/ppermute | solution.py:32
  9.7 2.5 %collective-permute-done.2.refs_4_ = bf16[16,4096]{1,0:T(8,128)(2,1)S(1)} collective-permute-done((bf16[16,4096]{1,0:T(8,128)(2,1)}, bf16[16,4096]{1,0:T(8,128)(2,1)S(1)}, u32[]{:S(2)}, u32[]{:S(2)}) %collective-permute-start.2) | collective-permute-done | bytes 131104 | tf_op jit(solution)/shard_map/ppermute | solution.py:32
  12.2 4.3 %collective-permute-done.1.refs_3_ = bf16[16,4096]{1,0:T(8,128)(2,1)S(1)} collective-permute-done((bf16[16,4096]{1,0:T(8,128)(2,1)}, bf16[16,4096]{1,0:T(8,128)(2,1)S(1)}, u32[]{:S(2)}, u32[]{:S(2)}) %collective-permute-start.1) | collective-permute-done | bytes 131104 | tf_op jit(solution)/shard_map/ppermute | solution.py:32
  16.9 1.6 %collective-permute-start.5 = (bf16[16,4096]{1,0:T(8,128)(2,1)S(1)}, bf16[16,4096]{1,0:T(8,128)(2,1)S(1)}, u32[]{:S(2)}, u32[]{:S(2)}) collective-permute-start(bf16[16,4096]{1,0:T(8,128)(2,1)S(1)} %collective-permute-done.1.refs_3_), channel_id=1, source_target_pairs={{2,0},{3,1},{0,2},{1,3},{6,4},{7,5},{4,6},{5,7},{10,8},{11,9},{8,1... | collective-permute-start | bytes 393224 | tf_op jit(solution)/shard_map/ppermute | solution.py:32
  19.0 0.7 copy-done.13
  20.8 2.0 %collective-permute-done.6.refs_8_ = bf16[16,4096]{1,0:T(8,128)(2,1)S(1)} collective-permute-done((bf16[16,4096]{1,0:T(8,128)(2,1)S(1)}, bf16[16,4096]{1,0:T(8,128)(2,1)S(1)}, u32[]{:S(2)}, u32[]{:S(2)}) %collective-permute-start.6) | collective-permute-done | bytes 131104 | tf_op jit(solution)/shard_map/ppermute | solution.py:32
  22.8 0.7 copy-done.17
  23.5 2.1 %collective-permute-done.5.refs_7_ = bf16[16,4096]{1,0:T(8,128)(2,1)S(1)} collective-permute-done((bf16[16,4096]{1,0:T(8,128)(2,1)S(1)}, bf16[16,4096]{1,0:T(8,128)(2,1)S(1)}, u32[]{:S(2)}, u32[]{:S(2)}) %collective-permute-start.5) | collective-permute-done | bytes 131104 | tf_op jit(solution)/shard_map/ppermute | solution.py:32
  25.6 0.7 copy-done.19
  26.3 1.1 %collective-permute-done.4.refs_6_ = bf16[16,4096]{1,0:T(8,128)(2,1)S(1)} collective-permute-done((bf16[16,4096]{1,0:T(8,128)(2,1)S(1)}, bf16[16,4096]{1,0:T(8,128)(2,1)S(1)}, u32[]{:S(2)}, u32[]{:S(2)}) %collective-permute-start.4) | collective-permute-done | bytes 131104 | tf_op jit(solution)/shard_map/ppermute | solution.py:32
  27.4 0.7 copy-done.21
  28.8 0.7 copy-done.25
  29.5 0.7 copy-done.27
  30.1 0.7 copy-done.29
  31.5 3.4 %copy-done = f32[4096,512]{1,0:T(8,128)S(1)} copy-done((f32[4096,512]{1,0:T(8,128)S(1)}, f32[4096,512]{1,0:T(8,128)}, u32[]{:S(2)}) %copy-start) | copy-done | bytes 8388632
  34.9 2.2 %copy-done.2 = bf16[4096,512]{1,0:T(8,128)(2,1)S(1)} copy-done((bf16[4096,512]{1,0:T(8,128)(2,1)S(1)}, bf16[4096,512]{1,0:T(8,128)(2,1)}, u32[]{:S(2)}) %copy-start.2) | copy-done | bytes 4194328
  37.0 2.2 %copy-done.3 = bf16[4096,512]{1,0:T(8,128)(2,1)S(1)} copy-done((bf16[4096,512]{1,0:T(8,128)(2,1)S(1)}, bf16[4096,512]{1,0:T(8,128)(2,1)}, u32[]{:S(2)}) %copy-start.3) | copy-done | bytes 4194328
  39.2 2.2 %copy-done.4 = bf16[4096,512]{1,0:T(8,128)(2,1)S(1)} copy-done((bf16[4096,512]{1,0:T(8,128)(2,1)S(1)}, bf16[4096,512]{1,0:T(8,128)(2,1)}, u32[]{:S(2)}) %copy-start.4) | copy-done | bytes 4194328
  41.4 0.9 %copy-done.7 = bf16[256,512]{1,0:T(8,128)(2,1)S(1)} copy-done((bf16[256,512]{1,0:T(8,128)(2,1)S(1)}, bf16[256,512]{1,0:T(8,128)(2,1)}, u32[]{:S(2)}) %copy-start.7) | copy-done | bytes 262168
  42.4 0.9 %copy-done.8 = bf16[16,4096]{1,0:T(8,128)(2,1)S(1)} copy-done((bf16[16,4096]{1,0:T(8,128)(2,1)S(1)}, bf16[16,4096]{1,0:T(8,128)(2,1)}, u32[]{:S(2)}) %copy-start.8) | copy-done | bytes 131096
  43.3 0.9 %copy-done.10 = bf16[16,4096]{1,0:T(8,128)(2,1)S(1)} copy-done((bf16[16,4096]{1,0:T(8,128)(2,1)S(1)}, bf16[16,4096]{1,0:T(8,128)(2,1)}, u32[]{:S(2)}) %copy-start.10) | copy-done | bytes 131096
  44.2 0.9 %copy-done.12 = bf16[16,4096]{1,0:T(8,128)(2,1)S(1)} copy-done((bf16[16,4096]{1,0:T(8,128)(2,1)S(1)}, bf16[16,4096]{1,0:T(8,128)(2,1)}, u32[]{:S(2)}) %copy-start.12) | copy-done | bytes 131096
  45.1 0.9 %copy-done.14 = bf16[16,4096]{1,0:T(8,128)(2,1)S(1)} copy-done((bf16[16,4096]{1,0:T(8,128)(2,1)S(1)}, bf16[16,4096]{1,0:T(8,128)(2,1)}, u32[]{:S(2)}) %copy-start.14) | copy-done | bytes 131096
  46.0 0.9 %copy-done.16 = bf16[16,4096]{1,0:T(8,128)(2,1)S(1)} copy-done((bf16[16,4096]{1,0:T(8,128)(2,1)S(1)}, bf16[16,4096]{1,0:T(8,128)(2,1)}, u32[]{:S(2)}) %copy-start.16) | copy-done | bytes 131096
  46.9 0.9 %copy-done.18 = bf16[16,4096]{1,0:T(8,128)(2,1)S(1)} copy-done((bf16[16,4096]{1,0:T(8,128)(2,1)S(1)}, bf16[16,4096]{1,0:T(8,128)(2,1)}, u32[]{:S(2)}) %copy-start.18) | copy-done | bytes 131096
  47.8 0.9 %copy-done.20 = bf16[16,4096]{1,0:T(8,128)(2,1)S(1)} copy-done((bf16[16,4096]{1,0:T(8,128)(2,1)S(1)}, bf16[16,4096]{1,0:T(8,128)(2,1)}, u32[]{:S(2)}) %copy-start.20) | copy-done | bytes 131096
  48.7 0.9 %copy-done.22 = bf16[16,4096]{1,0:T(8,128)(2,1)S(1)} copy-done((bf16[16,4096]{1,0:T(8,128)(2,1)S(1)}, bf16[16,4096]{1,0:T(8,128)(2,1)}, u32[]{:S(2)}) %copy-start.22) | copy-done | bytes 131096
  49.6 0.9 %copy-done.24 = bf16[16,4096]{1,0:T(8,128)(2,1)S(1)} copy-done((bf16[16,4096]{1,0:T(8,128)(2,1)S(1)}, bf16[16,4096]{1,0:T(8,128)(2,1)}, u32[]{:S(2)}) %copy-start.24) | copy-done | bytes 131096
  50.5 0.9 %copy-done.26 = bf16[16,4096]{1,0:T(8,128)(2,1)S(1)} copy-done((bf16[16,4096]{1,0:T(8,128)(2,1)S(1)}, bf16[16,4096]{1,0:T(8,128)(2,1)}, u32[]{:S(2)}) %copy-start.26) | copy-done | bytes 131096
  51.4 0.9 %copy-done.28 = bf16[16,4096]{1,0:T(8,128)(2,1)S(1)} copy-done((bf16[16,4096]{1,0:T(8,128)(2,1)S(1)}, bf16[16,4096]{1,0:T(8,128)(2,1)}, u32[]{:S(2)}) %copy-start.28) | copy-done | bytes 131096
  52.3 0.9 %copy-done.30 = bf16[16,4096]{1,0:T(8,128)(2,1)S(1)} copy-done((bf16[16,4096]{1,0:T(8,128)(2,1)S(1)}, bf16[16,4096]{1,0:T(8,128)(2,1)}, u32[]{:S(2)}) %copy-start.30) | copy-done | bytes 131096
  53.2 0.9 %copy-done.32 = bf16[16,4096]{1,0:T(8,128)(2,1)S(1)} copy-done((bf16[16,4096]{1,0:T(8,128)(2,1)S(1)}, bf16[16,4096]{1,0:T(8,128)(2,1)}, u32[]{:S(2)}) %copy-start.32) | copy-done | bytes 131096
  54.1 0.7 copy-done.33
  54.8 13.6 %replay.1 = (bf16[4096,256]{1,0:T(8,128)(2,1)S(1)}, f32[256,512]{1,0:T(8,128)S(1)}, f32[256,512]{1,0:T(8,128)S(1)}, f32[256,512]{1,0:T(8,128)S(1)}, f32[8,256]{1,0:T(8,128)S(1)}) custom-call(s32[16]{0:T(128)S(1)} %stack.67.refs_0_, bf16[16,4096]{1,0:T(8,128)(2,1)S(1)} %copy-done.8, bf16[16,4096]{1,0:T(8,128)(2,1)S(1)} %copy-done.10, ...), custom_call_target="tpu_custom_call" | custom-call | tf_op jit(solution)/shard_map/replay/pallas_call | solution.py:190
  68.4 0.8 copy-done.5
  69.2 1.2 %collective-permute-start.17 = (f32[8,256]{1,0:T(8,128)S(1)}, f32[8,256]{1,0:T(8,128)S(1)}, u32[]{:S(2)}, u32[]{:S(2)}) collective-permute-start(f32[8,256]{1,0:T(8,128)S(1)} %get-tuple-element.9.own), channel_id=1, source_target_pairs={{12,0},{13,1},{14,2},{15,3},{0,4},{1,5},{2,6},{3,7},{4,8},{5,9},{6... | collective-permute-start | bytes 24584 | tf_op jit(solution)/shard_map/ppermute | solution.py:32
  70.4 2.1 %collective-permute-start.16 = (f32[8,256]{1,0:T(8,128)S(1)}, f32[8,256]{1,0:T(8,128)S(1)}, u32[]{:S(2)}, u32[]{:S(2)}) collective-permute-start(f32[8,256]{1,0:T(8,128)S(1)} %get-tuple-element.9.own), channel_id=1, source_target_pairs={{8,0},{9,1},{10,2},{11,3},{12,4},{13,5},{14,6},{15,7},{0,8},{1,9},... | collective-permute-start | bytes 24584 | tf_op jit(solution)/shard_map/ppermute | solution.py:32
  72.5 2.2 %collective-permute-start.15 = (f32[8,256]{1,0:T(8,128)S(1)}, f32[8,256]{1,0:T(8,128)S(1)}, u32[]{:S(2)}, u32[]{:S(2)}) collective-permute-start(f32[8,256]{1,0:T(8,128)S(1)} %get-tuple-element.9.own), channel_id=1, source_target_pairs={{4,0},{5,1},{6,2},{7,3},{8,4},{9,5},{10,6},{11,7},{12,8},{13,9},{1... | collective-permute-start | bytes 24584 | tf_op jit(solution)/shard_map/ppermute | solution.py:32
  75.0 1.2 %collective-permute-done.15 = f32[8,256]{1,0:T(8,128)S(1)} collective-permute-done((f32[8,256]{1,0:T(8,128)S(1)}, f32[8,256]{1,0:T(8,128)S(1)}, u32[]{:S(2)}, u32[]{:S(2)}) %collective-permute-start.15) | collective-permute-done | bytes 8224 | tf_op jit(solution)/shard_map/ppermute | solution.py:32
  76.2 0.7 collective-permute-start.19
  76.8 1.2 %collective-permute-start.18 = (f32[8,256]{1,0:T(8,128)S(1)}, f32[8,256]{1,0:T(8,128)S(1)}, u32[]{:S(2)}, u32[]{:S(2)}) collective-permute-start(f32[8,256]{1,0:T(8,128)S(1)} %add_add_fusion.s0), channel_id=1, source_target_pairs={{1,0},{0,1},{3,2},{2,3},{5,4},{4,5},{7,6},{6,7},{9,8},{8,9},{11,10... | collective-permute-start | bytes 24584 | tf_op jit(solution)/shard_map/ppermute | solution.py:32
  78.0 1.2 %collective-permute-done.20.s3 = f32[8,256]{1,0:T(8,128)S(1)} collective-permute-done((f32[8,256]{1,0:T(8,128)S(1)}, f32[8,256]{1,0:T(8,128)S(1)}, u32[]{:S(2)}, u32[]{:S(2)}) %collective-permute-start.20) | collective-permute-done | bytes 8224 | tf_op jit(solution)/shard_map/ppermute | solution.py:32
  79.9 3.4 %copy-done.1 = f32[4096,512]{1,0:T(8,128)S(1)} copy-done((f32[4096,512]{1,0:T(8,128)S(1)}, f32[4096,512]{1,0:T(8,128)}, u32[]{:S(2)}) %copy-start.1) | copy-done | bytes 8388632
  83.3 1.0 %copy-done.6 = f32[256,512]{1,0:T(8,128)S(1)} copy-done((f32[256,512]{1,0:T(8,128)S(1)}, f32[256,512]{1,0:T(8,128)}, u32[]{:S(2)}) %copy-start.6) | copy-done | bytes 524312
  84.3 3.8 %theta.1 = (f32[4096,512]{1,0:T(8,128)}, f32[1,256]{1,0:T(1,128)S(1)}) custom-call(f32[8,256]{1,0:T(8,128)S(1)} %add_add_fusion.s0, f32[8,256]{1,0:T(8,128)S(1)} %collective-permute-done.18.s1, f32[8,256]{1,0:T(8,128)S(1)} %collective-permute-done.19.s2, f32[8,256]{1,0:T(8,128)S(1)} %collective-permute-done.20.s3, f32[8,256]{1,0:T(8,128)S(1)} %get-tuple-element.9.own, ...), custom_call_target="tpu_custom_call" | custom-call | tf_op jit(solution)/shard_map/theta/pallas_call | solution.py:252
  (67 shorter events, 5.6 us)
Async XLA Ops:
  0.6 8.6 %collective-permute-start.3 = (bf16[16,4096]{1,0:T(8,128)(2,1)}, bf16[16,4096]{1,0:T(8,128)(2,1)S(1)}, u32[]{:S(2)}, u32[]{:S(2)}) collective-permute-start(bf16[16,4096]{1,0:T(8,128)(2,1)} %refs_1_.1), channel_id=1, source_target_pairs={{2,0},{3,1},{0,2},{1,3},{6,4},{7,5},{4,6},{5,7},{10,8},{11,9},{8,1... | collective-permute-start | bytes 393224 | tf_op jit(solution)/shard_map/ppermute | solution.py:32
  3.7 8.5 %collective-permute-start.2 = (bf16[16,4096]{1,0:T(8,128)(2,1)}, bf16[16,4096]{1,0:T(8,128)(2,1)S(1)}, u32[]{:S(2)}, u32[]{:S(2)}) collective-permute-start(bf16[16,4096]{1,0:T(8,128)(2,1)} %refs_1_.1), channel_id=1, source_target_pairs={{12,0},{13,1},{14,2},{15,3},{0,4},{1,5},{2,6},{3,7},{4,8},{5,9},{6... | collective-permute-start | bytes 393224 | tf_op jit(solution)/shard_map/ppermute | solution.py:32
  5.2 11.2 %collective-permute-start.1 = (bf16[16,4096]{1,0:T(8,128)(2,1)}, bf16[16,4096]{1,0:T(8,128)(2,1)S(1)}, u32[]{:S(2)}, u32[]{:S(2)}) collective-permute-start(bf16[16,4096]{1,0:T(8,128)(2,1)} %refs_1_.1), channel_id=1, source_target_pairs={{8,0},{9,1},{10,2},{11,3},{12,4},{13,5},{14,6},{15,7},{0,8},{1,9},... | collective-permute-start | bytes 393224 | tf_op jit(solution)/shard_map/ppermute | solution.py:32
  7.8 9.1 %collective-permute-start = (bf16[16,4096]{1,0:T(8,128)(2,1)}, bf16[16,4096]{1,0:T(8,128)(2,1)S(1)}, u32[]{:S(2)}, u32[]{:S(2)}) collective-permute-start(bf16[16,4096]{1,0:T(8,128)(2,1)} %refs_1_.1), channel_id=1, source_target_pairs={{4,0},{5,1},{6,2},{7,3},{8,4},{9,5},{10,6},{11,7},{12,8},{13,9},{1... | collective-permute-start | bytes 393224 | tf_op jit(solution)/shard_map/ppermute | solution.py:32
  9.2 9.3 %collective-permute-start.7 = (bf16[16,4096]{1,0:T(8,128)(2,1)}, bf16[16,4096]{1,0:T(8,128)(2,1)S(1)}, u32[]{:S(2)}, u32[]{:S(2)}) collective-permute-start(bf16[16,4096]{1,0:T(8,128)(2,1)} %refs_1_.1), channel_id=1, source_target_pairs={{1,0},{0,1},{3,2},{2,3},{5,4},{4,5},{7,6},{6,7},{9,8},{8,9},{11,10... | collective-permute-start | bytes 393224 | tf_op jit(solution)/shard_map/ppermute | solution.py:32
  9.2 9.8 %collective-permute-start.8 = (bf16[16,4096]{1,0:T(8,128)(2,1)S(1)}, bf16[16,4096]{1,0:T(8,128)(2,1)S(1)}, u32[]{:S(2)}, u32[]{:S(2)}) collective-permute-start(bf16[16,4096]{1,0:T(8,128)(2,1)S(1)} %collective-permute-done.3.refs_5_), channel_id=1, source_target_pairs={{1,0},{0,1},{3,2},{2,3},{5,4},{4,5},{7,6},{6,7},{9,8},{8,9},{11,10... | collective-permute-start | bytes 393224 | tf_op jit(solution)/shard_map/ppermute | solution.py:32
  12.2 7.5 %collective-permute-start.13 = (bf16[16,4096]{1,0:T(8,128)(2,1)S(1)}, bf16[16,4096]{1,0:T(8,128)(2,1)S(1)}, u32[]{:S(2)}, u32[]{:S(2)}) collective-permute-start(bf16[16,4096]{1,0:T(8,128)(2,1)S(1)} %collective-permute-done.2.refs_4_), channel_id=1, source_target_pairs={{1,0},{0,1},{3,2},{2,3},{5,4},{4,5},{7,6},{6,7},{9,8},{8,9},{11,10... | collective-permute-start | bytes 393224 | tf_op jit(solution)/shard_map/ppermute | solution.py:32
  16.5 6.4 %collective-permute-start.6 = (bf16[16,4096]{1,0:T(8,128)(2,1)S(1)}, bf16[16,4096]{1,0:T(8,128)(2,1)S(1)}, u32[]{:S(2)}, u32[]{:S(2)}) collective-permute-start(bf16[16,4096]{1,0:T(8,128)(2,1)S(1)} %collective-permute-done.2.refs_4_), channel_id=1, source_target_pairs={{2,0},{3,1},{0,2},{1,3},{6,4},{7,5},{4,6},{5,7},{10,8},{11,9},{8,1... | collective-permute-start | bytes 393224 | tf_op jit(solution)/shard_map/ppermute | solution.py:32
  16.9 13.9 %copy-start.9 = (bf16[16,4096]{1,0:T(8,128)(2,1)}, bf16[16,4096]{1,0:T(8,128)(2,1)S(1)}, u32[]{:S(2)}) copy-start(bf16[16,4096]{1,0:T(8,128)(2,1)S(1)} %collective-permute-done.refs_2_) | copy-start | bytes 393220
  16.9 8.7 %collective-permute-start.5 = (bf16[16,4096]{1,0:T(8,128)(2,1)S(1)}, bf16[16,4096]{1,0:T(8,128)(2,1)S(1)}, u32[]{:S(2)}, u32[]{:S(2)}) collective-permute-start(bf16[16,4096]{1,0:T(8,128)(2,1)S(1)} %collective-permute-done.1.refs_3_), channel_id=1, source_target_pairs={{2,0},{3,1},{0,2},{1,3},{6,4},{7,5},{4,6},{5,7},{10,8},{11,9},{8,1... | collective-permute-start | bytes 393224 | tf_op jit(solution)/shard_map/ppermute | solution.py:32
  18.5 12.3 %copy-start.11 = (bf16[16,4096]{1,0:T(8,128)(2,1)}, bf16[16,4096]{1,0:T(8,128)(2,1)S(1)}, u32[]{:S(2)}) copy-start(bf16[16,4096]{1,0:T(8,128)(2,1)S(1)} %collective-permute-done.7.refs_9_) | copy-start | bytes 393220
  18.5 8.9 %collective-permute-start.4 = (bf16[16,4096]{1,0:T(8,128)(2,1)S(1)}, bf16[16,4096]{1,0:T(8,128)(2,1)S(1)}, u32[]{:S(2)}, u32[]{:S(2)}) collective-permute-start(bf16[16,4096]{1,0:T(8,128)(2,1)S(1)} %collective-permute-done.refs_2_), channel_id=1, source_target_pairs={{2,0},{3,1},{0,2},{1,3},{6,4},{7,5},{4,6},{5,7},{10,8},{11,9},{8,1... | collective-permute-start | bytes 393224 | tf_op jit(solution)/shard_map/ppermute | solution.py:32
  19.0 0.7 copy-start.13
  19.6 8.5 %collective-permute-start.11 = (bf16[16,4096]{1,0:T(8,128)(2,1)S(1)}, bf16[16,4096]{1,0:T(8,128)(2,1)S(1)}, u32[]{:S(2)}, u32[]{:S(2)}) collective-permute-start(bf16[16,4096]{1,0:T(8,128)(2,1)S(1)} %collective-permute-done.1.refs_3_), channel_id=1, source_target_pairs={{1,0},{0,1},{3,2},{2,3},{5,4},{4,5},{7,6},{6,7},{9,8},{8,9},{11,10... | collective-permute-start | bytes 393224 | tf_op jit(solution)/shard_map/ppermute | solution.py:32
  20.3 8.5 %collective-permute-start.9 = (bf16[16,4096]{1,0:T(8,128)(2,1)S(1)}, bf16[16,4096]{1,0:T(8,128)(2,1)S(1)}, u32[]{:S(2)}, u32[]{:S(2)}) collective-permute-start(bf16[16,4096]{1,0:T(8,128)(2,1)S(1)} %collective-permute-done.refs_2_), channel_id=1, source_target_pairs={{1,0},{0,1},{3,2},{2,3},{5,4},{4,5},{7,6},{6,7},{9,8},{8,9},{11,10... | collective-permute-start | bytes 393224 | tf_op jit(solution)/shard_map/ppermute | solution.py:32
  22.8 6.7 %collective-permute-start.14 = (bf16[16,4096]{1,0:T(8,128)(2,1)S(1)}, bf16[16,4096]{1,0:T(8,128)(2,1)S(1)}, u32[]{:S(2)}, u32[]{:S(2)}) collective-permute-start(bf16[16,4096]{1,0:T(8,128)(2,1)S(1)} %collective-permute-done.6.refs_8_), channel_id=1, source_target_pairs={{1,0},{0,1},{3,2},{2,3},{5,4},{4,5},{7,6},{6,7},{9,8},{8,9},{11,10... | collective-permute-start | bytes 393224 | tf_op jit(solution)/shard_map/ppermute | solution.py:32
  22.8 0.7 copy-start.17
  25.6 4.5 %collective-permute-start.12 = (bf16[16,4096]{1,0:T(8,128)(2,1)S(1)}, bf16[16,4096]{1,0:T(8,128)(2,1)S(1)}, u32[]{:S(2)}, u32[]{:S(2)}) collective-permute-start(bf16[16,4096]{1,0:T(8,128)(2,1)S(1)} %collective-permute-done.5.refs_7_), channel_id=1, source_target_pairs={{1,0},{0,1},{3,2},{2,3},{5,4},{4,5},{7,6},{6,7},{9,8},{8,9},{11,10... | collective-permute-start | bytes 393224 | tf_op jit(solution)/shard_map/ppermute | solution.py:32
  27.4 3.4 %collective-permute-start.10 = (bf16[16,4096]{1,0:T(8,128)(2,1)S(1)}, bf16[16,4096]{1,0:T(8,128)(2,1)S(1)}, u32[]{:S(2)}, u32[]{:S(2)}) collective-permute-start(bf16[16,4096]{1,0:T(8,128)(2,1)S(1)} %collective-permute-done.4.refs_6_), channel_id=1, source_target_pairs={{1,0},{0,1},{3,2},{2,3},{5,4},{4,5},{7,6},{6,7},{9,8},{8,9},{11,10... | collective-permute-start | bytes 393224 | tf_op jit(solution)/shard_map/ppermute | solution.py:32
  30.1 0.7 copy-start.29
  31.5 3.4 %copy-start = (f32[4096,512]{1,0:T(8,128)S(1)}, f32[4096,512]{1,0:T(8,128)}, u32[]{:S(2)}) copy-start(f32[4096,512]{1,0:T(8,128)} %adjoint.1) | copy-start | bytes 25165828
  34.9 2.2 %copy-start.2 = (bf16[4096,512]{1,0:T(8,128)(2,1)S(1)}, bf16[4096,512]{1,0:T(8,128)(2,1)}, u32[]{:S(2)}) copy-start(bf16[4096,512]{1,0:T(8,128)(2,1)} %refs_17_.1) | copy-start | bytes 12582916
  37.0 2.2 %copy-start.3 = (bf16[4096,512]{1,0:T(8,128)(2,1)S(1)}, bf16[4096,512]{1,0:T(8,128)(2,1)}, u32[]{:S(2)}) copy-start(bf16[4096,512]{1,0:T(8,128)(2,1)} %refs_20_.1) | copy-start | bytes 12582916
  39.2 2.2 %copy-start.4 = (bf16[4096,512]{1,0:T(8,128)(2,1)S(1)}, bf16[4096,512]{1,0:T(8,128)(2,1)}, u32[]{:S(2)}) copy-start(bf16[4096,512]{1,0:T(8,128)(2,1)} %refs_21_.1) | copy-start | bytes 12582916
  41.4 0.9 %copy-start.7 = (bf16[256,512]{1,0:T(8,128)(2,1)S(1)}, bf16[256,512]{1,0:T(8,128)(2,1)}, u32[]{:S(2)}) copy-start(bf16[256,512]{1,0:T(8,128)(2,1)} %refs_18_.1) | copy-start | bytes 786436
  42.4 0.9 %copy-start.8 = (bf16[16,4096]{1,0:T(8,128)(2,1)S(1)}, bf16[16,4096]{1,0:T(8,128)(2,1)}, u32[]{:S(2)}) copy-start(bf16[16,4096]{1,0:T(8,128)(2,1)} %refs_1_.1) | copy-start | bytes 393220
  43.3 0.9 %copy-start.10 = (bf16[16,4096]{1,0:T(8,128)(2,1)S(1)}, bf16[16,4096]{1,0:T(8,128)(2,1)}, u32[]{:S(2)}) copy-start(bf16[16,4096]{1,0:T(8,128)(2,1)} %copy-done.9) | copy-start | bytes 393220
  44.2 0.9 %copy-start.12 = (bf16[16,4096]{1,0:T(8,128)(2,1)S(1)}, bf16[16,4096]{1,0:T(8,128)(2,1)}, u32[]{:S(2)}) copy-start(bf16[16,4096]{1,0:T(8,128)(2,1)} %copy-done.11) | copy-start | bytes 393220
  45.1 0.9 %copy-start.14 = (bf16[16,4096]{1,0:T(8,128)(2,1)S(1)}, bf16[16,4096]{1,0:T(8,128)(2,1)}, u32[]{:S(2)}) copy-start(bf16[16,4096]{1,0:T(8,128)(2,1)} %copy-done.13) | copy-start | bytes 393220
  46.0 0.9 %copy-start.16 = (bf16[16,4096]{1,0:T(8,128)(2,1)S(1)}, bf16[16,4096]{1,0:T(8,128)(2,1)}, u32[]{:S(2)}) copy-start(bf16[16,4096]{1,0:T(8,128)(2,1)} %copy-done.15) | copy-start | bytes 393220
  46.9 0.9 %copy-start.18 = (bf16[16,4096]{1,0:T(8,128)(2,1)S(1)}, bf16[16,4096]{1,0:T(8,128)(2,1)}, u32[]{:S(2)}) copy-start(bf16[16,4096]{1,0:T(8,128)(2,1)} %copy-done.17) | copy-start | bytes 393220
  47.8 0.9 %copy-start.20 = (bf16[16,4096]{1,0:T(8,128)(2,1)S(1)}, bf16[16,4096]{1,0:T(8,128)(2,1)}, u32[]{:S(2)}) copy-start(bf16[16,4096]{1,0:T(8,128)(2,1)} %copy-done.19) | copy-start | bytes 393220
  48.7 0.9 %copy-start.22 = (bf16[16,4096]{1,0:T(8,128)(2,1)S(1)}, bf16[16,4096]{1,0:T(8,128)(2,1)}, u32[]{:S(2)}) copy-start(bf16[16,4096]{1,0:T(8,128)(2,1)} %copy-done.21) | copy-start | bytes 393220
  49.6 0.9 %copy-start.24 = (bf16[16,4096]{1,0:T(8,128)(2,1)S(1)}, bf16[16,4096]{1,0:T(8,128)(2,1)}, u32[]{:S(2)}) copy-start(bf16[16,4096]{1,0:T(8,128)(2,1)} %copy-done.23) | copy-start | bytes 393220
  50.5 0.9 %copy-start.26 = (bf16[16,4096]{1,0:T(8,128)(2,1)S(1)}, bf16[16,4096]{1,0:T(8,128)(2,1)}, u32[]{:S(2)}) copy-start(bf16[16,4096]{1,0:T(8,128)(2,1)} %copy-done.25) | copy-start | bytes 393220
  51.4 0.9 %copy-start.28 = (bf16[16,4096]{1,0:T(8,128)(2,1)S(1)}, bf16[16,4096]{1,0:T(8,128)(2,1)}, u32[]{:S(2)}) copy-start(bf16[16,4096]{1,0:T(8,128)(2,1)} %copy-done.27) | copy-start | bytes 393220
  52.3 0.9 %copy-start.30 = (bf16[16,4096]{1,0:T(8,128)(2,1)S(1)}, bf16[16,4096]{1,0:T(8,128)(2,1)}, u32[]{:S(2)}) copy-start(bf16[16,4096]{1,0:T(8,128)(2,1)} %copy-done.29) | copy-start | bytes 393220
  53.2 0.9 %copy-start.32 = (bf16[16,4096]{1,0:T(8,128)(2,1)S(1)}, bf16[16,4096]{1,0:T(8,128)(2,1)}, u32[]{:S(2)}) copy-start(bf16[16,4096]{1,0:T(8,128)(2,1)} %copy-done.31) | copy-start | bytes 393220
  54.1 0.7 copy-start.33
  68.4 0.8 copy-start.5
  69.2 5.5 %collective-permute-start.17 = (f32[8,256]{1,0:T(8,128)S(1)}, f32[8,256]{1,0:T(8,128)S(1)}, u32[]{:S(2)}, u32[]{:S(2)}) collective-permute-start(f32[8,256]{1,0:T(8,128)S(1)} %get-tuple-element.9.own), channel_id=1, source_target_pairs={{12,0},{13,1},{14,2},{15,3},{0,4},{1,5},{2,6},{3,7},{4,8},{5,9},{6... | collective-permute-start | bytes 24584 | tf_op jit(solution)/shard_map/ppermute | solution.py:32
  70.4 4.5 %collective-permute-start.16 = (f32[8,256]{1,0:T(8,128)S(1)}, f32[8,256]{1,0:T(8,128)S(1)}, u32[]{:S(2)}, u32[]{:S(2)}) collective-permute-start(f32[8,256]{1,0:T(8,128)S(1)} %get-tuple-element.9.own), channel_id=1, source_target_pairs={{8,0},{9,1},{10,2},{11,3},{12,4},{13,5},{14,6},{15,7},{0,8},{1,9},... | collective-permute-start | bytes 24584 | tf_op jit(solution)/shard_map/ppermute | solution.py:32
  72.5 3.7 %collective-permute-start.15 = (f32[8,256]{1,0:T(8,128)S(1)}, f32[8,256]{1,0:T(8,128)S(1)}, u32[]{:S(2)}, u32[]{:S(2)}) collective-permute-start(f32[8,256]{1,0:T(8,128)S(1)} %get-tuple-element.9.own), channel_id=1, source_target_pairs={{4,0},{5,1},{6,2},{7,3},{8,4},{9,5},{10,6},{11,7},{12,8},{13,9},{1... | collective-permute-start | bytes 24584 | tf_op jit(solution)/shard_map/ppermute | solution.py:32
  76.1 3.1 %collective-permute-start.20 = (f32[8,256]{1,0:T(8,128)S(1)}, f32[8,256]{1,0:T(8,128)S(1)}, u32[]{:S(2)}, u32[]{:S(2)}) collective-permute-start(f32[8,256]{1,0:T(8,128)S(1)} %add_add_fusion.s0), channel_id=1, source_target_pairs={{3,0},{2,1},{1,2},{0,3},{7,4},{6,5},{5,6},{4,7},{11,8},{10,9},{9,1... | collective-permute-start | bytes 24584 | tf_op jit(solution)/shard_map/ppermute | solution.py:32
  76.2 3.7 %collective-permute-start.19 = (f32[8,256]{1,0:T(8,128)S(1)}, f32[8,256]{1,0:T(8,128)S(1)}, u32[]{:S(2)}, u32[]{:S(2)}) collective-permute-start(f32[8,256]{1,0:T(8,128)S(1)} %add_add_fusion.s0), channel_id=1, source_target_pairs={{2,0},{3,1},{0,2},{1,3},{6,4},{7,5},{4,6},{5,7},{10,8},{11,9},{8,1... | collective-permute-start | bytes 24584 | tf_op jit(solution)/shard_map/ppermute | solution.py:32
  76.8 3.1 %collective-permute-start.18 = (f32[8,256]{1,0:T(8,128)S(1)}, f32[8,256]{1,0:T(8,128)S(1)}, u32[]{:S(2)}, u32[]{:S(2)}) collective-permute-start(f32[8,256]{1,0:T(8,128)S(1)} %add_add_fusion.s0), channel_id=1, source_target_pairs={{1,0},{0,1},{3,2},{2,3},{5,4},{4,5},{7,6},{6,7},{9,8},{8,9},{11,10... | collective-permute-start | bytes 24584 | tf_op jit(solution)/shard_map/ppermute | solution.py:32
  79.9 3.4 %copy-start.1 = (f32[4096,512]{1,0:T(8,128)S(1)}, f32[4096,512]{1,0:T(8,128)}, u32[]{:S(2)}) copy-start(f32[4096,512]{1,0:T(8,128)} %adjoint.1) | copy-start | bytes 25165828
  83.3 1.0 %copy-start.6 = (f32[256,512]{1,0:T(8,128)S(1)}, f32[256,512]{1,0:T(8,128)}, u32[]{:S(2)}) copy-start(f32[256,512]{1,0:T(8,128)} %copy-done.5) | copy-start | bytes 1572868
  (7 other events, 4.6 us)

commit v3 on v2

--- a/solution.py
+++ b/solution.py
@@ -10,7 +10,7 @@
 TILE = 512
 ROWS = 16
 SAMPLE = 256
-VMEM_BYTES = 18 << 20
+VMEM_BYTES = 28 << 20
 RATIO = 0.1 / 0.05**0.5
 
 
@@ -42,10 +42,14 @@
     for slow in range(z):
         for mid in range(y):
             parts[slow, mid, 1] = shift(parts[slow, mid, 0], n, 0, 0, 1)
+    return parts
+
+
+def owners(n, steps):
+    z, y, c = digits(n)
     me = lax.axis_index("dp")
-    mz, my, mc = me // (y * c), me // c % y, me % c
-    places = [((mz + a) % z * y + (my + b) % y) * c + (mc + d) % c for a, b, d in parts]
-    return list(parts.values()), jnp.stack(places).astype(jnp.int32)
+    mz, my, mc = me // (y * c), lax.rem(me // c, y), lax.rem(me, c)
+    return [(lax.rem(mz + a, z) * y + lax.rem(my + b, y)) * c + lax.rem(mc + d, c) for a, b, d in steps]
 
 
 def all_sum(value, n):
@@ -77,27 +81,52 @@
     return over, inv, first * inv
 
 
-def replay_kernel(n, *refs):
-    places, parts = refs[0], refs[1 : n + 1]
-    (weight, cot, token_weight, one, two, adjoint) = refs[n + 1 : n + 7]
-    (turned, along, across, bend, stats) = refs[n + 7 : n + 12]
-    (tokens, scaled, score, g0, g1, a0, a1, b0, b1, sums) = refs[n + 12 :]
+def replay_kernel(steps, *refs):
+    n = len(steps)
+    parts, far = refs[:n], refs[n : n + 6]
+    (adjoint, turned, along, across, bend, stats) = refs[n + 6 : n + 12]
+    (tokens, scaled, score, g0, g1, a0, a1, b0, b1, sums) = refs[n + 12 : n + 22]
+    (weight, one, two, cot, token_weight, part_sem, tile_sem) = refs[n + 22 :]
     grads, firsts, seconds = (g0, g1), (a0, a1), (b0, b1)
     height, depth = parts[0].shape
     count, width = cot.shape
     tiles = depth // TILE
 
-    for part, ref in enumerate(parts):
-        at = pl.multiple_of(places[part] * height, height)
-        tokens[pl.ds(at, height), :] = ref[...]
-
     def span(i):
         return pl.ds(pl.multiple_of(i * TILE, TILE), TILE)
 
+    places = owners(n, steps)
+
+    def part_copy(part):
+        at = pl.multiple_of(places[part] * height, height)
+        return pltpu.make_async_copy(parts[part], tokens.at[pl.ds(at, height), :], part_sem.at[part])
+
+    near = (weight, one, two, adjoint)
+
+    def tile_copy(which, i):
+        return pltpu.make_async_copy(far[which].at[span(i), :], near[which].at[span(i), :], tile_sem.at[which, i])
+
+    small = [
+        pltpu.make_async_copy(far[4 + k], ref, part_sem.at[n + k]) for k, ref in enumerate((cot, token_weight))
+    ]
+
+    for part in range(n):
+        part_copy(part).start()
+    for i in range(tiles):
+        tile_copy(0, i).start()
+    for i in range(tiles):
+        for which in (1, 2, 3):
+            tile_copy(which, i).start()
+    for copy in small:
+        copy.start()
+    for part in range(n):
+        part_copy(part).wait()
+
     along[...] = jnp.zeros_like(along)
     across[...] = jnp.zeros_like(across)
 
     def gate_step(i, _):
+        tile_copy(0, i).wait()
         here = tokens[:, span(i)]
         along[...] += f32dot(here, weight[span(i), :])
         turned[span(i), :] = here.T
@@ -106,6 +135,8 @@
     lax.fori_loop(0, tiles, gate_step, 0)
 
     gate = along[...]
+    for copy in small:
+        copy.wait()
     weights = over_columns(token_weight[...])
     cot_f = cot[...].astype(jnp.float32)
     sig = 1.0 / (1.0 + jnp.exp(-gate))
@@ -128,7 +159,12 @@
         at = pl.ds(pl.multiple_of(i * TILE + r, ROWS), ROWS)
         return grads[slot][r : r + ROWS, :], one[at, :], two[at, :], adjoint[at, :]
 
+    def arrive(i):
+        for which in (1, 2, 3):
+            tile_copy(which, i).wait()
+
     grad_tile(0, 0)
+    arrive(0)
     sq = jnp.zeros((8, width), jnp.float32)
     cross = jnp.zeros((8, width), jnp.float32)
     for r in range(0, SAMPLE, ROWS):
@@ -143,6 +179,8 @@
     sums[...] = jnp.zeros_like(sums)
 
     def update_tile(i, slot):
+        if not isinstance(i, int) or i > 0:
+            arrive(i)
         sq, cross = sums[0], sums[1]
         for r in range(0, TILE, ROWS):
             g, m1, m2, adj = rows_of(i, slot, r)
@@ -181,17 +219,21 @@
     stats[4:8, :] = jnp.broadcast_to(guess, (4, count))
 
 
-def replay_call(places, parts, weight, cot, token_weight, one, two, adjoint):
-    n = len(parts)
-    depth = parts[0].shape[1]
+def replay_call(parts, weight, cot, token_weight, one, two, adjoint):
+    steps = list(parts)
+    n = len(steps)
+    depth = weight.shape[0]
     count, width = cot.shape
     vmem = pl.BlockSpec(memory_space=pltpu.VMEM)
+    far = pl.BlockSpec(memory_space=pl.ANY)
     block = lambda dtype: pltpu.VMEM((TILE, width), dtype)
+    whole = lambda dtype: pltpu.VMEM((depth, width), dtype)
     return pl.pallas_call(
-        functools.partial(replay_kernel, n),
-        in_specs=[pl.BlockSpec(memory_space=pltpu.SMEM)] + [vmem] * (n + 6),
-        out_specs=[vmem] * 5,
+        functools.partial(replay_kernel, steps),
+        in_specs=[far] * (n + 6),
+        out_specs=[vmem] * 6,
         out_shape=[
+            pltpu.VMEM((depth, width), jnp.float32),
             pltpu.VMEM((depth, count), jnp.bfloat16),
             pltpu.VMEM((count, width), jnp.float32),
             pltpu.VMEM((count, width), jnp.float32),
@@ -209,17 +251,27 @@
             block(jnp.bfloat16),
             block(jnp.bfloat16),
             pltpu.VMEM((2, 8, width), jnp.float32),
+            whole(jnp.bfloat16),
+            whole(jnp.bfloat16),
+            whole(jnp.bfloat16),
+            pltpu.VMEM((count, width), jnp.bfloat16),
+            pltpu.VMEM((1, count), jnp.float32),
+            pltpu.SemaphoreType.DMA((n + 2,)),
+            pltpu.SemaphoreType.DMA((4, depth // TILE)),
         ],
         compiler_params=pltpu.CompilerParams(vmem_limit_bytes=VMEM_BYTES),
         name="replay",
-    )(places, *[resident(x) for x in (*parts, weight, cot, token_weight, one, two, adjoint)])
-
-
-def resident(x):
-    return pltpu.with_memory_space_constraint(x, pltpu.VMEM)
-
-
-def theta_kernel(entries, s0, s1, s2, s3, own, along, across, bend, turned, adjoint, theta, scores, ready, sent):
+    )(
+        *[in_hbm(x) if step == (0, 0, 0) else x for step, x in parts.items()],
+        *[in_hbm(x) for x in (weight, one, two, adjoint, cot, token_weight)],
+    )
+
+
+def in_hbm(x):
+    return pltpu.with_memory_space_constraint(x, pltpu.HBM)
+
+
+def theta_kernel(n, entries, s0, s1, s2, s3, own, along, across, bend, turned, adjoint, theta, scores, ready, sent):
     total = s0[...] + s1[...] + (s2[...] + s3[...])
     sq, cross = total[2:3, 0:1], total[3:4, 0:1]
     rms = jnp.sqrt(sq / entries)
@@ -227,7 +279,11 @@
     bind = jnp.where(rms > 1.0, 1.0 / (rms * rms * rms), 0.0)
     lead = -0.01 * scale
     rest = 0.01 * cross * bind / entries
-    scores[...] = lead * total[0:1, :] + rest * total[1:2, :]
+    mine = lead * total[0:8, :] + rest * pltpu.roll(total, 7, 0)
+    count = total.shape[1]
+    height = count // n
+    mine = pltpu.roll(mine, lax.rem(count - lax.axis_index("dp") * height, count), 1)
+    scores[...] = mine[0:1, 0:height]
     lead_here = RATIO * lead
     rest_here = RATIO**2 * rest + lead_here * own[4:5, 0:1]
     bent = (bend[...] * (lead_here * along[...] + rest_here * across[...])).astype(jnp.bfloat16)
@@ -245,35 +301,33 @@
         copy(i).wait()
 
 
-def theta_call(entries, sums, own, along, across, bend, turned, adjoint):
+def theta_call(n, entries, sums, own, along, across, bend, turned, adjoint):
     depth, width = adjoint.shape
     count = turned.shape[1]
     vmem = pl.BlockSpec(memory_space=pltpu.VMEM)
     return pl.pallas_call(
-        functools.partial(theta_kernel, entries),
+        functools.partial(theta_kernel, n, entries),
         in_specs=[vmem] * 10,
         out_specs=[pl.BlockSpec(memory_space=pl.ANY), vmem],
         out_shape=[
             jax.ShapeDtypeStruct((depth, width), jnp.float32),
-            jax.ShapeDtypeStruct((1, count), jnp.float32),
+            jax.ShapeDtypeStruct((1, count // n), jnp.float32),
         ],
         scratch_shapes=[pltpu.VMEM((depth, width), jnp.float32), pltpu.SemaphoreType.DMA((depth // TILE,))],
         compiler_params=pltpu.CompilerParams(vmem_limit_bytes=VMEM_BYTES),
         name="theta",
-    )(*[resident(x) for x in (*sums, own, along, across, bend, turned, adjoint)])
+    )(*sums, own, along, across, bend, turned, adjoint)
 
 
 def shards(n, tokens, cotangent, token_weight, weight, moment_one, moment_two, adjoint):
     entries = float(adjoint.shape[0] * adjoint.shape[1] * n)
-    parts, places = gather(tokens, n)
-    turned, along, across, bend, stats = replay_call(
-        places, parts, weight, cotangent, token_weight.reshape(1, -1), moment_one, moment_two, adjoint
+    parts = gather(tokens, n)
+    adjoint_near, turned, along, across, bend, stats = replay_call(
+        parts, weight, cotangent, token_weight.reshape(1, -1), moment_one, moment_two, adjoint
     )
     sums = all_sum(stats, n)
-    theta_bar, scores = theta_call(entries, sums, stats, along, across, bend, turned, adjoint)
-    height = tokens.shape[0]
-    token_scores = lax.dynamic_slice(scores[0], (lax.axis_index("dp") * height,), (height,))
-    return (theta_bar, token_scores)
+    theta_bar, scores = theta_call(n, entries, sums, stats, along, across, bend, turned, adjoint_near)
+    return (theta_bar, scores.reshape(-1))
 
 
 def solution(mesh):

time: 89.3 us -> 66.6 us (0.75)
  local copies, waits for them, and re-layouts: 35.8 us -> 0 us
  Pallas kernels: 17.4 us -> 26.9 us
  waiting for transfers between devices: 15.4 us -> 19.3 us
    unnamed x68 -> x0, local copies, waits for them, and re-layouts: 35.1 us -> none
    pallas_call x2, Pallas kernels: 17.4 us -> 26.9 us  [the longest x1 22.6 us: replay_call(): pl.pallas_call(functools.partial(replay_kernel, steps), in_specs=[far] *...]
    ppermute x21, waiting for transfers between devices: 15.4 us -> 19.3 us  [shift(): return lax.ppermute(value, 'dp', pairs)]
  transfers between devices with their start and end apart: 21 -> 21, of which waited for: 9 -> 10; matrix products, arithmetic and copies ran while one was open for 0% -> 0% of each run, Pallas kernels for 0% -> 0%
where the time goes in v3:
time: 66.6 us; the launch traced here: 66.4 us
  Pallas kernels  26.9 us (40%)
  starting transfers between devices  19.5 us (29%)
  waiting for transfers between devices  19.3 us (29%)
  between operations  0.68 us (1%)
    pallas_call x1, Pallas kernels, replay_call(): pl.pallas_call(functools.partial(replay_kernel, steps), in_specs=[far] *...  22.6 us
    ppermute x21, starting transfers between devices, shift(): return lax.ppermute(value, 'dp', pairs)  19.5 us
    ppermute x21, waiting for transfers between devices, shift(): return lax.ppermute(value, 'dp', pairs)  19.3 us
    pallas_call x1, Pallas kernels, theta_call(): pl.pallas_call(functools.partial(theta_kernel, n, entries), in_specs=[vme...  4.31 us
  transfers between devices with their start and end apart: 21, of which 10 were waited for; matrix products, arithmetic and copies ran while one was open for 0% of the time, Pallas kernels for 0%

profile of v3, /device:TPU:0, one launch (start us, length us, event | category | flops | bytes accessed | tf_op | source)
XLA Modules:
  0.0 66.4 jit_solution(7982122319647871384)
XLA Ops:
  0.6 3.0 %collective-permute-start.3 = (bf16[16,4096]{1,0:T(8,128)(2,1)}, bf16[16,4096]{1,0:T(8,128)(2,1)S(1)}, u32[]{:S(2)}, u32[]{:S(2)}) collective-permute-start(bf16[16,4096]{1,0:T(8,128)(2,1)} %refs_0_.1), channel_id=1, source_target_pairs={{2,0},{3,1},{0,2},{1,3},{6,4},{7,5},{4,6},{5,7},{10,8},{11,9},{8,1... | collective-permute-start | bytes 393224 | tf_op jit(solution)/shard_map/ppermute | solution.py:32
  3.7 1.6 %collective-permute-start.2 = (bf16[16,4096]{1,0:T(8,128)(2,1)}, bf16[16,4096]{1,0:T(8,128)(2,1)S(1)}, u32[]{:S(2)}, u32[]{:S(2)}) collective-permute-start(bf16[16,4096]{1,0:T(8,128)(2,1)} %refs_0_.1), channel_id=1, source_target_pairs={{12,0},{13,1},{14,2},{15,3},{0,4},{1,5},{2,6},{3,7},{4,8},{5,9},{6... | collective-permute-start | bytes 393224 | tf_op jit(solution)/shard_map/ppermute | solution.py:32
  5.2 2.6 %collective-permute-start.1 = (bf16[16,4096]{1,0:T(8,128)(2,1)}, bf16[16,4096]{1,0:T(8,128)(2,1)S(1)}, u32[]{:S(2)}, u32[]{:S(2)}) collective-permute-start(bf16[16,4096]{1,0:T(8,128)(2,1)} %refs_0_.1), channel_id=1, source_target_pairs={{8,0},{9,1},{10,2},{11,3},{12,4},{13,5},{14,6},{15,7},{0,8},{1,9},... | collective-permute-start | bytes 393224 | tf_op jit(solution)/shard_map/ppermute | solution.py:32
  7.8 1.3 %collective-permute-start = (bf16[16,4096]{1,0:T(8,128)(2,1)}, bf16[16,4096]{1,0:T(8,128)(2,1)S(1)}, u32[]{:S(2)}, u32[]{:S(2)}) collective-permute-start(bf16[16,4096]{1,0:T(8,128)(2,1)} %refs_0_.1), channel_id=1, source_target_pairs={{4,0},{5,1},{6,2},{7,3},{8,4},{9,5},{10,6},{11,7},{12,8},{13,9},{1... | collective-permute-start | bytes 393224 | tf_op jit(solution)/shard_map/ppermute | solution.py:32
  9.2 0.0 collective-permute-start.7
  9.2 0.0 collective-permute-done.3.refs_4_
  9.2 0.5 collective-permute-start.8
  9.7 2.5 %collective-permute-done.2.refs_3_ = bf16[16,4096]{1,0:T(8,128)(2,1)S(1)} collective-permute-done((bf16[16,4096]{1,0:T(8,128)(2,1)}, bf16[16,4096]{1,0:T(8,128)(2,1)S(1)}, u32[]{:S(2)}, u32[]{:S(2)}) %collective-permute-start.2) | collective-permute-done | bytes 131104 | tf_op jit(solution)/shard_map/ppermute | solution.py:32
  12.2 0.0 collective-permute-start.13
  12.2 4.3 %collective-permute-done.1.refs_2_ = bf16[16,4096]{1,0:T(8,128)(2,1)S(1)} collective-permute-done((bf16[16,4096]{1,0:T(8,128)(2,1)}, bf16[16,4096]{1,0:T(8,128)(2,1)S(1)}, u32[]{:S(2)}, u32[]{:S(2)}) %collective-permute-start.1) | collective-permute-done | bytes 131104 | tf_op jit(solution)/shard_map/ppermute | solution.py:32
  16.5 0.5 collective-permute-start.6
  16.9 0.0 collective-permute-done.refs_1_
  16.9 1.6 %collective-permute-start.5 = (bf16[16,4096]{1,0:T(8,128)(2,1)S(1)}, bf16[16,4096]{1,0:T(8,128)(2,1)S(1)}, u32[]{:S(2)}, u32[]{:S(2)}) collective-permute-start(bf16[16,4096]{1,0:T(8,128)(2,1)S(1)} %collective-permute-done.1.refs_2_), channel_id=1, source_target_pairs={{2,0},{3,1},{0,2},{1,3},{6,4},{7,5},{4,6},{5,7},{10,8},{11,9},{8,1... | collective-permute-start | bytes 393224 | tf_op jit(solution)/shard_map/ppermute | solution.py:32
  18.5 0.0 collective-permute-done.7.refs_8_
  18.5 0.5 collective-permute-start.4
  19.0 0.0 collective-permute-done.8.refs_9_
  19.0 0.0 collective-permute-start.11
  19.0 0.0 collective-permute-done.13.refs_14_
  19.0 0.5 collective-permute-start.9
  19.5 3.3 %collective-permute-done.6.refs_7_ = bf16[16,4096]{1,0:T(8,128)(2,1)S(1)} collective-permute-done((bf16[16,4096]{1,0:T(8,128)(2,1)S(1)}, bf16[16,4096]{1,0:T(8,128)(2,1)S(1)}, u32[]{:S(2)}, u32[]{:S(2)}) %collective-permute-start.6) | collective-permute-done | bytes 131104 | tf_op jit(solution)/shard_map/ppermute | solution.py:32
  22.8 0.0 collective-permute-start.14
  22.8 2.8 %collective-permute-done.5.refs_6_ = bf16[16,4096]{1,0:T(8,128)(2,1)S(1)} collective-permute-done((bf16[16,4096]{1,0:T(8,128)(2,1)S(1)}, bf16[16,4096]{1,0:T(8,128)(2,1)S(1)}, u32[]{:S(2)}, u32[]{:S(2)}) %collective-permute-start.5) | collective-permute-done | bytes 131104 | tf_op jit(solution)/shard_map/ppermute | solution.py:32
  25.6 0.0 collective-permute-start.12
  25.7 1.8 %collective-permute-done.4.refs_5_ = bf16[16,4096]{1,0:T(8,128)(2,1)S(1)} collective-permute-done((bf16[16,4096]{1,0:T(8,128)(2,1)S(1)}, bf16[16,4096]{1,0:T(8,128)(2,1)S(1)}, u32[]{:S(2)}, u32[]{:S(2)}) %collective-permute-start.4) | collective-permute-done | bytes 131104 | tf_op jit(solution)/shard_map/ppermute | solution.py:32
  27.4 0.0 collective-permute-start.10
  27.4 0.0 collective-permute-done.11.refs_12_
  27.4 0.0 collective-permute-done.9.refs_10_
  27.4 0.0 collective-permute-done.14.refs_15_
  27.4 0.0 collective-permute-done.12.refs_13_
  27.4 1.3 %collective-permute-done.10.refs_11_ = bf16[16,4096]{1,0:T(8,128)(2,1)S(1)} collective-permute-done((bf16[16,4096]{1,0:T(8,128)(2,1)S(1)}, bf16[16,4096]{1,0:T(8,128)(2,1)S(1)}, u32[]{:S(2)}, u32[]{:S(2)}) %collective-permute-start.10) | collective-permute-done | bytes 131104 | tf_op jit(solution)/shard_map/ppermute | solution.py:32
  28.8 22.6 %replay.1 = (f32[4096,512]{1,0:T(8,128)S(1)}, bf16[4096,256]{1,0:T(8,128)(2,1)S(1)}, f32[256,512]{1,0:T(8,128)S(1)}, f32[256,512]{1,0:T(8,128)S(1)}, f32[256,512]{1,0:T(8,128)S(1)}, /*index=5*/f32[8,256]{1,0:T(8,128)S(1)}) custom-call(bf16[16,4096]{1,0:T(8,128)(2,1)} %refs_0_.1, bf16[16,4096]{1,0:T(8,128)(2,1)S(1)} %collective-permute-done.refs_1_, ...), custom_call_target="tpu_custom_call" | custom-call | tf_op jit(solution)/shard_map/replay/pallas_call | solution.py:231
  51.4 1.3 %collective-permute-start.17 = (f32[8,256]{1,0:T(8,128)S(1)}, f32[8,256]{1,0:T(8,128)S(1)}, u32[]{:S(2)}, u32[]{:S(2)}) collective-permute-start(f32[8,256]{1,0:T(8,128)S(1)} %get-tuple-element.10.own), channel_id=1, source_target_pairs={{12,0},{13,1},{14,2},{15,3},{0,4},{1,5},{2,6},{3,7},{4,8},{5,9},{6... | collective-permute-start | bytes 24584 | tf_op jit(solution)/shard_map/ppermute | solution.py:32
  52.7 2.1 %collective-permute-start.16 = (f32[8,256]{1,0:T(8,128)S(1)}, f32[8,256]{1,0:T(8,128)S(1)}, u32[]{:S(2)}, u32[]{:S(2)}) collective-permute-start(f32[8,256]{1,0:T(8,128)S(1)} %get-tuple-element.10.own), channel_id=1, source_target_pairs={{8,0},{9,1},{10,2},{11,3},{12,4},{13,5},{14,6},{15,7},{0,8},{1,9},... | collective-permute-start | bytes 24584 | tf_op jit(solution)/shard_map/ppermute | solution.py:32
  54.7 2.2 %collective-permute-start.15 = (f32[8,256]{1,0:T(8,128)S(1)}, f32[8,256]{1,0:T(8,128)S(1)}, u32[]{:S(2)}, u32[]{:S(2)}) collective-permute-start(f32[8,256]{1,0:T(8,128)S(1)} %get-tuple-element.10.own), channel_id=1, source_target_pairs={{4,0},{5,1},{6,2},{7,3},{8,4},{9,5},{10,6},{11,7},{12,8},{13,9},{1... | collective-permute-start | bytes 24584 | tf_op jit(solution)/shard_map/ppermute | solution.py:32
  57.0 0.0 collective-permute-done.17
  57.0 0.2 collective-permute-done.16
  57.2 1.2 %collective-permute-done.15 = f32[8,256]{1,0:T(8,128)S(1)} collective-permute-done((f32[8,256]{1,0:T(8,128)S(1)}, f32[8,256]{1,0:T(8,128)S(1)}, u32[]{:S(2)}, u32[]{:S(2)}) %collective-permute-start.15) | collective-permute-done | bytes 8224 | tf_op jit(solution)/shard_map/ppermute | solution.py:32
  58.4 0.0 collective-permute-start.20
  58.4 0.6 collective-permute-start.19
  59.0 1.3 %collective-permute-start.18 = (f32[8,256]{1,0:T(8,128)S(1)}, f32[8,256]{1,0:T(8,128)S(1)}, u32[]{:S(2)}, u32[]{:S(2)}) collective-permute-start(f32[8,256]{1,0:T(8,128)S(1)} %add_add_fusion.s0), channel_id=1, source_target_pairs={{1,0},{0,1},{3,2},{2,3},{5,4},{4,5},{7,6},{6,7},{9,8},{8,9},{11,10... | collective-permute-start | bytes 24584 | tf_op jit(solution)/shard_map/ppermute | solution.py:32
  60.2 1.2 %collective-permute-done.20.s3 = f32[8,256]{1,0:T(8,128)S(1)} collective-permute-done((f32[8,256]{1,0:T(8,128)S(1)}, f32[8,256]{1,0:T(8,128)S(1)}, u32[]{:S(2)}, u32[]{:S(2)}) %collective-permute-start.20) | collective-permute-done | bytes 8224 | tf_op jit(solution)/shard_map/ppermute | solution.py:32
  61.5 0.6 collective-permute-done.19.s2
  62.1 0.0 collective-permute-done.18.s1
  62.1 4.3 %theta.1 = (f32[4096,512]{1,0:T(8,128)}, f32[1,16]{1,0:T(1,128)}) custom-call(f32[8,256]{1,0:T(8,128)S(1)} %add_add_fusion.s0, f32[8,256]{1,0:T(8,128)S(1)} %collective-permute-done.18.s1, f32[8,256]{1,0:T(8,128)S(1)} %collective-permute-done.19.s2, f32[8,256]{1,0:T(8,128)S(1)} %collective-permute-done.20.s3, f32[8,256]{1,0:T(8,128)S(1)} %get-tuple-element.10.own, ...), custom_call_target="tpu_custom_call" | custom-call | tf_op jit(solution)/shard_map/theta/pallas_call | solution.py:308
  (1 shorter events, 0.0 us)
Async XLA Ops:
  0.6 8.6 %collective-permute-start.3 = (bf16[16,4096]{1,0:T(8,128)(2,1)}, bf16[16,4096]{1,0:T(8,128)(2,1)S(1)}, u32[]{:S(2)}, u32[]{:S(2)}) collective-permute-start(bf16[16,4096]{1,0:T(8,128)(2,1)} %refs_0_.1), channel_id=1, source_target_pairs={{2,0},{3,1},{0,2},{1,3},{6,4},{7,5},{4,6},{5,7},{10,8},{11,9},{8,1... | collective-permute-start | bytes 393224 | tf_op jit(solution)/shard_map/ppermute | solution.py:32
  3.7 8.5 %collective-permute-start.2 = (bf16[16,4096]{1,0:T(8,128)(2,1)}, bf16[16,4096]{1,0:T(8,128)(2,1)S(1)}, u32[]{:S(2)}, u32[]{:S(2)}) collective-permute-start(bf16[16,4096]{1,0:T(8,128)(2,1)} %refs_0_.1), channel_id=1, source_target_pairs={{12,0},{13,1},{14,2},{15,3},{0,4},{1,5},{2,6},{3,7},{4,8},{5,9},{6... | collective-permute-start | bytes 393224 | tf_op jit(solution)/shard_map/ppermute | solution.py:32
  5.2 11.2 %collective-permute-start.1 = (bf16[16,4096]{1,0:T(8,128)(2,1)}, bf16[16,4096]{1,0:T(8,128)(2,1)S(1)}, u32[]{:S(2)}, u32[]{:S(2)}) collective-permute-start(bf16[16,4096]{1,0:T(8,128)(2,1)} %refs_0_.1), channel_id=1, source_target_pairs={{8,0},{9,1},{10,2},{11,3},{12,4},{13,5},{14,6},{15,7},{0,8},{1,9},... | collective-permute-start | bytes 393224 | tf_op jit(solution)/shard_map/ppermute | solution.py:32
  7.8 9.1 %collective-permute-start = (bf16[16,4096]{1,0:T(8,128)(2,1)}, bf16[16,4096]{1,0:T(8,128)(2,1)S(1)}, u32[]{:S(2)}, u32[]{:S(2)}) collective-permute-start(bf16[16,4096]{1,0:T(8,128)(2,1)} %refs_0_.1), channel_id=1, source_target_pairs={{4,0},{5,1},{6,2},{7,3},{8,4},{9,5},{10,6},{11,7},{12,8},{13,9},{1... | collective-permute-start | bytes 393224 | tf_op jit(solution)/shard_map/ppermute | solution.py:32
  9.2 9.3 %collective-permute-start.7 = (bf16[16,4096]{1,0:T(8,128)(2,1)}, bf16[16,4096]{1,0:T(8,128)(2,1)S(1)}, u32[]{:S(2)}, u32[]{:S(2)}) collective-permute-start(bf16[16,4096]{1,0:T(8,128)(2,1)} %refs_0_.1), channel_id=1, source_target_pairs={{1,0},{0,1},{3,2},{2,3},{5,4},{4,5},{7,6},{6,7},{9,8},{8,9},{11,10... | collective-permute-start | bytes 393224 | tf_op jit(solution)/shard_map/ppermute | solution.py:32
  9.2 9.8 %collective-permute-start.8 = (bf16[16,4096]{1,0:T(8,128)(2,1)S(1)}, bf16[16,4096]{1,0:T(8,128)(2,1)S(1)}, u32[]{:S(2)}, u32[]{:S(2)}) collective-permute-start(bf16[16,4096]{1,0:T(8,128)(2,1)S(1)} %collective-permute-done.3.refs_4_), channel_id=1, source_target_pairs={{1,0},{0,1},{3,2},{2,3},{5,4},{4,5},{7,6},{6,7},{9,8},{8,9},{11,10... | collective-permute-start | bytes 393224 | tf_op jit(solution)/shard_map/ppermute | solution.py:32
  12.2 6.8 %collective-permute-start.13 = (bf16[16,4096]{1,0:T(8,128)(2,1)S(1)}, bf16[16,4096]{1,0:T(8,128)(2,1)S(1)}, u32[]{:S(2)}, u32[]{:S(2)}) collective-permute-start(bf16[16,4096]{1,0:T(8,128)(2,1)S(1)} %collective-permute-done.2.refs_3_), channel_id=1, source_target_pairs={{1,0},{0,1},{3,2},{2,3},{5,4},{4,5},{7,6},{6,7},{9,8},{8,9},{11,10... | collective-permute-start | bytes 393224 | tf_op jit(solution)/shard_map/ppermute | solution.py:32
  16.5 6.4 %collective-permute-start.6 = (bf16[16,4096]{1,0:T(8,128)(2,1)S(1)}, bf16[16,4096]{1,0:T(8,128)(2,1)S(1)}, u32[]{:S(2)}, u32[]{:S(2)}) collective-permute-start(bf16[16,4096]{1,0:T(8,128)(2,1)S(1)} %collective-permute-done.2.refs_3_), channel_id=1, source_target_pairs={{2,0},{3,1},{0,2},{1,3},{6,4},{7,5},{4,6},{5,7},{10,8},{11,9},{8,1... | collective-permute-start | bytes 393224 | tf_op jit(solution)/shard_map/ppermute | solution.py:32
  16.9 8.7 %collective-permute-start.5 = (bf16[16,4096]{1,0:T(8,128)(2,1)S(1)}, bf16[16,4096]{1,0:T(8,128)(2,1)S(1)}, u32[]{:S(2)}, u32[]{:S(2)}) collective-permute-start(bf16[16,4096]{1,0:T(8,128)(2,1)S(1)} %collective-permute-done.1.refs_2_), channel_id=1, source_target_pairs={{2,0},{3,1},{0,2},{1,3},{6,4},{7,5},{4,6},{5,7},{10,8},{11,9},{8,1... | collective-permute-start | bytes 393224 | tf_op jit(solution)/shard_map/ppermute | solution.py:32
  18.5 8.9 %collective-permute-start.4 = (bf16[16,4096]{1,0:T(8,128)(2,1)S(1)}, bf16[16,4096]{1,0:T(8,128)(2,1)S(1)}, u32[]{:S(2)}, u32[]{:S(2)}) collective-permute-start(bf16[16,4096]{1,0:T(8,128)(2,1)S(1)} %collective-permute-done.refs_1_), channel_id=1, source_target_pairs={{2,0},{3,1},{0,2},{1,3},{6,4},{7,5},{4,6},{5,7},{10,8},{11,9},{8,1... | collective-permute-start | bytes 393224 | tf_op jit(solution)/shard_map/ppermute | solution.py:32
  19.0 8.4 %collective-permute-start.11 = (bf16[16,4096]{1,0:T(8,128)(2,1)S(1)}, bf16[16,4096]{1,0:T(8,128)(2,1)S(1)}, u32[]{:S(2)}, u32[]{:S(2)}) collective-permute-start(bf16[16,4096]{1,0:T(8,128)(2,1)S(1)} %collective-permute-done.1.refs_2_), channel_id=1, source_target_pairs={{1,0},{0,1},{3,2},{2,3},{5,4},{4,5},{7,6},{6,7},{9,8},{8,9},{11,10... | collective-permute-start | bytes 393224 | tf_op jit(solution)/shard_map/ppermute | solution.py:32
  19.0 8.4 %collective-permute-start.9 = (bf16[16,4096]{1,0:T(8,128)(2,1)S(1)}, bf16[16,4096]{1,0:T(8,128)(2,1)S(1)}, u32[]{:S(2)}, u32[]{:S(2)}) collective-permute-start(bf16[16,4096]{1,0:T(8,128)(2,1)S(1)} %collective-permute-done.refs_1_), channel_id=1, source_target_pairs={{1,0},{0,1},{3,2},{2,3},{5,4},{4,5},{7,6},{6,7},{9,8},{8,9},{11,10... | collective-permute-start | bytes 393224 | tf_op jit(solution)/shard_map/ppermute | solution.py:32
  22.8 4.6 %collective-permute-start.14 = (bf16[16,4096]{1,0:T(8,128)(2,1)S(1)}, bf16[16,4096]{1,0:T(8,128)(2,1)S(1)}, u32[]{:S(2)}, u32[]{:S(2)}) collective-permute-start(bf16[16,4096]{1,0:T(8,128)(2,1)S(1)} %collective-permute-done.6.refs_7_), channel_id=1, source_target_pairs={{1,0},{0,1},{3,2},{2,3},{5,4},{4,5},{7,6},{6,7},{9,8},{8,9},{11,10... | collective-permute-start | bytes 393224 | tf_op jit(solution)/shard_map/ppermute | solution.py:32
  25.6 1.8 %collective-permute-start.12 = (bf16[16,4096]{1,0:T(8,128)(2,1)S(1)}, bf16[16,4096]{1,0:T(8,128)(2,1)S(1)}, u32[]{:S(2)}, u32[]{:S(2)}) collective-permute-start(bf16[16,4096]{1,0:T(8,128)(2,1)S(1)} %collective-permute-done.5.refs_6_), channel_id=1, source_target_pairs={{1,0},{0,1},{3,2},{2,3},{5,4},{4,5},{7,6},{6,7},{9,8},{8,9},{11,10... | collective-permute-start | bytes 393224 | tf_op jit(solution)/shard_map/ppermute | solution.py:32
  27.4 1.3 %collective-permute-start.10 = (bf16[16,4096]{1,0:T(8,128)(2,1)S(1)}, bf16[16,4096]{1,0:T(8,128)(2,1)S(1)}, u32[]{:S(2)}, u32[]{:S(2)}) collective-permute-start(bf16[16,4096]{1,0:T(8,128)(2,1)S(1)} %collective-permute-done.4.refs_5_), channel_id=1, source_target_pairs={{1,0},{0,1},{3,2},{2,3},{5,4},{4,5},{7,6},{6,7},{9,8},{8,9},{11,10... | collective-permute-start | bytes 393224 | tf_op jit(solution)/shard_map/ppermute | solution.py:32
  51.4 5.6 %collective-permute-start.17 = (f32[8,256]{1,0:T(8,128)S(1)}, f32[8,256]{1,0:T(8,128)S(1)}, u32[]{:S(2)}, u32[]{:S(2)}) collective-permute-start(f32[8,256]{1,0:T(8,128)S(1)} %get-tuple-element.10.own), channel_id=1, source_target_pairs={{12,0},{13,1},{14,2},{15,3},{0,4},{1,5},{2,6},{3,7},{4,8},{5,9},{6... | collective-permute-start | bytes 24584 | tf_op jit(solution)/shard_map/ppermute | solution.py:32
  52.7 4.5 %collective-permute-start.16 = (f32[8,256]{1,0:T(8,128)S(1)}, f32[8,256]{1,0:T(8,128)S(1)}, u32[]{:S(2)}, u32[]{:S(2)}) collective-permute-start(f32[8,256]{1,0:T(8,128)S(1)} %get-tuple-element.10.own), channel_id=1, source_target_pairs={{8,0},{9,1},{10,2},{11,3},{12,4},{13,5},{14,6},{15,7},{0,8},{1,9},... | collective-permute-start | bytes 24584 | tf_op jit(solution)/shard_map/ppermute | solution.py:32
  54.7 3.7 %collective-permute-start.15 = (f32[8,256]{1,0:T(8,128)S(1)}, f32[8,256]{1,0:T(8,128)S(1)}, u32[]{:S(2)}, u32[]{:S(2)}) collective-permute-start(f32[8,256]{1,0:T(8,128)S(1)} %get-tuple-element.10.own), channel_id=1, source_target_pairs={{4,0},{5,1},{6,2},{7,3},{8,4},{9,5},{10,6},{11,7},{12,8},{13,9},{1... | collective-permute-start | bytes 24584 | tf_op jit(solution)/shard_map/ppermute | solution.py:32
  58.4 3.1 %collective-permute-start.20 = (f32[8,256]{1,0:T(8,128)S(1)}, f32[8,256]{1,0:T(8,128)S(1)}, u32[]{:S(2)}, u32[]{:S(2)}) collective-permute-start(f32[8,256]{1,0:T(8,128)S(1)} %add_add_fusion.s0), channel_id=1, source_target_pairs={{3,0},{2,1},{1,2},{0,3},{7,4},{6,5},{5,6},{4,7},{11,8},{10,9},{9,1... | collective-permute-start | bytes 24584 | tf_op jit(solution)/shard_map/ppermute | solution.py:32
  58.4 3.7 %collective-permute-start.19 = (f32[8,256]{1,0:T(8,128)S(1)}, f32[8,256]{1,0:T(8,128)S(1)}, u32[]{:S(2)}, u32[]{:S(2)}) collective-permute-start(f32[8,256]{1,0:T(8,128)S(1)} %add_add_fusion.s0), channel_id=1, source_target_pairs={{2,0},{3,1},{0,2},{1,3},{6,4},{7,5},{4,6},{5,7},{10,8},{11,9},{8,1... | collective-permute-start | bytes 24584 | tf_op jit(solution)/shard_map/ppermute | solution.py:32
  59.0 3.1 %collective-permute-start.18 = (f32[8,256]{1,0:T(8,128)S(1)}, f32[8,256]{1,0:T(8,128)S(1)}, u32[]{:S(2)}, u32[]{:S(2)}) collective-permute-start(f32[8,256]{1,0:T(8,128)S(1)} %add_add_fusion.s0), channel_id=1, source_target_pairs={{1,0},{0,1},{3,2},{2,3},{5,4},{4,5},{7,6},{6,7},{9,8},{8,9},{11,10... | collective-permute-start | bytes 24584 | tf_op jit(solution)/shard_map/ppermute | solution.py:32

commit v4 on v3

--- a/solution.py
+++ b/solution.py
@@ -10,7 +10,7 @@
 TILE = 512
 ROWS = 16
 SAMPLE = 256
-VMEM_BYTES = 28 << 20
+VMEM_BYTES = 12 << 20
 RATIO = 0.1 / 0.05**0.5
 
 
@@ -32,24 +32,54 @@
     return lax.ppermute(value, "dp", pairs)
 
 
-def gather(tokens, n):
-    z, y, c = digits(n)
-    parts = {(0, 0, 0): tokens}
-    for slow in range(1, z):
-        parts[slow, 0, 0] = shift(tokens, n, slow, 0, 0)
-    for slow in range(z):
-        parts[slow, 1, 0] = shift(parts[slow, 0, 0], n, 0, 1, 0)
-    for slow in range(z):
-        for mid in range(y):
-            parts[slow, mid, 1] = shift(parts[slow, mid, 0], n, 0, 0, 1)
-    return parts
+def ring(n):
+    chips = n // 2
+    return [*range(0, chips, 2), *range(chips - 1 - chips % 2, 0, -2)]
+
+
+def along_ring(value, n, way):
+    order = ring(n)
+    pairs = []
+    for i, chip in enumerate(order):
+        source = order[(i - way) % len(order)]
+        pairs += [(2 * source + core, 2 * chip + core) for core in (0, 1)]
+    return lax.ppermute(value, "dp", pairs)
+
+
+def gather(tokens, n, errands):
+    parts = {(0, 0): tokens}
+    chips = n // 2
+    done = []
+    token = None
+    for hop in range(1, chips // 2 + 1):
+        for way in (1, -1):
+            if 2 * hop == chips and way == -1:
+                continue
+            here = parts[way * (hop - 1), 0]
+            if token is not None:
+                here = lax.optimization_barrier((here, token))[0]
+            parts[way * hop, 0] = along_ring(here, n, way)
+        token = None
+        if errands[len(done) :]:
+            result, token = errands[len(done)](parts[hop - 1, 0])
+            done.append(result)
+    for back, core in list(parts):
+        parts[back, 1] = shift(parts[back, core], n, 0, 0, 1)
+    return parts, done
 
 
 def owners(n, steps):
-    z, y, c = digits(n)
+    order = ring(n)
     me = lax.axis_index("dp")
-    mz, my, mc = me // (y * c), lax.rem(me // c, y), lax.rem(me, c)
-    return [(lax.rem(mz + a, z) * y + lax.rem(my + b, y)) * c + lax.rem(mc + d, c) for a, b, d in steps]
+    chip, core = me // 2, lax.rem(me, 2)
+    at = jnp.where(lax.rem(chip, 2) == 0, chip // 2, n // 2 - 1 - chip // 2)
+    places = []
+    for back, other in steps:
+        there = lax.rem(at - back + len(order), len(order))
+        up = len(order) // 2
+        source = jnp.where(there < up, 2 * there, 2 * (len(order) - 1 - there) + 1)
+        places.append(2 * source + lax.rem(core + other, 2))
+    return places
 
 
 def all_sum(value, n):
@@ -74,19 +104,56 @@
 
 
 def update(grad, one, two):
-    first = 9.0 * one.astype(jnp.float32) + grad
-    second = 19.0 * two.astype(jnp.float32) + grad * grad
+    first = one + grad
+    second = two + grad * grad
     over = lax.rsqrt(second)
     inv = pltpu.reciprocal(second * over + 1e-08 / 0.05**0.5, approx=True)
     return over, inv, first * inv
 
 
+def fetch_kernel(factor, far, after, near, token, raw, sem):
+    target = near if factor is None else raw
+    tiles = far.shape[0] // TILE
+
+    def copy(i):
+        at = pl.ds(pl.multiple_of(i * TILE, TILE), TILE)
+        return pltpu.make_async_copy(far.at[at, :], target.at[at, :], sem.at[i])
+
+    for i in range(tiles):
+        copy(i).start()
+    token[...] = jnp.zeros_like(token)
+
+    def widen(i, _):
+        copy(i).wait()
+        if factor is not None:
+            at = pl.ds(pl.multiple_of(i * TILE, TILE), TILE)
+            near[at, :] = factor * raw[at, :].astype(jnp.float32)
+        return 0
+
+    lax.fori_loop(0, tiles, widen, 0)
+
+
+def fetch(x, after, factor=None):
+    dtype = x.dtype if factor is None else jnp.float32
+    raw = (8, 128) if factor is None else x.shape
+    return pl.pallas_call(
+        functools.partial(fetch_kernel, factor),
+        in_specs=[pl.BlockSpec(memory_space=pl.ANY)] * 2,
+        out_specs=[pl.BlockSpec(memory_space=pltpu.VMEM)] * 2,
+        out_shape=[pltpu.VMEM(x.shape, dtype), jax.ShapeDtypeStruct((8, 128), jnp.float32)],
+        scratch_shapes=[pltpu.VMEM(raw, x.dtype), pltpu.SemaphoreType.DMA((x.shape[0] // TILE,))],
+        compiler_params=pltpu.CompilerParams(vmem_limit_bytes=VMEM_BYTES),
+        cost_estimate=pl.CostEstimate(flops=0, bytes_accessed=8 << 20, transcendentals=0),
+        name="fetch",
+    )(in_hbm(x), after)
+
+
 def replay_kernel(steps, *refs):
     n = len(steps)
-    parts, far = refs[:n], refs[n : n + 6]
-    (adjoint, turned, along, across, bend, stats) = refs[n + 6 : n + 12]
-    (tokens, scaled, score, g0, g1, a0, a1, b0, b1, sums) = refs[n + 12 : n + 22]
-    (weight, one, two, cot, token_weight, part_sem, tile_sem) = refs[n + 22 :]
+    parts, far = refs[:n], refs[n : n + 2]
+    (weight, one, two, adjoint) = refs[n + 2 : n + 6]
+    (turned, along, across, bend, stats) = refs[n + 6 : n + 11]
+    (tokens, scaled, score, g0, g1, a0, a1, b0, b1, sums, cot, token_weight, part_sem) = refs[n + 11 :]
     grads, firsts, seconds = (g0, g1), (a0, a1), (b0, b1)
     height, depth = parts[0].shape
     count, width = cot.shape
@@ -101,22 +168,12 @@
         at = pl.multiple_of(places[part] * height, height)
         return pltpu.make_async_copy(parts[part], tokens.at[pl.ds(at, height), :], part_sem.at[part])
 
-    near = (weight, one, two, adjoint)
-
-    def tile_copy(which, i):
-        return pltpu.make_async_copy(far[which].at[span(i), :], near[which].at[span(i), :], tile_sem.at[which, i])
-
     small = [
-        pltpu.make_async_copy(far[4 + k], ref, part_sem.at[n + k]) for k, ref in enumerate((cot, token_weight))
+        pltpu.make_async_copy(far[k], ref, part_sem.at[n + k]) for k, ref in enumerate((cot, token_weight))
     ]
 
     for part in range(n):
         part_copy(part).start()
-    for i in range(tiles):
-        tile_copy(0, i).start()
-    for i in range(tiles):
-        for which in (1, 2, 3):
-            tile_copy(which, i).start()
     for copy in small:
         copy.start()
     for part in range(n):
@@ -126,7 +183,6 @@
     across[...] = jnp.zeros_like(across)
 
     def gate_step(i, _):
-        tile_copy(0, i).wait()
         here = tokens[:, span(i)]
         along[...] += f32dot(here, weight[span(i), :])
         turned[span(i), :] = here.T
@@ -159,12 +215,7 @@
         at = pl.ds(pl.multiple_of(i * TILE + r, ROWS), ROWS)
         return grads[slot][r : r + ROWS, :], one[at, :], two[at, :], adjoint[at, :]
 
-    def arrive(i):
-        for which in (1, 2, 3):
-            tile_copy(which, i).wait()
-
     grad_tile(0, 0)
-    arrive(0)
     sq = jnp.zeros((8, width), jnp.float32)
     cross = jnp.zeros((8, width), jnp.float32)
     for r in range(0, SAMPLE, ROWS):
@@ -179,8 +230,6 @@
     sums[...] = jnp.zeros_like(sums)
 
     def update_tile(i, slot):
-        if not isinstance(i, int) or i > 0:
-            arrive(i)
         sq, cross = sums[0], sums[1]
         for r in range(0, TILE, ROWS):
             g, m1, m2, adj = rows_of(i, slot, r)
@@ -219,7 +268,7 @@
     stats[4:8, :] = jnp.broadcast_to(guess, (4, count))
 
 
-def replay_call(parts, weight, cot, token_weight, one, two, adjoint):
+def replay_call(parts, cot, token_weight, weight, one, two, adjoint):
     steps = list(parts)
     n = len(steps)
     depth = weight.shape[0]
@@ -227,13 +276,11 @@
     vmem = pl.BlockSpec(memory_space=pltpu.VMEM)
     far = pl.BlockSpec(memory_space=pl.ANY)
     block = lambda dtype: pltpu.VMEM((TILE, width), dtype)
-    whole = lambda dtype: pltpu.VMEM((depth, width), dtype)
     return pl.pallas_call(
         functools.partial(replay_kernel, steps),
-        in_specs=[far] * (n + 6),
-        out_specs=[vmem] * 6,
+        in_specs=[far] * (n + 2) + [vmem] * 4,
+        out_specs=[vmem] * 5,
         out_shape=[
-            pltpu.VMEM((depth, width), jnp.float32),
             pltpu.VMEM((depth, count), jnp.bfloat16),
             pltpu.VMEM((count, width), jnp.float32),
             pltpu.VMEM((count, width), jnp.float32),
@@ -251,19 +298,19 @@
             block(jnp.bfloat16),
             block(jnp.bfloat16),
             pltpu.VMEM((2, 8, width), jnp.float32),
-            whole(jnp.bfloat16),
-            whole(jnp.bfloat16),
-            whole(jnp.bfloat16),
             pltpu.VMEM((count, width), jnp.bfloat16),
             pltpu.VMEM((1, count), jnp.float32),
             pltpu.SemaphoreType.DMA((n + 2,)),
-            pltpu.SemaphoreType.DMA((4, depth // TILE)),
         ],
         compiler_params=pltpu.CompilerParams(vmem_limit_bytes=VMEM_BYTES),
         name="replay",
     )(
-        *[in_hbm(x) if step == (0, 0, 0) else x for step, x in parts.items()],
-        *[in_hbm(x) for x in (weight, one, two, adjoint, cot, token_weight)],
+        *[in_hbm(x) if step == (0, 0) else x for step, x in parts.items()],
+        *[in_hbm(x) for x in (cot, token_weight)],
+        weight,
+        one,
+        two,
+        adjoint,
     )
 
 
@@ -321,9 +368,15 @@
 
 def shards(n, tokens, cotangent, token_weight, weight, moment_one, moment_two, adjoint):
     entries = float(adjoint.shape[0] * adjoint.shape[1] * n)
-    parts = gather(tokens, n)
-    adjoint_near, turned, along, across, bend, stats = replay_call(
-        parts, weight, cotangent, token_weight.reshape(1, -1), moment_one, moment_two, adjoint
+    errands = [
+        lambda after: fetch(weight, after),
+        lambda after: fetch(moment_one, after, 9.0),
+        lambda after: fetch(moment_two, after, 19.0),
+        lambda after: fetch(adjoint, after),
+    ]
+    parts, (weight_near, one, two, adjoint_near) = gather(tokens, n, errands)
+    turned, along, across, bend, stats = replay_call(
+        parts, cotangent, token_weight.reshape(1, -1), weight_near, one, two, adjoint_near
     )
     sums = all_sum(stats, n)
     theta_bar, scores = theta_call(n, entries, sums, stats, along, across, bend, turned, adjoint_near)

time: 66.6 us -> 61.2 us (0.919)
  waiting for transfers between devices: 19.3 us -> 9.09 us
  Pallas kernels: 26.9 us -> 32.1 us
  starting transfers between devices: 19.5 us -> 18.1 us
  local copies, waits for them, and re-layouts: 0 us -> 0.97 us
    ppermute x21 -> x14, waiting for transfers between devices: 19.3 us -> 4.18 us  [shift(): return lax.ppermute(value, 'dp', pairs)]
    pallas_call x0 -> x4, Pallas kernels: none -> 12.5 us  [fetch(): pl.pallas_call(functools.partial(fetch_kernel, factor), in_specs=[pl.Bloc...]
    ppermute x21 -> x14, starting transfers between devices: 19.5 us -> 8.94 us  [shift(): return lax.ppermute(value, 'dp', pairs)]
    ppermute x0 -> x7, starting transfers between devices: none -> 9.2 us  [along_ring(): return lax.ppermute(value, 'dp', pairs)]
    pallas_call x1, Pallas kernels: 22.6 us -> 15.2 us  [replay_call(): pl.pallas_call(functools.partial(replay_kernel, steps), in_specs=[far] *...]
    ppermute x0 -> x7, waiting for transfers between devices: none -> 4.91 us  [along_ring(): return lax.ppermute(value, 'dp', pairs)]
    unnamed x0 -> x4, local copies, waits for them, and re-layouts: none -> 0.97 us
  transfers between devices with their start and end apart: 21 -> 21, of which waited for: 10 -> 8; matrix products, arithmetic and copies ran while one was open for 0% -> 0% of each run, Pallas kernels for 0% -> 21%
where the time goes in v4:
time: 61.2 us; the launch traced here: 61 us
  Pallas kernels  32.1 us (52%)
  starting transfers between devices  18.1 us (30%)
  waiting for transfers between devices  9.09 us (15%)
  local copies, waits for them, and re-layouts  0.97 us (2%)
  between operations  0.74 us (1%)
    pallas_call x1, Pallas kernels, replay_call(): pl.pallas_call(functools.partial(replay_kernel, steps), in_specs=[far] *...  15.2 us
    pallas_call x4, Pallas kernels, fetch(): pl.pallas_call(functools.partial(fetch_kernel, factor), in_specs=[pl.Bloc...  12.5 us
    ppermute x7, starting transfers between devices, along_ring(): return lax.ppermute(value, 'dp', pairs)  9.2 us
    ppermute x14, starting transfers between devices, shift(): return lax.ppermute(value, 'dp', pairs)  8.94 us
    ppermute x7, waiting for transfers between devices, along_ring(): return lax.ppermute(value, 'dp', pairs)  4.91 us
    pallas_call x1, Pallas kernels, theta_call(): pl.pallas_call(functools.partial(theta_kernel, n, entries), in_specs=[vme...  4.29 us
    ppermute x14, waiting for transfers between devices, shift(): return lax.ppermute(value, 'dp', pairs)  4.18 us
  transfers between devices with their start and end apart: 21, of which 8 were waited for; matrix products, arithmetic and copies ran while one was open for 0% of the time, Pallas kernels for 21%

profile of v4, /device:TPU:0, one launch (start us, length us, event | category | flops | bytes accessed | tf_op | source)
XLA Modules:
  0.0 61.0 jit_solution(15060187289009627018)
XLA Ops:
  0.6 3.1 %collective-permute-start = (bf16[16,4096]{1,0:T(8,128)(2,1)}, bf16[16,4096]{1,0:T(8,128)(2,1)S(1)}, u32[]{:S(2)}, u32[]{:S(2)}) collective-permute-start(bf16[16,4096]{1,0:T(8,128)(2,1)} %refs_0_.1), channel_id=1, source_target_pairs={{2,0},{3,1},{0,4},{1,5},{4,8},{5,9},{8,12},{9,13},{12,14},{13,15},... | collective-permute-start | bytes 393224 | tf_op jit(solution)/shard_map/ppermute | solution.py:46
  3.7 0.0 collective-permute-start.1
  3.7 1.0 %copy-done = bf16[16,4096]{1,0:T(8,128)(2,1)S(1)} copy-done((bf16[16,4096]{1,0:T(8,128)(2,1)S(1)}, bf16[16,4096]{1,0:T(8,128)(2,1)}, u32[]{:S(2)}) %copy-start) | copy-done | bytes 131096
  4.7 2.8 %fetch.4 = (bf16[4096,512]{1,0:T(8,128)(2,1)S(1)}, f32[8,128]{1,0:T(8,128)}) custom-call(bf16[4096,512]{1,0:T(8,128)(2,1)} %far.4, bf16[16,4096]{1,0:T(8,128)(2,1)S(1)} %copy-done), custom_call_target="tpu_custom_call" | custom-call | bytes 8388608 | tf_op jit(solution)/shard_map/fetch/pallas_call | solution.py:139
  7.5 0.0 collective-permute-done.after.refs_1_
  7.5 2.0 %collective-permute-start.2 = (bf16[16,4096]{1,0:T(8,128)(2,1)S(1)}, bf16[16,4096]{1,0:T(8,128)(2,1)S(1)}, u32[]{:S(2)}, u32[]{:S(2)}) collective-permute-start(bf16[16,4096]{1,0:T(8,128)(2,1)S(1)} %collective-permute-done.after.refs_1_), channel_id=1, source_target_pairs={{2,0},{3,1},{0,4},{1,5},{4,8},{5,9},{8,12},{9,13},{12,14},{13,15},... | collective-permute-start | bytes 393224 | tf_op jit(solution)/shard_map/ppermute | solution.py:46
  9.6 0.0 collective-permute-done.1.refs_2_
  9.6 0.0 collective-permute-start.3
  9.6 2.8 %fetch.5 = (f32[4096,512]{1,0:T(8,128)S(1)}, f32[8,128]{1,0:T(8,128)}) custom-call(bf16[4096,512]{1,0:T(8,128)(2,1)} %far.5, bf16[16,4096]{1,0:T(8,128)(2,1)S(1)} %collective-permute-done.after.refs_1_), custom_call_target="tpu_custom_call" | custom-call | bytes 8388608 | tf_op jit(solution)/shard_map/fetch/pallas_call | solution.py:139
  12.4 0.1 collective-permute-done.2.after.refs_3_
  12.6 2.0 %collective-permute-start.4 = (bf16[16,4096]{1,0:T(8,128)(2,1)S(1)}, bf16[16,4096]{1,0:T(8,128)(2,1)S(1)}, u32[]{:S(2)}, u32[]{:S(2)}) collective-permute-start(bf16[16,4096]{1,0:T(8,128)(2,1)S(1)} %collective-permute-done.2.after.refs_3_), channel_id=1, source_target_pairs={{2,0},{3,1},{0,4},{1,5},{4,8},{5,9},{8,12},{9,13},{12,14},{13,15},... | collective-permute-start | bytes 393224 | tf_op jit(solution)/shard_map/ppermute | solution.py:46
  14.6 0.0 collective-permute-start.7
  14.6 0.5 collective-permute-start.9
  15.1 0.0 collective-permute-start.8
  15.1 0.0 collective-permute-done.3.refs_4_
  15.1 0.1 collective-permute-start.5
  15.1 2.4 %collective-permute-done.4.after.refs_5_ = bf16[16,4096]{1,0:T(8,128)(2,1)S(1)} collective-permute-done((bf16[16,4096]{1,0:T(8,128)(2,1)S(1)}, bf16[16,4096]{1,0:T(8,128)(2,1)S(1)}, u32[]{:S(2)}, u32[]{:S(2)}) %collective-permute-start.4) | collective-permute-done | bytes 131104 | tf_op jit(solution)/shard_map/ppermute | solution.py:46
  17.5 2.0 %collective-permute-start.6 = (bf16[16,4096]{1,0:T(8,128)(2,1)S(1)}, bf16[16,4096]{1,0:T(8,128)(2,1)S(1)}, u32[]{:S(2)}, u32[]{:S(2)}) collective-permute-start(bf16[16,4096]{1,0:T(8,128)(2,1)S(1)} %collective-permute-done.4.after.refs_5_), channel_id=1, source_target_pairs={{2,0},{3,1},{0,4},{1,5},{4,8},{5,9},{8,12},{9,13},{12,14},{13,15},... | collective-permute-start | bytes 393224 | tf_op jit(solution)/shard_map/ppermute | solution.py:46
  19.5 0.0 collective-permute-done.7.refs_8_
  19.5 0.0 collective-permute-start.10
  19.5 0.0 collective-permute-done.9.refs_10_
  19.5 0.5 collective-permute-start.11
  20.0 0.0 collective-permute-done.8.refs_9_
  20.0 0.1 collective-permute-start.12
  20.1 0.9 %collective-permute-done.5.refs_6_ = bf16[16,4096]{1,0:T(8,128)(2,1)S(1)} collective-permute-done((bf16[16,4096]{1,0:T(8,128)(2,1)S(1)}, bf16[16,4096]{1,0:T(8,128)(2,1)S(1)}, u32[]{:S(2)}, u32[]{:S(2)}) %collective-permute-start.5) | collective-permute-done | bytes 131104 | tf_op jit(solution)/shard_map/ppermute | solution.py:46
  21.0 0.0 collective-permute-start.13
  21.0 1.5 %collective-permute-done.6.refs_7_ = bf16[16,4096]{1,0:T(8,128)(2,1)S(1)} collective-permute-done((bf16[16,4096]{1,0:T(8,128)(2,1)S(1)}, bf16[16,4096]{1,0:T(8,128)(2,1)S(1)}, u32[]{:S(2)}, u32[]{:S(2)}) %collective-permute-start.6) | collective-permute-done | bytes 131104 | tf_op jit(solution)/shard_map/ppermute | solution.py:46
  22.5 0.0 collective-permute-start.14
  22.5 2.8 %fetch.6 = (f32[4096,512]{1,0:T(8,128)S(1)}, f32[8,128]{1,0:T(8,128)}) custom-call(bf16[4096,512]{1,0:T(8,128)(2,1)} %far.6, bf16[16,4096]{1,0:T(8,128)(2,1)S(1)} %collective-permute-done.2.after.refs_3_), custom_call_target="tpu_custom_call" | custom-call | bytes 8388608 | tf_op jit(solution)/shard_map/fetch/pallas_call | solution.py:139
  25.3 4.1 %fetch.7 = (f32[4096,512]{1,0:T(8,128)S(1)}, f32[8,128]{1,0:T(8,128)}) custom-call(f32[4096,512]{1,0:T(8,128)} %far.7, bf16[16,4096]{1,0:T(8,128)(2,1)S(1)} %collective-permute-done.4.after.refs_5_), custom_call_target="tpu_custom_call" | custom-call | bytes 8388608 | tf_op jit(solution)/shard_map/fetch/pallas_call | solution.py:139
  29.4 0.0 collective-permute-done.10.refs_11_
  29.4 0.0 collective-permute-done.11.refs_12_
  29.4 0.0 collective-permute-done.12.refs_13_
  29.4 0.0 collective-permute-done.13.refs_14_
  29.4 0.0 collective-permute-done.14.refs_15_
  29.4 15.2 %replay.1 = (bf16[4096,256]{1,0:T(8,128)(2,1)S(1)}, f32[256,512]{1,0:T(8,128)S(1)}, f32[256,512]{1,0:T(8,128)S(1)}, f32[256,512]{1,0:T(8,128)S(1)}, f32[8,256]{1,0:T(8,128)S(1)}) custom-call(bf16[16,4096]{1,0:T(8,128)(2,1)} %refs_0_.1, bf16[16,4096]{1,0:T(8,128)(2,1)S(1)} %collective-permute-done.after.refs_1_, ...), custom_call_target="tpu_custom_call" | custom-call | tf_op jit(solution)/shard_map/replay/pallas_call | solution.py:279
  44.7 2.0 %collective-permute-start.17 = (f32[8,256]{1,0:T(8,128)S(1)}, f32[8,256]{1,0:T(8,128)S(1)}, u32[]{:S(2)}, u32[]{:S(2)}) collective-permute-start(f32[8,256]{1,0:T(8,128)S(1)} %get-tuple-element.29.own), channel_id=1, source_target_pairs={{12,0},{13,1},{14,2},{15,3},{0,4},{1,5},{2,6},{3,7},{4,8},{5,9},{6... | collective-permute-start | bytes 24584 | tf_op jit(solution)/shard_map/ppermute | solution.py:32
  46.7 2.6 %collective-permute-start.16 = (f32[8,256]{1,0:T(8,128)S(1)}, f32[8,256]{1,0:T(8,128)S(1)}, u32[]{:S(2)}, u32[]{:S(2)}) collective-permute-start(f32[8,256]{1,0:T(8,128)S(1)} %get-tuple-element.29.own), channel_id=1, source_target_pairs={{8,0},{9,1},{10,2},{11,3},{12,4},{13,5},{14,6},{15,7},{0,8},{1,9},... | collective-permute-start | bytes 24584 | tf_op jit(solution)/shard_map/ppermute | solution.py:32
  49.3 1.3 %collective-permute-start.15 = (f32[8,256]{1,0:T(8,128)S(1)}, f32[8,256]{1,0:T(8,128)S(1)}, u32[]{:S(2)}, u32[]{:S(2)}) collective-permute-start(f32[8,256]{1,0:T(8,128)S(1)} %get-tuple-element.29.own), channel_id=1, source_target_pairs={{4,0},{5,1},{6,2},{7,3},{8,4},{9,5},{10,6},{11,7},{12,8},{13,9},{1... | collective-permute-start | bytes 24584 | tf_op jit(solution)/shard_map/ppermute | solution.py:32
  50.7 0.0 collective-permute-done.17
  50.7 0.6 collective-permute-done.16
  51.3 1.7 %collective-permute-done.15 = f32[8,256]{1,0:T(8,128)S(1)} collective-permute-done((f32[8,256]{1,0:T(8,128)S(1)}, f32[8,256]{1,0:T(8,128)S(1)}, u32[]{:S(2)}, u32[]{:S(2)}) %collective-permute-start.15) | collective-permute-done | bytes 8224 | tf_op jit(solution)/shard_map/ppermute | solution.py:32
  53.0 1.6 %collective-permute-start.19 = (f32[8,256]{1,0:T(8,128)S(1)}, f32[8,256]{1,0:T(8,128)S(1)}, u32[]{:S(2)}, u32[]{:S(2)}) collective-permute-start(f32[8,256]{1,0:T(8,128)S(1)} %add_add_fusion.s0), channel_id=1, source_target_pairs={{2,0},{3,1},{0,2},{1,3},{6,4},{7,5},{4,6},{5,7},{10,8},{11,9},{8,1... | collective-permute-start | bytes 24584 | tf_op jit(solution)/shard_map/ppermute | solution.py:32
  54.6 0.3 collective-permute-start.18
  54.8 1.2 %collective-permute-done.20.s3 = f32[8,256]{1,0:T(8,128)S(1)} collective-permute-done((f32[8,256]{1,0:T(8,128)S(1)}, f32[8,256]{1,0:T(8,128)S(1)}, u32[]{:S(2)}, u32[]{:S(2)}) %collective-permute-start.20) | collective-permute-done | bytes 8224 | tf_op jit(solution)/shard_map/ppermute | solution.py:32
  56.1 0.6 %collective-permute-done.19.s2 = f32[8,256]{1,0:T(8,128)S(1)} collective-permute-done((f32[8,256]{1,0:T(8,128)S(1)}, f32[8,256]{1,0:T(8,128)S(1)}, u32[]{:S(2)}, u32[]{:S(2)}) %collective-permute-start.19) | collective-permute-done | bytes 8224 | tf_op jit(solution)/shard_map/ppermute | solution.py:32
  56.7 0.0 collective-permute-done.18.s1
  56.7 4.3 %theta.1 = (f32[4096,512]{1,0:T(8,128)}, f32[1,16]{1,0:T(1,128)}) custom-call(f32[8,256]{1,0:T(8,128)S(1)} %add_add_fusion.s0, f32[8,256]{1,0:T(8,128)S(1)} %collective-permute-done.18.s1, f32[8,256]{1,0:T(8,128)S(1)} %collective-permute-done.19.s2, f32[8,256]{1,0:T(8,128)S(1)} %collective-permute-done.20.s3, f32[8,256]{1,0:T(8,128)S(1)} %get-tuple-element.29.own, ...), custom_call_target="tpu_custom_call" | custom-call | tf_op jit(solution)/shard_map/theta/pallas_call | solution.py:355
  (5 shorter events, 0.0 us)
Async XLA Ops:
  0.6 6.9 %collective-permute-start = (bf16[16,4096]{1,0:T(8,128)(2,1)}, bf16[16,4096]{1,0:T(8,128)(2,1)S(1)}, u32[]{:S(2)}, u32[]{:S(2)}) collective-permute-start(bf16[16,4096]{1,0:T(8,128)(2,1)} %refs_0_.1), channel_id=1, source_target_pairs={{2,0},{3,1},{0,4},{1,5},{4,8},{5,9},{8,12},{9,13},{12,14},{13,15},... | collective-permute-start | bytes 393224 | tf_op jit(solution)/shard_map/ppermute | solution.py:46
  3.7 5.9 %collective-permute-start.1 = (bf16[16,4096]{1,0:T(8,128)(2,1)}, bf16[16,4096]{1,0:T(8,128)(2,1)S(1)}, u32[]{:S(2)}, u32[]{:S(2)}) collective-permute-start(bf16[16,4096]{1,0:T(8,128)(2,1)} %refs_0_.1), channel_id=1, source_target_pairs={{4,0},{5,1},{8,4},{9,5},{12,8},{13,9},{14,12},{15,13},{10,14},{11,... | collective-permute-start | bytes 393224 | tf_op jit(solution)/shard_map/ppermute | solution.py:46
  3.7 1.0 %copy-start = (bf16[16,4096]{1,0:T(8,128)(2,1)S(1)}, bf16[16,4096]{1,0:T(8,128)(2,1)}, u32[]{:S(2)}) copy-start(bf16[16,4096]{1,0:T(8,128)(2,1)} %refs_0_.1) | copy-start | bytes 393220
  4.7 9.9 %copy-start.1 = (bf16[16,4096]{1,0:T(8,128)(2,1)S(1)}, bf16[16,4096]{1,0:T(8,128)(2,1)}, u32[]{:S(2)}) copy-start(bf16[16,4096]{1,0:T(8,128)(2,1)} %refs_0_.1) | copy-start | bytes 393220
  7.5 5.0 %collective-permute-start.2 = (bf16[16,4096]{1,0:T(8,128)(2,1)S(1)}, bf16[16,4096]{1,0:T(8,128)(2,1)S(1)}, u32[]{:S(2)}, u32[]{:S(2)}) collective-permute-start(bf16[16,4096]{1,0:T(8,128)(2,1)S(1)} %collective-permute-done.after.refs_1_), channel_id=1, source_target_pairs={{2,0},{3,1},{0,4},{1,5},{4,8},{5,9},{8,12},{9,13},{12,14},{13,15},... | collective-permute-start | bytes 393224 | tf_op jit(solution)/shard_map/ppermute | solution.py:46
  9.6 5.5 %collective-permute-start.3 = (bf16[16,4096]{1,0:T(8,128)(2,1)S(1)}, bf16[16,4096]{1,0:T(8,128)(2,1)S(1)}, u32[]{:S(2)}, u32[]{:S(2)}) collective-permute-start(bf16[16,4096]{1,0:T(8,128)(2,1)S(1)} %collective-permute-done.1.refs_2_), channel_id=1, source_target_pairs={{4,0},{5,1},{8,4},{9,5},{12,8},{13,9},{14,12},{15,13},{10,14},{11,... | collective-permute-start | bytes 393224 | tf_op jit(solution)/shard_map/ppermute | solution.py:46
  12.6 5.0 %collective-permute-start.4 = (bf16[16,4096]{1,0:T(8,128)(2,1)S(1)}, bf16[16,4096]{1,0:T(8,128)(2,1)S(1)}, u32[]{:S(2)}, u32[]{:S(2)}) collective-permute-start(bf16[16,4096]{1,0:T(8,128)(2,1)S(1)} %collective-permute-done.2.after.refs_3_), channel_id=1, source_target_pairs={{2,0},{3,1},{0,4},{1,5},{4,8},{5,9},{8,12},{9,13},{12,14},{13,15},... | collective-permute-start | bytes 393224 | tf_op jit(solution)/shard_map/ppermute | solution.py:46
  14.6 5.0 %collective-permute-start.7 = (bf16[16,4096]{1,0:T(8,128)(2,1)S(1)}, bf16[16,4096]{1,0:T(8,128)(2,1)S(1)}, u32[]{:S(2)}, u32[]{:S(2)}) collective-permute-start(bf16[16,4096]{1,0:T(8,128)(2,1)S(1)} %copy-done.1), channel_id=1, source_target_pairs={{1,0},{0,1},{3,2},{2,3},{5,4},{4,5},{7,6},{6,7},{9,8},{8,9},{11,10... | collective-permute-start | bytes 393224 | tf_op jit(solution)/shard_map/ppermute | solution.py:32
  14.6 5.0 %collective-permute-start.9 = (bf16[16,4096]{1,0:T(8,128)(2,1)S(1)}, bf16[16,4096]{1,0:T(8,128)(2,1)S(1)}, u32[]{:S(2)}, u32[]{:S(2)}) collective-permute-start(bf16[16,4096]{1,0:T(8,128)(2,1)S(1)} %collective-permute-done.1.refs_2_), channel_id=1, source_target_pairs={{1,0},{0,1},{3,2},{2,3},{5,4},{4,5},{7,6},{6,7},{9,8},{8,9},{11,10... | collective-permute-start | bytes 393224 | tf_op jit(solution)/shard_map/ppermute | solution.py:32
  15.1 5.0 %collective-permute-start.8 = (bf16[16,4096]{1,0:T(8,128)(2,1)S(1)}, bf16[16,4096]{1,0:T(8,128)(2,1)S(1)}, u32[]{:S(2)}, u32[]{:S(2)}) collective-permute-start(bf16[16,4096]{1,0:T(8,128)(2,1)S(1)} %collective-permute-done.after.refs_1_), channel_id=1, source_target_pairs={{1,0},{0,1},{3,2},{2,3},{5,4},{4,5},{7,6},{6,7},{9,8},{8,9},{11,10... | collective-permute-start | bytes 393224 | tf_op jit(solution)/shard_map/ppermute | solution.py:32
  15.1 5.9 %collective-permute-start.5 = (bf16[16,4096]{1,0:T(8,128)(2,1)S(1)}, bf16[16,4096]{1,0:T(8,128)(2,1)S(1)}, u32[]{:S(2)}, u32[]{:S(2)}) collective-permute-start(bf16[16,4096]{1,0:T(8,128)(2,1)S(1)} %collective-permute-done.3.refs_4_), channel_id=1, source_target_pairs={{4,0},{5,1},{8,4},{9,5},{12,8},{13,9},{14,12},{15,13},{10,14},{11,... | collective-permute-start | bytes 393224 | tf_op jit(solution)/shard_map/ppermute | solution.py:46
  17.5 5.0 %collective-permute-start.6 = (bf16[16,4096]{1,0:T(8,128)(2,1)S(1)}, bf16[16,4096]{1,0:T(8,128)(2,1)S(1)}, u32[]{:S(2)}, u32[]{:S(2)}) collective-permute-start(bf16[16,4096]{1,0:T(8,128)(2,1)S(1)} %collective-permute-done.4.after.refs_5_), channel_id=1, source_target_pairs={{2,0},{3,1},{0,4},{1,5},{4,8},{5,9},{8,12},{9,13},{12,14},{13,15},... | collective-permute-start | bytes 393224 | tf_op jit(solution)/shard_map/ppermute | solution.py:46
  19.5 9.9 %collective-permute-start.10 = (bf16[16,4096]{1,0:T(8,128)(2,1)S(1)}, bf16[16,4096]{1,0:T(8,128)(2,1)S(1)}, u32[]{:S(2)}, u32[]{:S(2)}) collective-permute-start(bf16[16,4096]{1,0:T(8,128)(2,1)S(1)} %collective-permute-done.2.after.refs_3_), channel_id=1, source_target_pairs={{1,0},{0,1},{3,2},{2,3},{5,4},{4,5},{7,6},{6,7},{9,8},{8,9},{11,10... | collective-permute-start | bytes 393224 | tf_op jit(solution)/shard_map/ppermute | solution.py:32
  19.5 9.9 %collective-permute-start.11 = (bf16[16,4096]{1,0:T(8,128)(2,1)S(1)}, bf16[16,4096]{1,0:T(8,128)(2,1)S(1)}, u32[]{:S(2)}, u32[]{:S(2)}) collective-permute-start(bf16[16,4096]{1,0:T(8,128)(2,1)S(1)} %collective-permute-done.3.refs_4_), channel_id=1, source_target_pairs={{1,0},{0,1},{3,2},{2,3},{5,4},{4,5},{7,6},{6,7},{9,8},{8,9},{11,10... | collective-permute-start | bytes 393224 | tf_op jit(solution)/shard_map/ppermute | solution.py:32
  20.0 9.4 %collective-permute-start.12 = (bf16[16,4096]{1,0:T(8,128)(2,1)S(1)}, bf16[16,4096]{1,0:T(8,128)(2,1)S(1)}, u32[]{:S(2)}, u32[]{:S(2)}) collective-permute-start(bf16[16,4096]{1,0:T(8,128)(2,1)S(1)} %collective-permute-done.4.after.refs_5_), channel_id=1, source_target_pairs={{1,0},{0,1},{3,2},{2,3},{5,4},{4,5},{7,6},{6,7},{9,8},{8,9},{11,10... | collective-permute-start | bytes 393224 | tf_op jit(solution)/shard_map/ppermute | solution.py:32
  21.0 8.4 %collective-permute-start.13 = (bf16[16,4096]{1,0:T(8,128)(2,1)S(1)}, bf16[16,4096]{1,0:T(8,128)(2,1)S(1)}, u32[]{:S(2)}, u32[]{:S(2)}) collective-permute-start(bf16[16,4096]{1,0:T(8,128)(2,1)S(1)} %collective-permute-done.5.refs_6_), channel_id=1, source_target_pairs={{1,0},{0,1},{3,2},{2,3},{5,4},{4,5},{7,6},{6,7},{9,8},{8,9},{11,10... | collective-permute-start | bytes 393224 | tf_op jit(solution)/shard_map/ppermute | solution.py:32
  22.5 6.9 %collective-permute-start.14 = (bf16[16,4096]{1,0:T(8,128)(2,1)S(1)}, bf16[16,4096]{1,0:T(8,128)(2,1)S(1)}, u32[]{:S(2)}, u32[]{:S(2)}) collective-permute-start(bf16[16,4096]{1,0:T(8,128)(2,1)S(1)} %collective-permute-done.6.refs_7_), channel_id=1, source_target_pairs={{1,0},{0,1},{3,2},{2,3},{5,4},{4,5},{7,6},{6,7},{9,8},{8,9},{11,10... | collective-permute-start | bytes 393224 | tf_op jit(solution)/shard_map/ppermute | solution.py:32
  44.7 6.0 %collective-permute-start.17 = (f32[8,256]{1,0:T(8,128)S(1)}, f32[8,256]{1,0:T(8,128)S(1)}, u32[]{:S(2)}, u32[]{:S(2)}) collective-permute-start(f32[8,256]{1,0:T(8,128)S(1)} %get-tuple-element.29.own), channel_id=1, source_target_pairs={{12,0},{13,1},{14,2},{15,3},{0,4},{1,5},{2,6},{3,7},{4,8},{5,9},{6... | collective-permute-start | bytes 24584 | tf_op jit(solution)/shard_map/ppermute | solution.py:32
  46.7 4.5 %collective-permute-start.16 = (f32[8,256]{1,0:T(8,128)S(1)}, f32[8,256]{1,0:T(8,128)S(1)}, u32[]{:S(2)}, u32[]{:S(2)}) collective-permute-start(f32[8,256]{1,0:T(8,128)S(1)} %get-tuple-element.29.own), channel_id=1, source_target_pairs={{8,0},{9,1},{10,2},{11,3},{12,4},{13,5},{14,6},{15,7},{0,8},{1,9},... | collective-permute-start | bytes 24584 | tf_op jit(solution)/shard_map/ppermute | solution.py:32
  49.3 3.7 %collective-permute-start.15 = (f32[8,256]{1,0:T(8,128)S(1)}, f32[8,256]{1,0:T(8,128)S(1)}, u32[]{:S(2)}, u32[]{:S(2)}) collective-permute-start(f32[8,256]{1,0:T(8,128)S(1)} %get-tuple-element.29.own), channel_id=1, source_target_pairs={{4,0},{5,1},{6,2},{7,3},{8,4},{9,5},{10,6},{11,7},{12,8},{13,9},{1... | collective-permute-start | bytes 24584 | tf_op jit(solution)/shard_map/ppermute | solution.py:32
  53.0 3.1 %collective-permute-start.20 = (f32[8,256]{1,0:T(8,128)S(1)}, f32[8,256]{1,0:T(8,128)S(1)}, u32[]{:S(2)}, u32[]{:S(2)}) collective-permute-start(f32[8,256]{1,0:T(8,128)S(1)} %add_add_fusion.s0), channel_id=1, source_target_pairs={{3,0},{2,1},{1,2},{0,3},{7,4},{6,5},{5,6},{4,7},{11,8},{10,9},{9,1... | collective-permute-start | bytes 24584 | tf_op jit(solution)/shard_map/ppermute | solution.py:32
  53.0 3.7 %collective-permute-start.19 = (f32[8,256]{1,0:T(8,128)S(1)}, f32[8,256]{1,0:T(8,128)S(1)}, u32[]{:S(2)}, u32[]{:S(2)}) collective-permute-start(f32[8,256]{1,0:T(8,128)S(1)} %add_add_fusion.s0), channel_id=1, source_target_pairs={{2,0},{3,1},{0,2},{1,3},{6,4},{7,5},{4,6},{5,7},{10,8},{11,9},{8,1... | collective-permute-start | bytes 24584 | tf_op jit(solution)/shard_map/ppermute | solution.py:32
  54.6 2.1 %collective-permute-start.18 = (f32[8,256]{1,0:T(8,128)S(1)}, f32[8,256]{1,0:T(8,128)S(1)}, u32[]{:S(2)}, u32[]{:S(2)}) collective-permute-start(f32[8,256]{1,0:T(8,128)S(1)} %add_add_fusion.s0), channel_id=1, source_target_pairs={{1,0},{0,1},{3,2},{2,3},{5,4},{4,5},{7,6},{6,7},{9,8},{8,9},{11,10... | collective-permute-start | bytes 24584 | tf_op jit(solution)/shard_map/ppermute | solution.py:32

commit v5 on v4

--- a/solution.py
+++ b/solution.py
@@ -10,7 +10,7 @@
 TILE = 512
 ROWS = 16
 SAMPLE = 256
-VMEM_BYTES = 12 << 20
+VMEM_BYTES = 16 << 20
 RATIO = 0.1 / 0.05**0.5
 
 
@@ -18,18 +18,8 @@
     return jnp.dot(a, b, preferred_element_type=jnp.float32)
 
 
-def digits(n):
-    return (n // 4, 2, 2)
-
-
-def shift(value, n, slow, mid, core):
-    z, y, c = digits(n)
-    pairs = []
-    for d in range(n):
-        dz, dy, dc = d // (y * c), d // c % y, d % c
-        source = ((dz + slow) % z * y + (dy + mid) % y) * c + (dc + core) % c
-        pairs.append((source, d))
-    return lax.ppermute(value, "dp", pairs)
+def swapped(value, n, mask):
+    return lax.ppermute(value, "dp", [(d ^ mask, d) for d in range(n)])
 
 
 def ring(n):
@@ -64,7 +54,7 @@
             result, token = errands[len(done)](parts[hop - 1, 0])
             done.append(result)
     for back, core in list(parts):
-        parts[back, 1] = shift(parts[back, core], n, 0, 0, 1)
+        parts[back, 1] = swapped(parts[back, core], n, 1)
     return parts, done
 
 
@@ -83,11 +73,10 @@
 
 
 def all_sum(value, n):
-    z, y, c = digits(n)
     total = value
-    for slow in range(1, z):
-        total = total + shift(value, n, slow, 0, 0)
-    return [total] + [shift(total, n, 0, a, b) for a, b in ((0, 1), (1, 0), (1, 1))]
+    for mask in range(4, n, 4):
+        total = total + swapped(value, n, mask)
+    return [total] + [swapped(total, n, mask) for mask in (1, 2, 3)]
 
 
 def over_columns(row):
@@ -105,7 +94,7 @@
 
 def update(grad, one, two):
     first = one + grad
-    second = two + grad * grad
+    second = 19.0 * two.astype(jnp.float32) + grad * grad
     over = lax.rsqrt(second)
     inv = pltpu.reciprocal(second * over + 1e-08 / 0.05**0.5, approx=True)
     return over, inv, first * inv
@@ -150,10 +139,10 @@
 
 def replay_kernel(steps, *refs):
     n = len(steps)
-    parts, far = refs[:n], refs[n : n + 2]
-    (weight, one, two, adjoint) = refs[n + 2 : n + 6]
-    (turned, along, across, bend, stats) = refs[n + 6 : n + 11]
-    (tokens, scaled, score, g0, g1, a0, a1, b0, b1, sums, cot, token_weight, part_sem) = refs[n + 11 :]
+    parts, far, (weight, one) = refs[:n], refs[n : n + 4], refs[n + 4 : n + 6]
+    (adjoint, turned, along, across, bend, stats) = refs[n + 6 : n + 12]
+    (tokens, scaled, score, g0, g1, a0, a1, b0, b1, sums) = refs[n + 12 : n + 22]
+    (two, cot, token_weight, part_sem, tile_sem) = refs[n + 22 :]
     grads, firsts, seconds = (g0, g1), (a0, a1), (b0, b1)
     height, depth = parts[0].shape
     count, width = cot.shape
@@ -171,6 +160,11 @@
     small = [
         pltpu.make_async_copy(far[k], ref, part_sem.at[n + k]) for k, ref in enumerate((cot, token_weight))
     ]
+
+    near = (two, adjoint)
+
+    def tile_copy(which, i):
+        return pltpu.make_async_copy(far[2 + which].at[span(i), :], near[which].at[span(i), :], tile_sem.at[which, i])
 
     for part in range(n):
         part_copy(part).start()
@@ -183,6 +177,8 @@
     across[...] = jnp.zeros_like(across)
 
     def gate_step(i, _):
+        tile_copy(0, i).start()
+        tile_copy(1, i).start()
         here = tokens[:, span(i)]
         along[...] += f32dot(here, weight[span(i), :])
         turned[span(i), :] = here.T
@@ -215,7 +211,12 @@
         at = pl.ds(pl.multiple_of(i * TILE + r, ROWS), ROWS)
         return grads[slot][r : r + ROWS, :], one[at, :], two[at, :], adjoint[at, :]
 
+    def arrive(i):
+        tile_copy(0, i).wait()
+        tile_copy(1, i).wait()
+
     grad_tile(0, 0)
+    arrive(0)
     sq = jnp.zeros((8, width), jnp.float32)
     cross = jnp.zeros((8, width), jnp.float32)
     for r in range(0, SAMPLE, ROWS):
@@ -230,6 +231,8 @@
     sums[...] = jnp.zeros_like(sums)
 
     def update_tile(i, slot):
+        if not isinstance(i, int) or i > 0:
+            arrive(i)
         sq, cross = sums[0], sums[1]
         for r in range(0, TILE, ROWS):
             g, m1, m2, adj = rows_of(i, slot, r)
@@ -268,7 +271,7 @@
     stats[4:8, :] = jnp.broadcast_to(guess, (4, count))
 
 
-def replay_call(parts, cot, token_weight, weight, one, two, adjoint):
+def replay_call(parts, cot, token_weight, two, adjoint, weight, one):
     steps = list(parts)
     n = len(steps)
     depth = weight.shape[0]
@@ -278,9 +281,10 @@
     block = lambda dtype: pltpu.VMEM((TILE, width), dtype)
     return pl.pallas_call(
         functools.partial(replay_kernel, steps),
-        in_specs=[far] * (n + 2) + [vmem] * 4,
-        out_specs=[vmem] * 5,
+        in_specs=[far] * (n + 4) + [vmem] * 2,
+        out_specs=[vmem] * 6,
         out_shape=[
+            pltpu.VMEM((depth, width), jnp.float32),
             pltpu.VMEM((depth, count), jnp.bfloat16),
             pltpu.VMEM((count, width), jnp.float32),
             pltpu.VMEM((count, width), jnp.float32),
@@ -298,19 +302,19 @@
             block(jnp.bfloat16),
             block(jnp.bfloat16),
             pltpu.VMEM((2, 8, width), jnp.float32),
+            pltpu.VMEM((depth, width), jnp.bfloat16),
             pltpu.VMEM((count, width), jnp.bfloat16),
             pltpu.VMEM((1, count), jnp.float32),
             pltpu.SemaphoreType.DMA((n + 2,)),
+            pltpu.SemaphoreType.DMA((2, depth // TILE)),
         ],
         compiler_params=pltpu.CompilerParams(vmem_limit_bytes=VMEM_BYTES),
         name="replay",
     )(
         *[in_hbm(x) if step == (0, 0) else x for step, x in parts.items()],
-        *[in_hbm(x) for x in (cot, token_weight)],
+        *[in_hbm(x) for x in (cot, token_weight, two, adjoint)],
         weight,
         one,
-        two,
-        adjoint,
     )
 
 
@@ -371,12 +375,10 @@
     errands = [
         lambda after: fetch(weight, after),
         lambda after: fetch(moment_one, after, 9.0),
-        lambda after: fetch(moment_two, after, 19.0),
-        lambda after: fetch(adjoint, after),
     ]
-    parts, (weight_near, one, two, adjoint_near) = gather(tokens, n, errands)
-    turned, along, across, bend, stats = replay_call(
-        parts, cotangent, token_weight.reshape(1, -1), weight_near, one, two, adjoint_near
+    parts, (weight_near, one_near) = gather(tokens, n, errands)
+    adjoint_near, turned, along, across, bend, stats = replay_call(
+        parts, cotangent, token_weight.reshape(1, -1), moment_two, adjoint, weight_near, one_near
     )
     sums = all_sum(stats, n)
     theta_bar, scores = theta_call(n, entries, sums, stats, along, across, bend, turned, adjoint_near)

time: 61.2 us -> 58.3 us (0.953)
  Pallas kernels: 32.1 us -> 27.5 us
  waiting for transfers between devices: 9.09 us -> 12 us
  starting transfers between devices: 18.1 us -> 16.9 us
    pallas_call x4 -> x2, Pallas kernels: 12.5 us -> 5.65 us  [fetch(): pl.pallas_call(functools.partial(fetch_kernel, factor), in_specs=[pl.Bloc...]
    ppermute x14, waiting for transfers between devices: 4.18 us -> 7.11 us  [swapped(): return lax.ppermute(value, 'dp', [(d ^ mask, d) for d in range(n)])]
    pallas_call x1, Pallas kernels: 15.2 us -> 17.5 us  [replay_call(): pl.pallas_call(functools.partial(replay_kernel, steps), in_specs=[far] *...]
    ppermute x14, starting transfers between devices: 8.94 us -> 7.74 us  [swapped(): return lax.ppermute(value, 'dp', [(d ^ mask, d) for d in range(n)])]
  transfers between devices with their start and end apart: 21 -> 21, of which waited for: 8 -> 9; matrix products, arithmetic and copies ran while one was open for 0% -> 0% of each run, Pallas kernels for 21% -> 10%
where the time goes in v5:
time: 58.3 us; the launch traced here: 58.1 us
  Pallas kernels  27.5 us (47%)
  starting transfers between devices  16.9 us (29%)
  waiting for transfers between devices  12 us (21%)
  local copies, waits for them, and re-layouts  0.97 us (2%)
  between operations  0.71 us (1%)
    pallas_call x1, Pallas kernels, replay_call(): pl.pallas_call(functools.partial(replay_kernel, steps), in_specs=[far] *...  17.5 us
    ppermute x7, starting transfers between devices, along_ring(): return lax.ppermute(value, 'dp', pairs)  9.2 us
    ppermute x14, starting transfers between devices, swapped(): return lax.ppermute(value, 'dp', [(d ^ mask, d) for d in range(n)])  7.74 us
    ppermute x14, waiting for transfers between devices, swapped(): return lax.ppermute(value, 'dp', [(d ^ mask, d) for d in range(n)])  7.11 us
    pallas_call x2, Pallas kernels, fetch(): pl.pallas_call(functools.partial(fetch_kernel, factor), in_specs=[pl.Bloc...  5.65 us
    ppermute x7, waiting for transfers between devices, along_ring(): return lax.ppermute(value, 'dp', pairs)  4.91 us
    pallas_call x1, Pallas kernels, theta_call(): pl.pallas_call(functools.partial(theta_kernel, n, entries), in_specs=[vme...  4.3 us
  transfers between devices with their start and end apart: 21, of which 9 were waited for; matrix products, arithmetic and copies ran while one was open for 0% of the time, Pallas kernels for 10%

profile of v5, /device:TPU:0, one launch (start us, length us, event | category | flops | bytes accessed | tf_op | source)
XLA Modules:
  0.0 58.1 jit_solution(6151207008755690035)
XLA Ops:
  0.6 3.1 %collective-permute-start = (bf16[16,4096]{1,0:T(8,128)(2,1)}, bf16[16,4096]{1,0:T(8,128)(2,1)S(1)}, u32[]{:S(2)}, u32[]{:S(2)}) collective-permute-start(bf16[16,4096]{1,0:T(8,128)(2,1)} %refs_0_.1), channel_id=1, source_target_pairs={{2,0},{3,1},{0,4},{1,5},{4,8},{5,9},{8,12},{9,13},{12,14},{13,15},... | collective-permute-start | bytes 393224 | tf_op jit(solution)/shard_map/ppermute | solution.py:36
  3.7 0.0 collective-permute-start.1
  3.7 1.0 %copy-done = bf16[16,4096]{1,0:T(8,128)(2,1)S(1)} copy-done((bf16[16,4096]{1,0:T(8,128)(2,1)S(1)}, bf16[16,4096]{1,0:T(8,128)(2,1)}, u32[]{:S(2)}) %copy-start) | copy-done | bytes 131096
  4.7 2.8 %fetch.2 = (bf16[4096,512]{1,0:T(8,128)(2,1)S(1)}, f32[8,128]{1,0:T(8,128)}) custom-call(bf16[4096,512]{1,0:T(8,128)(2,1)} %far.2, bf16[16,4096]{1,0:T(8,128)(2,1)S(1)} %copy-done), custom_call_target="tpu_custom_call" | custom-call | bytes 8388608 | tf_op jit(solution)/shard_map/fetch/pallas_call | solution.py:128
  7.5 0.0 collective-permute-done.after.refs_1_
  7.5 2.0 %collective-permute-start.2 = (bf16[16,4096]{1,0:T(8,128)(2,1)S(1)}, bf16[16,4096]{1,0:T(8,128)(2,1)S(1)}, u32[]{:S(2)}, u32[]{:S(2)}) collective-permute-start(bf16[16,4096]{1,0:T(8,128)(2,1)S(1)} %collective-permute-done.after.refs_1_), channel_id=1, source_target_pairs={{2,0},{3,1},{0,4},{1,5},{4,8},{5,9},{8,12},{9,13},{12,14},{13,15},... | collective-permute-start | bytes 393224 | tf_op jit(solution)/shard_map/ppermute | solution.py:36
  9.6 0.0 collective-permute-done.1.refs_2_
  9.6 0.0 collective-permute-start.3
  9.6 2.8 %fetch.3 = (f32[4096,512]{1,0:T(8,128)S(1)}, f32[8,128]{1,0:T(8,128)}) custom-call(bf16[4096,512]{1,0:T(8,128)(2,1)} %far.3, bf16[16,4096]{1,0:T(8,128)(2,1)S(1)} %collective-permute-done.after.refs_1_), custom_call_target="tpu_custom_call" | custom-call | bytes 8388608 | tf_op jit(solution)/shard_map/fetch/pallas_call | solution.py:128
  12.4 0.1 collective-permute-done.2.refs_3_
  12.6 2.0 %collective-permute-start.4 = (bf16[16,4096]{1,0:T(8,128)(2,1)S(1)}, bf16[16,4096]{1,0:T(8,128)(2,1)S(1)}, u32[]{:S(2)}, u32[]{:S(2)}) collective-permute-start(bf16[16,4096]{1,0:T(8,128)(2,1)S(1)} %collective-permute-done.2.refs_3_), channel_id=1, source_target_pairs={{2,0},{3,1},{0,4},{1,5},{4,8},{5,9},{8,12},{9,13},{12,14},{13,15},... | collective-permute-start | bytes 393224 | tf_op jit(solution)/shard_map/ppermute | solution.py:36
  14.6 0.0 copy-done.1
  14.6 0.0 collective-permute-start.7
  14.6 0.5 collective-permute-start.9
  15.1 0.0 collective-permute-start.8
  15.1 0.0 collective-permute-done.3.refs_4_
  15.1 0.1 collective-permute-start.5
  15.1 2.4 %collective-permute-done.4.refs_5_ = bf16[16,4096]{1,0:T(8,128)(2,1)S(1)} collective-permute-done((bf16[16,4096]{1,0:T(8,128)(2,1)S(1)}, bf16[16,4096]{1,0:T(8,128)(2,1)S(1)}, u32[]{:S(2)}, u32[]{:S(2)}) %collective-permute-start.4) | collective-permute-done | bytes 131104 | tf_op jit(solution)/shard_map/ppermute | solution.py:36
  17.5 2.0 %collective-permute-start.6 = (bf16[16,4096]{1,0:T(8,128)(2,1)S(1)}, bf16[16,4096]{1,0:T(8,128)(2,1)S(1)}, u32[]{:S(2)}, u32[]{:S(2)}) collective-permute-start(bf16[16,4096]{1,0:T(8,128)(2,1)S(1)} %collective-permute-done.4.refs_5_), channel_id=1, source_target_pairs={{2,0},{3,1},{0,4},{1,5},{4,8},{5,9},{8,12},{9,13},{12,14},{13,15},... | collective-permute-start | bytes 393224 | tf_op jit(solution)/shard_map/ppermute | solution.py:36
  19.5 0.0 collective-permute-done.7.refs_8_
  19.5 0.0 collective-permute-start.10
  19.5 0.0 collective-permute-done.9.refs_10_
  19.5 0.5 collective-permute-start.11
  20.0 0.0 collective-permute-done.8.refs_9_
  20.0 0.1 collective-permute-start.12
  20.1 0.9 %collective-permute-done.5.refs_6_ = bf16[16,4096]{1,0:T(8,128)(2,1)S(1)} collective-permute-done((bf16[16,4096]{1,0:T(8,128)(2,1)S(1)}, bf16[16,4096]{1,0:T(8,128)(2,1)S(1)}, u32[]{:S(2)}, u32[]{:S(2)}) %collective-permute-start.5) | collective-permute-done | bytes 131104 | tf_op jit(solution)/shard_map/ppermute | solution.py:36
  21.0 0.0 collective-permute-start.13
  21.0 1.5 %collective-permute-done.6.refs_7_ = bf16[16,4096]{1,0:T(8,128)(2,1)S(1)} collective-permute-done((bf16[16,4096]{1,0:T(8,128)(2,1)S(1)}, bf16[16,4096]{1,0:T(8,128)(2,1)S(1)}, u32[]{:S(2)}, u32[]{:S(2)}) %collective-permute-start.6) | collective-permute-done | bytes 131104 | tf_op jit(solution)/shard_map/ppermute | solution.py:36
  22.5 0.0 collective-permute-start.14
  22.5 0.0 collective-permute-done.10.refs_11_
  22.5 0.0 collective-permute-done.11.refs_12_
  22.5 0.0 collective-permute-done.12.refs_13_
  22.5 0.0 collective-permute-done.13.refs_14_
  22.5 1.3 %collective-permute-done.14.refs_15_ = bf16[16,4096]{1,0:T(8,128)(2,1)S(1)} collective-permute-done((bf16[16,4096]{1,0:T(8,128)(2,1)S(1)}, bf16[16,4096]{1,0:T(8,128)(2,1)S(1)}, u32[]{:S(2)}, u32[]{:S(2)}) %collective-permute-start.14) | collective-permute-done | bytes 131104 | tf_op jit(solution)/shard_map/ppermute | solution.py:22
  23.8 17.5 %replay.1 = (f32[4096,512]{1,0:T(8,128)S(1)}, bf16[4096,256]{1,0:T(8,128)(2,1)S(1)}, f32[256,512]{1,0:T(8,128)S(1)}, f32[256,512]{1,0:T(8,128)S(1)}, f32[256,512]{1,0:T(8,128)S(1)}, /*index=5*/f32[8,256]{1,0:T(8,128)S(1)}) custom-call(bf16[16,4096]{1,0:T(8,128)(2,1)} %refs_0_.1, bf16[16,4096]{1,0:T(8,128)(2,1)S(1)} %collective-permute-done.after.refs_1_, ...), custom_call_target="tpu_custom_call" | custom-call | tf_op jit(solution)/shard_map/replay/pallas_call | solution.py:282
  41.4 4.1 %collective-permute-start.17 = (f32[8,256]{1,0:T(8,128)S(1)}, f32[8,256]{1,0:T(8,128)S(1)}, u32[]{:S(2)}, u32[]{:S(2)}) collective-permute-start(f32[8,256]{1,0:T(8,128)S(1)} %get-tuple-element.26.own), channel_id=1, source_target_pairs={{12,0},{13,1},{14,2},{15,3},{8,4},{9,5},{10,6},{11,7},{4,8},{5,9},... | collective-permute-start | bytes 24584 | tf_op jit(solution)/shard_map/ppermute | solution.py:22
  45.4 0.0 collective-permute-start.16
  45.5 0.6 %collective-permute-start.15 = (f32[8,256]{1,0:T(8,128)S(1)}, f32[8,256]{1,0:T(8,128)S(1)}, u32[]{:S(2)}, u32[]{:S(2)}) collective-permute-start(f32[8,256]{1,0:T(8,128)S(1)} %get-tuple-element.26.own), channel_id=1, source_target_pairs={{4,0},{5,1},{6,2},{7,3},{0,4},{1,5},{2,6},{3,7},{12,8},{13,9},{14,... | collective-permute-start | bytes 24584 | tf_op jit(solution)/shard_map/ppermute | solution.py:22
  46.1 1.0 %collective-permute-done.17 = f32[8,256]{1,0:T(8,128)S(1)} collective-permute-done((f32[8,256]{1,0:T(8,128)S(1)}, f32[8,256]{1,0:T(8,128)S(1)}, u32[]{:S(2)}, u32[]{:S(2)}) %collective-permute-start.17) | collective-permute-done | bytes 8224 | tf_op jit(solution)/shard_map/ppermute | solution.py:22
  47.1 2.9 %collective-permute-done.16 = f32[8,256]{1,0:T(8,128)S(1)} collective-permute-done((f32[8,256]{1,0:T(8,128)S(1)}, f32[8,256]{1,0:T(8,128)S(1)}, u32[]{:S(2)}, u32[]{:S(2)}) %collective-permute-start.16) | collective-permute-done | bytes 8224 | tf_op jit(solution)/shard_map/ppermute | solution.py:22
  50.0 0.0 collective-permute-done.15
  50.0 0.1 collective-permute-start.20
  50.1 1.6 %collective-permute-start.19 = (f32[8,256]{1,0:T(8,128)S(1)}, f32[8,256]{1,0:T(8,128)S(1)}, u32[]{:S(2)}, u32[]{:S(2)}) collective-permute-start(f32[8,256]{1,0:T(8,128)S(1)} %add_add_fusion.s0), channel_id=1, source_target_pairs={{2,0},{3,1},{0,2},{1,3},{6,4},{7,5},{4,6},{5,7},{10,8},{11,9},{8,1... | collective-permute-start | bytes 24584 | tf_op jit(solution)/shard_map/ppermute | solution.py:22
  51.7 0.3 collective-permute-start.18
  51.9 1.2 %collective-permute-done.20.s3 = f32[8,256]{1,0:T(8,128)S(1)} collective-permute-done((f32[8,256]{1,0:T(8,128)S(1)}, f32[8,256]{1,0:T(8,128)S(1)}, u32[]{:S(2)}, u32[]{:S(2)}) %collective-permute-start.20) | collective-permute-done | bytes 8224 | tf_op jit(solution)/shard_map/ppermute | solution.py:22
  53.2 0.6 %collective-permute-done.19.s2 = f32[8,256]{1,0:T(8,128)S(1)} collective-permute-done((f32[8,256]{1,0:T(8,128)S(1)}, f32[8,256]{1,0:T(8,128)S(1)}, u32[]{:S(2)}, u32[]{:S(2)}) %collective-permute-start.19) | collective-permute-done | bytes 8224 | tf_op jit(solution)/shard_map/ppermute | solution.py:22
  53.8 0.0 collective-permute-done.18.s1
  53.8 4.3 %theta.1 = (f32[4096,512]{1,0:T(8,128)}, f32[1,16]{1,0:T(1,128)}) custom-call(f32[8,256]{1,0:T(8,128)S(1)} %add_add_fusion.s0, f32[8,256]{1,0:T(8,128)S(1)} %collective-permute-done.18.s1, f32[8,256]{1,0:T(8,128)S(1)} %collective-permute-done.19.s2, f32[8,256]{1,0:T(8,128)S(1)} %collective-permute-done.20.s3, f32[8,256]{1,0:T(8,128)S(1)} %get-tuple-element.26.own, ...), custom_call_target="tpu_custom_call" | custom-call | tf_op jit(solution)/shard_map/theta/pallas_call | solution.py:359
  (3 shorter events, 0.0 us)
Async XLA Ops:
  0.6 6.9 %collective-permute-start = (bf16[16,4096]{1,0:T(8,128)(2,1)}, bf16[16,4096]{1,0:T(8,128)(2,1)S(1)}, u32[]{:S(2)}, u32[]{:S(2)}) collective-permute-start(bf16[16,4096]{1,0:T(8,128)(2,1)} %refs_0_.1), channel_id=1, source_target_pairs={{2,0},{3,1},{0,4},{1,5},{4,8},{5,9},{8,12},{9,13},{12,14},{13,15},... | collective-permute-start | bytes 393224 | tf_op jit(solution)/shard_map/ppermute | solution.py:36
  3.7 5.9 %collective-permute-start.1 = (bf16[16,4096]{1,0:T(8,128)(2,1)}, bf16[16,4096]{1,0:T(8,128)(2,1)S(1)}, u32[]{:S(2)}, u32[]{:S(2)}) collective-permute-start(bf16[16,4096]{1,0:T(8,128)(2,1)} %refs_0_.1), channel_id=1, source_target_pairs={{4,0},{5,1},{8,4},{9,5},{12,8},{13,9},{14,12},{15,13},{10,14},{11,... | collective-permute-start | bytes 393224 | tf_op jit(solution)/shard_map/ppermute | solution.py:36
  3.7 1.0 %copy-start = (bf16[16,4096]{1,0:T(8,128)(2,1)S(1)}, bf16[16,4096]{1,0:T(8,128)(2,1)}, u32[]{:S(2)}) copy-start(bf16[16,4096]{1,0:T(8,128)(2,1)} %refs_0_.1) | copy-start | bytes 393220
  4.7 9.9 %copy-start.1 = (bf16[16,4096]{1,0:T(8,128)(2,1)S(1)}, bf16[16,4096]{1,0:T(8,128)(2,1)}, u32[]{:S(2)}) copy-start(bf16[16,4096]{1,0:T(8,128)(2,1)} %refs_0_.1) | copy-start | bytes 393220
  7.5 5.0 %collective-permute-start.2 = (bf16[16,4096]{1,0:T(8,128)(2,1)S(1)}, bf16[16,4096]{1,0:T(8,128)(2,1)S(1)}, u32[]{:S(2)}, u32[]{:S(2)}) collective-permute-start(bf16[16,4096]{1,0:T(8,128)(2,1)S(1)} %collective-permute-done.after.refs_1_), channel_id=1, source_target_pairs={{2,0},{3,1},{0,4},{1,5},{4,8},{5,9},{8,12},{9,13},{12,14},{13,15},... | collective-permute-start | bytes 393224 | tf_op jit(solution)/shard_map/ppermute | solution.py:36
  9.6 5.5 %collective-permute-start.3 = (bf16[16,4096]{1,0:T(8,128)(2,1)S(1)}, bf16[16,4096]{1,0:T(8,128)(2,1)S(1)}, u32[]{:S(2)}, u32[]{:S(2)}) collective-permute-start(bf16[16,4096]{1,0:T(8,128)(2,1)S(1)} %collective-permute-done.1.refs_2_), channel_id=1, source_target_pairs={{4,0},{5,1},{8,4},{9,5},{12,8},{13,9},{14,12},{15,13},{10,14},{11,... | collective-permute-start | bytes 393224 | tf_op jit(solution)/shard_map/ppermute | solution.py:36
  12.6 5.0 %collective-permute-start.4 = (bf16[16,4096]{1,0:T(8,128)(2,1)S(1)}, bf16[16,4096]{1,0:T(8,128)(2,1)S(1)}, u32[]{:S(2)}, u32[]{:S(2)}) collective-permute-start(bf16[16,4096]{1,0:T(8,128)(2,1)S(1)} %collective-permute-done.2.refs_3_), channel_id=1, source_target_pairs={{2,0},{3,1},{0,4},{1,5},{4,8},{5,9},{8,12},{9,13},{12,14},{13,15},... | collective-permute-start | bytes 393224 | tf_op jit(solution)/shard_map/ppermute | solution.py:36
  14.6 5.0 %collective-permute-start.7 = (bf16[16,4096]{1,0:T(8,128)(2,1)S(1)}, bf16[16,4096]{1,0:T(8,128)(2,1)S(1)}, u32[]{:S(2)}, u32[]{:S(2)}) collective-permute-start(bf16[16,4096]{1,0:T(8,128)(2,1)S(1)} %copy-done.1), channel_id=1, source_target_pairs={{1,0},{0,1},{3,2},{2,3},{5,4},{4,5},{7,6},{6,7},{9,8},{8,9},{11,10... | collective-permute-start | bytes 393224 | tf_op jit(solution)/shard_map/ppermute | solution.py:22
  14.6 5.0 %collective-permute-start.9 = (bf16[16,4096]{1,0:T(8,128)(2,1)S(1)}, bf16[16,4096]{1,0:T(8,128)(2,1)S(1)}, u32[]{:S(2)}, u32[]{:S(2)}) collective-permute-start(bf16[16,4096]{1,0:T(8,128)(2,1)S(1)} %collective-permute-done.1.refs_2_), channel_id=1, source_target_pairs={{1,0},{0,1},{3,2},{2,3},{5,4},{4,5},{7,6},{6,7},{9,8},{8,9},{11,10... | collective-permute-start | bytes 393224 | tf_op jit(solution)/shard_map/ppermute | solution.py:22
  15.1 5.0 %collective-permute-start.8 = (bf16[16,4096]{1,0:T(8,128)(2,1)S(1)}, bf16[16,4096]{1,0:T(8,128)(2,1)S(1)}, u32[]{:S(2)}, u32[]{:S(2)}) collective-permute-start(bf16[16,4096]{1,0:T(8,128)(2,1)S(1)} %collective-permute-done.after.refs_1_), channel_id=1, source_target_pairs={{1,0},{0,1},{3,2},{2,3},{5,4},{4,5},{7,6},{6,7},{9,8},{8,9},{11,10... | collective-permute-start | bytes 393224 | tf_op jit(solution)/shard_map/ppermute | solution.py:22
  15.1 5.9 %collective-permute-start.5 = (bf16[16,4096]{1,0:T(8,128)(2,1)S(1)}, bf16[16,4096]{1,0:T(8,128)(2,1)S(1)}, u32[]{:S(2)}, u32[]{:S(2)}) collective-permute-start(bf16[16,4096]{1,0:T(8,128)(2,1)S(1)} %collective-permute-done.3.refs_4_), channel_id=1, source_target_pairs={{4,0},{5,1},{8,4},{9,5},{12,8},{13,9},{14,12},{15,13},{10,14},{11,... | collective-permute-start | bytes 393224 | tf_op jit(solution)/shard_map/ppermute | solution.py:36
  17.5 5.0 %collective-permute-start.6 = (bf16[16,4096]{1,0:T(8,128)(2,1)S(1)}, bf16[16,4096]{1,0:T(8,128)(2,1)S(1)}, u32[]{:S(2)}, u32[]{:S(2)}) collective-permute-start(bf16[16,4096]{1,0:T(8,128)(2,1)S(1)} %collective-permute-done.4.refs_5_), channel_id=1, source_target_pairs={{2,0},{3,1},{0,4},{1,5},{4,8},{5,9},{8,12},{9,13},{12,14},{13,15},... | collective-permute-start | bytes 393224 | tf_op jit(solution)/shard_map/ppermute | solution.py:36
  19.5 3.0 %collective-permute-start.10 = (bf16[16,4096]{1,0:T(8,128)(2,1)S(1)}, bf16[16,4096]{1,0:T(8,128)(2,1)S(1)}, u32[]{:S(2)}, u32[]{:S(2)}) collective-permute-start(bf16[16,4096]{1,0:T(8,128)(2,1)S(1)} %collective-permute-done.2.refs_3_), channel_id=1, source_target_pairs={{1,0},{0,1},{3,2},{2,3},{5,4},{4,5},{7,6},{6,7},{9,8},{8,9},{11,10... | collective-permute-start | bytes 393224 | tf_op jit(solution)/shard_map/ppermute | solution.py:22
  19.5 3.0 %collective-permute-start.11 = (bf16[16,4096]{1,0:T(8,128)(2,1)S(1)}, bf16[16,4096]{1,0:T(8,128)(2,1)S(1)}, u32[]{:S(2)}, u32[]{:S(2)}) collective-permute-start(bf16[16,4096]{1,0:T(8,128)(2,1)S(1)} %collective-permute-done.3.refs_4_), channel_id=1, source_target_pairs={{1,0},{0,1},{3,2},{2,3},{5,4},{4,5},{7,6},{6,7},{9,8},{8,9},{11,10... | collective-permute-start | bytes 393224 | tf_op jit(solution)/shard_map/ppermute | solution.py:22
  20.0 2.5 %collective-permute-start.12 = (bf16[16,4096]{1,0:T(8,128)(2,1)S(1)}, bf16[16,4096]{1,0:T(8,128)(2,1)S(1)}, u32[]{:S(2)}, u32[]{:S(2)}) collective-permute-start(bf16[16,4096]{1,0:T(8,128)(2,1)S(1)} %collective-permute-done.4.refs_5_), channel_id=1, source_target_pairs={{1,0},{0,1},{3,2},{2,3},{5,4},{4,5},{7,6},{6,7},{9,8},{8,9},{11,10... | collective-permute-start | bytes 393224 | tf_op jit(solution)/shard_map/ppermute | solution.py:22
  21.0 1.5 %collective-permute-start.13 = (bf16[16,4096]{1,0:T(8,128)(2,1)S(1)}, bf16[16,4096]{1,0:T(8,128)(2,1)S(1)}, u32[]{:S(2)}, u32[]{:S(2)}) collective-permute-start(bf16[16,4096]{1,0:T(8,128)(2,1)S(1)} %collective-permute-done.5.refs_6_), channel_id=1, source_target_pairs={{1,0},{0,1},{3,2},{2,3},{5,4},{4,5},{7,6},{6,7},{9,8},{8,9},{11,10... | collective-permute-start | bytes 393224 | tf_op jit(solution)/shard_map/ppermute | solution.py:22
  22.5 1.3 %collective-permute-start.14 = (bf16[16,4096]{1,0:T(8,128)(2,1)S(1)}, bf16[16,4096]{1,0:T(8,128)(2,1)S(1)}, u32[]{:S(2)}, u32[]{:S(2)}) collective-permute-start(bf16[16,4096]{1,0:T(8,128)(2,1)S(1)} %collective-permute-done.6.refs_7_), channel_id=1, source_target_pairs={{1,0},{0,1},{3,2},{2,3},{5,4},{4,5},{7,6},{6,7},{9,8},{8,9},{11,10... | collective-permute-start | bytes 393224 | tf_op jit(solution)/shard_map/ppermute | solution.py:22
  41.4 5.7 %collective-permute-start.17 = (f32[8,256]{1,0:T(8,128)S(1)}, f32[8,256]{1,0:T(8,128)S(1)}, u32[]{:S(2)}, u32[]{:S(2)}) collective-permute-start(f32[8,256]{1,0:T(8,128)S(1)} %get-tuple-element.26.own), channel_id=1, source_target_pairs={{12,0},{13,1},{14,2},{15,3},{8,4},{9,5},{10,6},{11,7},{4,8},{5,9},... | collective-permute-start | bytes 24584 | tf_op jit(solution)/shard_map/ppermute | solution.py:22
  45.4 4.5 %collective-permute-start.16 = (f32[8,256]{1,0:T(8,128)S(1)}, f32[8,256]{1,0:T(8,128)S(1)}, u32[]{:S(2)}, u32[]{:S(2)}) collective-permute-start(f32[8,256]{1,0:T(8,128)S(1)} %get-tuple-element.26.own), channel_id=1, source_target_pairs={{8,0},{9,1},{10,2},{11,3},{12,4},{13,5},{14,6},{15,7},{0,8},{1,9},... | collective-permute-start | bytes 24584 | tf_op jit(solution)/shard_map/ppermute | solution.py:22
  45.5 4.5 %collective-permute-start.15 = (f32[8,256]{1,0:T(8,128)S(1)}, f32[8,256]{1,0:T(8,128)S(1)}, u32[]{:S(2)}, u32[]{:S(2)}) collective-permute-start(f32[8,256]{1,0:T(8,128)S(1)} %get-tuple-element.26.own), channel_id=1, source_target_pairs={{4,0},{5,1},{6,2},{7,3},{0,4},{1,5},{2,6},{3,7},{12,8},{13,9},{14,... | collective-permute-start | bytes 24584 | tf_op jit(solution)/shard_map/ppermute | solution.py:22
  50.0 3.2 %collective-permute-start.20 = (f32[8,256]{1,0:T(8,128)S(1)}, f32[8,256]{1,0:T(8,128)S(1)}, u32[]{:S(2)}, u32[]{:S(2)}) collective-permute-start(f32[8,256]{1,0:T(8,128)S(1)} %add_add_fusion.s0), channel_id=1, source_target_pairs={{3,0},{2,1},{1,2},{0,3},{7,4},{6,5},{5,6},{4,7},{11,8},{10,9},{9,1... | collective-permute-start | bytes 24584 | tf_op jit(solution)/shard_map/ppermute | solution.py:22
  50.1 3.7 %collective-permute-start.19 = (f32[8,256]{1,0:T(8,128)S(1)}, f32[8,256]{1,0:T(8,128)S(1)}, u32[]{:S(2)}, u32[]{:S(2)}) collective-permute-start(f32[8,256]{1,0:T(8,128)S(1)} %add_add_fusion.s0), channel_id=1, source_target_pairs={{2,0},{3,1},{0,2},{1,3},{6,4},{7,5},{4,6},{5,7},{10,8},{11,9},{8,1... | collective-permute-start | bytes 24584 | tf_op jit(solution)/shard_map/ppermute | solution.py:22
  51.7 2.1 %collective-permute-start.18 = (f32[8,256]{1,0:T(8,128)S(1)}, f32[8,256]{1,0:T(8,128)S(1)}, u32[]{:S(2)}, u32[]{:S(2)}) collective-permute-start(f32[8,256]{1,0:T(8,128)S(1)} %add_add_fusion.s0), channel_id=1, source_target_pairs={{1,0},{0,1},{3,2},{2,3},{5,4},{4,5},{7,6},{6,7},{9,8},{8,9},{11,10... | collective-permute-start | bytes 24584 | tf_op jit(solution)/shard_map/ppermute | solution.py:22

commit v6 on v5

--- a/solution.py
+++ b/solution.py
@@ -8,7 +8,9 @@
 from jax.sharding import PartitionSpec as P
 
 TILE = 512
+HALF = 256
 ROWS = 16
+COLUMNS = 256
 SAMPLE = 256
 VMEM_BYTES = 16 << 20
 RATIO = 0.1 / 0.05**0.5
@@ -51,7 +53,8 @@
             parts[way * hop, 0] = along_ring(here, n, way)
         token = None
         if errands[len(done) :]:
-            result, token = errands[len(done)](parts[hop - 1, 0])
+            after = parts[hop - 1, 0]
+            result, token = errands[len(done)](in_hbm(after) if hop == 1 else after)
             done.append(result)
     for back, core in list(parts):
         parts[back, 1] = swapped(parts[back, core], n, 1)
@@ -199,67 +202,72 @@
     score[...] = cot_f * slope
     along[...] = jnp.zeros_like(along)
 
-    def grad_tile(i, slot):
-        grads[slot][...] = f32dot(turned[span(i), :], scaled[...])
-
-    def probe_tile(i, slot):
-        here = tokens[:, span(i)]
-        along[...] += f32dot(here, firsts[slot][...])
-        across[...] += f32dot(here, seconds[slot][...])
-
-    def rows_of(i, slot, r):
-        at = pl.ds(pl.multiple_of(i * TILE + r, ROWS), ROWS)
-        return grads[slot][r : r + ROWS, :], one[at, :], two[at, :], adjoint[at, :]
+    def grad_rows(i, slot, r):
+        at = pl.ds(pl.multiple_of(i * TILE + r, HALF), HALF)
+        grads[slot][r : r + HALF, :] = f32dot(turned[at, :], scaled[...])
+
+    def probe(i, slot, target, terms):
+        target[...] += f32dot(tokens[:, span(i)], terms[slot][...])
 
     def arrive(i):
         tile_copy(0, i).wait()
         tile_copy(1, i).wait()
 
-    grad_tile(0, 0)
+    def pieces(i, slot, first, last):
+        for r in range(first, last, ROWS):
+            at = pl.ds(pl.multiple_of(i * TILE + r, ROWS), ROWS)
+            for c in range(0, width, COLUMNS):
+                cols = slice(c, min(c + COLUMNS, width))
+                yield r, cols, grads[slot][r : r + ROWS, cols], one[at, cols], two[at, cols], adjoint[at, cols]
+
     arrive(0)
-    sq = jnp.zeros((8, width), jnp.float32)
-    cross = jnp.zeros((8, width), jnp.float32)
-    for r in range(0, SAMPLE, ROWS):
-        g, m1, m2, adj = rows_of(0, 0, r)
+    grad_rows(0, 0, 0)
+    grad_rows(0, 0, HALF)
+    sq, cross = {}, {}
+    for r, cols, g, m1, m2, adj in pieces(0, 0, 0, SAMPLE):
         _, _, upd = update(g, m1, m2)
-        sq += fold(upd * upd)
-        cross += fold(adj * upd)
-    sq = jnp.sum(sq, keepdims=True)
+        sq[cols.start] = sq.get(cols.start, 0.0) + fold(upd * upd)
+        cross[cols.start] = cross.get(cols.start, 0.0) + fold(adj * upd)
+    sq = jnp.sum(sum(sq.values()), keepdims=True)
+    cross = jnp.sum(sum(cross.values()), keepdims=True)
     clipped = sq * RATIO**2 > float(SAMPLE * width)
-    guess = jnp.where(clipped, jnp.sum(cross, keepdims=True) / jnp.maximum(sq, 1.0), 0.0)
+    guess = jnp.where(clipped, cross / jnp.maximum(sq, 1.0), 0.0)
 
     sums[...] = jnp.zeros_like(sums)
 
-    def update_tile(i, slot):
-        if not isinstance(i, int) or i > 0:
-            arrive(i)
-        sq, cross = sums[0], sums[1]
-        for r in range(0, TILE, ROWS):
-            g, m1, m2, adj = rows_of(i, slot, r)
+    def update_rows(i, slot, first):
+        sq, cross = {}, {}
+        for r, cols, g, m1, m2, adj in pieces(i, slot, first, first + HALF):
             over, inv, upd = update(g, m1, m2)
-            sq += fold(upd * upd)
-            cross += fold(adj * upd)
+            sq[cols.start] = sq.get(cols.start, 0.0) + fold(upd * upd)
+            cross[cols.start] = cross.get(cols.start, 0.0) + fold(adj * upd)
             pull = inv * (1.0 - g * (upd * over))
-            firsts[slot][r : r + ROWS, :] = ((adj - guess * upd) * pull).astype(jnp.bfloat16)
-            seconds[slot][r : r + ROWS, :] = (upd * pull).astype(jnp.bfloat16)
-        sums[0] = sq
-        sums[1] = cross
-
-    grad_tile(1, 1)
-    update_tile(0, 0)
+            firsts[slot][r : r + ROWS, cols] = ((adj - guess * upd) * pull).astype(jnp.bfloat16)
+            seconds[slot][r : r + ROWS, cols] = (upd * pull).astype(jnp.bfloat16)
+        sums[0] += sum(sq.values())
+        sums[1] += sum(cross.values())
+
+    def body(i, slot, ahead=True, behind=True):
+        if ahead:
+            arrive(i + 1)
+        for r, target, terms in ((0, along, firsts), (HALF, across, seconds)):
+            if ahead:
+                grad_rows(i + 1, 1 - slot, r)
+            update_rows(i, slot, r)
+            if behind:
+                probe(i - 1, 1 - slot, target, terms)
+
+    body(0, 0, behind=False)
 
     def pair(k, _):
-        i = 2 * k + 1
-        for j, slot in ((0, 1), (1, 0)):
-            grad_tile(i + j + 1, 1 - slot)
-            update_tile(i + j, slot)
-            probe_tile(i + j - 1, 1 - slot)
+        body(2 * k + 1, 1)
+        body(2 * k + 2, 0)
         return 0
 
     lax.fori_loop(0, tiles // 2 - 1, pair, 0)
-    update_tile(tiles - 1, 1)
-    probe_tile(tiles - 2, 0)
-    probe_tile(tiles - 1, 1)
+    body(tiles - 1, 1, ahead=False)
+    probe(tiles - 1, 1, along, firsts)
+    probe(tiles - 1, 1, across, seconds)
 
     b = score[...] * across[...]
     a = score[...] * along[...] + guess * b
@@ -301,7 +309,7 @@
             block(jnp.bfloat16),
             block(jnp.bfloat16),
             block(jnp.bfloat16),
-            pltpu.VMEM((2, 8, width), jnp.float32),
+            pltpu.VMEM((2, 8, min(COLUMNS, width)), jnp.float32),
             pltpu.VMEM((depth, width), jnp.bfloat16),
             pltpu.VMEM((count, width), jnp.bfloat16),
             pltpu.VMEM((1, count), jnp.float32),

time: 58.3 us -> 57.1 us (0.979)
  waiting for transfers between devices: 12 us -> 13.1 us
  local copies, waits for them, and re-layouts: 0.97 us -> 0.01 us
  Pallas kernels: 27.5 us -> 26.7 us
    ppermute x7, waiting for transfers between devices: 4.91 us -> 5.96 us  [along_ring(): return lax.ppermute(value, 'dp', pairs)]
    unnamed x4 -> x2, local copies, waits for them, and re-layouts: 0.97 us -> 0.01 us
    pallas_call x1, Pallas kernels: 17.5 us -> 16.7 us  [replay_call(): pl.pallas_call(functools.partial(replay_kernel, steps), in_specs=[far] *...]
  transfers between devices with their start and end apart: 21 -> 21, of which waited for: 9 -> 10; matrix products, arithmetic and copies ran while one was open for 0% -> 0% of each run, Pallas kernels for 10% -> 10%
where the time goes in v6:
time: 57.1 us; the launch traced here: 56.9 us
  Pallas kernels  26.7 us (47%)
  starting transfers between devices  16.4 us (29%)
  waiting for transfers between devices  13.1 us (23%)
  between operations  0.71 us (1%)
    pallas_call x1, Pallas kernels, replay_call(): pl.pallas_call(functools.partial(replay_kernel, steps), in_specs=[far] *...  16.7 us
    ppermute x7, starting transfers between devices, along_ring(): return lax.ppermute(value, 'dp', pairs)  8.93 us
    ppermute x14, starting transfers between devices, swapped(): return lax.ppermute(value, 'dp', [(d ^ mask, d) for d in range(n)])  7.52 us
    ppermute x14, waiting for transfers between devices, swapped(): return lax.ppermute(value, 'dp', [(d ^ mask, d) for d in range(n)])  7.11 us
    ppermute x7, waiting for transfers between devices, along_ring(): return lax.ppermute(value, 'dp', pairs)  5.96 us
    pallas_call x2, Pallas kernels, fetch(): pl.pallas_call(functools.partial(fetch_kernel, factor), in_specs=[pl.Bloc...  5.61 us
    pallas_call x1, Pallas kernels, theta_call(): pl.pallas_call(functools.partial(theta_kernel, n, entries), in_specs=[vme...  4.29 us
  transfers between devices with their start and end apart: 21, of which 10 were waited for; matrix products, arithmetic and copies ran while one was open for 0% of the time, Pallas kernels for 10%

profile of v6, /device:TPU:0, one launch (start us, length us, event | category | flops | bytes accessed | tf_op | source)
XLA Modules:
  0.0 56.9 jit_solution(393660565200586716)
XLA Ops:
  0.6 0.0 copy-start
  0.6 3.1 %collective-permute-start = (bf16[16,4096]{1,0:T(8,128)(2,1)}, bf16[16,4096]{1,0:T(8,128)(2,1)S(1)}, u32[]{:S(2)}, u32[]{:S(2)}) collective-permute-start(bf16[16,4096]{1,0:T(8,128)(2,1)} %refs_0_.1), channel_id=1, source_target_pairs={{2,0},{3,1},{0,4},{1,5},{4,8},{5,9},{8,12},{9,13},{12,14},{13,15},... | collective-permute-start | bytes 393224 | tf_op jit(solution)/shard_map/ppermute | solution.py:38
  3.7 0.0 collective-permute-start.1
  3.7 2.8 %fetch.2 = (bf16[4096,512]{1,0:T(8,128)(2,1)S(1)}, f32[8,128]{1,0:T(8,128)}) custom-call(bf16[4096,512]{1,0:T(8,128)(2,1)} %far.2, bf16[16,4096]{1,0:T(8,128)(2,1)} %refs_0_.1), custom_call_target="tpu_custom_call" | custom-call | bytes 8388608 | tf_op jit(solution)/shard_map/fetch/pallas_call | solution.py:131
  6.5 0.8 %collective-permute-done.after.refs_1_ = bf16[16,4096]{1,0:T(8,128)(2,1)S(1)} collective-permute-done((bf16[16,4096]{1,0:T(8,128)(2,1)}, bf16[16,4096]{1,0:T(8,128)(2,1)S(1)}, u32[]{:S(2)}, u32[]{:S(2)}) %collective-permute-start) | collective-permute-done | bytes 131104 | tf_op jit(solution)/shard_map/ppermute | solution.py:38
  7.4 1.8 %collective-permute-start.2 = (bf16[16,4096]{1,0:T(8,128)(2,1)S(1)}, bf16[16,4096]{1,0:T(8,128)(2,1)S(1)}, u32[]{:S(2)}, u32[]{:S(2)}) collective-permute-start(bf16[16,4096]{1,0:T(8,128)(2,1)S(1)} %collective-permute-done.after.refs_1_), channel_id=1, source_target_pairs={{2,0},{3,1},{0,4},{1,5},{4,8},{5,9},{8,12},{9,13},{12,14},{13,15},... | collective-permute-start | bytes 393224 | tf_op jit(solution)/shard_map/ppermute | solution.py:38
  9.2 0.0 collective-permute-done.1.refs_2_
  9.2 0.2 collective-permute-start.3
  9.4 2.8 %fetch.3 = (f32[4096,512]{1,0:T(8,128)S(1)}, f32[8,128]{1,0:T(8,128)}) custom-call(bf16[4096,512]{1,0:T(8,128)(2,1)} %far.3, bf16[16,4096]{1,0:T(8,128)(2,1)S(1)} %collective-permute-done.after.refs_1_), custom_call_target="tpu_custom_call" | custom-call | bytes 8388608 | tf_op jit(solution)/shard_map/fetch/pallas_call | solution.py:131
  12.2 0.1 collective-permute-done.2.refs_3_
  12.3 1.8 %collective-permute-start.4 = (bf16[16,4096]{1,0:T(8,128)(2,1)S(1)}, bf16[16,4096]{1,0:T(8,128)(2,1)S(1)}, u32[]{:S(2)}, u32[]{:S(2)}) collective-permute-start(bf16[16,4096]{1,0:T(8,128)(2,1)S(1)} %collective-permute-done.2.refs_3_), channel_id=1, source_target_pairs={{2,0},{3,1},{0,4},{1,5},{4,8},{5,9},{8,12},{9,13},{12,14},{13,15},... | collective-permute-start | bytes 393224 | tf_op jit(solution)/shard_map/ppermute | solution.py:38
  14.1 0.0 copy-done
  14.1 0.0 collective-permute-start.7
  14.1 0.5 collective-permute-start.9
  14.6 0.0 collective-permute-start.8
  14.7 0.0 collective-permute-done.3.refs_4_
  14.7 0.2 collective-permute-start.5
  14.9 2.4 %collective-permute-done.4.refs_5_ = bf16[16,4096]{1,0:T(8,128)(2,1)S(1)} collective-permute-done((bf16[16,4096]{1,0:T(8,128)(2,1)S(1)}, bf16[16,4096]{1,0:T(8,128)(2,1)S(1)}, u32[]{:S(2)}, u32[]{:S(2)}) %collective-permute-start.4) | collective-permute-done | bytes 131104 | tf_op jit(solution)/shard_map/ppermute | solution.py:38
  17.3 1.8 %collective-permute-start.6 = (bf16[16,4096]{1,0:T(8,128)(2,1)S(1)}, bf16[16,4096]{1,0:T(8,128)(2,1)S(1)}, u32[]{:S(2)}, u32[]{:S(2)}) collective-permute-start(bf16[16,4096]{1,0:T(8,128)(2,1)S(1)} %collective-permute-done.4.refs_5_), channel_id=1, source_target_pairs={{2,0},{3,1},{0,4},{1,5},{4,8},{5,9},{8,12},{9,13},{12,14},{13,15},... | collective-permute-start | bytes 393224 | tf_op jit(solution)/shard_map/ppermute | solution.py:38
  19.1 0.0 collective-permute-done.7.refs_8_
  19.1 0.0 collective-permute-start.10
  19.1 0.0 collective-permute-done.9.refs_10_
  19.1 0.5 collective-permute-start.11
  19.6 0.0 collective-permute-done.8.refs_9_
  19.6 0.1 collective-permute-start.12
  19.7 0.9 %collective-permute-done.5.refs_6_ = bf16[16,4096]{1,0:T(8,128)(2,1)S(1)} collective-permute-done((bf16[16,4096]{1,0:T(8,128)(2,1)S(1)}, bf16[16,4096]{1,0:T(8,128)(2,1)S(1)}, u32[]{:S(2)}, u32[]{:S(2)}) %collective-permute-start.5) | collective-permute-done | bytes 131104 | tf_op jit(solution)/shard_map/ppermute | solution.py:38
  20.6 0.0 collective-permute-start.13
  20.6 1.7 %collective-permute-done.6.refs_7_ = bf16[16,4096]{1,0:T(8,128)(2,1)S(1)} collective-permute-done((bf16[16,4096]{1,0:T(8,128)(2,1)S(1)}, bf16[16,4096]{1,0:T(8,128)(2,1)S(1)}, u32[]{:S(2)}, u32[]{:S(2)}) %collective-permute-start.6) | collective-permute-done | bytes 131104 | tf_op jit(solution)/shard_map/ppermute | solution.py:38
  22.3 0.0 collective-permute-start.14
  22.3 0.0 collective-permute-done.10.refs_11_
  22.3 0.0 collective-permute-done.11.refs_12_
  22.3 0.0 collective-permute-done.12.refs_13_
  22.3 0.0 collective-permute-done.13.refs_14_
  22.3 1.3 %collective-permute-done.14.refs_15_ = bf16[16,4096]{1,0:T(8,128)(2,1)S(1)} collective-permute-done((bf16[16,4096]{1,0:T(8,128)(2,1)S(1)}, bf16[16,4096]{1,0:T(8,128)(2,1)S(1)}, u32[]{:S(2)}, u32[]{:S(2)}) %collective-permute-start.14) | collective-permute-done | bytes 131104 | tf_op jit(solution)/shard_map/ppermute | solution.py:24
  23.6 16.7 %replay.1 = (f32[4096,512]{1,0:T(8,128)S(1)}, bf16[4096,256]{1,0:T(8,128)(2,1)S(1)}, f32[256,512]{1,0:T(8,128)S(1)}, f32[256,512]{1,0:T(8,128)S(1)}, f32[256,512]{1,0:T(8,128)S(1)}, /*index=5*/f32[8,256]{1,0:T(8,128)S(1)}) custom-call(bf16[16,4096]{1,0:T(8,128)(2,1)} %refs_0_.1, bf16[16,4096]{1,0:T(8,128)(2,1)S(1)} %collective-permute-done.after.refs_1_, ...), custom_call_target="tpu_custom_call" | custom-call | tf_op jit(solution)/shard_map/replay/pallas_call | solution.py:290
  40.4 3.9 %collective-permute-start.17 = (f32[8,256]{1,0:T(8,128)S(1)}, f32[8,256]{1,0:T(8,128)S(1)}, u32[]{:S(2)}, u32[]{:S(2)}) collective-permute-start(f32[8,256]{1,0:T(8,128)S(1)} %get-tuple-element.26.own), channel_id=1, source_target_pairs={{12,0},{13,1},{14,2},{15,3},{8,4},{9,5},{10,6},{11,7},{4,8},{5,9},... | collective-permute-start | bytes 24584 | tf_op jit(solution)/shard_map/ppermute | solution.py:24
  44.2 0.0 collective-permute-start.16
  44.3 0.6 %collective-permute-start.15 = (f32[8,256]{1,0:T(8,128)S(1)}, f32[8,256]{1,0:T(8,128)S(1)}, u32[]{:S(2)}, u32[]{:S(2)}) collective-permute-start(f32[8,256]{1,0:T(8,128)S(1)} %get-tuple-element.26.own), channel_id=1, source_target_pairs={{4,0},{5,1},{6,2},{7,3},{0,4},{1,5},{2,6},{3,7},{12,8},{13,9},{14,... | collective-permute-start | bytes 24584 | tf_op jit(solution)/shard_map/ppermute | solution.py:24
  44.9 1.0 %collective-permute-done.17 = f32[8,256]{1,0:T(8,128)S(1)} collective-permute-done((f32[8,256]{1,0:T(8,128)S(1)}, f32[8,256]{1,0:T(8,128)S(1)}, u32[]{:S(2)}, u32[]{:S(2)}) %collective-permute-start.17) | collective-permute-done | bytes 8224 | tf_op jit(solution)/shard_map/ppermute | solution.py:24
  45.9 2.9 %collective-permute-done.16 = f32[8,256]{1,0:T(8,128)S(1)} collective-permute-done((f32[8,256]{1,0:T(8,128)S(1)}, f32[8,256]{1,0:T(8,128)S(1)}, u32[]{:S(2)}, u32[]{:S(2)}) %collective-permute-start.16) | collective-permute-done | bytes 8224 | tf_op jit(solution)/shard_map/ppermute | solution.py:24
  48.8 0.0 collective-permute-done.15
  48.8 0.1 collective-permute-start.20
  48.9 1.6 %collective-permute-start.19 = (f32[8,256]{1,0:T(8,128)S(1)}, f32[8,256]{1,0:T(8,128)S(1)}, u32[]{:S(2)}, u32[]{:S(2)}) collective-permute-start(f32[8,256]{1,0:T(8,128)S(1)} %add_add_fusion.s0), channel_id=1, source_target_pairs={{2,0},{3,1},{0,2},{1,3},{6,4},{7,5},{4,6},{5,7},{10,8},{11,9},{8,1... | collective-permute-start | bytes 24584 | tf_op jit(solution)/shard_map/ppermute | solution.py:24
  50.5 0.3 collective-permute-start.18
  50.7 1.2 %collective-permute-done.20.s3 = f32[8,256]{1,0:T(8,128)S(1)} collective-permute-done((f32[8,256]{1,0:T(8,128)S(1)}, f32[8,256]{1,0:T(8,128)S(1)}, u32[]{:S(2)}, u32[]{:S(2)}) %collective-permute-start.20) | collective-permute-done | bytes 8224 | tf_op jit(solution)/shard_map/ppermute | solution.py:24
  52.0 0.6 %collective-permute-done.19.s2 = f32[8,256]{1,0:T(8,128)S(1)} collective-permute-done((f32[8,256]{1,0:T(8,128)S(1)}, f32[8,256]{1,0:T(8,128)S(1)}, u32[]{:S(2)}, u32[]{:S(2)}) %collective-permute-start.19) | collective-permute-done | bytes 8224 | tf_op jit(solution)/shard_map/ppermute | solution.py:24
  52.6 0.0 collective-permute-done.18.s1
  52.6 4.3 %theta.1 = (f32[4096,512]{1,0:T(8,128)}, f32[1,16]{1,0:T(1,128)}) custom-call(f32[8,256]{1,0:T(8,128)S(1)} %add_add_fusion.s0, f32[8,256]{1,0:T(8,128)S(1)} %collective-permute-done.18.s1, f32[8,256]{1,0:T(8,128)S(1)} %collective-permute-done.19.s2, f32[8,256]{1,0:T(8,128)S(1)} %collective-permute-done.20.s3, f32[8,256]{1,0:T(8,128)S(1)} %get-tuple-element.26.own, ...), custom_call_target="tpu_custom_call" | custom-call | tf_op jit(solution)/shard_map/theta/pallas_call | solution.py:367
  (1 shorter events, 0.0 us)
Async XLA Ops:
  0.6 13.5 %copy-start = (bf16[16,4096]{1,0:T(8,128)(2,1)S(1)}, bf16[16,4096]{1,0:T(8,128)(2,1)}, u32[]{:S(2)}) copy-start(bf16[16,4096]{1,0:T(8,128)(2,1)} %refs_0_.1) | copy-start | bytes 393220
  0.6 6.7 %collective-permute-start = (bf16[16,4096]{1,0:T(8,128)(2,1)}, bf16[16,4096]{1,0:T(8,128)(2,1)S(1)}, u32[]{:S(2)}, u32[]{:S(2)}) collective-permute-start(bf16[16,4096]{1,0:T(8,128)(2,1)} %refs_0_.1), channel_id=1, source_target_pairs={{2,0},{3,1},{0,4},{1,5},{4,8},{5,9},{8,12},{9,13},{12,14},{13,15},... | collective-permute-start | bytes 393224 | tf_op jit(solution)/shard_map/ppermute | solution.py:38
  3.7 5.5 %collective-permute-start.1 = (bf16[16,4096]{1,0:T(8,128)(2,1)}, bf16[16,4096]{1,0:T(8,128)(2,1)S(1)}, u32[]{:S(2)}, u32[]{:S(2)}) collective-permute-start(bf16[16,4096]{1,0:T(8,128)(2,1)} %refs_0_.1), channel_id=1, source_target_pairs={{4,0},{5,1},{8,4},{9,5},{12,8},{13,9},{14,12},{15,13},{10,14},{11,... | collective-permute-start | bytes 393224 | tf_op jit(solution)/shard_map/ppermute | solution.py:38
  7.4 5.0 %collective-permute-start.2 = (bf16[16,4096]{1,0:T(8,128)(2,1)S(1)}, bf16[16,4096]{1,0:T(8,128)(2,1)S(1)}, u32[]{:S(2)}, u32[]{:S(2)}) collective-permute-start(bf16[16,4096]{1,0:T(8,128)(2,1)S(1)} %collective-permute-done.after.refs_1_), channel_id=1, source_target_pairs={{2,0},{3,1},{0,4},{1,5},{4,8},{5,9},{8,12},{9,13},{12,14},{13,15},... | collective-permute-start | bytes 393224 | tf_op jit(solution)/shard_map/ppermute | solution.py:38
  9.2 5.5 %collective-permute-start.3 = (bf16[16,4096]{1,0:T(8,128)(2,1)S(1)}, bf16[16,4096]{1,0:T(8,128)(2,1)S(1)}, u32[]{:S(2)}, u32[]{:S(2)}) collective-permute-start(bf16[16,4096]{1,0:T(8,128)(2,1)S(1)} %collective-permute-done.1.refs_2_), channel_id=1, source_target_pairs={{4,0},{5,1},{8,4},{9,5},{12,8},{13,9},{14,12},{15,13},{10,14},{11,... | collective-permute-start | bytes 393224 | tf_op jit(solution)/shard_map/ppermute | solution.py:38
  12.3 5.0 %collective-permute-start.4 = (bf16[16,4096]{1,0:T(8,128)(2,1)S(1)}, bf16[16,4096]{1,0:T(8,128)(2,1)S(1)}, u32[]{:S(2)}, u32[]{:S(2)}) collective-permute-start(bf16[16,4096]{1,0:T(8,128)(2,1)S(1)} %collective-permute-done.2.refs_3_), channel_id=1, source_target_pairs={{2,0},{3,1},{0,4},{1,5},{4,8},{5,9},{8,12},{9,13},{12,14},{13,15},... | collective-permute-start | bytes 393224 | tf_op jit(solution)/shard_map/ppermute | solution.py:38
  14.1 5.0 %collective-permute-start.7 = (bf16[16,4096]{1,0:T(8,128)(2,1)S(1)}, bf16[16,4096]{1,0:T(8,128)(2,1)S(1)}, u32[]{:S(2)}, u32[]{:S(2)}) collective-permute-start(bf16[16,4096]{1,0:T(8,128)(2,1)S(1)} %copy-done), channel_id=1, source_target_pairs={{1,0},{0,1},{3,2},{2,3},{5,4},{4,5},{7,6},{6,7},{9,8},{8,9},{11,10... | collective-permute-start | bytes 393224 | tf_op jit(solution)/shard_map/ppermute | solution.py:24
  14.1 5.0 %collective-permute-start.9 = (bf16[16,4096]{1,0:T(8,128)(2,1)S(1)}, bf16[16,4096]{1,0:T(8,128)(2,1)S(1)}, u32[]{:S(2)}, u32[]{:S(2)}) collective-permute-start(bf16[16,4096]{1,0:T(8,128)(2,1)S(1)} %collective-permute-done.1.refs_2_), channel_id=1, source_target_pairs={{1,0},{0,1},{3,2},{2,3},{5,4},{4,5},{7,6},{6,7},{9,8},{8,9},{11,10... | collective-permute-start | bytes 393224 | tf_op jit(solution)/shard_map/ppermute | solution.py:24
  14.6 5.0 %collective-permute-start.8 = (bf16[16,4096]{1,0:T(8,128)(2,1)S(1)}, bf16[16,4096]{1,0:T(8,128)(2,1)S(1)}, u32[]{:S(2)}, u32[]{:S(2)}) collective-permute-start(bf16[16,4096]{1,0:T(8,128)(2,1)S(1)} %collective-permute-done.after.refs_1_), channel_id=1, source_target_pairs={{1,0},{0,1},{3,2},{2,3},{5,4},{4,5},{7,6},{6,7},{9,8},{8,9},{11,10... | collective-permute-start | bytes 393224 | tf_op jit(solution)/shard_map/ppermute | solution.py:24
  14.7 5.9 %collective-permute-start.5 = (bf16[16,4096]{1,0:T(8,128)(2,1)S(1)}, bf16[16,4096]{1,0:T(8,128)(2,1)S(1)}, u32[]{:S(2)}, u32[]{:S(2)}) collective-permute-start(bf16[16,4096]{1,0:T(8,128)(2,1)S(1)} %collective-permute-done.3.refs_4_), channel_id=1, source_target_pairs={{4,0},{5,1},{8,4},{9,5},{12,8},{13,9},{14,12},{15,13},{10,14},{11,... | collective-permute-start | bytes 393224 | tf_op jit(solution)/shard_map/ppermute | solution.py:38
  17.3 5.0 %collective-permute-start.6 = (bf16[16,4096]{1,0:T(8,128)(2,1)S(1)}, bf16[16,4096]{1,0:T(8,128)(2,1)S(1)}, u32[]{:S(2)}, u32[]{:S(2)}) collective-permute-start(bf16[16,4096]{1,0:T(8,128)(2,1)S(1)} %collective-permute-done.4.refs_5_), channel_id=1, source_target_pairs={{2,0},{3,1},{0,4},{1,5},{4,8},{5,9},{8,12},{9,13},{12,14},{13,15},... | collective-permute-start | bytes 393224 | tf_op jit(solution)/shard_map/ppermute | solution.py:38
  19.1 3.2 %collective-permute-start.10 = (bf16[16,4096]{1,0:T(8,128)(2,1)S(1)}, bf16[16,4096]{1,0:T(8,128)(2,1)S(1)}, u32[]{:S(2)}, u32[]{:S(2)}) collective-permute-start(bf16[16,4096]{1,0:T(8,128)(2,1)S(1)} %collective-permute-done.2.refs_3_), channel_id=1, source_target_pairs={{1,0},{0,1},{3,2},{2,3},{5,4},{4,5},{7,6},{6,7},{9,8},{8,9},{11,10... | collective-permute-start | bytes 393224 | tf_op jit(solution)/shard_map/ppermute | solution.py:24
  19.1 3.2 %collective-permute-start.11 = (bf16[16,4096]{1,0:T(8,128)(2,1)S(1)}, bf16[16,4096]{1,0:T(8,128)(2,1)S(1)}, u32[]{:S(2)}, u32[]{:S(2)}) collective-permute-start(bf16[16,4096]{1,0:T(8,128)(2,1)S(1)} %collective-permute-done.3.refs_4_), channel_id=1, source_target_pairs={{1,0},{0,1},{3,2},{2,3},{5,4},{4,5},{7,6},{6,7},{9,8},{8,9},{11,10... | collective-permute-start | bytes 393224 | tf_op jit(solution)/shard_map/ppermute | solution.py:24
  19.6 2.7 %collective-permute-start.12 = (bf16[16,4096]{1,0:T(8,128)(2,1)S(1)}, bf16[16,4096]{1,0:T(8,128)(2,1)S(1)}, u32[]{:S(2)}, u32[]{:S(2)}) collective-permute-start(bf16[16,4096]{1,0:T(8,128)(2,1)S(1)} %collective-permute-done.4.refs_5_), channel_id=1, source_target_pairs={{1,0},{0,1},{3,2},{2,3},{5,4},{4,5},{7,6},{6,7},{9,8},{8,9},{11,10... | collective-permute-start | bytes 393224 | tf_op jit(solution)/shard_map/ppermute | solution.py:24
  20.6 1.7 %collective-permute-start.13 = (bf16[16,4096]{1,0:T(8,128)(2,1)S(1)}, bf16[16,4096]{1,0:T(8,128)(2,1)S(1)}, u32[]{:S(2)}, u32[]{:S(2)}) collective-permute-start(bf16[16,4096]{1,0:T(8,128)(2,1)S(1)} %collective-permute-done.5.refs_6_), channel_id=1, source_target_pairs={{1,0},{0,1},{3,2},{2,3},{5,4},{4,5},{7,6},{6,7},{9,8},{8,9},{11,10... | collective-permute-start | bytes 393224 | tf_op jit(solution)/shard_map/ppermute | solution.py:24
  22.3 1.3 %collective-permute-start.14 = (bf16[16,4096]{1,0:T(8,128)(2,1)S(1)}, bf16[16,4096]{1,0:T(8,128)(2,1)S(1)}, u32[]{:S(2)}, u32[]{:S(2)}) collective-permute-start(bf16[16,4096]{1,0:T(8,128)(2,1)S(1)} %collective-permute-done.6.refs_7_), channel_id=1, source_target_pairs={{1,0},{0,1},{3,2},{2,3},{5,4},{4,5},{7,6},{6,7},{9,8},{8,9},{11,10... | collective-permute-start | bytes 393224 | tf_op jit(solution)/shard_map/ppermute | solution.py:24
  40.4 5.5 %collective-permute-start.17 = (f32[8,256]{1,0:T(8,128)S(1)}, f32[8,256]{1,0:T(8,128)S(1)}, u32[]{:S(2)}, u32[]{:S(2)}) collective-permute-start(f32[8,256]{1,0:T(8,128)S(1)} %get-tuple-element.26.own), channel_id=1, source_target_pairs={{12,0},{13,1},{14,2},{15,3},{8,4},{9,5},{10,6},{11,7},{4,8},{5,9},... | collective-permute-start | bytes 24584 | tf_op jit(solution)/shard_map/ppermute | solution.py:24
  44.2 4.5 %collective-permute-start.16 = (f32[8,256]{1,0:T(8,128)S(1)}, f32[8,256]{1,0:T(8,128)S(1)}, u32[]{:S(2)}, u32[]{:S(2)}) collective-permute-start(f32[8,256]{1,0:T(8,128)S(1)} %get-tuple-element.26.own), channel_id=1, source_target_pairs={{8,0},{9,1},{10,2},{11,3},{12,4},{13,5},{14,6},{15,7},{0,8},{1,9},... | collective-permute-start | bytes 24584 | tf_op jit(solution)/shard_map/ppermute | solution.py:24
  44.3 4.5 %collective-permute-start.15 = (f32[8,256]{1,0:T(8,128)S(1)}, f32[8,256]{1,0:T(8,128)S(1)}, u32[]{:S(2)}, u32[]{:S(2)}) collective-permute-start(f32[8,256]{1,0:T(8,128)S(1)} %get-tuple-element.26.own), channel_id=1, source_target_pairs={{4,0},{5,1},{6,2},{7,3},{0,4},{1,5},{2,6},{3,7},{12,8},{13,9},{14,... | collective-permute-start | bytes 24584 | tf_op jit(solution)/shard_map/ppermute | solution.py:24
  48.8 3.1 %collective-permute-start.20 = (f32[8,256]{1,0:T(8,128)S(1)}, f32[8,256]{1,0:T(8,128)S(1)}, u32[]{:S(2)}, u32[]{:S(2)}) collective-permute-start(f32[8,256]{1,0:T(8,128)S(1)} %add_add_fusion.s0), channel_id=1, source_target_pairs={{3,0},{2,1},{1,2},{0,3},{7,4},{6,5},{5,6},{4,7},{11,8},{10,9},{9,1... | collective-permute-start | bytes 24584 | tf_op jit(solution)/shard_map/ppermute | solution.py:24
  48.9 3.7 %collective-permute-start.19 = (f32[8,256]{1,0:T(8,128)S(1)}, f32[8,256]{1,0:T(8,128)S(1)}, u32[]{:S(2)}, u32[]{:S(2)}) collective-permute-start(f32[8,256]{1,0:T(8,128)S(1)} %add_add_fusion.s0), channel_id=1, source_target_pairs={{2,0},{3,1},{0,2},{1,3},{6,4},{7,5},{4,6},{5,7},{10,8},{11,9},{8,1... | collective-permute-start | bytes 24584 | tf_op jit(solution)/shard_map/ppermute | solution.py:24
  50.5 2.1 %collective-permute-start.18 = (f32[8,256]{1,0:T(8,128)S(1)}, f32[8,256]{1,0:T(8,128)S(1)}, u32[]{:S(2)}, u32[]{:S(2)}) collective-permute-start(f32[8,256]{1,0:T(8,128)S(1)} %add_add_fusion.s0), channel_id=1, source_target_pairs={{1,0},{0,1},{3,2},{2,3},{5,4},{4,5},{7,6},{6,7},{9,8},{8,9},{11,10... | collective-permute-start | bytes 24584 | tf_op jit(solution)/shard_map/ppermute | solution.py:24

commit v7 on v6

v7 whole, which is shorter than its diff:
```python
import functools

import jax
import jax.numpy as jnp
from jax import lax
from jax.experimental import pallas as pl
from jax.experimental.pallas import tpu as pltpu
from jax.sharding import PartitionSpec as P

TILE = 512
HALF = 256
ROWS = 16
COLUMNS = 256
COST = 4 << 30
SAMPLE = 256
VMEM_BYTES = 12 << 20
RATIO = 0.1 / 0.05**0.5


def f32dot(a, b):
    return jnp.dot(a, b, preferred_element_type=jnp.float32)


def swapped(value, n, mask):
    return lax.ppermute(value, "dp", [(d ^ mask, d) for d in range(n)])


def ring(n):
    chips = n // 2
    return [*range(0, chips, 2), *range(chips - 1 - chips % 2, 0, -2)]


def onward(value, n):
    order = ring(n)
    pairs = []
    for i, chip in enumerate(order):
        pairs.append((2 * order[i - 1], 2 * chip))
        pairs.append((2 * order[(i + 1) % len(order)] + 1, 2 * chip + 1))
    return lax.ppermute(value, "dp", pairs)


def gather(tokens, n, errands):
    hops = n // 4
    done = []
    token = None
    own = jnp.concatenate([tokens, swapped(tokens, n, 1)], axis=0)
    blocks = [own]
    here = own
    for hop in range(1, hops + 1):
        after = in_hbm(tokens) if hop == 1 else here
        if token is not None:
            here = lax.optimization_barrier((here, token))[0]
        here = onward(here, n)
        token = None
        if errands[len(done) :]:
            result, token = errands[len(done)](after)
            done.append(result)
        blocks.append(here)
        if hop < hops:
            blocks.append(swapped(here, n, 1))
    return blocks, done


def owners(n):
    chips = n // 2
    me = lax.axis_index("dp")
    chip, core = me // 2, lax.rem(me, 2)
    at = jnp.where(lax.rem(chip, 2) == 0, chip // 2, chips - 1 - chip // 2)
    way = 2 * core - 1
    blocks = [(0, core)]
    for hop in range(1, chips // 2 + 1):
        blocks.append((way * hop, core))
        if 2 * hop < chips:
            blocks.append((-way * hop, 1 - core))
    places = []
    for step, first in blocks:
        there = lax.rem(at + step + chips, chips)
        source = jnp.where(there < chips // 2, 2 * there, 2 * (chips - 1 - there) + 1)
        places += [2 * source + first, 2 * source + 1 - first]
    return places


def all_sum(value, n):
    total = value
    for mask in range(4, n, 4):
        total = total + swapped(value, n, mask)
    return [total] + [swapped(total, n, mask) for mask in (1, 2, 3)]


def over_columns(row):
    return jnp.transpose(jnp.broadcast_to(row, (8, row.shape[1])))[:, :1]


def fold(x):
    return jnp.sum(x.reshape(x.shape[0] // 8, 8, x.shape[1]), axis=0)


def update(grad, one, two):
    first = 9.0 * one.astype(jnp.float32) + grad
    second = 19.0 * two.astype(jnp.float32) + grad * grad
    over = lax.rsqrt(second)
    inv = pltpu.reciprocal(second * over + 1e-08 / 0.05**0.5, approx=True)
    return over, inv, first * inv


def fetch_kernel(far, after, near, token, sem):
    copy = pltpu.make_async_copy(far, near, sem.at[0])
    copy.start()
    token[...] = jnp.zeros_like(token)
    copy.wait()


def fetch(x, after):
    return pl.pallas_call(
        fetch_kernel,
        in_specs=[pl.BlockSpec(memory_space=pl.ANY)] * 2,
        out_specs=[pl.BlockSpec(memory_space=pltpu.VMEM)] * 2,
        out_shape=[pltpu.VMEM(x.shape, x.dtype), jax.ShapeDtypeStruct((8, 128), jnp.float32)],
        scratch_shapes=[pltpu.SemaphoreType.DMA((1,))],
        compiler_params=pltpu.CompilerParams(vmem_limit_bytes=1 << 20),
        cost_estimate=pl.CostEstimate(flops=COST, bytes_accessed=8 << 20, transcendentals=0),
        name="fetch",
    )(in_hbm(x), after)


def span(i):
    return pl.ds(pl.multiple_of(i * TILE, TILE), TILE)


def gate_rows(blocks, first, sems, weight, tokens, turned, gate):
    height, depth = blocks[0].shape
    count = len(blocks) * height
    rows = slice(first, first + count)
    copies = [
        pltpu.make_async_copy(ref, tokens.at[pl.ds(first + k * height, height), :], sems.at[k])
        for k, ref in enumerate(blocks)
    ]
    for copy in copies:
        copy.start()
    gate[rows, :] = jnp.zeros((count, gate.shape[1]), jnp.float32)
    for copy in copies:
        copy.wait()

    def step(i, _):
        here = tokens[rows, span(i)]
        gate[rows, :] += f32dot(here, weight[span(i), :])
        turned[span(i), rows] = here.T
        return 0

    lax.fori_loop(0, depth // TILE, step, 0)


def early_kernel(n, half, *refs):
    blocks, (far_cot, far_weight, far_adjoint, weight, _) = refs[:half], refs[half : half + 5]
    (tokens, turned, gate, cot, weights, adjoint) = refs[half + 5 : half + 11]
    (token_weight, upright, sems, cot_sems, far_sems) = refs[half + 11 :]
    height = cot.shape[0] // n
    places = owners(n)
    adjoint_copy = pltpu.make_async_copy(far_adjoint, adjoint, far_sems.at[0])
    weight_copy = pltpu.make_async_copy(far_weight, token_weight, far_sems.at[1])
    cot_copies = [
        pltpu.make_async_copy(
            far_cot.at[pl.ds(pl.multiple_of(place * height, height), height), :],
            cot.at[pl.ds(k * height, height), :],
            cot_sems.at[k],
        )
        for k, place in enumerate(places)
    ]
    weight_copy.start()
    for copy in cot_copies:
        copy.start()
    gate_rows(blocks, 0, sems, weight, tokens, turned, gate)
    adjoint_copy.start()
    weight_copy.wait()
    upright[...] = jnp.broadcast_to(over_columns(token_weight[...]), upright.shape)
    for k, place in enumerate(places):
        weights[k * height : (k + 1) * height, :] = upright[pl.ds(pl.multiple_of(place * height, height), height), :]
    for copy in cot_copies:
        copy.wait()
    adjoint_copy.wait()


def early_call(n, blocks, cot, token_weight, adjoint, weight, token):
    half = len(blocks)
    count, width = cot.shape
    depth = weight.shape[0]
    far = pl.BlockSpec(memory_space=pl.ANY)
    vmem = pl.BlockSpec(memory_space=pltpu.VMEM)
    return pl.pallas_call(
        functools.partial(early_kernel, n, half),
        in_specs=[far] * (half + 3) + [vmem, far],
        out_specs=[vmem] * 6,
        out_shape=[
            pltpu.VMEM((count, depth), jnp.bfloat16),
            pltpu.VMEM((depth, count), jnp.bfloat16),
            pltpu.VMEM((count, width), jnp.float32),
            pltpu.VMEM((count, width), jnp.bfloat16),
            pltpu.VMEM((count, 128), jnp.float32),
            pltpu.VMEM((depth, width), jnp.float32),
        ],
        scratch_shapes=[
            pltpu.VMEM((1, count), jnp.float32),
            pltpu.VMEM((count, 128), jnp.float32),
            pltpu.SemaphoreType.DMA((half,)),
            pltpu.SemaphoreType.DMA((n,)),
            pltpu.SemaphoreType.DMA((2,)),
        ],
        compiler_params=pltpu.CompilerParams(vmem_limit_bytes=VMEM_BYTES),
        cost_estimate=pl.CostEstimate(flops=COST, bytes_accessed=12 << 20, transcendentals=0),
        name="early",
    )(*blocks, *[in_hbm(x) for x in (cot, token_weight, adjoint)], weight, token)


def late_kernel(half, *refs):
    blocks, (weight, cot, weights) = refs[:half], refs[half : half + 3]
    (tokens, turned, gate, scaled, bend, score, sems) = refs[half + 6 :]
    count, width = cot.shape
    gate_rows(blocks, count // 2, sems, weight, tokens, turned, gate)
    for r in range(0, count, 64):
        at = slice(r, r + 64)
        x = gate[at, :]
        token_weight = weights[at, 0:1]
        cot_f = cot[at, :].astype(jnp.float32)
        sig = 1.0 / (1.0 + jnp.exp(-x))
        slope = sig * (1.0 + x * (1.0 - sig))
        curve = sig * (1.0 - sig) * (2.0 + x * (1.0 - 2.0 * sig))
        scaled[at, :] = (token_weight * cot_f * slope).astype(jnp.bfloat16)
        bend[at, :] = token_weight * cot_f * curve
        score[at, :] = cot_f * slope


def late_call(blocks, weight, cot, weights, tokens, turned, gate):
    half = len(blocks)
    count, width = cot.shape
    far = pl.BlockSpec(memory_space=pl.ANY)
    vmem = pl.BlockSpec(memory_space=pltpu.VMEM)
    like = lambda x: pltpu.VMEM(x.shape, x.dtype)
    return pl.pallas_call(
        functools.partial(late_kernel, half),
        in_specs=[far] * half + [vmem] * 6,
        out_specs=[vmem] * 6,
        out_shape=[
            like(tokens),
            like(turned),
            like(gate),
            pltpu.VMEM((count, width), jnp.bfloat16),
            pltpu.VMEM((count, width), jnp.float32),
            pltpu.VMEM((count, width), jnp.float32),
        ],
        scratch_shapes=[pltpu.SemaphoreType.DMA((half,))],
        input_output_aliases={half + 3: 0, half + 4: 1, half + 5: 2},
        compiler_params=pltpu.CompilerParams(vmem_limit_bytes=VMEM_BYTES),
        name="late",
    )(*blocks, weight, cot, weights, tokens, turned, gate)


def step_kernel(n, tokens, turned, scaled, score, one, two, adjoint, along, across, stats, *scratch):
    (g0, g1, a0, a1, b0, b1, sums, upright) = scratch
    grads, firsts, seconds = (g0, g1), (a0, a1), (b0, b1)
    depth = one.shape[0]
    count, width = scaled.shape
    tiles = depth // TILE
    along[...] = jnp.zeros_like(along)
    across[...] = jnp.zeros_like(across)

    def grad_rows(i, slot, r):
        at = pl.ds(pl.multiple_of(i * TILE + r, HALF), HALF)
        grads[slot][r : r + HALF, :] = f32dot(turned[at, :], scaled[...])

    def probe(i, slot, target, terms):
        target[...] += f32dot(tokens[:, span(i)], terms[slot][...])

    def pieces(i, slot, first, last):
        for r in range(first, last, ROWS):
            at = pl.ds(pl.multiple_of(i * TILE + r, ROWS), ROWS)
            for c in range(0, width, COLUMNS):
                cols = slice(c, min(c + COLUMNS, width))
                yield r, cols, grads[slot][r : r + ROWS, cols], one[at, cols], two[at, cols], adjoint[at, cols]

    grad_rows(0, 0, 0)
    grad_rows(0, 0, HALF)
    sq, cross = {}, {}
    for r, cols, g, m1, m2, adj in pieces(0, 0, 0, SAMPLE):
        _, _, upd = update(g, m1, m2)
        sq[cols.start] = sq.get(cols.start, 0.0) + fold(upd * upd)
        cross[cols.start] = cross.get(cols.start, 0.0) + fold(adj * upd)
    sq = jnp.sum(sum(sq.values()), keepdims=True)
    cross = jnp.sum(sum(cross.values()), keepdims=True)
    clipped = sq * RATIO**2 > float(SAMPLE * width)
    guess = jnp.where(clipped, cross / jnp.maximum(sq, 1.0), 0.0)

    sums[...] = jnp.zeros_like(sums)

    def update_rows(i, slot, first):
        sq, cross = {}, {}
        for r, cols, g, m1, m2, adj in pieces(i, slot, first, first + HALF):
            over, inv, upd = update(g, m1, m2)
            sq[cols.start] = sq.get(cols.start, 0.0) + fold(upd * upd)
            cross[cols.start] = cross.get(cols.start, 0.0) + fold(adj * upd)
            pull = inv * (1.0 - g * (upd * over))
            firsts[slot][r : r + ROWS, cols] = ((adj - guess * upd) * pull).astype(jnp.bfloat16)
            seconds[slot][r : r + ROWS, cols] = (upd * pull).astype(jnp.bfloat16)
        sums[0] += sum(sq.values())
        sums[1] += sum(cross.values())

    def body(i, slot, ahead=True, behind=True):
        for r, target, terms in ((0, along, firsts), (HALF, across, seconds)):
            if ahead:
                grad_rows(i + 1, 1 - slot, r)
            update_rows(i, slot, r)
            if behind:
                probe(i - 1, 1 - slot, target, terms)

    body(0, 0, behind=False)

    def pair(k, _):
        body(2 * k + 1, 1)
        body(2 * k + 2, 0)
        return 0

    lax.fori_loop(0, tiles // 2 - 1, pair, 0)
    body(tiles - 1, 1, ahead=False)
    probe(tiles - 1, 1, along, firsts)
    probe(tiles - 1, 1, across, seconds)

    height = count // n
    places = owners(n)

    def spread(x):
        x = sum(x[:, i : i + 128] for i in range(0, width, 128))
        for k, place in enumerate(places):
            upright[pl.ds(pl.multiple_of(place * height, height), height), :] = x[k * height : (k + 1) * height, :]
        return jnp.sum(jnp.transpose(upright[...]), axis=0, keepdims=True)

    b = score[...] * across[...]
    a = score[...] * along[...] + guess * b
    whole = lambda x: jnp.broadcast_to(jnp.sum(x, keepdims=True), (1, count))
    stats[0:1, :] = RATIO * spread(a)
    stats[1:2, :] = RATIO**2 * spread(b)
    stats[2:3, :] = RATIO**2 * whole(sums[0])
    stats[3:4, :] = RATIO * whole(sums[1])
    stats[4:8, :] = jnp.broadcast_to(guess, (4, count))


def step_call(n, tokens, turned, scaled, score, one, two, adjoint):
    count, width = scaled.shape
    vmem = pl.BlockSpec(memory_space=pltpu.VMEM)
    block = lambda dtype: pltpu.VMEM((TILE, width), dtype)
    return pl.pallas_call(
        functools.partial(step_kernel, n),
        in_specs=[vmem] * 7,
        out_specs=[vmem] * 3,
        out_shape=[
            pltpu.VMEM((count, width), jnp.float32),
            pltpu.VMEM((count, width), jnp.float32),
            pltpu.VMEM((8, count), jnp.float32),
        ],
        scratch_shapes=[
            block(jnp.float32),
            block(jnp.float32),
            block(jnp.bfloat16),
            block(jnp.bfloat16),
            block(jnp.bfloat16),
            block(jnp.bfloat16),
            pltpu.VMEM((2, 8, min(COLUMNS, width)), jnp.float32),
            pltpu.VMEM((count, 128), jnp.float32),
        ],
        compiler_params=pltpu.CompilerParams(vmem_limit_bytes=VMEM_BYTES),
        name="step",
    )(tokens, turned, scaled, score, one, two, adjoint)


def in_hbm(x):
    return pltpu.with_memory_space_constraint(x, pltpu.HBM)


def theta_kernel(n, entries, s0, s1, s2, s3, own, along, across, bend, turned, adjoint, theta, scores, ready, sent):
    total = s0[...] + s1[...] + (s2[...] + s3[...])
    sq, cross = total[2:3, 0:1], total[3:4, 0:1]
    rms = jnp.sqrt(sq / entries)
    scale = 1.0 / jnp.maximum(1.0, rms)
    bind = jnp.where(rms > 1.0, 1.0 / (rms * rms * rms), 0.0)
    lead = -0.01 * scale
    rest = 0.01 * cross * bind / entries
    mine = lead * total[0:8, :] + rest * pltpu.roll(total, 7, 0)
    count = total.shape[1]
    height = count // n
    mine = pltpu.roll(mine, lax.rem(count - lax.axis_index("dp") * height, count), 1)
    scores[...] = mine[0:1, 0:height]
    lead_here = RATIO * lead
    rest_here = RATIO**2 * rest + lead_here * own[4:5, 0:1]
    bent = (bend[...] * (lead_here * along[...] + rest_here * across[...])).astype(jnp.bfloat16)

    def copy(i):
        at = pl.ds(i * TILE, TILE)
        return pltpu.make_async_copy(ready.at[at, :], theta.at[at, :], sent.at[i])

    tiles = theta.shape[0] // TILE
    for i in range(tiles):
        at = pl.ds(i * TILE, TILE)
        ready[at, :] = 0.999 * adjoint[at, :] + f32dot(turned[at, :], bent)
        copy(i).start()
    for i in range(tiles):
        copy(i).wait()


def theta_call(n, entries, sums, own, along, across, bend, turned, adjoint):
    depth, width = adjoint.shape
    count = turned.shape[1]
    vmem = pl.BlockSpec(memory_space=pltpu.VMEM)
    return pl.pallas_call(
        functools.partial(theta_kernel, n, entries),
        in_specs=[vmem] * 10,
        out_specs=[pl.BlockSpec(memory_space=pl.ANY), vmem],
        out_shape=[
            jax.ShapeDtypeStruct((depth, width), jnp.float32),
            jax.ShapeDtypeStruct((1, count // n), jnp.float32),
        ],
        scratch_shapes=[pltpu.VMEM((depth, width), jnp.float32), pltpu.SemaphoreType.DMA((depth // TILE,))],
        compiler_params=pltpu.CompilerParams(vmem_limit_bytes=VMEM_BYTES),
        name="theta",
    )(*sums, own, along, across, bend, turned, adjoint)


def shards(n, tokens, cotangent, token_weight, weight, moment_one, moment_two, adjoint):
    entries = float(adjoint.shape[0] * adjoint.shape[1] * n)
    errands = [
        lambda after: fetch(weight, after),
        lambda after: fetch(moment_one, after),
        lambda after: fetch(moment_two, after),
    ]
    blocks, (weight_near, one, two) = gather(tokens, n, errands)
    half = len(blocks) // 2
    rows, turned, gate, cot, weights, adjoint_near = early_call(
        n, blocks[:half], cotangent, token_weight.reshape(1, -1), adjoint, weight_near, two
    )
    rows, turned, gate, scaled, bend, score = late_call(blocks[half:], weight_near, cot, weights, rows, turned, gate)
    along, across, stats = step_call(n, rows, turned, scaled, score, one, two, adjoint_near)
    sums = all_sum(stats, n)
    theta_bar, scores = theta_call(n, entries, sums, stats, along, across, bend, turned, adjoint_near)
    return (theta_bar, scores.reshape(-1))


def solution(mesh):
    in_specs = (
        P(("group", "dp"), None),
        P("group", "dp"),
        P("group"),
        P(None, "dp"),
        P(None, "dp"),
        P(None, "dp"),
        P(None, "dp"),
    )
    out_specs = (P("group", "dp"), P(("group", "dp")))
    body = functools.partial(shards, mesh.shape["dp"])
    return jax.shard_map(body, mesh=mesh, in_specs=in_specs, out_specs=out_specs, check_vma=False)
```

time: 57.1 us -> 59.6 us (1.044)
  Pallas kernels: 26.7 us -> 30.9 us
  waiting for transfers between devices: 13.1 us -> 10.6 us
  local copies, waits for them, and re-layouts: 0.01 us -> 0.92 us
    pallas_call x3 -> x6, Pallas kernels: 22.4 us -> 26.6 us  [the longest x1 10.4 us: step_call(): pl.pallas_call(functools.partial(step_kernel, n), in_specs=[vmem] * 7, ou...]
    ppermute x7 -> x4, waiting for transfers between devices: 5.96 us -> 4.49 us  [onward(): return lax.ppermute(value, 'dp', pairs)]
    ppermute x14 -> x10, waiting for transfers between devices: 7.11 us -> 6.15 us  [swapped(): return lax.ppermute(value, 'dp', [(d ^ mask, d) for d in range(n)])]
    unnamed x2 -> x1, local copies, waits for them, and re-layouts: 0.01 us -> 0.91 us
    ppermute x14 -> x10, starting transfers between devices: 7.52 us -> 6.84 us  [swapped(): return lax.ppermute(value, 'dp', [(d ^ mask, d) for d in range(n)])]
    ppermute x7 -> x4, starting transfers between devices: 8.93 us -> 9.22 us  [onward(): return lax.ppermute(value, 'dp', pairs)]
  transfers between devices with their start and end apart: 21 -> 14, of which waited for: 10 -> 9; matrix products, arithmetic and copies ran while one was open for 0% -> 2% of each run, Pallas kernels for 10% -> 23%
where the time goes in v7:
time: 59.6 us; the launch traced here: 59.3 us
  Pallas kernels  30.9 us (52%)
  starting transfers between devices  16.1 us (27%)
  waiting for transfers between devices  10.6 us (18%)
  local copies, waits for them, and re-layouts  0.92 us (2%)
  between operations  0.71 us (1%)
    pallas_call x1, Pallas kernels, step_call(): pl.pallas_call(functools.partial(step_kernel, n), in_specs=[vmem] * 7, ou...  10.4 us
    ppermute x4, starting transfers between devices, onward(): return lax.ppermute(value, 'dp', pairs)  9.22 us
    pallas_call x3, Pallas kernels, fetch(): pl.pallas_call(fetch_kernel, in_specs=[pl.BlockSpec(memory_space=pl.ANY)]...  8.36 us
    ppermute x10, starting transfers between devices, swapped(): return lax.ppermute(value, 'dp', [(d ^ mask, d) for d in range(n)])  6.84 us
    ppermute x10, waiting for transfers between devices, swapped(): return lax.ppermute(value, 'dp', [(d ^ mask, d) for d in range(n)])  6.15 us
    pallas_call x1, Pallas kernels, early_call(): pl.pallas_call(functools.partial(early_kernel, n, half), in_specs=[far] *...  5.47 us
    ppermute x4, waiting for transfers between devices, onward(): return lax.ppermute(value, 'dp', pairs)  4.49 us
    pallas_call x1, Pallas kernels, theta_call(): pl.pallas_call(functools.partial(theta_kernel, n, entries), in_specs=[vme...  4.31 us
  transfers between devices with their start and end apart: 14, of which 9 were waited for; matrix products, arithmetic and copies ran while one was open for 2% of the time, Pallas kernels for 23%

profile of v7, /device:TPU:0, one launch (start us, length us, event | category | flops | bytes accessed | tf_op | source)
XLA Modules:
  0.0 59.3 jit_solution(16105383170292559057)
XLA Ops:
  0.6 0.5 collective-permute-start
  1.1 0.9 %constant_dynamic-update-slice_fusion.1 = bf16[32,4096]{1,0:T(8,128)(2,1)S(1)} fusion(bf16[16,4096]{1,0:T(8,128)(2,1)} %after.1), kind=kLoop, calls=%fused_computation.2 | loop fusion | bytes 262144
  2.1 0.3 collective-permute-done
  2.4 3.0 %collective-permute-start.1 = (bf16[32,4096]{1,0:T(8,128)(2,1)S(1)}, bf16[32,4096]{1,0:T(8,128)(2,1)S(1)}, u32[]{:S(2)}, u32[]{:S(2)}) collective-permute-start(bf16[32,4096]{1,0:T(8,128)(2,1)S(1)} %constant_dynamic-update-slice_fusion.refs_0_), channel_id=1, source_target_pairs={{2,0},{5,1},{0,4},{9,5},{4,8},{13,9},{8,12},{15,13},{12,14},{11,15... | collective-permute-start | bytes 786440 | tf_op jit(solution)/shard_map/ppermute | solution.py:39
  5.3 2.8 %fetch.3 = (bf16[4096,512]{1,0:T(8,128)(2,1)S(1)}, f32[8,128]{1,0:T(8,128)}) custom-call(bf16[4096,512]{1,0:T(8,128)(2,1)} %far.3, bf16[16,4096]{1,0:T(8,128)(2,1)} %after.1), custom_call_target="tpu_custom_call" | custom-call | flops 4294967296 | bytes 8388608 | tf_op jit(solution)/shard_map/fetch/pallas_call | solution.py:114
  8.1 1.5 %collective-permute-done.1.refs_1_.after = bf16[32,4096]{1,0:T(8,128)(2,1)S(1)} collective-permute-done((bf16[32,4096]{1,0:T(8,128)(2,1)S(1)}, bf16[32,4096]{1,0:T(8,128)(2,1)S(1)}, u32[]{:S(2)}, u32[]{:S(2)}) %collective-permute-start.1) | collective-permute-done | bytes 262176 | tf_op jit(solution)/shard_map/ppermute | solution.py:39
  9.6 2.1 %collective-permute-start.2 = (bf16[32,4096]{1,0:T(8,128)(2,1)S(1)}, bf16[32,4096]{1,0:T(8,128)(2,1)S(1)}, u32[]{:S(2)}, u32[]{:S(2)}) collective-permute-start(bf16[32,4096]{1,0:T(8,128)(2,1)S(1)} %collective-permute-done.1.refs_1_.after), channel_id=1, source_target_pairs={{2,0},{5,1},{0,4},{9,5},{4,8},{13,9},{8,12},{15,13},{12,14},{11,15... | collective-permute-start | bytes 786440 | tf_op jit(solution)/shard_map/ppermute | solution.py:39
  11.7 0.0 collective-permute-start.7
  11.7 2.8 %fetch.5 = (bf16[4096,512]{1,0:T(8,128)(2,1)S(1)}, f32[8,128]{1,0:T(8,128)}) custom-call(bf16[4096,512]{1,0:T(8,128)(2,1)} %far.5, bf16[32,4096]{1,0:T(8,128)(2,1)S(1)} %collective-permute-done.1.refs_1_.after), custom_call_target="tpu_custom_call" | custom-call | flops 4294967296 | bytes 8388608 | tf_op jit(solution)/shard_map/fetch/pallas_call | solution.py:114
  14.5 1.5 %collective-permute-done.2.after.refs_3_ = bf16[32,4096]{1,0:T(8,128)(2,1)S(1)} collective-permute-done((bf16[32,4096]{1,0:T(8,128)(2,1)S(1)}, bf16[32,4096]{1,0:T(8,128)(2,1)S(1)}, u32[]{:S(2)}, u32[]{:S(2)}) %collective-permute-start.2) | collective-permute-done | bytes 262176 | tf_op jit(solution)/shard_map/ppermute | solution.py:39
  16.0 2.1 %collective-permute-start.4 = (bf16[32,4096]{1,0:T(8,128)(2,1)S(1)}, bf16[32,4096]{1,0:T(8,128)(2,1)S(1)}, u32[]{:S(2)}, u32[]{:S(2)}) collective-permute-start(bf16[32,4096]{1,0:T(8,128)(2,1)S(1)} %collective-permute-done.2.after.refs_3_), channel_id=1, source_target_pairs={{2,0},{5,1},{0,4},{9,5},{4,8},{13,9},{8,12},{15,13},{12,14},{11,15... | collective-permute-start | bytes 786440 | tf_op jit(solution)/shard_map/ppermute | solution.py:39
  18.1 0.0 collective-permute-start.3
  18.1 2.8 %fetch.4 = (bf16[4096,512]{1,0:T(8,128)(2,1)S(1)}, f32[8,128]{1,0:T(8,128)}) custom-call(bf16[4096,512]{1,0:T(8,128)(2,1)} %far.4, bf16[32,4096]{1,0:T(8,128)(2,1)S(1)} %collective-permute-done.2.after.refs_3_), custom_call_target="tpu_custom_call" | custom-call | flops 4294967296 | bytes 8388608 | tf_op jit(solution)/shard_map/fetch/pallas_call | solution.py:114
  20.9 1.5 %collective-permute-done.4.refs_1_ = bf16[32,4096]{1,0:T(8,128)(2,1)S(1)} collective-permute-done((bf16[32,4096]{1,0:T(8,128)(2,1)S(1)}, bf16[32,4096]{1,0:T(8,128)(2,1)S(1)}, u32[]{:S(2)}, u32[]{:S(2)}) %collective-permute-start.4) | collective-permute-done | bytes 262176 | tf_op jit(solution)/shard_map/ppermute | solution.py:39
  22.4 2.1 %collective-permute-start.6 = (bf16[32,4096]{1,0:T(8,128)(2,1)S(1)}, bf16[32,4096]{1,0:T(8,128)(2,1)S(1)}, u32[]{:S(2)}, u32[]{:S(2)}) collective-permute-start(bf16[32,4096]{1,0:T(8,128)(2,1)S(1)} %collective-permute-done.4.refs_1_), channel_id=1, source_target_pairs={{2,0},{5,1},{0,4},{9,5},{4,8},{13,9},{8,12},{15,13},{12,14},{11,15... | collective-permute-start | bytes 786440 | tf_op jit(solution)/shard_map/ppermute | solution.py:39
  24.5 0.0 collective-permute-start.5
  24.5 0.0 collective-permute-done.7.refs_2_
  24.5 5.5 %early.1 = (bf16[256,4096]{1,0:T(8,128)(2,1)S(1)}, bf16[4096,256]{1,0:T(8,128)(2,1)S(1)}, f32[256,512]{1,0:T(8,128)S(1)}, bf16[256,512]{1,0:T(8,128)(2,1)S(1)}, ...) custom-call(bf16[32,4096]{1,0:T(8,128)(2,1)S(1)} %constant_dynamic-update-slice_fusion.refs_0_, ...), custom_call_target="tpu_custom_call" | custom-call | flops 4294967296 | bytes 12582912 | tf_op jit(solution)/shard_map/early/pallas_call | solution.py:189
  29.9 0.0 collective-permute-done.3.refs_0_
  30.0 0.0 collective-permute-done.5.refs_2_
  30.0 0.0 collective-permute-done.6.refs_3_
  30.0 2.4 %late.1 = (bf16[256,4096]{1,0:T(8,128)(2,1)S(1)}, bf16[4096,256]{1,0:T(8,128)(2,1)S(1)}, f32[256,512]{1,0:T(8,128)S(1)}, bf16[256,512]{1,0:T(8,128)(2,1)S(1)}, f...) custom-call(bf16[32,4096]{1,0:T(8,128)(2,1)S(1)} %collective-permute-don, ...), custom_call_target="tpu_custom_call", output_to_operand_aliasing={{0}: (7, {}), {1}: (8, {}), {2}: (9, {})} | custom-call | tf_op jit(solution)/shard_map/late/pallas_call | solution.py:238
  32.4 10.4 %step.1 = (f32[256,512]{1,0:T(8,128)S(1)}, f32[256,512]{1,0:T(8,128)S(1)}, f32[8,256]{1,0:T(8,128)S(1)}) custom-call(bf16[256,4096]{1,0:T(8,128)(2,1)S(1)} %get-tuple-element.28.tokens, bf16[4096,256]{1,0:T(8,128)(2,1)S(1)} %get-tuple-element.29.turned, bf16[256,512]{1,0:T(8,128)(2,1)S(1)} %get-tuple-element.30.scaled, ...), custom_call_target="tpu_custom_call" | custom-call | tf_op jit(solution)/shard_map/step/pallas_call | solution.py:349
  42.8 3.6 %collective-permute-start.10 = (f32[8,256]{1,0:T(8,128)S(1)}, f32[8,256]{1,0:T(8,128)S(1)}, u32[]{:S(2)}, u32[]{:S(2)}) collective-permute-start(f32[8,256]{1,0:T(8,128)S(1)} %get-tuple-element.34.own), channel_id=1, source_target_pairs={{12,0},{13,1},{14,2},{15,3},{8,4},{9,5},{10,6},{11,7},{4,8},{5,9},... | collective-permute-start | bytes 24584 | tf_op jit(solution)/shard_map/ppermute | solution.py:25
  46.4 0.0 collective-permute-start.8
  46.4 0.8 %collective-permute-start.9 = (f32[8,256]{1,0:T(8,128)S(1)}, f32[8,256]{1,0:T(8,128)S(1)}, u32[]{:S(2)}, u32[]{:S(2)}) collective-permute-start(f32[8,256]{1,0:T(8,128)S(1)} %get-tuple-element.34.own), channel_id=1, source_target_pairs={{8,0},{9,1},{10,2},{11,3},{12,4},{13,5},{14,6},{15,7},{0,8},{1,9},... | collective-permute-start | bytes 24584 | tf_op jit(solution)/shard_map/ppermute | solution.py:25
  47.2 1.1 %collective-permute-done.10 = f32[8,256]{1,0:T(8,128)S(1)} collective-permute-done((f32[8,256]{1,0:T(8,128)S(1)}, f32[8,256]{1,0:T(8,128)S(1)}, u32[]{:S(2)}, u32[]{:S(2)}) %collective-permute-start.10) | collective-permute-done | bytes 8224 | tf_op jit(solution)/shard_map/ppermute | solution.py:25
  48.3 1.7 %collective-permute-done.8 = f32[8,256]{1,0:T(8,128)S(1)} collective-permute-done((f32[8,256]{1,0:T(8,128)S(1)}, f32[8,256]{1,0:T(8,128)S(1)}, u32[]{:S(2)}, u32[]{:S(2)}) %collective-permute-start.8) | collective-permute-done | bytes 8224 | tf_op jit(solution)/shard_map/ppermute | solution.py:25
  50.0 0.9 %collective-permute-done.9 = f32[8,256]{1,0:T(8,128)S(1)} collective-permute-done((f32[8,256]{1,0:T(8,128)S(1)}, f32[8,256]{1,0:T(8,128)S(1)}, u32[]{:S(2)}, u32[]{:S(2)}) %collective-permute-start.9) | collective-permute-done | bytes 8224 | tf_op jit(solution)/shard_map/ppermute | solution.py:25
  51.0 0.0 collective-permute-start.11
  51.0 0.9 %collective-permute-start.12 = (f32[8,256]{1,0:T(8,128)S(1)}, f32[8,256]{1,0:T(8,128)S(1)}, u32[]{:S(2)}, u32[]{:S(2)}) collective-permute-start(f32[8,256]{1,0:T(8,128)S(1)} %add_add_fusion.s0), channel_id=1, source_target_pairs={{2,0},{3,1},{0,2},{1,3},{6,4},{7,5},{4,6},{5,7},{10,8},{11,9},{8,1... | collective-permute-start | bytes 24584 | tf_op jit(solution)/shard_map/ppermute | solution.py:25
  51.9 0.9 %collective-permute-start.13 = (f32[8,256]{1,0:T(8,128)S(1)}, f32[8,256]{1,0:T(8,128)S(1)}, u32[]{:S(2)}, u32[]{:S(2)}) collective-permute-start(f32[8,256]{1,0:T(8,128)S(1)} %add_add_fusion.s0), channel_id=1, source_target_pairs={{3,0},{2,1},{1,2},{0,3},{7,4},{6,5},{5,6},{4,7},{11,8},{10,9},{9,1... | collective-permute-start | bytes 24584 | tf_op jit(solution)/shard_map/ppermute | solution.py:25
  52.8 0.0 collective-permute-done.11.s1
  52.8 1.9 %collective-permute-done.12.s2 = f32[8,256]{1,0:T(8,128)S(1)} collective-permute-done((f32[8,256]{1,0:T(8,128)S(1)}, f32[8,256]{1,0:T(8,128)S(1)}, u32[]{:S(2)}, u32[]{:S(2)}) %collective-permute-start.12) | collective-permute-done | bytes 8224 | tf_op jit(solution)/shard_map/ppermute | solution.py:25
  54.7 0.3 collective-permute-done.13.s3
  55.0 4.3 %theta.1 = (f32[4096,512]{1,0:T(8,128)}, f32[1,16]{1,0:T(1,128)}) custom-call(f32[8,256]{1,0:T(8,128)S(1)} %add_add_fusion.s0, f32[8,256]{1,0:T(8,128)S(1)} %collective-permute-done.11.s1, f32[8,256]{1,0:T(8,128)S(1)} %collective-permute-done.12.s2, f32[8,256]{1,0:T(8,128)S(1)} %collective-permute-done.13.s3, f32[8,256]{1,0:T(8,128)S(1)} %get-tuple-element.34.own, ...), custom_call_target="tpu_custom_call" | custom-call | tf_op jit(solution)/shard_map/theta/pallas_call | solution.py:411
  (2 shorter events, 0.0 us)
Async XLA Ops:
  0.6 1.7 %collective-permute-start = (bf16[16,4096]{1,0:T(8,128)(2,1)}, bf16[16,4096]{1,0:T(8,128)(2,1)S(1)}, u32[]{:S(2)}, u32[]{:S(2)}) collective-permute-start(bf16[16,4096]{1,0:T(8,128)(2,1)} %after.1), channel_id=1, source_target_pairs={{1,0},{0,1},{3,2},{2,3},{5,4},{4,5},{7,6},{6,7},{9,8},{8,9},{11,10... | collective-permute-start | bytes 393224 | tf_op jit(solution)/shard_map/ppermute | solution.py:25
  2.4 7.3 %collective-permute-start.1 = (bf16[32,4096]{1,0:T(8,128)(2,1)S(1)}, bf16[32,4096]{1,0:T(8,128)(2,1)S(1)}, u32[]{:S(2)}, u32[]{:S(2)}) collective-permute-start(bf16[32,4096]{1,0:T(8,128)(2,1)S(1)} %constant_dynamic-update-slice_fusion.refs_0_), channel_id=1, source_target_pairs={{2,0},{5,1},{0,4},{9,5},{4,8},{13,9},{8,12},{15,13},{12,14},{11,15... | collective-permute-start | bytes 786440 | tf_op jit(solution)/shard_map/ppermute | solution.py:39
  9.6 6.4 %collective-permute-start.2 = (bf16[32,4096]{1,0:T(8,128)(2,1)S(1)}, bf16[32,4096]{1,0:T(8,128)(2,1)S(1)}, u32[]{:S(2)}, u32[]{:S(2)}) collective-permute-start(bf16[32,4096]{1,0:T(8,128)(2,1)S(1)} %collective-permute-done.1.refs_1_.after), channel_id=1, source_target_pairs={{2,0},{5,1},{0,4},{9,5},{4,8},{13,9},{8,12},{15,13},{12,14},{11,15... | collective-permute-start | bytes 786440 | tf_op jit(solution)/shard_map/ppermute | solution.py:39
  11.7 12.8 %collective-permute-start.7 = (bf16[32,4096]{1,0:T(8,128)(2,1)S(1)}, bf16[32,4096]{1,0:T(8,128)(2,1)S(1)}, u32[]{:S(2)}, u32[]{:S(2)}) collective-permute-start(bf16[32,4096]{1,0:T(8,128)(2,1)S(1)} %collective-permute-done.1.refs_1_.after), channel_id=1, source_target_pairs={{1,0},{0,1},{3,2},{2,3},{5,4},{4,5},{7,6},{6,7},{9,8},{8,9},{11,10... | collective-permute-start | bytes 786440 | tf_op jit(solution)/shard_map/ppermute | solution.py:25
  16.0 6.4 %collective-permute-start.4 = (bf16[32,4096]{1,0:T(8,128)(2,1)S(1)}, bf16[32,4096]{1,0:T(8,128)(2,1)S(1)}, u32[]{:S(2)}, u32[]{:S(2)}) collective-permute-start(bf16[32,4096]{1,0:T(8,128)(2,1)S(1)} %collective-permute-done.2.after.refs_3_), channel_id=1, source_target_pairs={{2,0},{5,1},{0,4},{9,5},{4,8},{13,9},{8,12},{15,13},{12,14},{11,15... | collective-permute-start | bytes 786440 | tf_op jit(solution)/shard_map/ppermute | solution.py:39
  18.1 11.9 %collective-permute-start.3 = (bf16[32,4096]{1,0:T(8,128)(2,1)S(1)}, bf16[32,4096]{1,0:T(8,128)(2,1)S(1)}, u32[]{:S(2)}, u32[]{:S(2)}) collective-permute-start(bf16[32,4096]{1,0:T(8,128)(2,1)S(1)} %collective-permute-done.2.after.refs_3_), channel_id=1, source_target_pairs={{1,0},{0,1},{3,2},{2,3},{5,4},{4,5},{7,6},{6,7},{9,8},{8,9},{11,10... | collective-permute-start | bytes 786440 | tf_op jit(solution)/shard_map/ppermute | solution.py:25
  22.4 7.6 %collective-permute-start.6 = (bf16[32,4096]{1,0:T(8,128)(2,1)S(1)}, bf16[32,4096]{1,0:T(8,128)(2,1)S(1)}, u32[]{:S(2)}, u32[]{:S(2)}) collective-permute-start(bf16[32,4096]{1,0:T(8,128)(2,1)S(1)} %collective-permute-done.4.refs_1_), channel_id=1, source_target_pairs={{2,0},{5,1},{0,4},{9,5},{4,8},{13,9},{8,12},{15,13},{12,14},{11,15... | collective-permute-start | bytes 786440 | tf_op jit(solution)/shard_map/ppermute | solution.py:39
  24.5 5.5 %collective-permute-start.5 = (bf16[32,4096]{1,0:T(8,128)(2,1)S(1)}, bf16[32,4096]{1,0:T(8,128)(2,1)S(1)}, u32[]{:S(2)}, u32[]{:S(2)}) collective-permute-start(bf16[32,4096]{1,0:T(8,128)(2,1)S(1)} %collective-permute-done.4.refs_1_), channel_id=1, source_target_pairs={{1,0},{0,1},{3,2},{2,3},{5,4},{4,5},{7,6},{6,7},{9,8},{8,9},{11,10... | collective-permute-start | bytes 786440 | tf_op jit(solution)/shard_map/ppermute | solution.py:25
  42.8 5.5 %collective-permute-start.10 = (f32[8,256]{1,0:T(8,128)S(1)}, f32[8,256]{1,0:T(8,128)S(1)}, u32[]{:S(2)}, u32[]{:S(2)}) collective-permute-start(f32[8,256]{1,0:T(8,128)S(1)} %get-tuple-element.34.own), channel_id=1, source_target_pairs={{12,0},{13,1},{14,2},{15,3},{8,4},{9,5},{10,6},{11,7},{4,8},{5,9},... | collective-permute-start | bytes 24584 | tf_op jit(solution)/shard_map/ppermute | solution.py:25
  46.4 3.7 %collective-permute-start.8 = (f32[8,256]{1,0:T(8,128)S(1)}, f32[8,256]{1,0:T(8,128)S(1)}, u32[]{:S(2)}, u32[]{:S(2)}) collective-permute-start(f32[8,256]{1,0:T(8,128)S(1)} %get-tuple-element.34.own), channel_id=1, source_target_pairs={{4,0},{5,1},{6,2},{7,3},{0,4},{1,5},{2,6},{3,7},{12,8},{13,9},{14,... | collective-permute-start | bytes 24584 | tf_op jit(solution)/shard_map/ppermute | solution.py:25
  46.4 4.5 %collective-permute-start.9 = (f32[8,256]{1,0:T(8,128)S(1)}, f32[8,256]{1,0:T(8,128)S(1)}, u32[]{:S(2)}, u32[]{:S(2)}) collective-permute-start(f32[8,256]{1,0:T(8,128)S(1)} %get-tuple-element.34.own), channel_id=1, source_target_pairs={{8,0},{9,1},{10,2},{11,3},{12,4},{13,5},{14,6},{15,7},{0,8},{1,9},... | collective-permute-start | bytes 24584 | tf_op jit(solution)/shard_map/ppermute | solution.py:25
  51.0 1.9 %collective-permute-start.11 = (f32[8,256]{1,0:T(8,128)S(1)}, f32[8,256]{1,0:T(8,128)S(1)}, u32[]{:S(2)}, u32[]{:S(2)}) collective-permute-start(f32[8,256]{1,0:T(8,128)S(1)} %add_add_fusion.s0), channel_id=1, source_target_pairs={{1,0},{0,1},{3,2},{2,3},{5,4},{4,5},{7,6},{6,7},{9,8},{8,9},{11,10... | collective-permute-start | bytes 24584 | tf_op jit(solution)/shard_map/ppermute | solution.py:25
  51.0 3.7 %collective-permute-start.12 = (f32[8,256]{1,0:T(8,128)S(1)}, f32[8,256]{1,0:T(8,128)S(1)}, u32[]{:S(2)}, u32[]{:S(2)}) collective-permute-start(f32[8,256]{1,0:T(8,128)S(1)} %add_add_fusion.s0), channel_id=1, source_target_pairs={{2,0},{3,1},{0,2},{1,3},{6,4},{7,5},{4,6},{5,7},{10,8},{11,9},{8,1... | collective-permute-start | bytes 24584 | tf_op jit(solution)/shard_map/ppermute | solution.py:25
  51.9 3.1 %collective-permute-start.13 = (f32[8,256]{1,0:T(8,128)S(1)}, f32[8,256]{1,0:T(8,128)S(1)}, u32[]{:S(2)}, u32[]{:S(2)}) collective-permute-start(f32[8,256]{1,0:T(8,128)S(1)} %add_add_fusion.s0), channel_id=1, source_target_pairs={{3,0},{2,1},{1,2},{0,3},{7,4},{6,5},{5,6},{4,7},{11,8},{10,9},{9,1... | collective-permute-start | bytes 24584 | tf_op jit(solution)/shard_map/ppermute | solution.py:25

commit v8 on v7

--- a/solution.py
+++ b/solution.py
@@ -42,23 +42,17 @@
 def gather(tokens, n, errands):
     hops = n // 4
     done = []
-    token = None
-    own = jnp.concatenate([tokens, swapped(tokens, n, 1)], axis=0)
-    blocks = [own]
-    here = own
+    here = [tokens, swapped(tokens, n, 1)]
+    parts = list(here)
     for hop in range(1, hops + 1):
-        after = in_hbm(tokens) if hop == 1 else here
-        if token is not None:
-            here = lax.optimization_barrier((here, token))[0]
-        here = onward(here, n)
-        token = None
+        after = in_hbm(tokens) if hop == 1 else here[0]
+        here = [onward(x, n) for x in here]
         if errands[len(done) :]:
-            result, token = errands[len(done)](after)
-            done.append(result)
-        blocks.append(here)
+            done.append(errands[len(done)](after))
+        parts += here
         if hop < hops:
-            blocks.append(swapped(here, n, 1))
-    return blocks, done
+            parts += [swapped(x, n, 1) for x in here]
+    return parts, done
 
 
 def owners(n):
@@ -103,10 +97,9 @@
     return over, inv, first * inv
 
 
-def fetch_kernel(far, after, near, token, sem):
+def fetch_kernel(far, after, near, sem):
     copy = pltpu.make_async_copy(far, near, sem.at[0])
     copy.start()
-    token[...] = jnp.zeros_like(token)
     copy.wait()
 
 
@@ -114,8 +107,8 @@
     return pl.pallas_call(
         fetch_kernel,
         in_specs=[pl.BlockSpec(memory_space=pl.ANY)] * 2,
-        out_specs=[pl.BlockSpec(memory_space=pltpu.VMEM)] * 2,
-        out_shape=[pltpu.VMEM(x.shape, x.dtype), jax.ShapeDtypeStruct((8, 128), jnp.float32)],
+        out_specs=pl.BlockSpec(memory_space=pltpu.VMEM),
+        out_shape=pltpu.VMEM(x.shape, x.dtype),
         scratch_shapes=[pltpu.SemaphoreType.DMA((1,))],
         compiler_params=pltpu.CompilerParams(vmem_limit_bytes=1 << 20),
         cost_estimate=pl.CostEstimate(flops=COST, bytes_accessed=8 << 20, transcendentals=0),
@@ -127,7 +120,7 @@
     return pl.ds(pl.multiple_of(i * TILE, TILE), TILE)
 
 
-def gate_rows(blocks, first, sems, weight, tokens, turned, gate):
+def gate_rows(blocks, first, sems, weight, tokens, turned, gate, beside):
     height, depth = blocks[0].shape
     count = len(blocks) * height
     rows = slice(first, first + count)
@@ -142,6 +135,7 @@
         copy.wait()
 
     def step(i, _):
+        beside(i)
         here = tokens[rows, span(i)]
         gate[rows, :] += f32dot(here, weight[span(i), :])
         turned[span(i), rows] = here.T
@@ -151,13 +145,12 @@
 
 
 def early_kernel(n, half, *refs):
-    blocks, (far_cot, far_weight, far_adjoint, weight, _) = refs[:half], refs[half : half + 5]
-    (tokens, turned, gate, cot, weights, adjoint) = refs[half + 5 : half + 11]
-    (token_weight, upright, sems, cot_sems, far_sems) = refs[half + 11 :]
+    blocks, (far_cot, far_weight, weight) = refs[:half], refs[half : half + 3]
+    (tokens, turned, gate, cot, weights) = refs[half + 3 : half + 8]
+    (token_weight, upright, sems, cot_sems, far_sems) = refs[half + 8 :]
     height = cot.shape[0] // n
     places = owners(n)
-    adjoint_copy = pltpu.make_async_copy(far_adjoint, adjoint, far_sems.at[0])
-    weight_copy = pltpu.make_async_copy(far_weight, token_weight, far_sems.at[1])
+    weight_copy = pltpu.make_async_copy(far_weight, token_weight, far_sems.at[0])
     cot_copies = [
         pltpu.make_async_copy(
             far_cot.at[pl.ds(pl.multiple_of(place * height, height), height), :],
@@ -169,18 +162,16 @@
     weight_copy.start()
     for copy in cot_copies:
         copy.start()
-    gate_rows(blocks, 0, sems, weight, tokens, turned, gate)
-    adjoint_copy.start()
+    gate_rows(blocks, 0, sems, weight, tokens, turned, gate, lambda i: None)
     weight_copy.wait()
     upright[...] = jnp.broadcast_to(over_columns(token_weight[...]), upright.shape)
     for k, place in enumerate(places):
         weights[k * height : (k + 1) * height, :] = upright[pl.ds(pl.multiple_of(place * height, height), height), :]
     for copy in cot_copies:
         copy.wait()
-    adjoint_copy.wait()
-
-
-def early_call(n, blocks, cot, token_weight, adjoint, weight, token):
+
+
+def early_call(n, blocks, cot, token_weight, weight):
     half = len(blocks)
     count, width = cot.shape
     depth = weight.shape[0]
@@ -188,34 +179,51 @@
     vmem = pl.BlockSpec(memory_space=pltpu.VMEM)
     return pl.pallas_call(
         functools.partial(early_kernel, n, half),
-        in_specs=[far] * (half + 3) + [vmem, far],
-        out_specs=[vmem] * 6,
+        in_specs=[far] * (half + 2) + [vmem],
+        out_specs=[vmem] * 5,
         out_shape=[
             pltpu.VMEM((count, depth), jnp.bfloat16),
             pltpu.VMEM((depth, count), jnp.bfloat16),
             pltpu.VMEM((count, width), jnp.float32),
             pltpu.VMEM((count, width), jnp.bfloat16),
             pltpu.VMEM((count, 128), jnp.float32),
-            pltpu.VMEM((depth, width), jnp.float32),
         ],
         scratch_shapes=[
             pltpu.VMEM((1, count), jnp.float32),
             pltpu.VMEM((count, 128), jnp.float32),
             pltpu.SemaphoreType.DMA((half,)),
             pltpu.SemaphoreType.DMA((n,)),
-            pltpu.SemaphoreType.DMA((2,)),
+            pltpu.SemaphoreType.DMA((1,)),
         ],
         compiler_params=pltpu.CompilerParams(vmem_limit_bytes=VMEM_BYTES),
         cost_estimate=pl.CostEstimate(flops=COST, bytes_accessed=12 << 20, transcendentals=0),
         name="early",
-    )(*blocks, *[in_hbm(x) for x in (cot, token_weight, adjoint)], weight, token)
-
-
-def late_kernel(half, *refs):
-    blocks, (weight, cot, weights) = refs[:half], refs[half : half + 3]
-    (tokens, turned, gate, scaled, bend, score, sems) = refs[half + 6 :]
-    count, width = cot.shape
-    gate_rows(blocks, count // 2, sems, weight, tokens, turned, gate)
+    )(*blocks, *[in_hbm(x) for x in (cot, token_weight)], weight)
+
+
+def replay_kernel(n, half, *refs):
+    blocks, far = refs[:half], refs[half : half + 2]
+    (weight, cot, weights, one) = refs[half + 2 : half + 6]
+    (tokens, turned, gate, adjoint, along, across, bend, stats) = refs[half + 9 : half + 17]
+    (scaled, score, two, g0, g1, a0, a1, b0, b1, sums, upright, sems, tile_sems) = refs[half + 17 :]
+    grads, firsts, seconds = (g0, g1), (a0, a1), (b0, b1)
+    near = (two, adjoint)
+    depth = one.shape[0]
+    count, width = scaled.shape
+    tiles = depth // TILE
+
+    def tile_copy(which, i):
+        return pltpu.make_async_copy(far[which].at[span(i), :], near[which].at[span(i), :], tile_sems.at[which, i])
+
+    def start(i):
+        tile_copy(0, i).start()
+        tile_copy(1, i).start()
+
+    def arrive(i):
+        tile_copy(0, i).wait()
+        tile_copy(1, i).wait()
+
+    gate_rows(blocks, count // 2, sems, weight, tokens, turned, gate, start)
     for r in range(0, count, 64):
         at = slice(r, r + 64)
         x = gate[at, :]
@@ -228,38 +236,6 @@
         bend[at, :] = token_weight * cot_f * curve
         score[at, :] = cot_f * slope
 
-
-def late_call(blocks, weight, cot, weights, tokens, turned, gate):
-    half = len(blocks)
-    count, width = cot.shape
-    far = pl.BlockSpec(memory_space=pl.ANY)
-    vmem = pl.BlockSpec(memory_space=pltpu.VMEM)
-    like = lambda x: pltpu.VMEM(x.shape, x.dtype)
-    return pl.pallas_call(
-        functools.partial(late_kernel, half),
-        in_specs=[far] * half + [vmem] * 6,
-        out_specs=[vmem] * 6,
-        out_shape=[
-            like(tokens),
-            like(turned),
-            like(gate),
-            pltpu.VMEM((count, width), jnp.bfloat16),
-            pltpu.VMEM((count, width), jnp.float32),
-            pltpu.VMEM((count, width), jnp.float32),
-        ],
-        scratch_shapes=[pltpu.SemaphoreType.DMA((half,))],
-        input_output_aliases={half + 3: 0, half + 4: 1, half + 5: 2},
-        compiler_params=pltpu.CompilerParams(vmem_limit_bytes=VMEM_BYTES),
-        name="late",
-    )(*blocks, weight, cot, weights, tokens, turned, gate)
-
-
-def step_kernel(n, tokens, turned, scaled, score, one, two, adjoint, along, across, stats, *scratch):
-    (g0, g1, a0, a1, b0, b1, sums, upright) = scratch
-    grads, firsts, seconds = (g0, g1), (a0, a1), (b0, b1)
-    depth = one.shape[0]
-    count, width = scaled.shape
-    tiles = depth // TILE
     along[...] = jnp.zeros_like(along)
     across[...] = jnp.zeros_like(across)
 
@@ -277,6 +253,7 @@
                 cols = slice(c, min(c + COLUMNS, width))
                 yield r, cols, grads[slot][r : r + ROWS, cols], one[at, cols], two[at, cols], adjoint[at, cols]
 
+    arrive(0)
     grad_rows(0, 0, 0)
     grad_rows(0, 0, HALF)
     sq, cross = {}, {}
@@ -304,6 +281,8 @@
         sums[1] += sum(cross.values())
 
     def body(i, slot, ahead=True, behind=True):
+        if ahead:
+            arrive(i + 1)
         for r, target, terms in ((0, along, firsts), (HALF, across, seconds)):
             if ahead:
                 grad_rows(i + 1, 1 - slot, r)
@@ -342,20 +321,32 @@
     stats[4:8, :] = jnp.broadcast_to(guess, (4, count))
 
 
-def step_call(n, tokens, turned, scaled, score, one, two, adjoint):
-    count, width = scaled.shape
+def replay_call(n, blocks, two, adjoint, weight, cot, weights, one, tokens, turned, gate):
+    half = len(blocks)
+    depth = one.shape[0]
+    count, width = cot.shape
+    far = pl.BlockSpec(memory_space=pl.ANY)
     vmem = pl.BlockSpec(memory_space=pltpu.VMEM)
+    like = lambda x: pltpu.VMEM(x.shape, x.dtype)
     block = lambda dtype: pltpu.VMEM((TILE, width), dtype)
     return pl.pallas_call(
-        functools.partial(step_kernel, n),
-        in_specs=[vmem] * 7,
-        out_specs=[vmem] * 3,
+        functools.partial(replay_kernel, n, half),
+        in_specs=[far] * (half + 2) + [vmem] * 7,
+        out_specs=[vmem] * 8,
         out_shape=[
+            like(tokens),
+            like(turned),
+            like(gate),
+            pltpu.VMEM((depth, width), jnp.float32),
+            pltpu.VMEM((count, width), jnp.float32),
             pltpu.VMEM((count, width), jnp.float32),
             pltpu.VMEM((count, width), jnp.float32),
             pltpu.VMEM((8, count), jnp.float32),
         ],
         scratch_shapes=[
+            pltpu.VMEM((count, width), jnp.bfloat16),
+            pltpu.VMEM((count, width), jnp.float32),
+            pltpu.VMEM((depth, width), jnp.bfloat16),
             block(jnp.float32),
             block(jnp.float32),
             block(jnp.bfloat16),
@@ -364,10 +355,13 @@
             block(jnp.bfloat16),
             pltpu.VMEM((2, 8, min(COLUMNS, width)), jnp.float32),
             pltpu.VMEM((count, 128), jnp.float32),
+            pltpu.SemaphoreType.DMA((half,)),
+            pltpu.SemaphoreType.DMA((2, depth // TILE)),
         ],
+        input_output_aliases={half + 6: 0, half + 7: 1, half + 8: 2},
         compiler_params=pltpu.CompilerParams(vmem_limit_bytes=VMEM_BYTES),
-        name="step",
-    )(tokens, turned, scaled, score, one, two, adjoint)
+        name="replay",
+    )(*blocks, in_hbm(two), in_hbm(adjoint), weight, cot, weights, one, tokens, turned, gate)
 
 
 def in_hbm(x):
@@ -424,18 +418,13 @@
 
 def shards(n, tokens, cotangent, token_weight, weight, moment_one, moment_two, adjoint):
     entries = float(adjoint.shape[0] * adjoint.shape[1] * n)
-    errands = [
-        lambda after: fetch(weight, after),
-        lambda after: fetch(moment_one, after),
-        lambda after: fetch(moment_two, after),
-    ]
-    blocks, (weight_near, one, two) = gather(tokens, n, errands)
+    errands = [lambda after: fetch(weight, after), lambda after: fetch(moment_one, after)]
+    blocks, (weight_near, one) = gather(tokens, n, errands)
     half = len(blocks) // 2
-    rows, turned, gate, cot, weights, adjoint_near = early_call(
-        n, blocks[:half], cotangent, token_weight.reshape(1, -1), adjoint, weight_near, two
+    rows, turned, gate, cot, weights = early_call(n, blocks[:half], cotangent, token_weight.reshape(1, -1), weight_near)
+    _, turned, _, adjoint_near, along, across, bend, stats = replay_call(
+        n, blocks[half:], moment_two, adjoint, weight_near, cot, weights, one, rows, turned, gate
     )
-    rows, turned, gate, scaled, bend, score = late_call(blocks[half:], weight_near, cot, weights, rows, turned, gate)
-    along, across, stats = step_call(n, rows, turned, scaled, score, one, two, adjoint_near)
     sums = all_sum(stats, n)
     theta_bar, scores = theta_call(n, entries, sums, stats, along, across, bend, turned, adjoint_near)
     return (theta_bar, scores.reshape(-1))

time: 59.6 us -> 56.1 us (0.941)
  starting transfers between devices: 16.1 us -> 21.2 us
  waiting for transfers between devices: 10.6 us -> 5.98 us
  Pallas kernels: 30.9 us -> 27.9 us
  local copies, waits for them, and re-layouts: 0.92 us -> 0.01 us
    ppermute x4 -> x8, starting transfers between devices: 9.22 us -> 13.7 us  [onward(): return lax.ppermute(value, 'dp', pairs)]
    pallas_call x3 -> x2, Pallas kernels: 8.36 us -> 4.39 us  [fetch(): pl.pallas_call(fetch_kernel, in_specs=[pl.BlockSpec(memory_space=pl.ANY)]...]
    ppermute x4 -> x8, waiting for transfers between devices: 4.49 us -> 1.54 us  [onward(): return lax.ppermute(value, 'dp', pairs)]
    pallas_call x2 -> x1, Pallas kernels: 12.8 us -> 15 us  [replay_call(): pl.pallas_call(functools.partial(replay_kernel, n, half), in_specs=[far]...]
    ppermute x10 -> x13, waiting for transfers between devices: 6.15 us -> 4.44 us  [swapped(): return lax.ppermute(value, 'dp', [(d ^ mask, d) for d in range(n)])]
    pallas_call x1, Pallas kernels: 5.47 us -> 4.18 us  [early_call(): pl.pallas_call(functools.partial(early_kernel, n, half), in_specs=[far] *...]
    unnamed x1 -> x2, local copies, waits for them, and re-layouts: 0.91 us -> 0.01 us
    ppermute x10 -> x13, starting transfers between devices: 6.84 us -> 7.54 us  [swapped(): return lax.ppermute(value, 'dp', [(d ^ mask, d) for d in range(n)])]
  transfers between devices with their start and end apart: 14 -> 21, of which waited for: 9 -> 5; matrix products, arithmetic and copies ran while one was open for 2% -> 0% of each run, Pallas kernels for 23% -> 15%
where the time goes in v8:
time: 56.1 us; the launch traced here: 55.9 us
  Pallas kernels  27.9 us (50%)
  starting transfers between devices  21.2 us (38%)
  waiting for transfers between devices  5.98 us (11%)
  between operations  0.77 us (1%)
    pallas_call x1, Pallas kernels, replay_call(): pl.pallas_call(functools.partial(replay_kernel, n, half), in_specs=[far]...  15 us
    ppermute x8, starting transfers between devices, onward(): return lax.ppermute(value, 'dp', pairs)  13.7 us
    ppermute x13, starting transfers between devices, swapped(): return lax.ppermute(value, 'dp', [(d ^ mask, d) for d in range(n)])  7.54 us
    ppermute x13, waiting for transfers between devices, swapped(): return lax.ppermute(value, 'dp', [(d ^ mask, d) for d in range(n)])  4.44 us
    pallas_call x2, Pallas kernels, fetch(): pl.pallas_call(fetch_kernel, in_specs=[pl.BlockSpec(memory_space=pl.ANY)]...  4.39 us
    pallas_call x1, Pallas kernels, theta_call(): pl.pallas_call(functools.partial(theta_kernel, n, entries), in_specs=[vme...  4.31 us
    pallas_call x1, Pallas kernels, early_call(): pl.pallas_call(functools.partial(early_kernel, n, half), in_specs=[far] *...  4.18 us
    ppermute x8, waiting for transfers between devices, onward(): return lax.ppermute(value, 'dp', pairs)  1.54 us
  transfers between devices with their start and end apart: 21, of which 5 were waited for; matrix products, arithmetic and copies ran while one was open for 0% of the time, Pallas kernels for 15%

profile of v8, /device:TPU:0, one launch (start us, length us, event | category | flops | bytes accessed | tf_op | source)
XLA Modules:
  0.0 55.9 jit_solution(1469553862529215454)
XLA Ops:
  0.6 0.5 collective-permute-start.3
  1.1 2.6 %collective-permute-start = (bf16[16,4096]{1,0:T(8,128)(2,1)}, bf16[16,4096]{1,0:T(8,128)(2,1)S(1)}, u32[]{:S(2)}, u32[]{:S(2)}) collective-permute-start(bf16[16,4096]{1,0:T(8,128)(2,1)} %refs_0_.1), channel_id=1, source_target_pairs={{2,0},{5,1},{0,4},{9,5},{4,8},{13,9},{8,12},{15,13},{12,14},{11,15... | collective-permute-start | bytes 393224 | tf_op jit(solution)/shard_map/ppermute | solution.py:39
  3.8 0.0 collective-permute-done.3.refs_1_
  3.8 1.6 %collective-permute-start.4 = (bf16[16,4096]{1,0:T(8,128)(2,1)S(1)}, bf16[16,4096]{1,0:T(8,128)(2,1)S(1)}, u32[]{:S(2)}, u32[]{:S(2)}) collective-permute-start(bf16[16,4096]{1,0:T(8,128)(2,1)S(1)} %collective-permute-done.3.refs_1_), channel_id=1, source_target_pairs={{2,0},{5,1},{0,4},{9,5},{4,8},{13,9},{8,12},{15,13},{12,14},{11,15... | collective-permute-start | bytes 393224 | tf_op jit(solution)/shard_map/ppermute | solution.py:39
  5.4 1.5 %collective-permute-done.refs_2_.after = bf16[16,4096]{1,0:T(8,128)(2,1)S(1)} collective-permute-done((bf16[16,4096]{1,0:T(8,128)(2,1)}, bf16[16,4096]{1,0:T(8,128)(2,1)S(1)}, u32[]{:S(2)}, u32[]{:S(2)}) %collective-permute-start) | collective-permute-done | bytes 131104 | tf_op jit(solution)/shard_map/ppermute | solution.py:39
  6.9 2.1 %collective-permute-start.1 = (bf16[16,4096]{1,0:T(8,128)(2,1)S(1)}, bf16[16,4096]{1,0:T(8,128)(2,1)S(1)}, u32[]{:S(2)}, u32[]{:S(2)}) collective-permute-start(bf16[16,4096]{1,0:T(8,128)(2,1)S(1)} %collective-permute-done.refs_2_.after), channel_id=1, source_target_pairs={{2,0},{5,1},{0,4},{9,5},{4,8},{13,9},{8,12},{15,13},{12,14},{11,15... | collective-permute-start | bytes 393224 | tf_op jit(solution)/shard_map/ppermute | solution.py:39
  9.0 0.0 collective-permute-done.4.refs_3_
  9.0 1.6 %collective-permute-start.5 = (bf16[16,4096]{1,0:T(8,128)(2,1)S(1)}, bf16[16,4096]{1,0:T(8,128)(2,1)S(1)}, u32[]{:S(2)}, u32[]{:S(2)}) collective-permute-start(bf16[16,4096]{1,0:T(8,128)(2,1)S(1)} %collective-permute-done.4.refs_3_), channel_id=1, source_target_pairs={{2,0},{5,1},{0,4},{9,5},{4,8},{13,9},{8,12},{15,13},{12,14},{11,15... | collective-permute-start | bytes 393224 | tf_op jit(solution)/shard_map/ppermute | solution.py:39
  10.5 2.2 %fetch.2.refs_10_ = bf16[4096,512]{1,0:T(8,128)(2,1)S(1)} custom-call(bf16[4096,512]{1,0:T(8,128)(2,1)} %far.2, bf16[16,4096]{1,0:T(8,128)(2,1)} %refs_0_.1), custom_call_target="tpu_custom_call" | custom-call | flops 4294967296 | bytes 8388608 | tf_op jit(solution)/shard_map/fetch/pallas_call | solution.py:107
  12.7 0.0 copy-start
  12.8 0.1 collective-permute-start.13
  12.8 0.5 collective-permute-start.14
  13.3 0.0 collective-permute-done.1.refs_6_
  13.3 1.6 %collective-permute-start.7 = (bf16[16,4096]{1,0:T(8,128)(2,1)S(1)}, bf16[16,4096]{1,0:T(8,128)(2,1)S(1)}, u32[]{:S(2)}, u32[]{:S(2)}) collective-permute-start(bf16[16,4096]{1,0:T(8,128)(2,1)S(1)} %collective-permute-done.1.refs_6_), channel_id=1, source_target_pairs={{2,0},{5,1},{0,4},{9,5},{4,8},{13,9},{8,12},{15,13},{12,14},{11,15... | collective-permute-start | bytes 393224 | tf_op jit(solution)/shard_map/ppermute | solution.py:39
  14.9 0.0 collective-permute-start.2
  14.9 0.0 collective-permute-done.5.refs_7_
  14.9 1.5 %collective-permute-start.8 = (bf16[16,4096]{1,0:T(8,128)(2,1)S(1)}, bf16[16,4096]{1,0:T(8,128)(2,1)S(1)}, u32[]{:S(2)}, u32[]{:S(2)}) collective-permute-start(bf16[16,4096]{1,0:T(8,128)(2,1)S(1)} %collective-permute-done.5.refs_7_), channel_id=1, source_target_pairs={{2,0},{5,1},{0,4},{9,5},{4,8},{13,9},{8,12},{15,13},{12,14},{11,15... | collective-permute-start | bytes 393224 | tf_op jit(solution)/shard_map/ppermute | solution.py:39
  16.4 2.2 %fetch.3.refs_13_ = bf16[4096,512]{1,0:T(8,128)(2,1)S(1)} custom-call(bf16[4096,512]{1,0:T(8,128)(2,1)} %far.3, bf16[16,4096]{1,0:T(8,128)(2,1)S(1)} %collective-permute-done.refs_2_.after), custom_call_target="tpu_custom_call" | custom-call | flops 4294967296 | bytes 8388608 | tf_op jit(solution)/shard_map/fetch/pallas_call | solution.py:107
  18.6 0.0 collective-permute-done.13.refs_4_
  18.7 0.1 collective-permute-start.6
  18.7 0.0 collective-permute-done.7.refs_2_
  18.7 1.5 %collective-permute-start.11 = (bf16[16,4096]{1,0:T(8,128)(2,1)S(1)}, bf16[16,4096]{1,0:T(8,128)(2,1)S(1)}, u32[]{:S(2)}, u32[]{:S(2)}) collective-permute-start(bf16[16,4096]{1,0:T(8,128)(2,1)S(1)} %collective-permute-done.7.refs_2_), channel_id=1, source_target_pairs={{2,0},{5,1},{0,4},{9,5},{4,8},{13,9},{8,12},{15,13},{12,14},{11,15... | collective-permute-start | bytes 393224 | tf_op jit(solution)/shard_map/ppermute | solution.py:39
  20.2 0.0 collective-permute-done.14.refs_5_
  20.2 0.0 collective-permute-start.9
  20.2 0.0 collective-permute-done.8.refs_3_
  20.2 1.3 %collective-permute-start.12 = (bf16[16,4096]{1,0:T(8,128)(2,1)S(1)}, bf16[16,4096]{1,0:T(8,128)(2,1)S(1)}, u32[]{:S(2)}, u32[]{:S(2)}) collective-permute-start(bf16[16,4096]{1,0:T(8,128)(2,1)S(1)} %collective-permute-done.8.refs_3_), channel_id=1, source_target_pairs={{2,0},{5,1},{0,4},{9,5},{4,8},{13,9},{8,12},{15,13},{12,14},{11,15... | collective-permute-start | bytes 393224 | tf_op jit(solution)/shard_map/ppermute | solution.py:39
  21.5 0.0 collective-permute-done.2.refs_0_
  21.5 0.0 collective-permute-start.10
  21.5 4.2 %early.1 = (bf16[256,4096]{1,0:T(8,128)(2,1)S(1)}, bf16[4096,256]{1,0:T(8,128)(2,1)S(1)}, f32[256,512]{1,0:T(8,128)S(1)}, bf16[256,512]{1,0:T(8,128)(2,1)S(1)}, f32[256,128]{1,0:T(8,128)S(1)}) custom-call(bf16[16,4096]{1,0:T(8,128)(2,1)S(1)} %copy-done, bf16[16,4096]{1,0:T(8,128)(2,1)S(1)} %collective-permute-done.3.refs_1_, ...), custom_call_target="tpu_custom_call" | custom-call | flops 4294967296 | bytes 12582912 | tf_op jit(solution)/shard_map/early/pallas_call | solution.py:180
  25.7 0.0 collective-permute-done.6.refs_1_
  25.7 0.0 collective-permute-done.11.refs_6_
  25.7 0.0 collective-permute-done.9.refs_4_
  25.7 0.0 collective-permute-done.12.refs_7_
  25.7 0.0 collective-permute-done.10.refs_5_
  25.7 15.0 %replay.1 = (bf16[256,4096]{1,0:T(8,128)(2,1)S(1)}, bf16[4096,256]{1,0:T(8,128)(2,1)S(1)}, f32[256,512]{1,0:T(8,128)S(1)}, f32[4096,512]{1,0:T(8,128)S(1)}, f32[...) custom-call(bf16[16,4096]{1,0:T(8,128)(2,1)S(1)} %collective-permute, ...), custom_call_target="tpu_custom_call", output_to_operand_aliasing={{0}: (14, {}), {1}: (15, {}), {2}: (16, {})} | custom-call | tf_op jit(solution)/shard_map/replay/pallas_call | solution.py:332
  40.8 2.5 %collective-permute-start.17 = (f32[8,256]{1,0:T(8,128)S(1)}, f32[8,256]{1,0:T(8,128)S(1)}, u32[]{:S(2)}, u32[]{:S(2)}) collective-permute-start(f32[8,256]{1,0:T(8,128)S(1)} %get-tuple-element.20.own), channel_id=1, source_target_pairs={{12,0},{13,1},{14,2},{15,3},{8,4},{9,5},{10,6},{11,7},{4,8},{5,9},... | collective-permute-start | bytes 24584 | tf_op jit(solution)/shard_map/ppermute | solution.py:25
  43.2 0.5 collective-permute-start.16
  43.7 1.5 %collective-permute-start.15 = (f32[8,256]{1,0:T(8,128)S(1)}, f32[8,256]{1,0:T(8,128)S(1)}, u32[]{:S(2)}, u32[]{:S(2)}) collective-permute-start(f32[8,256]{1,0:T(8,128)S(1)} %get-tuple-element.20.own), channel_id=1, source_target_pairs={{4,0},{5,1},{6,2},{7,3},{0,4},{1,5},{2,6},{3,7},{12,8},{13,9},{14,... | collective-permute-start | bytes 24584 | tf_op jit(solution)/shard_map/ppermute | solution.py:25
  45.2 1.1 %collective-permute-done.17 = f32[8,256]{1,0:T(8,128)S(1)} collective-permute-done((f32[8,256]{1,0:T(8,128)S(1)}, f32[8,256]{1,0:T(8,128)S(1)}, u32[]{:S(2)}, u32[]{:S(2)}) %collective-permute-start.17) | collective-permute-done | bytes 8224 | tf_op jit(solution)/shard_map/ppermute | solution.py:25
  46.4 1.4 %collective-permute-done.16 = f32[8,256]{1,0:T(8,128)S(1)} collective-permute-done((f32[8,256]{1,0:T(8,128)S(1)}, f32[8,256]{1,0:T(8,128)S(1)}, u32[]{:S(2)}, u32[]{:S(2)}) %collective-permute-start.16) | collective-permute-done | bytes 8224 | tf_op jit(solution)/shard_map/ppermute | solution.py:25
  47.8 0.0 collective-permute-done.15
  47.8 0.1 collective-permute-start.20
  47.9 0.8 %collective-permute-start.19 = (f32[8,256]{1,0:T(8,128)S(1)}, f32[8,256]{1,0:T(8,128)S(1)}, u32[]{:S(2)}, u32[]{:S(2)}) collective-permute-start(f32[8,256]{1,0:T(8,128)S(1)} %add_add_fusion.s0), channel_id=1, source_target_pairs={{2,0},{3,1},{0,2},{1,3},{6,4},{7,5},{4,6},{5,7},{10,8},{11,9},{8,1... | collective-permute-start | bytes 24584 | tf_op jit(solution)/shard_map/ppermute | solution.py:25
  48.7 1.0 %collective-permute-start.18 = (f32[8,256]{1,0:T(8,128)S(1)}, f32[8,256]{1,0:T(8,128)S(1)}, u32[]{:S(2)}, u32[]{:S(2)}) collective-permute-start(f32[8,256]{1,0:T(8,128)S(1)} %add_add_fusion.s0), channel_id=1, source_target_pairs={{1,0},{0,1},{3,2},{2,3},{5,4},{4,5},{7,6},{6,7},{9,8},{8,9},{11,10... | collective-permute-start | bytes 24584 | tf_op jit(solution)/shard_map/ppermute | solution.py:25
  49.7 1.2 %collective-permute-done.20.s3 = f32[8,256]{1,0:T(8,128)S(1)} collective-permute-done((f32[8,256]{1,0:T(8,128)S(1)}, f32[8,256]{1,0:T(8,128)S(1)}, u32[]{:S(2)}, u32[]{:S(2)}) %collective-permute-start.20) | collective-permute-done | bytes 8224 | tf_op jit(solution)/shard_map/ppermute | solution.py:25
  50.9 0.7 %collective-permute-done.19.s2 = f32[8,256]{1,0:T(8,128)S(1)} collective-permute-done((f32[8,256]{1,0:T(8,128)S(1)}, f32[8,256]{1,0:T(8,128)S(1)}, u32[]{:S(2)}, u32[]{:S(2)}) %collective-permute-start.19) | collective-permute-done | bytes 8224 | tf_op jit(solution)/shard_map/ppermute | solution.py:25
  51.6 0.0 collective-permute-done.18.s1
  51.6 4.3 %theta.1 = (f32[4096,512]{1,0:T(8,128)}, f32[1,16]{1,0:T(1,128)}) custom-call(f32[8,256]{1,0:T(8,128)S(1)} %add_add_fusion.s0, f32[8,256]{1,0:T(8,128)S(1)} %collective-permute-done.18.s1, f32[8,256]{1,0:T(8,128)S(1)} %collective-permute-done.19.s2, f32[8,256]{1,0:T(8,128)S(1)} %collective-permute-done.20.s3, f32[8,256]{1,0:T(8,128)S(1)} %get-tuple-element.20.own, ...), custom_call_target="tpu_custom_call" | custom-call | tf_op jit(solution)/shard_map/theta/pallas_call | solution.py:405
  (2 shorter events, 0.0 us)
Async XLA Ops:
  0.6 3.2 %collective-permute-start.3 = (bf16[16,4096]{1,0:T(8,128)(2,1)}, bf16[16,4096]{1,0:T(8,128)(2,1)S(1)}, u32[]{:S(2)}, u32[]{:S(2)}) collective-permute-start(bf16[16,4096]{1,0:T(8,128)(2,1)} %refs_0_.1), channel_id=1, source_target_pairs={{1,0},{0,1},{3,2},{2,3},{5,4},{4,5},{7,6},{6,7},{9,8},{8,9},{11,10... | collective-permute-start | bytes 393224 | tf_op jit(solution)/shard_map/ppermute | solution.py:25
  1.1 5.7 %collective-permute-start = (bf16[16,4096]{1,0:T(8,128)(2,1)}, bf16[16,4096]{1,0:T(8,128)(2,1)S(1)}, u32[]{:S(2)}, u32[]{:S(2)}) collective-permute-start(bf16[16,4096]{1,0:T(8,128)(2,1)} %refs_0_.1), channel_id=1, source_target_pairs={{2,0},{5,1},{0,4},{9,5},{4,8},{13,9},{8,12},{15,13},{12,14},{11,15... | collective-permute-start | bytes 393224 | tf_op jit(solution)/shard_map/ppermute | solution.py:39
  3.8 5.2 %collective-permute-start.4 = (bf16[16,4096]{1,0:T(8,128)(2,1)S(1)}, bf16[16,4096]{1,0:T(8,128)(2,1)S(1)}, u32[]{:S(2)}, u32[]{:S(2)}) collective-permute-start(bf16[16,4096]{1,0:T(8,128)(2,1)S(1)} %collective-permute-done.3.refs_1_), channel_id=1, source_target_pairs={{2,0},{5,1},{0,4},{9,5},{4,8},{13,9},{8,12},{15,13},{12,14},{11,15... | collective-permute-start | bytes 393224 | tf_op jit(solution)/shard_map/ppermute | solution.py:39
  6.9 6.5 %collective-permute-start.1 = (bf16[16,4096]{1,0:T(8,128)(2,1)S(1)}, bf16[16,4096]{1,0:T(8,128)(2,1)S(1)}, u32[]{:S(2)}, u32[]{:S(2)}) collective-permute-start(bf16[16,4096]{1,0:T(8,128)(2,1)S(1)} %collective-permute-done.refs_2_.after), channel_id=1, source_target_pairs={{2,0},{5,1},{0,4},{9,5},{4,8},{13,9},{8,12},{15,13},{12,14},{11,15... | collective-permute-start | bytes 393224 | tf_op jit(solution)/shard_map/ppermute | solution.py:39
  9.0 6.0 %collective-permute-start.5 = (bf16[16,4096]{1,0:T(8,128)(2,1)S(1)}, bf16[16,4096]{1,0:T(8,128)(2,1)S(1)}, u32[]{:S(2)}, u32[]{:S(2)}) collective-permute-start(bf16[16,4096]{1,0:T(8,128)(2,1)S(1)} %collective-permute-done.4.refs_3_), channel_id=1, source_target_pairs={{2,0},{5,1},{0,4},{9,5},{4,8},{13,9},{8,12},{15,13},{12,14},{11,15... | collective-permute-start | bytes 393224 | tf_op jit(solution)/shard_map/ppermute | solution.py:39
  12.7 8.7 %copy-start = (bf16[16,4096]{1,0:T(8,128)(2,1)S(1)}, bf16[16,4096]{1,0:T(8,128)(2,1)}, u32[]{:S(2)}) copy-start(bf16[16,4096]{1,0:T(8,128)(2,1)} %refs_0_.1) | copy-start | bytes 393220
  12.8 5.9 %collective-permute-start.13 = (bf16[16,4096]{1,0:T(8,128)(2,1)S(1)}, bf16[16,4096]{1,0:T(8,128)(2,1)S(1)}, u32[]{:S(2)}, u32[]{:S(2)}) collective-permute-start(bf16[16,4096]{1,0:T(8,128)(2,1)S(1)} %collective-permute-done.refs_2_.after), channel_id=1, source_target_pairs={{1,0},{0,1},{3,2},{2,3},{5,4},{4,5},{7,6},{6,7},{9,8},{8,9},{11,10... | collective-permute-start | bytes 393224 | tf_op jit(solution)/shard_map/ppermute | solution.py:25
  12.8 7.4 %collective-permute-start.14 = (bf16[16,4096]{1,0:T(8,128)(2,1)S(1)}, bf16[16,4096]{1,0:T(8,128)(2,1)S(1)}, u32[]{:S(2)}, u32[]{:S(2)}) collective-permute-start(bf16[16,4096]{1,0:T(8,128)(2,1)S(1)} %collective-permute-done.4.refs_3_), channel_id=1, source_target_pairs={{1,0},{0,1},{3,2},{2,3},{5,4},{4,5},{7,6},{6,7},{9,8},{8,9},{11,10... | collective-permute-start | bytes 393224 | tf_op jit(solution)/shard_map/ppermute | solution.py:25
  13.3 5.4 %collective-permute-start.7 = (bf16[16,4096]{1,0:T(8,128)(2,1)S(1)}, bf16[16,4096]{1,0:T(8,128)(2,1)S(1)}, u32[]{:S(2)}, u32[]{:S(2)}) collective-permute-start(bf16[16,4096]{1,0:T(8,128)(2,1)S(1)} %collective-permute-done.1.refs_6_), channel_id=1, source_target_pairs={{2,0},{5,1},{0,4},{9,5},{4,8},{13,9},{8,12},{15,13},{12,14},{11,15... | collective-permute-start | bytes 393224 | tf_op jit(solution)/shard_map/ppermute | solution.py:39
  14.9 6.6 %collective-permute-start.2 = (bf16[16,4096]{1,0:T(8,128)(2,1)S(1)}, bf16[16,4096]{1,0:T(8,128)(2,1)S(1)}, u32[]{:S(2)}, u32[]{:S(2)}) collective-permute-start(bf16[16,4096]{1,0:T(8,128)(2,1)S(1)} %collective-permute-done.1.refs_6_), channel_id=1, source_target_pairs={{1,0},{0,1},{3,2},{2,3},{5,4},{4,5},{7,6},{6,7},{9,8},{8,9},{11,10... | collective-permute-start | bytes 393224 | tf_op jit(solution)/shard_map/ppermute | solution.py:25
  14.9 5.3 %collective-permute-start.8 = (bf16[16,4096]{1,0:T(8,128)(2,1)S(1)}, bf16[16,4096]{1,0:T(8,128)(2,1)S(1)}, u32[]{:S(2)}, u32[]{:S(2)}) collective-permute-start(bf16[16,4096]{1,0:T(8,128)(2,1)S(1)} %collective-permute-done.5.refs_7_), channel_id=1, source_target_pairs={{2,0},{5,1},{0,4},{9,5},{4,8},{13,9},{8,12},{15,13},{12,14},{11,15... | collective-permute-start | bytes 393224 | tf_op jit(solution)/shard_map/ppermute | solution.py:39
  18.7 7.0 %collective-permute-start.6 = (bf16[16,4096]{1,0:T(8,128)(2,1)S(1)}, bf16[16,4096]{1,0:T(8,128)(2,1)S(1)}, u32[]{:S(2)}, u32[]{:S(2)}) collective-permute-start(bf16[16,4096]{1,0:T(8,128)(2,1)S(1)} %collective-permute-done.5.refs_7_), channel_id=1, source_target_pairs={{1,0},{0,1},{3,2},{2,3},{5,4},{4,5},{7,6},{6,7},{9,8},{8,9},{11,10... | collective-permute-start | bytes 393224 | tf_op jit(solution)/shard_map/ppermute | solution.py:25
  18.7 6.9 %collective-permute-start.11 = (bf16[16,4096]{1,0:T(8,128)(2,1)S(1)}, bf16[16,4096]{1,0:T(8,128)(2,1)S(1)}, u32[]{:S(2)}, u32[]{:S(2)}) collective-permute-start(bf16[16,4096]{1,0:T(8,128)(2,1)S(1)} %collective-permute-done.7.refs_2_), channel_id=1, source_target_pairs={{2,0},{5,1},{0,4},{9,5},{4,8},{13,9},{8,12},{15,13},{12,14},{11,15... | collective-permute-start | bytes 393224 | tf_op jit(solution)/shard_map/ppermute | solution.py:39
  20.2 5.5 %collective-permute-start.9 = (bf16[16,4096]{1,0:T(8,128)(2,1)S(1)}, bf16[16,4096]{1,0:T(8,128)(2,1)S(1)}, u32[]{:S(2)}, u32[]{:S(2)}) collective-permute-start(bf16[16,4096]{1,0:T(8,128)(2,1)S(1)} %collective-permute-done.7.refs_2_), channel_id=1, source_target_pairs={{1,0},{0,1},{3,2},{2,3},{5,4},{4,5},{7,6},{6,7},{9,8},{8,9},{11,10... | collective-permute-start | bytes 393224 | tf_op jit(solution)/shard_map/ppermute | solution.py:25
  20.2 5.5 %collective-permute-start.12 = (bf16[16,4096]{1,0:T(8,128)(2,1)S(1)}, bf16[16,4096]{1,0:T(8,128)(2,1)S(1)}, u32[]{:S(2)}, u32[]{:S(2)}) collective-permute-start(bf16[16,4096]{1,0:T(8,128)(2,1)S(1)} %collective-permute-done.8.refs_3_), channel_id=1, source_target_pairs={{2,0},{5,1},{0,4},{9,5},{4,8},{13,9},{8,12},{15,13},{12,14},{11,15... | collective-permute-start | bytes 393224 | tf_op jit(solution)/shard_map/ppermute | solution.py:39
  21.5 4.2 %collective-permute-start.10 = (bf16[16,4096]{1,0:T(8,128)(2,1)S(1)}, bf16[16,4096]{1,0:T(8,128)(2,1)S(1)}, u32[]{:S(2)}, u32[]{:S(2)}) collective-permute-start(bf16[16,4096]{1,0:T(8,128)(2,1)S(1)} %collective-permute-done.8.refs_3_), channel_id=1, source_target_pairs={{1,0},{0,1},{3,2},{2,3},{5,4},{4,5},{7,6},{6,7},{9,8},{8,9},{11,10... | collective-permute-start | bytes 393224 | tf_op jit(solution)/shard_map/ppermute | solution.py:25
  40.8 5.6 %collective-permute-start.17 = (f32[8,256]{1,0:T(8,128)S(1)}, f32[8,256]{1,0:T(8,128)S(1)}, u32[]{:S(2)}, u32[]{:S(2)}) collective-permute-start(f32[8,256]{1,0:T(8,128)S(1)} %get-tuple-element.20.own), channel_id=1, source_target_pairs={{12,0},{13,1},{14,2},{15,3},{8,4},{9,5},{10,6},{11,7},{4,8},{5,9},... | collective-permute-start | bytes 24584 | tf_op jit(solution)/shard_map/ppermute | solution.py:25
  43.2 4.5 %collective-permute-start.16 = (f32[8,256]{1,0:T(8,128)S(1)}, f32[8,256]{1,0:T(8,128)S(1)}, u32[]{:S(2)}, u32[]{:S(2)}) collective-permute-start(f32[8,256]{1,0:T(8,128)S(1)} %get-tuple-element.20.own), channel_id=1, source_target_pairs={{8,0},{9,1},{10,2},{11,3},{12,4},{13,5},{14,6},{15,7},{0,8},{1,9},... | collective-permute-start | bytes 24584 | tf_op jit(solution)/shard_map/ppermute | solution.py:25
  43.7 4.1 %collective-permute-start.15 = (f32[8,256]{1,0:T(8,128)S(1)}, f32[8,256]{1,0:T(8,128)S(1)}, u32[]{:S(2)}, u32[]{:S(2)}) collective-permute-start(f32[8,256]{1,0:T(8,128)S(1)} %get-tuple-element.20.own), channel_id=1, source_target_pairs={{4,0},{5,1},{6,2},{7,3},{0,4},{1,5},{2,6},{3,7},{12,8},{13,9},{14,... | collective-permute-start | bytes 24584 | tf_op jit(solution)/shard_map/ppermute | solution.py:25
  47.8 3.1 %collective-permute-start.20 = (f32[8,256]{1,0:T(8,128)S(1)}, f32[8,256]{1,0:T(8,128)S(1)}, u32[]{:S(2)}, u32[]{:S(2)}) collective-permute-start(f32[8,256]{1,0:T(8,128)S(1)} %add_add_fusion.s0), channel_id=1, source_target_pairs={{3,0},{2,1},{1,2},{0,3},{7,4},{6,5},{5,6},{4,7},{11,8},{10,9},{9,1... | collective-permute-start | bytes 24584 | tf_op jit(solution)/shard_map/ppermute | solution.py:25
  47.9 3.7 %collective-permute-start.19 = (f32[8,256]{1,0:T(8,128)S(1)}, f32[8,256]{1,0:T(8,128)S(1)}, u32[]{:S(2)}, u32[]{:S(2)}) collective-permute-start(f32[8,256]{1,0:T(8,128)S(1)} %add_add_fusion.s0), channel_id=1, source_target_pairs={{2,0},{3,1},{0,2},{1,3},{6,4},{7,5},{4,6},{5,7},{10,8},{11,9},{8,1... | collective-permute-start | bytes 24584 | tf_op jit(solution)/shard_map/ppermute | solution.py:25
  48.7 2.9 %collective-permute-start.18 = (f32[8,256]{1,0:T(8,128)S(1)}, f32[8,256]{1,0:T(8,128)S(1)}, u32[]{:S(2)}, u32[]{:S(2)}) collective-permute-start(f32[8,256]{1,0:T(8,128)S(1)} %add_add_fusion.s0), channel_id=1, source_target_pairs={{1,0},{0,1},{3,2},{2,3},{5,4},{4,5},{7,6},{6,7},{9,8},{8,9},{11,10... | collective-permute-start | bytes 24584 | tf_op jit(solution)/shard_map/ppermute | solution.py:25

commit v9 on v8

--- a/solution.py
+++ b/solution.py
@@ -58,8 +58,8 @@
 def owners(n):
     chips = n // 2
     me = lax.axis_index("dp")
-    chip, core = me // 2, lax.rem(me, 2)
-    at = jnp.where(lax.rem(chip, 2) == 0, chip // 2, chips - 1 - chip // 2)
+    chip, core = me >> 1, me & 1
+    at = jnp.where(chip & 1 == 0, chip >> 1, chips - 1 - (chip >> 1))
     way = 2 * core - 1
     blocks = [(0, core)]
     for hop in range(1, chips // 2 + 1):
@@ -68,7 +68,8 @@
             blocks.append((-way * hop, 1 - core))
     places = []
     for step, first in blocks:
-        there = lax.rem(at + step + chips, chips)
+        there = at + step
+        there = jnp.where(there < 0, there + chips, jnp.where(there >= chips, there - chips, there))
         source = jnp.where(there < chips // 2, 2 * there, 2 * (chips - 1 - there) + 1)
         places += [2 * source + first, 2 * source + 1 - first]
     return places
@@ -90,30 +91,94 @@
 
 
 def update(grad, one, two):
-    first = 9.0 * one.astype(jnp.float32) + grad
-    second = 19.0 * two.astype(jnp.float32) + grad * grad
+    first = one + grad
+    second = two + grad * grad
     over = lax.rsqrt(second)
     inv = pltpu.reciprocal(second * over + 1e-08 / 0.05**0.5, approx=True)
     return over, inv, first * inv
 
 
-def fetch_kernel(far, after, near, sem):
-    copy = pltpu.make_async_copy(far, near, sem.at[0])
-    copy.start()
-    copy.wait()
-
-
-def fetch(x, after):
+def fetch_params():
+    return {
+        "compiler_params": pltpu.CompilerParams(vmem_limit_bytes=6 << 20),
+        "cost_estimate": pl.CostEstimate(flops=COST, bytes_accessed=8 << 20, transcendentals=0),
+    }
+
+
+def widen_kernel(factor, far, after, near, raw, sems):
+    tiles = far.shape[0] // TILE
+
+    def copy(i):
+        return pltpu.make_async_copy(far.at[span(i), :], raw.at[span(i), :], sems.at[i])
+
+    for i in range(tiles):
+        copy(i).start()
+
+    def step(i, _):
+        copy(i).wait()
+        near[span(i), :] = factor * raw[span(i), :].astype(jnp.float32)
+        return 0
+
+    lax.fori_loop(0, tiles, step, 0)
+
+
+def fetch_wide(x, factor, after):
     return pl.pallas_call(
-        fetch_kernel,
+        functools.partial(widen_kernel, factor),
         in_specs=[pl.BlockSpec(memory_space=pl.ANY)] * 2,
         out_specs=pl.BlockSpec(memory_space=pltpu.VMEM),
-        out_shape=pltpu.VMEM(x.shape, x.dtype),
-        scratch_shapes=[pltpu.SemaphoreType.DMA((1,))],
-        compiler_params=pltpu.CompilerParams(vmem_limit_bytes=1 << 20),
-        cost_estimate=pl.CostEstimate(flops=COST, bytes_accessed=8 << 20, transcendentals=0),
+        out_shape=pltpu.VMEM(x.shape, jnp.float32),
+        scratch_shapes=[pltpu.VMEM(x.shape, x.dtype), pltpu.SemaphoreType.DMA((x.shape[0] // TILE,))],
+        name="widen",
+        **fetch_params(),
+    )(in_hbm(x), after)
+
+
+def fetch_kernel(n, far, far_cot, far_weight, after, near, cot, weights, token_weight, upright, sems, cot_sems):
+    height = cot.shape[0] // n
+    copy = pltpu.make_async_copy(far, near, sems.at[0])
+    weight_copy = pltpu.make_async_copy(far_weight, token_weight, sems.at[1])
+    weight_copy.start()
+    copy.start()
+    places = [pl.multiple_of(place * height, height) for place in owners(n)]
+    cot_copies = [
+        pltpu.make_async_copy(
+            far_cot.at[pl.ds(place, height), :], cot.at[pl.ds(k * height, height), :], cot_sems.at[k]
+        )
+        for k, place in enumerate(places)
+    ]
+    for cot_copy in cot_copies:
+        cot_copy.start()
+    weight_copy.wait()
+    upright[...] = jnp.broadcast_to(over_columns(token_weight[...]), upright.shape)
+    for k, place in enumerate(places):
+        weights[k * height : (k + 1) * height, :] = upright[pl.ds(place, height), :]
+    for cot_copy in cot_copies:
+        cot_copy.wait()
+    copy.wait()
+
+
+def fetch(n, weight, cot, token_weight, after):
+    count = cot.shape[0]
+    vmem = pl.BlockSpec(memory_space=pltpu.VMEM)
+    return pl.pallas_call(
+        functools.partial(fetch_kernel, n),
+        in_specs=[pl.BlockSpec(memory_space=pl.ANY)] * 4,
+        out_specs=[vmem] * 3,
+        out_shape=[
+            pltpu.VMEM(weight.shape, weight.dtype),
+            pltpu.VMEM(cot.shape, cot.dtype),
+            pltpu.VMEM((count, 128), jnp.float32),
+        ],
+        scratch_shapes=[
+            pltpu.VMEM((1, count), jnp.float32),
+            pltpu.VMEM((count, 128), jnp.float32),
+            pltpu.SemaphoreType.DMA((2,)),
+            pltpu.SemaphoreType.DMA((n,)),
+        ],
         name="fetch",
-    )(in_hbm(x), after)
+        **fetch_params(),
+    )(in_hbm(weight), in_hbm(cot), in_hbm(token_weight), after)
 
 
 def span(i):
@@ -144,86 +209,44 @@
     lax.fori_loop(0, depth // TILE, step, 0)
 
 
-def early_kernel(n, half, *refs):
-    blocks, (far_cot, far_weight, weight) = refs[:half], refs[half : half + 3]
-    (tokens, turned, gate, cot, weights) = refs[half + 3 : half + 8]
-    (token_weight, upright, sems, cot_sems, far_sems) = refs[half + 8 :]
-    height = cot.shape[0] // n
-    places = owners(n)
-    weight_copy = pltpu.make_async_copy(far_weight, token_weight, far_sems.at[0])
-    cot_copies = [
-        pltpu.make_async_copy(
-            far_cot.at[pl.ds(pl.multiple_of(place * height, height), height), :],
-            cot.at[pl.ds(k * height, height), :],
-            cot_sems.at[k],
-        )
-        for k, place in enumerate(places)
-    ]
-    weight_copy.start()
-    for copy in cot_copies:
-        copy.start()
+def early_kernel(half, *refs):
+    blocks, weight, (tokens, turned, gate, sems) = refs[:half], refs[half], refs[half + 1 :]
     gate_rows(blocks, 0, sems, weight, tokens, turned, gate, lambda i: None)
-    weight_copy.wait()
-    upright[...] = jnp.broadcast_to(over_columns(token_weight[...]), upright.shape)
-    for k, place in enumerate(places):
-        weights[k * height : (k + 1) * height, :] = upright[pl.ds(pl.multiple_of(place * height, height), height), :]
-    for copy in cot_copies:
-        copy.wait()
-
-
-def early_call(n, blocks, cot, token_weight, weight):
+
+
+def early_call(blocks, weight, count):
     half = len(blocks)
-    count, width = cot.shape
-    depth = weight.shape[0]
-    far = pl.BlockSpec(memory_space=pl.ANY)
+    depth, width = weight.shape
     vmem = pl.BlockSpec(memory_space=pltpu.VMEM)
     return pl.pallas_call(
-        functools.partial(early_kernel, n, half),
-        in_specs=[far] * (half + 2) + [vmem],
-        out_specs=[vmem] * 5,
+        functools.partial(early_kernel, half),
+        in_specs=[pl.BlockSpec(memory_space=pl.ANY)] * half + [vmem],
+        out_specs=[vmem] * 3,
         out_shape=[
             pltpu.VMEM((count, depth), jnp.bfloat16),
             pltpu.VMEM((depth, count), jnp.bfloat16),
             pltpu.VMEM((count, width), jnp.float32),
-            pltpu.VMEM((count, width), jnp.bfloat16),
-            pltpu.VMEM((count, 128), jnp.float32),
-        ],
-        scratch_shapes=[
-            pltpu.VMEM((1, count), jnp.float32),
-            pltpu.VMEM((count, 128), jnp.float32),
-            pltpu.SemaphoreType.DMA((half,)),
-            pltpu.SemaphoreType.DMA((n,)),
-            pltpu.SemaphoreType.DMA((1,)),
-        ],
-        compiler_params=pltpu.CompilerParams(vmem_limit_bytes=VMEM_BYTES),
+        ],
+        scratch_shapes=[pltpu.SemaphoreType.DMA((half,))],
+        compiler_params=pltpu.CompilerParams(vmem_limit_bytes=4 << 20),
         cost_estimate=pl.CostEstimate(flops=COST, bytes_accessed=12 << 20, transcendentals=0),
         name="early",
-    )(*blocks, *[in_hbm(x) for x in (cot, token_weight)], weight)
+    )(*blocks, weight)
 
 
 def replay_kernel(n, half, *refs):
-    blocks, far = refs[:half], refs[half : half + 2]
-    (weight, cot, weights, one) = refs[half + 2 : half + 6]
+    blocks, (far, weight, cot, weights, one, two) = refs[:half], refs[half : half + 6]
     (tokens, turned, gate, adjoint, along, across, bend, stats) = refs[half + 9 : half + 17]
-    (scaled, score, two, g0, g1, a0, a1, b0, b1, sums, upright, sems, tile_sems) = refs[half + 17 :]
+    (scaled, score, g0, g1, a0, a1, b0, b1, sums, upright, sems, tile_sems) = refs[half + 17 :]
     grads, firsts, seconds = (g0, g1), (a0, a1), (b0, b1)
-    near = (two, adjoint)
     depth = one.shape[0]
     count, width = scaled.shape
     tiles = depth // TILE
 
-    def tile_copy(which, i):
-        return pltpu.make_async_copy(far[which].at[span(i), :], near[which].at[span(i), :], tile_sems.at[which, i])
-
-    def start(i):
-        tile_copy(0, i).start()
-        tile_copy(1, i).start()
-
-    def arrive(i):
-        tile_copy(0, i).wait()
-        tile_copy(1, i).wait()
-
-    gate_rows(blocks, count // 2, sems, weight, tokens, turned, gate, start)
+    def tile_copy(i):
+        return pltpu.make_async_copy(far.at[span(i), :], adjoint.at[span(i), :], tile_sems.at[i])
+
+    gate_rows(blocks, count // 2, sems, weight, tokens, turned, gate, lambda i: tile_copy(i).start())
     for r in range(0, count, 64):
         at = slice(r, r + 64)
         x = gate[at, :]
@@ -253,7 +276,8 @@
                 cols = slice(c, min(c + COLUMNS, width))
                 yield r, cols, grads[slot][r : r + ROWS, cols], one[at, cols], two[at, cols], adjoint[at, cols]
 
-    arrive(0)
+    for i in range(2):
+        tile_copy(i).wait()
     grad_rows(0, 0, 0)
     grad_rows(0, 0, HALF)
     sq, cross = {}, {}
@@ -281,8 +305,6 @@
         sums[1] += sum(cross.values())
 
     def body(i, slot, ahead=True, behind=True):
-        if ahead:
-            arrive(i + 1)
         for r, target, terms in ((0, along, firsts), (HALF, across, seconds)):
             if ahead:
                 grad_rows(i + 1, 1 - slot, r)
@@ -293,6 +315,8 @@
     body(0, 0, behind=False)
 
     def pair(k, _):
+        tile_copy(2 * k + 2).wait()
+        tile_copy(2 * k + 3).wait()
         body(2 * k + 1, 1)
         body(2 * k + 2, 0)
         return 0
@@ -321,7 +345,7 @@
     stats[4:8, :] = jnp.broadcast_to(guess, (4, count))
 
 
-def replay_call(n, blocks, two, adjoint, weight, cot, weights, one, tokens, turned, gate):
+def replay_call(n, blocks, adjoint, weight, cot, weights, one, two, tokens, turned, gate):
     half = len(blocks)
     depth = one.shape[0]
     count, width = cot.shape
@@ -331,7 +355,7 @@
     block = lambda dtype: pltpu.VMEM((TILE, width), dtype)
     return pl.pallas_call(
         functools.partial(replay_kernel, n, half),
-        in_specs=[far] * (half + 2) + [vmem] * 7,
+        in_specs=[far] * (half + 1) + [vmem] * 8,
         out_specs=[vmem] * 8,
         out_shape=[
             like(tokens),
@@ -346,7 +370,6 @@
         scratch_shapes=[
             pltpu.VMEM((count, width), jnp.bfloat16),
             pltpu.VMEM((count, width), jnp.float32),
-            pltpu.VMEM((depth, width), jnp.bfloat16),
             block(jnp.float32),
             block(jnp.float32),
             block(jnp.bfloat16),
@@ -356,12 +379,12 @@
             pltpu.VMEM((2, 8, min(COLUMNS, width)), jnp.float32),
             pltpu.VMEM((count, 128), jnp.float32),
             pltpu.SemaphoreType.DMA((half,)),
-            pltpu.SemaphoreType.DMA((2, depth // TILE)),
+            pltpu.SemaphoreType.DMA((depth // TILE,)),
         ],
         input_output_aliases={half + 6: 0, half + 7: 1, half + 8: 2},
         compiler_params=pltpu.CompilerParams(vmem_limit_bytes=VMEM_BYTES),
         name="replay",
-    )(*blocks, in_hbm(two), in_hbm(adjoint), weight, cot, weights, one, tokens, turned, gate)
+    )(*blocks, in_hbm(adjoint), weight, cot, weights, one, two, tokens, turned, gate)
 
 
 def in_hbm(x):
@@ -418,12 +441,16 @@
 
 def shards(n, tokens, cotangent, token_weight, weight, moment_one, moment_two, adjoint):
     entries = float(adjoint.shape[0] * adjoint.shape[1] * n)
-    errands = [lambda after: fetch(weight, after), lambda after: fetch(moment_one, after)]
-    blocks, (weight_near, one) = gather(tokens, n, errands)
+    errands = [
+        lambda after: fetch(n, weight, cotangent, token_weight.reshape(1, -1), after),
+        lambda after: fetch_wide(moment_one, 9.0, after),
+        lambda after: fetch_wide(moment_two, 19.0, after),
+    ]
+    blocks, ((weight_near, cot, weights), one, two) = gather(tokens, n, errands)
     half = len(blocks) // 2
-    rows, turned, gate, cot, weights = early_call(n, blocks[:half], cotangent, token_weight.reshape(1, -1), weight_near)
+    rows, turned, gate = early_call(blocks[:half], weight_near, cot.shape[0])
     _, turned, _, adjoint_near, along, across, bend, stats = replay_call(
-        n, blocks[half:], moment_two, adjoint, weight_near, cot, weights, one, rows, turned, gate
+        n, blocks[half:], adjoint, weight_near, cot, weights, one, two, rows, turned, gate
     )
     sums = all_sum(stats, n)
     theta_bar, scores = theta_call(n, entries, sums, stats, along, across, bend, turned, adjoint_near)

time: 56.1 us -> 53.9 us (0.961)
  starting transfers between devices: 21.2 us -> 20 us
  waiting for transfers between devices: 5.98 us -> 5.01 us
    pallas_call x1, Pallas kernels: 15 us -> 13.1 us  [replay_call(): pl.pallas_call(functools.partial(replay_kernel, n, half), in_specs=[far]...]
    pallas_call x3 -> x4, Pallas kernels: 8.57 us -> 10.4 us  [the longest x2 4.57 us: fetch_wide(): pl.pallas_call(functools.partial(widen_kernel, factor), in_specs=[pl.Bloc...]
    ppermute x8, waiting for transfers between devices: 1.54 us -> 0.24 us  [onward(): return lax.ppermute(value, 'dp', pairs)]
    ppermute x8, starting transfers between devices: 13.7 us -> 12.9 us  [onward(): return lax.ppermute(value, 'dp', pairs)]
  transfers between devices with their start and end apart: 21 -> 21, of which waited for: 5 -> 6; matrix products, arithmetic and copies ran while one was open for 0% -> 0% of each run, Pallas kernels for 15% -> 19%
where the time goes in v9:
time: 53.9 us; the launch traced here: 53.6 us
  Pallas kernels  27.8 us (52%)
  starting transfers between devices  20 us (37%)
  waiting for transfers between devices  5.01 us (9%)
  between operations  0.78 us (1%)
    pallas_call x1, Pallas kernels, replay_call(): pl.pallas_call(functools.partial(replay_kernel, n, half), in_specs=[far]...  13.1 us
    ppermute x8, starting transfers between devices, onward(): return lax.ppermute(value, 'dp', pairs)  12.9 us
    ppermute x13, starting transfers between devices, swapped(): return lax.ppermute(value, 'dp', [(d ^ mask, d) for d in range(n)])  7.12 us
    ppermute x13, waiting for transfers between devices, swapped(): return lax.ppermute(value, 'dp', [(d ^ mask, d) for d in range(n)])  4.77 us
    pallas_call x2, Pallas kernels, fetch_wide(): pl.pallas_call(functools.partial(widen_kernel, factor), in_specs=[pl.Bloc...  4.57 us
    pallas_call x1, Pallas kernels, theta_call(): pl.pallas_call(functools.partial(theta_kernel, n, entries), in_specs=[vme...  4.29 us
    pallas_call x1, Pallas kernels, early_call(): pl.pallas_call(functools.partial(early_kernel, half), in_specs=[pl.BlockS...  3.35 us
    pallas_call x1, Pallas kernels, fetch(): pl.pallas_call(functools.partial(fetch_kernel, n), in_specs=[pl.BlockSpec...  2.52 us
  transfers between devices with their start and end apart: 21, of which 6 were waited for; matrix products, arithmetic and copies ran while one was open for 0% of the time, Pallas kernels for 19%

profile of v9, /device:TPU:0, one launch (start us, length us, event | category | flops | bytes accessed | tf_op | source)
XLA Modules:
  0.0 53.6 jit_solution(5879244066382179763)
XLA Ops:
  0.6 0.5 collective-permute-start.3
  1.1 2.6 %collective-permute-start = (bf16[16,4096]{1,0:T(8,128)(2,1)}, bf16[16,4096]{1,0:T(8,128)(2,1)S(1)}, u32[]{:S(2)}, u32[]{:S(2)}) collective-permute-start(bf16[16,4096]{1,0:T(8,128)(2,1)} %refs_0_.1), channel_id=1, source_target_pairs={{2,0},{5,1},{0,4},{9,5},{4,8},{13,9},{8,12},{15,13},{12,14},{11,15... | collective-permute-start | bytes 393224 | tf_op jit(solution)/shard_map/ppermute | solution.py:39
  3.8 0.0 collective-permute-done.3.refs_1_
  3.8 1.6 %collective-permute-start.4 = (bf16[16,4096]{1,0:T(8,128)(2,1)S(1)}, bf16[16,4096]{1,0:T(8,128)(2,1)S(1)}, u32[]{:S(2)}, u32[]{:S(2)}) collective-permute-start(bf16[16,4096]{1,0:T(8,128)(2,1)S(1)} %collective-permute-done.3.refs_1_), channel_id=1, source_target_pairs={{2,0},{5,1},{0,4},{9,5},{4,8},{13,9},{8,12},{15,13},{12,14},{11,15... | collective-permute-start | bytes 393224 | tf_op jit(solution)/shard_map/ppermute | solution.py:39
  5.4 2.5 %fetch.1 = (bf16[4096,512]{1,0:T(8,128)(2,1)S(1)}, bf16[256,512]{1,0:T(8,128)(2,1)S(1)}, f32[256,128]{1,0:T(8,128)S(1)}) custom-call(bf16[4096,512]{1,0:T(8,128)(2,1)} %far.3, bf16[256,512]{1,0:T(8,128)(2,1)} %far_cot.1, f32[1,256]{1,0:T(1,128)} %bitcast.2, bf16[16,4096]{1,0:T(8,128)(2,1)} %refs_0_.1), custom_call_target="tpu_custom_call" | custom-call | flops 4294967296 | bytes 8388608 | tf_op jit(solution)/shard_map/fetch/pallas_call | solution.py:164
  7.9 0.0 collective-permute-done.after.refs_2_
  7.9 0.1 collective-permute-start.13
  8.0 1.6 %collective-permute-start.1 = (bf16[16,4096]{1,0:T(8,128)(2,1)S(1)}, bf16[16,4096]{1,0:T(8,128)(2,1)S(1)}, u32[]{:S(2)}, u32[]{:S(2)}) collective-permute-start(bf16[16,4096]{1,0:T(8,128)(2,1)S(1)} %collective-permute-done.after.refs_2_), channel_id=1, source_target_pairs={{2,0},{5,1},{0,4},{9,5},{4,8},{13,9},{8,12},{15,13},{12,14},{11,15... | collective-permute-start | bytes 393224 | tf_op jit(solution)/shard_map/ppermute | solution.py:39
  9.6 0.0 collective-permute-done.4.refs_3_
  9.6 1.5 %collective-permute-start.5 = (bf16[16,4096]{1,0:T(8,128)(2,1)S(1)}, bf16[16,4096]{1,0:T(8,128)(2,1)S(1)}, u32[]{:S(2)}, u32[]{:S(2)}) collective-permute-start(bf16[16,4096]{1,0:T(8,128)(2,1)S(1)} %collective-permute-done.4.refs_3_), channel_id=1, source_target_pairs={{2,0},{5,1},{0,4},{9,5},{4,8},{13,9},{8,12},{15,13},{12,14},{11,15... | collective-permute-start | bytes 393224 | tf_op jit(solution)/shard_map/ppermute | solution.py:39
  11.1 2.3 %widen.2.refs_12_ = f32[4096,512]{1,0:T(8,128)S(1)} custom-call(bf16[4096,512]{1,0:T(8,128)(2,1)} %far.4, bf16[16,4096]{1,0:T(8,128)(2,1)S(1)} %collective-permute-done.after.refs_2_), custom_call_target="tpu_custom_call" | custom-call | flops 4294967296 | bytes 8388608 | tf_op jit(solution)/shard_map/widen/pallas_call | solution.py:126
  13.4 0.0 copy-start
  13.4 0.1 collective-permute-start.14
  13.5 0.0 collective-permute-done.1.after.refs_6_
  13.5 1.5 %collective-permute-start.7 = (bf16[16,4096]{1,0:T(8,128)(2,1)S(1)}, bf16[16,4096]{1,0:T(8,128)(2,1)S(1)}, u32[]{:S(2)}, u32[]{:S(2)}) collective-permute-start(bf16[16,4096]{1,0:T(8,128)(2,1)S(1)} %collective-permute-done.1.after.refs_6_), channel_id=1, source_target_pairs={{2,0},{5,1},{0,4},{9,5},{4,8},{13,9},{8,12},{15,13},{12,14},{11,15... | collective-permute-start | bytes 393224 | tf_op jit(solution)/shard_map/ppermute | solution.py:39
  15.1 0.0 collective-permute-start.2
  15.1 0.0 collective-permute-done.5.refs_7_
  15.1 1.0 %collective-permute-start.8 = (bf16[16,4096]{1,0:T(8,128)(2,1)S(1)}, bf16[16,4096]{1,0:T(8,128)(2,1)S(1)}, u32[]{:S(2)}, u32[]{:S(2)}) collective-permute-start(bf16[16,4096]{1,0:T(8,128)(2,1)S(1)} %collective-permute-done.5.refs_7_), channel_id=1, source_target_pairs={{2,0},{5,1},{0,4},{9,5},{4,8},{13,9},{8,12},{15,13},{12,14},{11,15... | collective-permute-start | bytes 393224 | tf_op jit(solution)/shard_map/ppermute | solution.py:39
  16.1 2.3 %widen.3.refs_13_ = f32[4096,512]{1,0:T(8,128)S(1)} custom-call(bf16[4096,512]{1,0:T(8,128)(2,1)} %far.5, bf16[16,4096]{1,0:T(8,128)(2,1)S(1)} %collective-permute-done.1.after.refs_6_), custom_call_target="tpu_custom_call" | custom-call | flops 4294967296 | bytes 8388608 | tf_op jit(solution)/shard_map/widen/pallas_call | solution.py:126
  18.4 0.0 collective-permute-done.13.refs_4_
  18.4 0.1 collective-permute-start.6
  18.5 0.1 collective-permute-done.7.refs_2_
  18.6 1.5 %collective-permute-start.11 = (bf16[16,4096]{1,0:T(8,128)(2,1)S(1)}, bf16[16,4096]{1,0:T(8,128)(2,1)S(1)}, u32[]{:S(2)}, u32[]{:S(2)}) collective-permute-start(bf16[16,4096]{1,0:T(8,128)(2,1)S(1)} %collective-permute-done.7.refs_2_), channel_id=1, source_target_pairs={{2,0},{5,1},{0,4},{9,5},{4,8},{13,9},{8,12},{15,13},{12,14},{11,15... | collective-permute-start | bytes 393224 | tf_op jit(solution)/shard_map/ppermute | solution.py:39
  20.0 0.0 collective-permute-done.14.refs_5_
  20.0 0.0 collective-permute-start.9
  20.1 0.0 collective-permute-done.8.refs_3_
  20.1 1.4 %collective-permute-start.12 = (bf16[16,4096]{1,0:T(8,128)(2,1)S(1)}, bf16[16,4096]{1,0:T(8,128)(2,1)S(1)}, u32[]{:S(2)}, u32[]{:S(2)}) collective-permute-start(bf16[16,4096]{1,0:T(8,128)(2,1)S(1)} %collective-permute-done.8.refs_3_), channel_id=1, source_target_pairs={{2,0},{5,1},{0,4},{9,5},{4,8},{13,9},{8,12},{15,13},{12,14},{11,15... | collective-permute-start | bytes 393224 | tf_op jit(solution)/shard_map/ppermute | solution.py:39
  21.5 0.0 collective-permute-done.2.refs_0_
  21.5 0.0 collective-permute-start.10
  21.5 3.4 %early.1 = (bf16[256,4096]{1,0:T(8,128)(2,1)S(1)}, bf16[4096,256]{1,0:T(8,128)(2,1)S(1)}, f32[256,512]{1,0:T(8,128)S(1)}) custom-call(bf16[16,4096]{1,0:T(8,128)(2,1)S(1)} %copy-done, bf16[16,4096]{1,0:T(8,128)(2,1)S(1)} %collective-permute-done.3.refs_1_, bf16[16,4096]{1,0:T(8,128)(2,1)S(1)} %collective-permute-done.after.refs_2_, ...), custom_call_target="tpu_custom_call" | custom-call | flops 4294967296 | bytes 12582912 | tf_op jit(solution)/shard_map/early/pallas_call | solution.py:221
  24.9 0.0 collective-permute-done.6.refs_1_
  24.9 0.0 collective-permute-done.9.refs_4_
  24.9 0.2 collective-permute-done.12.refs_7_
  25.1 0.0 collective-permute-done.10.refs_5_
  25.1 13.1 %replay.1 = (bf16[256,4096]{1,0:T(8,128)(2,1)S(1)}, bf16[4096,256]{1,0:T(8,128)(2,1)S(1)}, f32[256,512]{1,0:T(8,128)S(1)}, f32[4096,512]{1,0:T(8,128)S(1)}, f32[...) custom-call(bf16[16,4096]{1,0:T(8,128)(2,1)S(1)} %collective-permute, ...), custom_call_target="tpu_custom_call", output_to_operand_aliasing={{0}: (14, {}), {1}: (15, {}), {2}: (16, {})} | custom-call | tf_op jit(solution)/shard_map/replay/pallas_call | solution.py:356
  38.2 2.8 %collective-permute-start.17 = (f32[8,256]{1,0:T(8,128)S(1)}, f32[8,256]{1,0:T(8,128)S(1)}, u32[]{:S(2)}, u32[]{:S(2)}) collective-permute-start(f32[8,256]{1,0:T(8,128)S(1)} %get-tuple-element.22.own), channel_id=1, source_target_pairs={{12,0},{13,1},{14,2},{15,3},{8,4},{9,5},{10,6},{11,7},{4,8},{5,9},... | collective-permute-start | bytes 24584 | tf_op jit(solution)/shard_map/ppermute | solution.py:25
  41.0 0.1 collective-permute-start.16
  41.1 1.5 %collective-permute-start.15 = (f32[8,256]{1,0:T(8,128)S(1)}, f32[8,256]{1,0:T(8,128)S(1)}, u32[]{:S(2)}, u32[]{:S(2)}) collective-permute-start(f32[8,256]{1,0:T(8,128)S(1)} %get-tuple-element.22.own), channel_id=1, source_target_pairs={{4,0},{5,1},{6,2},{7,3},{0,4},{1,5},{2,6},{3,7},{12,8},{13,9},{14,... | collective-permute-start | bytes 24584 | tf_op jit(solution)/shard_map/ppermute | solution.py:25
  42.6 1.1 %collective-permute-done.17 = f32[8,256]{1,0:T(8,128)S(1)} collective-permute-done((f32[8,256]{1,0:T(8,128)S(1)}, f32[8,256]{1,0:T(8,128)S(1)}, u32[]{:S(2)}, u32[]{:S(2)}) %collective-permute-start.17) | collective-permute-done | bytes 8224 | tf_op jit(solution)/shard_map/ppermute | solution.py:25
  43.7 1.8 %collective-permute-done.16 = f32[8,256]{1,0:T(8,128)S(1)} collective-permute-done((f32[8,256]{1,0:T(8,128)S(1)}, f32[8,256]{1,0:T(8,128)S(1)}, u32[]{:S(2)}, u32[]{:S(2)}) %collective-permute-start.16) | collective-permute-done | bytes 8224 | tf_op jit(solution)/shard_map/ppermute | solution.py:25
  45.5 0.0 collective-permute-done.15
  45.5 0.1 collective-permute-start.20
  45.6 1.1 %collective-permute-start.19 = (f32[8,256]{1,0:T(8,128)S(1)}, f32[8,256]{1,0:T(8,128)S(1)}, u32[]{:S(2)}, u32[]{:S(2)}) collective-permute-start(f32[8,256]{1,0:T(8,128)S(1)} %add_add_fusion.s0), channel_id=1, source_target_pairs={{2,0},{3,1},{0,2},{1,3},{6,4},{7,5},{4,6},{5,7},{10,8},{11,9},{8,1... | collective-permute-start | bytes 24584 | tf_op jit(solution)/shard_map/ppermute | solution.py:25
  46.7 0.8 %collective-permute-start.18 = (f32[8,256]{1,0:T(8,128)S(1)}, f32[8,256]{1,0:T(8,128)S(1)}, u32[]{:S(2)}, u32[]{:S(2)}) collective-permute-start(f32[8,256]{1,0:T(8,128)S(1)} %add_add_fusion.s0), channel_id=1, source_target_pairs={{1,0},{0,1},{3,2},{2,3},{5,4},{4,5},{7,6},{6,7},{9,8},{8,9},{11,10... | collective-permute-start | bytes 24584 | tf_op jit(solution)/shard_map/ppermute | solution.py:25
  47.4 1.2 %collective-permute-done.20.s3 = f32[8,256]{1,0:T(8,128)S(1)} collective-permute-done((f32[8,256]{1,0:T(8,128)S(1)}, f32[8,256]{1,0:T(8,128)S(1)}, u32[]{:S(2)}, u32[]{:S(2)}) %collective-permute-start.20) | collective-permute-done | bytes 8224 | tf_op jit(solution)/shard_map/ppermute | solution.py:25
  48.7 0.7 %collective-permute-done.19.s2 = f32[8,256]{1,0:T(8,128)S(1)} collective-permute-done((f32[8,256]{1,0:T(8,128)S(1)}, f32[8,256]{1,0:T(8,128)S(1)}, u32[]{:S(2)}, u32[]{:S(2)}) %collective-permute-start.19) | collective-permute-done | bytes 8224 | tf_op jit(solution)/shard_map/ppermute | solution.py:25
  49.3 0.0 collective-permute-done.18.s1
  49.3 4.3 %theta.1 = (f32[4096,512]{1,0:T(8,128)}, f32[1,16]{1,0:T(1,128)}) custom-call(f32[8,256]{1,0:T(8,128)S(1)} %add_add_fusion.s0, f32[8,256]{1,0:T(8,128)S(1)} %collective-permute-done.18.s1, f32[8,256]{1,0:T(8,128)S(1)} %collective-permute-done.19.s2, f32[8,256]{1,0:T(8,128)S(1)} %collective-permute-done.20.s3, f32[8,256]{1,0:T(8,128)S(1)} %get-tuple-element.22.own, ...), custom_call_target="tpu_custom_call" | custom-call | tf_op jit(solution)/shard_map/theta/pallas_call | solution.py:428
  (3 shorter events, 0.0 us)
Async XLA Ops:
  0.6 3.2 %collective-permute-start.3 = (bf16[16,4096]{1,0:T(8,128)(2,1)}, bf16[16,4096]{1,0:T(8,128)(2,1)S(1)}, u32[]{:S(2)}, u32[]{:S(2)}) collective-permute-start(bf16[16,4096]{1,0:T(8,128)(2,1)} %refs_0_.1), channel_id=1, source_target_pairs={{1,0},{0,1},{3,2},{2,3},{5,4},{4,5},{7,6},{6,7},{9,8},{8,9},{11,10... | collective-permute-start | bytes 393224 | tf_op jit(solution)/shard_map/ppermute | solution.py:25
  1.1 6.8 %collective-permute-start = (bf16[16,4096]{1,0:T(8,128)(2,1)}, bf16[16,4096]{1,0:T(8,128)(2,1)S(1)}, u32[]{:S(2)}, u32[]{:S(2)}) collective-permute-start(bf16[16,4096]{1,0:T(8,128)(2,1)} %refs_0_.1), channel_id=1, source_target_pairs={{2,0},{5,1},{0,4},{9,5},{4,8},{13,9},{8,12},{15,13},{12,14},{11,15... | collective-permute-start | bytes 393224 | tf_op jit(solution)/shard_map/ppermute | solution.py:39
  3.8 5.8 %collective-permute-start.4 = (bf16[16,4096]{1,0:T(8,128)(2,1)S(1)}, bf16[16,4096]{1,0:T(8,128)(2,1)S(1)}, u32[]{:S(2)}, u32[]{:S(2)}) collective-permute-start(bf16[16,4096]{1,0:T(8,128)(2,1)S(1)} %collective-permute-done.3.refs_1_), channel_id=1, source_target_pairs={{2,0},{5,1},{0,4},{9,5},{4,8},{13,9},{8,12},{15,13},{12,14},{11,15... | collective-permute-start | bytes 393224 | tf_op jit(solution)/shard_map/ppermute | solution.py:39
  7.9 10.5 %collective-permute-start.13 = (bf16[16,4096]{1,0:T(8,128)(2,1)S(1)}, bf16[16,4096]{1,0:T(8,128)(2,1)S(1)}, u32[]{:S(2)}, u32[]{:S(2)}) collective-permute-start(bf16[16,4096]{1,0:T(8,128)(2,1)S(1)} %collective-permute-done.after.refs_2_), channel_id=1, source_target_pairs={{1,0},{0,1},{3,2},{2,3},{5,4},{4,5},{7,6},{6,7},{9,8},{8,9},{11,10... | collective-permute-start | bytes 393224 | tf_op jit(solution)/shard_map/ppermute | solution.py:25
  8.0 5.5 %collective-permute-start.1 = (bf16[16,4096]{1,0:T(8,128)(2,1)S(1)}, bf16[16,4096]{1,0:T(8,128)(2,1)S(1)}, u32[]{:S(2)}, u32[]{:S(2)}) collective-permute-start(bf16[16,4096]{1,0:T(8,128)(2,1)S(1)} %collective-permute-done.after.refs_2_), channel_id=1, source_target_pairs={{2,0},{5,1},{0,4},{9,5},{4,8},{13,9},{8,12},{15,13},{12,14},{11,15... | collective-permute-start | bytes 393224 | tf_op jit(solution)/shard_map/ppermute | solution.py:39
  9.6 5.5 %collective-permute-start.5 = (bf16[16,4096]{1,0:T(8,128)(2,1)S(1)}, bf16[16,4096]{1,0:T(8,128)(2,1)S(1)}, u32[]{:S(2)}, u32[]{:S(2)}) collective-permute-start(bf16[16,4096]{1,0:T(8,128)(2,1)S(1)} %collective-permute-done.4.refs_3_), channel_id=1, source_target_pairs={{2,0},{5,1},{0,4},{9,5},{4,8},{13,9},{8,12},{15,13},{12,14},{11,15... | collective-permute-start | bytes 393224 | tf_op jit(solution)/shard_map/ppermute | solution.py:39
  13.4 8.1 %copy-start = (bf16[16,4096]{1,0:T(8,128)(2,1)S(1)}, bf16[16,4096]{1,0:T(8,128)(2,1)}, u32[]{:S(2)}) copy-start(bf16[16,4096]{1,0:T(8,128)(2,1)} %refs_0_.1) | copy-start | bytes 393220
  13.4 6.6 %collective-permute-start.14 = (bf16[16,4096]{1,0:T(8,128)(2,1)S(1)}, bf16[16,4096]{1,0:T(8,128)(2,1)S(1)}, u32[]{:S(2)}, u32[]{:S(2)}) collective-permute-start(bf16[16,4096]{1,0:T(8,128)(2,1)S(1)} %collective-permute-done.4.refs_3_), channel_id=1, source_target_pairs={{1,0},{0,1},{3,2},{2,3},{5,4},{4,5},{7,6},{6,7},{9,8},{8,9},{11,10... | collective-permute-start | bytes 393224 | tf_op jit(solution)/shard_map/ppermute | solution.py:25
  13.5 5.0 %collective-permute-start.7 = (bf16[16,4096]{1,0:T(8,128)(2,1)S(1)}, bf16[16,4096]{1,0:T(8,128)(2,1)S(1)}, u32[]{:S(2)}, u32[]{:S(2)}) collective-permute-start(bf16[16,4096]{1,0:T(8,128)(2,1)S(1)} %collective-permute-done.1.after.refs_6_), channel_id=1, source_target_pairs={{2,0},{5,1},{0,4},{9,5},{4,8},{13,9},{8,12},{15,13},{12,14},{11,15... | collective-permute-start | bytes 393224 | tf_op jit(solution)/shard_map/ppermute | solution.py:39
  15.1 6.4 %collective-permute-start.2 = (bf16[16,4096]{1,0:T(8,128)(2,1)S(1)}, bf16[16,4096]{1,0:T(8,128)(2,1)S(1)}, u32[]{:S(2)}, u32[]{:S(2)}) collective-permute-start(bf16[16,4096]{1,0:T(8,128)(2,1)S(1)} %collective-permute-done.1.after.refs_6_), channel_id=1, source_target_pairs={{1,0},{0,1},{3,2},{2,3},{5,4},{4,5},{7,6},{6,7},{9,8},{8,9},{11,10... | collective-permute-start | bytes 393224 | tf_op jit(solution)/shard_map/ppermute | solution.py:25
  15.1 5.0 %collective-permute-start.8 = (bf16[16,4096]{1,0:T(8,128)(2,1)S(1)}, bf16[16,4096]{1,0:T(8,128)(2,1)S(1)}, u32[]{:S(2)}, u32[]{:S(2)}) collective-permute-start(bf16[16,4096]{1,0:T(8,128)(2,1)S(1)} %collective-permute-done.5.refs_7_), channel_id=1, source_target_pairs={{2,0},{5,1},{0,4},{9,5},{4,8},{13,9},{8,12},{15,13},{12,14},{11,15... | collective-permute-start | bytes 393224 | tf_op jit(solution)/shard_map/ppermute | solution.py:39
  18.4 6.5 %collective-permute-start.6 = (bf16[16,4096]{1,0:T(8,128)(2,1)S(1)}, bf16[16,4096]{1,0:T(8,128)(2,1)S(1)}, u32[]{:S(2)}, u32[]{:S(2)}) collective-permute-start(bf16[16,4096]{1,0:T(8,128)(2,1)S(1)} %collective-permute-done.5.refs_7_), channel_id=1, source_target_pairs={{1,0},{0,1},{3,2},{2,3},{5,4},{4,5},{7,6},{6,7},{9,8},{8,9},{11,10... | collective-permute-start | bytes 393224 | tf_op jit(solution)/shard_map/ppermute | solution.py:25
  18.6 6.3 %collective-permute-start.11 = (bf16[16,4096]{1,0:T(8,128)(2,1)S(1)}, bf16[16,4096]{1,0:T(8,128)(2,1)S(1)}, u32[]{:S(2)}, u32[]{:S(2)}) collective-permute-start(bf16[16,4096]{1,0:T(8,128)(2,1)S(1)} %collective-permute-done.7.refs_2_), channel_id=1, source_target_pairs={{2,0},{5,1},{0,4},{9,5},{4,8},{13,9},{8,12},{15,13},{12,14},{11,15... | collective-permute-start | bytes 393224 | tf_op jit(solution)/shard_map/ppermute | solution.py:39
  20.0 4.9 %collective-permute-start.9 = (bf16[16,4096]{1,0:T(8,128)(2,1)S(1)}, bf16[16,4096]{1,0:T(8,128)(2,1)S(1)}, u32[]{:S(2)}, u32[]{:S(2)}) collective-permute-start(bf16[16,4096]{1,0:T(8,128)(2,1)S(1)} %collective-permute-done.7.refs_2_), channel_id=1, source_target_pairs={{1,0},{0,1},{3,2},{2,3},{5,4},{4,5},{7,6},{6,7},{9,8},{8,9},{11,10... | collective-permute-start | bytes 393224 | tf_op jit(solution)/shard_map/ppermute | solution.py:25
  20.1 5.0 %collective-permute-start.12 = (bf16[16,4096]{1,0:T(8,128)(2,1)S(1)}, bf16[16,4096]{1,0:T(8,128)(2,1)S(1)}, u32[]{:S(2)}, u32[]{:S(2)}) collective-permute-start(bf16[16,4096]{1,0:T(8,128)(2,1)S(1)} %collective-permute-done.8.refs_3_), channel_id=1, source_target_pairs={{2,0},{5,1},{0,4},{9,5},{4,8},{13,9},{8,12},{15,13},{12,14},{11,15... | collective-permute-start | bytes 393224 | tf_op jit(solution)/shard_map/ppermute | solution.py:39
  21.5 3.6 %collective-permute-start.10 = (bf16[16,4096]{1,0:T(8,128)(2,1)S(1)}, bf16[16,4096]{1,0:T(8,128)(2,1)S(1)}, u32[]{:S(2)}, u32[]{:S(2)}) collective-permute-start(bf16[16,4096]{1,0:T(8,128)(2,1)S(1)} %collective-permute-done.8.refs_3_), channel_id=1, source_target_pairs={{1,0},{0,1},{3,2},{2,3},{5,4},{4,5},{7,6},{6,7},{9,8},{8,9},{11,10... | collective-permute-start | bytes 393224 | tf_op jit(solution)/shard_map/ppermute | solution.py:25
  38.2 5.5 %collective-permute-start.17 = (f32[8,256]{1,0:T(8,128)S(1)}, f32[8,256]{1,0:T(8,128)S(1)}, u32[]{:S(2)}, u32[]{:S(2)}) collective-permute-start(f32[8,256]{1,0:T(8,128)S(1)} %get-tuple-element.22.own), channel_id=1, source_target_pairs={{12,0},{13,1},{14,2},{15,3},{8,4},{9,5},{10,6},{11,7},{4,8},{5,9},... | collective-permute-start | bytes 24584 | tf_op jit(solution)/shard_map/ppermute | solution.py:25
  41.0 4.5 %collective-permute-start.16 = (f32[8,256]{1,0:T(8,128)S(1)}, f32[8,256]{1,0:T(8,128)S(1)}, u32[]{:S(2)}, u32[]{:S(2)}) collective-permute-start(f32[8,256]{1,0:T(8,128)S(1)} %get-tuple-element.22.own), channel_id=1, source_target_pairs={{8,0},{9,1},{10,2},{11,3},{12,4},{13,5},{14,6},{15,7},{0,8},{1,9},... | collective-permute-start | bytes 24584 | tf_op jit(solution)/shard_map/ppermute | solution.py:25
  41.1 4.4 %collective-permute-start.15 = (f32[8,256]{1,0:T(8,128)S(1)}, f32[8,256]{1,0:T(8,128)S(1)}, u32[]{:S(2)}, u32[]{:S(2)}) collective-permute-start(f32[8,256]{1,0:T(8,128)S(1)} %get-tuple-element.22.own), channel_id=1, source_target_pairs={{4,0},{5,1},{6,2},{7,3},{0,4},{1,5},{2,6},{3,7},{12,8},{13,9},{14,... | collective-permute-start | bytes 24584 | tf_op jit(solution)/shard_map/ppermute | solution.py:25
  45.5 3.1 %collective-permute-start.20 = (f32[8,256]{1,0:T(8,128)S(1)}, f32[8,256]{1,0:T(8,128)S(1)}, u32[]{:S(2)}, u32[]{:S(2)}) collective-permute-start(f32[8,256]{1,0:T(8,128)S(1)} %add_add_fusion.s0), channel_id=1, source_target_pairs={{3,0},{2,1},{1,2},{0,3},{7,4},{6,5},{5,6},{4,7},{11,8},{10,9},{9,1... | collective-permute-start | bytes 24584 | tf_op jit(solution)/shard_map/ppermute | solution.py:25
  45.6 3.7 %collective-permute-start.19 = (f32[8,256]{1,0:T(8,128)S(1)}, f32[8,256]{1,0:T(8,128)S(1)}, u32[]{:S(2)}, u32[]{:S(2)}) collective-permute-start(f32[8,256]{1,0:T(8,128)S(1)} %add_add_fusion.s0), channel_id=1, source_target_pairs={{2,0},{3,1},{0,2},{1,3},{6,4},{7,5},{4,6},{5,7},{10,8},{11,9},{8,1... | collective-permute-start | bytes 24584 | tf_op jit(solution)/shard_map/ppermute | solution.py:25
  46.7 2.6 %collective-permute-start.18 = (f32[8,256]{1,0:T(8,128)S(1)}, f32[8,256]{1,0:T(8,128)S(1)}, u32[]{:S(2)}, u32[]{:S(2)}) collective-permute-start(f32[8,256]{1,0:T(8,128)S(1)} %add_add_fusion.s0), channel_id=1, source_target_pairs={{1,0},{0,1},{3,2},{2,3},{5,4},{4,5},{7,6},{6,7},{9,8},{8,9},{11,10... | collective-permute-start | bytes 24584 | tf_op jit(solution)/shard_map/ppermute | solution.py:25

commit v10 on v9

--- a/solution.py
+++ b/solution.py
@@ -8,7 +8,7 @@
 from jax.sharding import PartitionSpec as P
 
 TILE = 512
-HALF = 256
+QUARTER = 128
 ROWS = 16
 COLUMNS = 256
 COST = 4 << 30
@@ -263,11 +263,18 @@
     across[...] = jnp.zeros_like(across)
 
     def grad_rows(i, slot, r):
-        at = pl.ds(pl.multiple_of(i * TILE + r, HALF), HALF)
-        grads[slot][r : r + HALF, :] = f32dot(turned[at, :], scaled[...])
-
-    def probe(i, slot, target, terms):
-        target[...] += f32dot(tokens[:, span(i)], terms[slot][...])
+        at = pl.ds(pl.multiple_of(i * TILE + r, QUARTER), QUARTER)
+        grads[slot][r : r + QUARTER, :] = f32dot(turned[at, :], scaled[...])
+
+    units = [
+        (target, terms, slice(c, min(c + COLUMNS, width)))
+        for target, terms in ((along, firsts), (across, seconds))
+        for c in range(0, width, COLUMNS)
+    ]
+
+    def probe(i, slot, unit):
+        target, terms, cols = unit
+        target[:, cols] += f32dot(tokens[:, span(i)], terms[slot][:, cols])
 
     def pieces(i, slot, first, last):
         for r in range(first, last, ROWS):
@@ -278,8 +285,8 @@
 
     for i in range(2):
         tile_copy(i).wait()
-    grad_rows(0, 0, 0)
-    grad_rows(0, 0, HALF)
+    for r in range(0, TILE, QUARTER):
+        grad_rows(0, 0, r)
     sq, cross = {}, {}
     for r, cols, g, m1, m2, adj in pieces(0, 0, 0, SAMPLE):
         _, _, upd = update(g, m1, m2)
@@ -292,9 +299,9 @@
 
     sums[...] = jnp.zeros_like(sums)
 
-    def update_rows(i, slot, first):
+    def update_rows(i, slot, first, last):
         sq, cross = {}, {}
-        for r, cols, g, m1, m2, adj in pieces(i, slot, first, first + HALF):
+        for r, cols, g, m1, m2, adj in pieces(i, slot, first, last):
             over, inv, upd = update(g, m1, m2)
             sq[cols.start] = sq.get(cols.start, 0.0) + fold(upd * upd)
             cross[cols.start] = cross.get(cols.start, 0.0) + fold(adj * upd)
@@ -305,12 +312,16 @@
         sums[1] += sum(cross.values())
 
     def body(i, slot, ahead=True, behind=True):
-        for r, target, terms in ((0, along, firsts), (HALF, across, seconds)):
+        quarters = TILE // QUARTER
+        for q in range(quarters):
+            r = q * QUARTER
             if ahead:
                 grad_rows(i + 1, 1 - slot, r)
-            update_rows(i, slot, r)
+            update_rows(i, slot, r, r + QUARTER // 2)
             if behind:
-                probe(i - 1, 1 - slot, target, terms)
+                for unit in units[q::quarters]:
+                    probe(i - 1, 1 - slot, unit)
+            update_rows(i, slot, r + QUARTER // 2, r + QUARTER)
 
     body(0, 0, behind=False)
 
@@ -323,8 +334,8 @@
 
     lax.fori_loop(0, tiles // 2 - 1, pair, 0)
     body(tiles - 1, 1, ahead=False)
-    probe(tiles - 1, 1, along, firsts)
-    probe(tiles - 1, 1, across, seconds)
+    for unit in units:
+        probe(tiles - 1, 1, unit)
 
     height = count // n
     places = owners(n)
@@ -409,12 +420,12 @@
     bent = (bend[...] * (lead_here * along[...] + rest_here * across[...])).astype(jnp.bfloat16)
 
     def copy(i):
-        at = pl.ds(i * TILE, TILE)
+        at = pl.ds(i * SAMPLE, SAMPLE)
         return pltpu.make_async_copy(ready.at[at, :], theta.at[at, :], sent.at[i])
 
-    tiles = theta.shape[0] // TILE
+    tiles = theta.shape[0] // SAMPLE
     for i in range(tiles):
-        at = pl.ds(i * TILE, TILE)
+        at = pl.ds(i * SAMPLE, SAMPLE)
         ready[at, :] = 0.999 * adjoint[at, :] + f32dot(turned[at, :], bent)
         copy(i).start()
     for i in range(tiles):
@@ -433,7 +444,7 @@
             jax.ShapeDtypeStruct((depth, width), jnp.float32),
             jax.ShapeDtypeStruct((1, count // n), jnp.float32),
         ],
-        scratch_shapes=[pltpu.VMEM((depth, width), jnp.float32), pltpu.SemaphoreType.DMA((depth // TILE,))],
+        scratch_shapes=[pltpu.VMEM((depth, width), jnp.float32), pltpu.SemaphoreType.DMA((depth // SAMPLE,))],
         compiler_params=pltpu.CompilerParams(vmem_limit_bytes=VMEM_BYTES),
         name="theta",
     )(*sums, own, along, across, bend, turned, adjoint)

time: 53.9 us -> 54.1 us (level)
  no operation moved by 1% of the time
where the time goes in v10:
time: 54.1 us; the launch traced here: 53.9 us
  Pallas kernels  28 us (52%)
  starting transfers between devices  20 us (37%)
  waiting for transfers between devices  5.03 us (9%)
  between operations  0.78 us (1%)
    pallas_call x1, Pallas kernels, replay_call(): pl.pallas_call(functools.partial(replay_kernel, n, half), in_specs=[far]...  13.3 us
    ppermute x8, starting transfers between devices, onward(): return lax.ppermute(value, 'dp', pairs)  12.9 us
    ppermute x13, starting transfers between devices, swapped(): return lax.ppermute(value, 'dp', [(d ^ mask, d) for d in range(n)])  7.11 us
    ppermute x13, waiting for transfers between devices, swapped(): return lax.ppermute(value, 'dp', [(d ^ mask, d) for d in range(n)])  4.79 us
    pallas_call x2, Pallas kernels, fetch_wide(): pl.pallas_call(functools.partial(widen_kernel, factor), in_specs=[pl.Bloc...  4.57 us
    pallas_call x1, Pallas kernels, theta_call(): pl.pallas_call(functools.partial(theta_kernel, n, entries), in_specs=[vme...  4.28 us
    pallas_call x1, Pallas kernels, early_call(): pl.pallas_call(functools.partial(early_kernel, half), in_specs=[pl.BlockS...  3.35 us
    pallas_call x1, Pallas kernels, fetch(): pl.pallas_call(functools.partial(fetch_kernel, n), in_specs=[pl.BlockSpec...  2.52 us
  transfers between devices with their start and end apart: 21, of which 6 were waited for; matrix products, arithmetic and copies ran while one was open for 0% of the time, Pallas kernels for 19%

profile of v10, /device:TPU:0, one launch (start us, length us, event | category | flops | bytes accessed | tf_op | source)
XLA Modules:
  0.0 53.9 jit_solution(14306424033275556260)
XLA Ops:
  0.6 0.5 collective-permute-start.3
  1.1 2.6 %collective-permute-start = (bf16[16,4096]{1,0:T(8,128)(2,1)}, bf16[16,4096]{1,0:T(8,128)(2,1)S(1)}, u32[]{:S(2)}, u32[]{:S(2)}) collective-permute-start(bf16[16,4096]{1,0:T(8,128)(2,1)} %refs_0_.1), channel_id=1, source_target_pairs={{2,0},{5,1},{0,4},{9,5},{4,8},{13,9},{8,12},{15,13},{12,14},{11,15... | collective-permute-start | bytes 393224 | tf_op jit(solution)/shard_map/ppermute | solution.py:39
  3.8 0.0 collective-permute-done.3.refs_1_
  3.8 1.6 %collective-permute-start.4 = (bf16[16,4096]{1,0:T(8,128)(2,1)S(1)}, bf16[16,4096]{1,0:T(8,128)(2,1)S(1)}, u32[]{:S(2)}, u32[]{:S(2)}) collective-permute-start(bf16[16,4096]{1,0:T(8,128)(2,1)S(1)} %collective-permute-done.3.refs_1_), channel_id=1, source_target_pairs={{2,0},{5,1},{0,4},{9,5},{4,8},{13,9},{8,12},{15,13},{12,14},{11,15... | collective-permute-start | bytes 393224 | tf_op jit(solution)/shard_map/ppermute | solution.py:39
  5.4 2.5 %fetch.1 = (bf16[4096,512]{1,0:T(8,128)(2,1)S(1)}, bf16[256,512]{1,0:T(8,128)(2,1)S(1)}, f32[256,128]{1,0:T(8,128)S(1)}) custom-call(bf16[4096,512]{1,0:T(8,128)(2,1)} %far.3, bf16[256,512]{1,0:T(8,128)(2,1)} %far_cot.1, f32[1,256]{1,0:T(1,128)} %bitcast.2, bf16[16,4096]{1,0:T(8,128)(2,1)} %refs_0_.1), custom_call_target="tpu_custom_call" | custom-call | flops 4294967296 | bytes 8388608 | tf_op jit(solution)/shard_map/fetch/pallas_call | solution.py:164
  7.9 0.0 collective-permute-done.after.refs_2_
  7.9 0.1 collective-permute-start.13
  8.0 1.6 %collective-permute-start.1 = (bf16[16,4096]{1,0:T(8,128)(2,1)S(1)}, bf16[16,4096]{1,0:T(8,128)(2,1)S(1)}, u32[]{:S(2)}, u32[]{:S(2)}) collective-permute-start(bf16[16,4096]{1,0:T(8,128)(2,1)S(1)} %collective-permute-done.after.refs_2_), channel_id=1, source_target_pairs={{2,0},{5,1},{0,4},{9,5},{4,8},{13,9},{8,12},{15,13},{12,14},{11,15... | collective-permute-start | bytes 393224 | tf_op jit(solution)/shard_map/ppermute | solution.py:39
  9.6 0.0 collective-permute-done.4.refs_3_
  9.6 1.5 %collective-permute-start.5 = (bf16[16,4096]{1,0:T(8,128)(2,1)S(1)}, bf16[16,4096]{1,0:T(8,128)(2,1)S(1)}, u32[]{:S(2)}, u32[]{:S(2)}) collective-permute-start(bf16[16,4096]{1,0:T(8,128)(2,1)S(1)} %collective-permute-done.4.refs_3_), channel_id=1, source_target_pairs={{2,0},{5,1},{0,4},{9,5},{4,8},{13,9},{8,12},{15,13},{12,14},{11,15... | collective-permute-start | bytes 393224 | tf_op jit(solution)/shard_map/ppermute | solution.py:39
  11.1 2.3 %widen.2.refs_12_ = f32[4096,512]{1,0:T(8,128)S(1)} custom-call(bf16[4096,512]{1,0:T(8,128)(2,1)} %far.4, bf16[16,4096]{1,0:T(8,128)(2,1)S(1)} %collective-permute-done.after.refs_2_), custom_call_target="tpu_custom_call" | custom-call | flops 4294967296 | bytes 8388608 | tf_op jit(solution)/shard_map/widen/pallas_call | solution.py:126
  13.4 0.0 copy-start
  13.4 0.1 collective-permute-start.14
  13.5 0.0 collective-permute-done.1.after.refs_6_
  13.5 1.5 %collective-permute-start.7 = (bf16[16,4096]{1,0:T(8,128)(2,1)S(1)}, bf16[16,4096]{1,0:T(8,128)(2,1)S(1)}, u32[]{:S(2)}, u32[]{:S(2)}) collective-permute-start(bf16[16,4096]{1,0:T(8,128)(2,1)S(1)} %collective-permute-done.1.after.refs_6_), channel_id=1, source_target_pairs={{2,0},{5,1},{0,4},{9,5},{4,8},{13,9},{8,12},{15,13},{12,14},{11,15... | collective-permute-start | bytes 393224 | tf_op jit(solution)/shard_map/ppermute | solution.py:39
  15.1 0.0 collective-permute-start.2
  15.1 0.0 collective-permute-done.5.refs_7_
  15.1 1.0 %collective-permute-start.8 = (bf16[16,4096]{1,0:T(8,128)(2,1)S(1)}, bf16[16,4096]{1,0:T(8,128)(2,1)S(1)}, u32[]{:S(2)}, u32[]{:S(2)}) collective-permute-start(bf16[16,4096]{1,0:T(8,128)(2,1)S(1)} %collective-permute-done.5.refs_7_), channel_id=1, source_target_pairs={{2,0},{5,1},{0,4},{9,5},{4,8},{13,9},{8,12},{15,13},{12,14},{11,15... | collective-permute-start | bytes 393224 | tf_op jit(solution)/shard_map/ppermute | solution.py:39
  16.1 2.3 %widen.3.refs_13_ = f32[4096,512]{1,0:T(8,128)S(1)} custom-call(bf16[4096,512]{1,0:T(8,128)(2,1)} %far.5, bf16[16,4096]{1,0:T(8,128)(2,1)S(1)} %collective-permute-done.1.after.refs_6_), custom_call_target="tpu_custom_call" | custom-call | flops 4294967296 | bytes 8388608 | tf_op jit(solution)/shard_map/widen/pallas_call | solution.py:126
  18.4 0.0 collective-permute-done.13.refs_4_
  18.4 0.1 collective-permute-start.6
  18.5 0.1 collective-permute-done.7.refs_2_
  18.6 1.5 %collective-permute-start.11 = (bf16[16,4096]{1,0:T(8,128)(2,1)S(1)}, bf16[16,4096]{1,0:T(8,128)(2,1)S(1)}, u32[]{:S(2)}, u32[]{:S(2)}) collective-permute-start(bf16[16,4096]{1,0:T(8,128)(2,1)S(1)} %collective-permute-done.7.refs_2_), channel_id=1, source_target_pairs={{2,0},{5,1},{0,4},{9,5},{4,8},{13,9},{8,12},{15,13},{12,14},{11,15... | collective-permute-start | bytes 393224 | tf_op jit(solution)/shard_map/ppermute | solution.py:39
  20.0 0.0 collective-permute-done.14.refs_5_
  20.0 0.0 collective-permute-start.9
  20.1 0.0 collective-permute-done.8.refs_3_
  20.1 1.4 %collective-permute-start.12 = (bf16[16,4096]{1,0:T(8,128)(2,1)S(1)}, bf16[16,4096]{1,0:T(8,128)(2,1)S(1)}, u32[]{:S(2)}, u32[]{:S(2)}) collective-permute-start(bf16[16,4096]{1,0:T(8,128)(2,1)S(1)} %collective-permute-done.8.refs_3_), channel_id=1, source_target_pairs={{2,0},{5,1},{0,4},{9,5},{4,8},{13,9},{8,12},{15,13},{12,14},{11,15... | collective-permute-start | bytes 393224 | tf_op jit(solution)/shard_map/ppermute | solution.py:39
  21.5 0.0 collective-permute-done.2.refs_0_
  21.5 0.0 collective-permute-start.10
  21.5 3.4 %early.1 = (bf16[256,4096]{1,0:T(8,128)(2,1)S(1)}, bf16[4096,256]{1,0:T(8,128)(2,1)S(1)}, f32[256,512]{1,0:T(8,128)S(1)}) custom-call(bf16[16,4096]{1,0:T(8,128)(2,1)S(1)} %copy-done, bf16[16,4096]{1,0:T(8,128)(2,1)S(1)} %collective-permute-done.3.refs_1_, bf16[16,4096]{1,0:T(8,128)(2,1)S(1)} %collective-permute-done.after.refs_2_, ...), custom_call_target="tpu_custom_call" | custom-call | flops 4294967296 | bytes 12582912 | tf_op jit(solution)/shard_map/early/pallas_call | solution.py:221
  24.9 0.0 collective-permute-done.6.refs_1_
  24.9 0.0 collective-permute-done.11.refs_6_
  24.9 0.0 collective-permute-done.9.refs_4_
  24.9 0.2 collective-permute-done.12.refs_7_
  25.1 0.0 collective-permute-done.10.refs_5_
  25.1 13.3 %replay.1 = (bf16[256,4096]{1,0:T(8,128)(2,1)S(1)}, bf16[4096,256]{1,0:T(8,128)(2,1)S(1)}, f32[256,512]{1,0:T(8,128)S(1)}, f32[4096,512]{1,0:T(8,128)S(1)}, f32[...) custom-call(bf16[16,4096]{1,0:T(8,128)(2,1)S(1)} %collective-permute, ...), custom_call_target="tpu_custom_call", output_to_operand_aliasing={{0}: (14, {}), {1}: (15, {}), {2}: (16, {})} | custom-call | tf_op jit(solution)/shard_map/replay/pallas_call | solution.py:367
  38.4 2.8 %collective-permute-start.17 = (f32[8,256]{1,0:T(8,128)S(1)}, f32[8,256]{1,0:T(8,128)S(1)}, u32[]{:S(2)}, u32[]{:S(2)}) collective-permute-start(f32[8,256]{1,0:T(8,128)S(1)} %get-tuple-element.22.own), channel_id=1, source_target_pairs={{12,0},{13,1},{14,2},{15,3},{8,4},{9,5},{10,6},{11,7},{4,8},{5,9},... | collective-permute-start | bytes 24584 | tf_op jit(solution)/shard_map/ppermute | solution.py:25
  41.2 0.1 collective-permute-start.16
  41.3 1.5 %collective-permute-start.15 = (f32[8,256]{1,0:T(8,128)S(1)}, f32[8,256]{1,0:T(8,128)S(1)}, u32[]{:S(2)}, u32[]{:S(2)}) collective-permute-start(f32[8,256]{1,0:T(8,128)S(1)} %get-tuple-element.22.own), channel_id=1, source_target_pairs={{4,0},{5,1},{6,2},{7,3},{0,4},{1,5},{2,6},{3,7},{12,8},{13,9},{14,... | collective-permute-start | bytes 24584 | tf_op jit(solution)/shard_map/ppermute | solution.py:25
  42.9 1.1 %collective-permute-done.17 = f32[8,256]{1,0:T(8,128)S(1)} collective-permute-done((f32[8,256]{1,0:T(8,128)S(1)}, f32[8,256]{1,0:T(8,128)S(1)}, u32[]{:S(2)}, u32[]{:S(2)}) %collective-permute-start.17) | collective-permute-done | bytes 8224 | tf_op jit(solution)/shard_map/ppermute | solution.py:25
  43.9 1.8 %collective-permute-done.16 = f32[8,256]{1,0:T(8,128)S(1)} collective-permute-done((f32[8,256]{1,0:T(8,128)S(1)}, f32[8,256]{1,0:T(8,128)S(1)}, u32[]{:S(2)}, u32[]{:S(2)}) %collective-permute-start.16) | collective-permute-done | bytes 8224 | tf_op jit(solution)/shard_map/ppermute | solution.py:25
  45.8 0.0 collective-permute-done.15
  45.8 0.1 collective-permute-start.20
  45.9 1.1 %collective-permute-start.19 = (f32[8,256]{1,0:T(8,128)S(1)}, f32[8,256]{1,0:T(8,128)S(1)}, u32[]{:S(2)}, u32[]{:S(2)}) collective-permute-start(f32[8,256]{1,0:T(8,128)S(1)} %add_add_fusion.s0), channel_id=1, source_target_pairs={{2,0},{3,1},{0,2},{1,3},{6,4},{7,5},{4,6},{5,7},{10,8},{11,9},{8,1... | collective-permute-start | bytes 24584 | tf_op jit(solution)/shard_map/ppermute | solution.py:25
  46.9 0.8 %collective-permute-start.18 = (f32[8,256]{1,0:T(8,128)S(1)}, f32[8,256]{1,0:T(8,128)S(1)}, u32[]{:S(2)}, u32[]{:S(2)}) collective-permute-start(f32[8,256]{1,0:T(8,128)S(1)} %add_add_fusion.s0), channel_id=1, source_target_pairs={{1,0},{0,1},{3,2},{2,3},{5,4},{4,5},{7,6},{6,7},{9,8},{8,9},{11,10... | collective-permute-start | bytes 24584 | tf_op jit(solution)/shard_map/ppermute | solution.py:25
  47.7 1.2 %collective-permute-done.20.s3 = f32[8,256]{1,0:T(8,128)S(1)} collective-permute-done((f32[8,256]{1,0:T(8,128)S(1)}, f32[8,256]{1,0:T(8,128)S(1)}, u32[]{:S(2)}, u32[]{:S(2)}) %collective-permute-start.20) | collective-permute-done | bytes 8224 | tf_op jit(solution)/shard_map/ppermute | solution.py:25
  48.9 0.7 %collective-permute-done.19.s2 = f32[8,256]{1,0:T(8,128)S(1)} collective-permute-done((f32[8,256]{1,0:T(8,128)S(1)}, f32[8,256]{1,0:T(8,128)S(1)}, u32[]{:S(2)}, u32[]{:S(2)}) %collective-permute-start.19) | collective-permute-done | bytes 8224 | tf_op jit(solution)/shard_map/ppermute | solution.py:25
  49.6 4.3 %theta.1 = (f32[4096,512]{1,0:T(8,128)}, f32[1,16]{1,0:T(1,128)}) custom-call(f32[8,256]{1,0:T(8,128)S(1)} %add_add_fusion.s0, f32[8,256]{1,0:T(8,128)S(1)} %collective-permute-done.18.s1, f32[8,256]{1,0:T(8,128)S(1)} %collective-permute-done.19.s2, f32[8,256]{1,0:T(8,128)S(1)} %collective-permute-done.20.s3, f32[8,256]{1,0:T(8,128)S(1)} %get-tuple-element.22.own, ...), custom_call_target="tpu_custom_call" | custom-call | tf_op jit(solution)/shard_map/theta/pallas_call | solution.py:439
  (3 shorter events, 0.0 us)
Async XLA Ops:
  0.6 3.2 %collective-permute-start.3 = (bf16[16,4096]{1,0:T(8,128)(2,1)}, bf16[16,4096]{1,0:T(8,128)(2,1)S(1)}, u32[]{:S(2)}, u32[]{:S(2)}) collective-permute-start(bf16[16,4096]{1,0:T(8,128)(2,1)} %refs_0_.1), channel_id=1, source_target_pairs={{1,0},{0,1},{3,2},{2,3},{5,4},{4,5},{7,6},{6,7},{9,8},{8,9},{11,10... | collective-permute-start | bytes 393224 | tf_op jit(solution)/shard_map/ppermute | solution.py:25
  1.1 6.8 %collective-permute-start = (bf16[16,4096]{1,0:T(8,128)(2,1)}, bf16[16,4096]{1,0:T(8,128)(2,1)S(1)}, u32[]{:S(2)}, u32[]{:S(2)}) collective-permute-start(bf16[16,4096]{1,0:T(8,128)(2,1)} %refs_0_.1), channel_id=1, source_target_pairs={{2,0},{5,1},{0,4},{9,5},{4,8},{13,9},{8,12},{15,13},{12,14},{11,15... | collective-permute-start | bytes 393224 | tf_op jit(solution)/shard_map/ppermute | solution.py:39
  3.8 5.8 %collective-permute-start.4 = (bf16[16,4096]{1,0:T(8,128)(2,1)S(1)}, bf16[16,4096]{1,0:T(8,128)(2,1)S(1)}, u32[]{:S(2)}, u32[]{:S(2)}) collective-permute-start(bf16[16,4096]{1,0:T(8,128)(2,1)S(1)} %collective-permute-done.3.refs_1_), channel_id=1, source_target_pairs={{2,0},{5,1},{0,4},{9,5},{4,8},{13,9},{8,12},{15,13},{12,14},{11,15... | collective-permute-start | bytes 393224 | tf_op jit(solution)/shard_map/ppermute | solution.py:39
  7.9 10.5 %collective-permute-start.13 = (bf16[16,4096]{1,0:T(8,128)(2,1)S(1)}, bf16[16,4096]{1,0:T(8,128)(2,1)S(1)}, u32[]{:S(2)}, u32[]{:S(2)}) collective-permute-start(bf16[16,4096]{1,0:T(8,128)(2,1)S(1)} %collective-permute-done.after.refs_2_), channel_id=1, source_target_pairs={{1,0},{0,1},{3,2},{2,3},{5,4},{4,5},{7,6},{6,7},{9,8},{8,9},{11,10... | collective-permute-start | bytes 393224 | tf_op jit(solution)/shard_map/ppermute | solution.py:25
  8.0 5.5 %collective-permute-start.1 = (bf16[16,4096]{1,0:T(8,128)(2,1)S(1)}, bf16[16,4096]{1,0:T(8,128)(2,1)S(1)}, u32[]{:S(2)}, u32[]{:S(2)}) collective-permute-start(bf16[16,4096]{1,0:T(8,128)(2,1)S(1)} %collective-permute-done.after.refs_2_), channel_id=1, source_target_pairs={{2,0},{5,1},{0,4},{9,5},{4,8},{13,9},{8,12},{15,13},{12,14},{11,15... | collective-permute-start | bytes 393224 | tf_op jit(solution)/shard_map/ppermute | solution.py:39
  9.6 5.5 %collective-permute-start.5 = (bf16[16,4096]{1,0:T(8,128)(2,1)S(1)}, bf16[16,4096]{1,0:T(8,128)(2,1)S(1)}, u32[]{:S(2)}, u32[]{:S(2)}) collective-permute-start(bf16[16,4096]{1,0:T(8,128)(2,1)S(1)} %collective-permute-done.4.refs_3_), channel_id=1, source_target_pairs={{2,0},{5,1},{0,4},{9,5},{4,8},{13,9},{8,12},{15,13},{12,14},{11,15... | collective-permute-start | bytes 393224 | tf_op jit(solution)/shard_map/ppermute | solution.py:39
  13.4 8.1 %copy-start = (bf16[16,4096]{1,0:T(8,128)(2,1)S(1)}, bf16[16,4096]{1,0:T(8,128)(2,1)}, u32[]{:S(2)}) copy-start(bf16[16,4096]{1,0:T(8,128)(2,1)} %refs_0_.1) | copy-start | bytes 393220
  13.4 6.6 %collective-permute-start.14 = (bf16[16,4096]{1,0:T(8,128)(2,1)S(1)}, bf16[16,4096]{1,0:T(8,128)(2,1)S(1)}, u32[]{:S(2)}, u32[]{:S(2)}) collective-permute-start(bf16[16,4096]{1,0:T(8,128)(2,1)S(1)} %collective-permute-done.4.refs_3_), channel_id=1, source_target_pairs={{1,0},{0,1},{3,2},{2,3},{5,4},{4,5},{7,6},{6,7},{9,8},{8,9},{11,10... | collective-permute-start | bytes 393224 | tf_op jit(solution)/shard_map/ppermute | solution.py:25
  13.5 5.0 %collective-permute-start.7 = (bf16[16,4096]{1,0:T(8,128)(2,1)S(1)}, bf16[16,4096]{1,0:T(8,128)(2,1)S(1)}, u32[]{:S(2)}, u32[]{:S(2)}) collective-permute-start(bf16[16,4096]{1,0:T(8,128)(2,1)S(1)} %collective-permute-done.1.after.refs_6_), channel_id=1, source_target_pairs={{2,0},{5,1},{0,4},{9,5},{4,8},{13,9},{8,12},{15,13},{12,14},{11,15... | collective-permute-start | bytes 393224 | tf_op jit(solution)/shard_map/ppermute | solution.py:39
  15.1 6.4 %collective-permute-start.2 = (bf16[16,4096]{1,0:T(8,128)(2,1)S(1)}, bf16[16,4096]{1,0:T(8,128)(2,1)S(1)}, u32[]{:S(2)}, u32[]{:S(2)}) collective-permute-start(bf16[16,4096]{1,0:T(8,128)(2,1)S(1)} %collective-permute-done.1.after.refs_6_), channel_id=1, source_target_pairs={{1,0},{0,1},{3,2},{2,3},{5,4},{4,5},{7,6},{6,7},{9,8},{8,9},{11,10... | collective-permute-start | bytes 393224 | tf_op jit(solution)/shard_map/ppermute | solution.py:25
  15.1 5.0 %collective-permute-start.8 = (bf16[16,4096]{1,0:T(8,128)(2,1)S(1)}, bf16[16,4096]{1,0:T(8,128)(2,1)S(1)}, u32[]{:S(2)}, u32[]{:S(2)}) collective-permute-start(bf16[16,4096]{1,0:T(8,128)(2,1)S(1)} %collective-permute-done.5.refs_7_), channel_id=1, source_target_pairs={{2,0},{5,1},{0,4},{9,5},{4,8},{13,9},{8,12},{15,13},{12,14},{11,15... | collective-permute-start | bytes 393224 | tf_op jit(solution)/shard_map/ppermute | solution.py:39
  18.4 6.5 %collective-permute-start.6 = (bf16[16,4096]{1,0:T(8,128)(2,1)S(1)}, bf16[16,4096]{1,0:T(8,128)(2,1)S(1)}, u32[]{:S(2)}, u32[]{:S(2)}) collective-permute-start(bf16[16,4096]{1,0:T(8,128)(2,1)S(1)} %collective-permute-done.5.refs_7_), channel_id=1, source_target_pairs={{1,0},{0,1},{3,2},{2,3},{5,4},{4,5},{7,6},{6,7},{9,8},{8,9},{11,10... | collective-permute-start | bytes 393224 | tf_op jit(solution)/shard_map/ppermute | solution.py:25
  18.6 6.3 %collective-permute-start.11 = (bf16[16,4096]{1,0:T(8,128)(2,1)S(1)}, bf16[16,4096]{1,0:T(8,128)(2,1)S(1)}, u32[]{:S(2)}, u32[]{:S(2)}) collective-permute-start(bf16[16,4096]{1,0:T(8,128)(2,1)S(1)} %collective-permute-done.7.refs_2_), channel_id=1, source_target_pairs={{2,0},{5,1},{0,4},{9,5},{4,8},{13,9},{8,12},{15,13},{12,14},{11,15... | collective-permute-start | bytes 393224 | tf_op jit(solution)/shard_map/ppermute | solution.py:39
  20.0 4.9 %collective-permute-start.9 = (bf16[16,4096]{1,0:T(8,128)(2,1)S(1)}, bf16[16,4096]{1,0:T(8,128)(2,1)S(1)}, u32[]{:S(2)}, u32[]{:S(2)}) collective-permute-start(bf16[16,4096]{1,0:T(8,128)(2,1)S(1)} %collective-permute-done.7.refs_2_), channel_id=1, source_target_pairs={{1,0},{0,1},{3,2},{2,3},{5,4},{4,5},{7,6},{6,7},{9,8},{8,9},{11,10... | collective-permute-start | bytes 393224 | tf_op jit(solution)/shard_map/ppermute | solution.py:25
  20.1 5.0 %collective-permute-start.12 = (bf16[16,4096]{1,0:T(8,128)(2,1)S(1)}, bf16[16,4096]{1,0:T(8,128)(2,1)S(1)}, u32[]{:S(2)}, u32[]{:S(2)}) collective-permute-start(bf16[16,4096]{1,0:T(8,128)(2,1)S(1)} %collective-permute-done.8.refs_3_), channel_id=1, source_target_pairs={{2,0},{5,1},{0,4},{9,5},{4,8},{13,9},{8,12},{15,13},{12,14},{11,15... | collective-permute-start | bytes 393224 | tf_op jit(solution)/shard_map/ppermute | solution.py:39
  21.5 3.6 %collective-permute-start.10 = (bf16[16,4096]{1,0:T(8,128)(2,1)S(1)}, bf16[16,4096]{1,0:T(8,128)(2,1)S(1)}, u32[]{:S(2)}, u32[]{:S(2)}) collective-permute-start(bf16[16,4096]{1,0:T(8,128)(2,1)S(1)} %collective-permute-done.8.refs_3_), channel_id=1, source_target_pairs={{1,0},{0,1},{3,2},{2,3},{5,4},{4,5},{7,6},{6,7},{9,8},{8,9},{11,10... | collective-permute-start | bytes 393224 | tf_op jit(solution)/shard_map/ppermute | solution.py:25
  38.4 5.5 %collective-permute-start.17 = (f32[8,256]{1,0:T(8,128)S(1)}, f32[8,256]{1,0:T(8,128)S(1)}, u32[]{:S(2)}, u32[]{:S(2)}) collective-permute-start(f32[8,256]{1,0:T(8,128)S(1)} %get-tuple-element.22.own), channel_id=1, source_target_pairs={{12,0},{13,1},{14,2},{15,3},{8,4},{9,5},{10,6},{11,7},{4,8},{5,9},... | collective-permute-start | bytes 24584 | tf_op jit(solution)/shard_map/ppermute | solution.py:25
  41.2 4.5 %collective-permute-start.16 = (f32[8,256]{1,0:T(8,128)S(1)}, f32[8,256]{1,0:T(8,128)S(1)}, u32[]{:S(2)}, u32[]{:S(2)}) collective-permute-start(f32[8,256]{1,0:T(8,128)S(1)} %get-tuple-element.22.own), channel_id=1, source_target_pairs={{8,0},{9,1},{10,2},{11,3},{12,4},{13,5},{14,6},{15,7},{0,8},{1,9},... | collective-permute-start | bytes 24584 | tf_op jit(solution)/shard_map/ppermute | solution.py:25
  41.3 4.4 %collective-permute-start.15 = (f32[8,256]{1,0:T(8,128)S(1)}, f32[8,256]{1,0:T(8,128)S(1)}, u32[]{:S(2)}, u32[]{:S(2)}) collective-permute-start(f32[8,256]{1,0:T(8,128)S(1)} %get-tuple-element.22.own), channel_id=1, source_target_pairs={{4,0},{5,1},{6,2},{7,3},{0,4},{1,5},{2,6},{3,7},{12,8},{13,9},{14,... | collective-permute-start | bytes 24584 | tf_op jit(solution)/shard_map/ppermute | solution.py:25
  45.8 3.1 %collective-permute-start.20 = (f32[8,256]{1,0:T(8,128)S(1)}, f32[8,256]{1,0:T(8,128)S(1)}, u32[]{:S(2)}, u32[]{:S(2)}) collective-permute-start(f32[8,256]{1,0:T(8,128)S(1)} %add_add_fusion.s0), channel_id=1, source_target_pairs={{3,0},{2,1},{1,2},{0,3},{7,4},{6,5},{5,6},{4,7},{11,8},{10,9},{9,1... | collective-permute-start | bytes 24584 | tf_op jit(solution)/shard_map/ppermute | solution.py:25
  45.9 3.7 %collective-permute-start.19 = (f32[8,256]{1,0:T(8,128)S(1)}, f32[8,256]{1,0:T(8,128)S(1)}, u32[]{:S(2)}, u32[]{:S(2)}) collective-permute-start(f32[8,256]{1,0:T(8,128)S(1)} %add_add_fusion.s0), channel_id=1, source_target_pairs={{2,0},{3,1},{0,2},{1,3},{6,4},{7,5},{4,6},{5,7},{10,8},{11,9},{8,1... | collective-permute-start | bytes 24584 | tf_op jit(solution)/shard_map/ppermute | solution.py:25
  46.9 2.7 %collective-permute-start.18 = (f32[8,256]{1,0:T(8,128)S(1)}, f32[8,256]{1,0:T(8,128)S(1)}, u32[]{:S(2)}, u32[]{:S(2)}) collective-permute-start(f32[8,256]{1,0:T(8,128)S(1)} %add_add_fusion.s0), channel_id=1, source_target_pairs={{1,0},{0,1},{3,2},{2,3},{5,4},{4,5},{7,6},{6,7},{9,8},{8,9},{11,10... | collective-permute-start | bytes 24584 | tf_op jit(solution)/shard_map/ppermute | solution.py:25

commit v11 on v9

--- a/solution.py
+++ b/solution.py
@@ -14,6 +14,7 @@
 COST = 4 << 30
 SAMPLE = 256
 VMEM_BYTES = 12 << 20
+TN = (((0,), (0,)), ((), ()))
 RATIO = 0.1 / 0.05**0.5
 
 
@@ -237,8 +238,8 @@
 def replay_kernel(n, half, *refs):
     blocks, (far, weight, cot, weights, one, two) = refs[:half], refs[half : half + 6]
     (tokens, turned, gate, adjoint, along, across, bend, stats) = refs[half + 9 : half + 17]
-    (scaled, score, g0, g1, a0, a1, b0, b1, sums, upright, sems, tile_sems) = refs[half + 17 :]
-    grads, firsts, seconds = (g0, g1), (a0, a1), (b0, b1)
+    (scaled, score, g0, g1, t0, t1, probes, sums, upright, sems, tile_sems) = refs[half + 17 :]
+    grads, terms = (g0, g1), (t0, t1)
     depth = one.shape[0]
     count, width = scaled.shape
     tiles = depth // TILE
@@ -259,15 +260,16 @@
         bend[at, :] = token_weight * cot_f * curve
         score[at, :] = cot_f * slope
 
-    along[...] = jnp.zeros_like(along)
-    across[...] = jnp.zeros_like(across)
+    probes[...] = jnp.zeros_like(probes)
 
     def grad_rows(i, slot, r):
         at = pl.ds(pl.multiple_of(i * TILE + r, HALF), HALF)
         grads[slot][r : r + HALF, :] = f32dot(turned[at, :], scaled[...])
 
-    def probe(i, slot, target, terms):
-        target[...] += f32dot(tokens[:, span(i)], terms[slot][...])
+    def probe(i, slot):
+        probes[...] += lax.dot_general(
+            terms[slot][...], turned[span(i), :], TN, preferred_element_type=jnp.float32
+        )
 
     def pieces(i, slot, first, last):
         for r in range(first, last, ROWS):
@@ -278,8 +280,8 @@
 
     for i in range(2):
         tile_copy(i).wait()
-    grad_rows(0, 0, 0)
-    grad_rows(0, 0, HALF)
+    for r in range(0, TILE, HALF):
+        grad_rows(0, 0, r)
     sq, cross = {}, {}
     for r, cols, g, m1, m2, adj in pieces(0, 0, 0, SAMPLE):
         _, _, upd = update(g, m1, m2)
@@ -292,25 +294,26 @@
 
     sums[...] = jnp.zeros_like(sums)
 
-    def update_rows(i, slot, first):
+    def update_rows(i, slot, first, last):
         sq, cross = {}, {}
-        for r, cols, g, m1, m2, adj in pieces(i, slot, first, first + HALF):
+        for r, cols, g, m1, m2, adj in pieces(i, slot, first, last):
             over, inv, upd = update(g, m1, m2)
             sq[cols.start] = sq.get(cols.start, 0.0) + fold(upd * upd)
             cross[cols.start] = cross.get(cols.start, 0.0) + fold(adj * upd)
             pull = inv * (1.0 - g * (upd * over))
-            firsts[slot][r : r + ROWS, cols] = ((adj - guess * upd) * pull).astype(jnp.bfloat16)
-            seconds[slot][r : r + ROWS, cols] = (upd * pull).astype(jnp.bfloat16)
+            others = slice(width + cols.start, width + cols.stop)
+            terms[slot][r : r + ROWS, cols] = ((adj - guess * upd) * pull).astype(jnp.bfloat16)
+            terms[slot][r : r + ROWS, others] = (upd * pull).astype(jnp.bfloat16)
         sums[0] += sum(sq.values())
         sums[1] += sum(cross.values())
 
     def body(i, slot, ahead=True, behind=True):
-        for r, target, terms in ((0, along, firsts), (HALF, across, seconds)):
+        for r in range(0, TILE, HALF):
             if ahead:
                 grad_rows(i + 1, 1 - slot, r)
-            update_rows(i, slot, r)
-            if behind:
-                probe(i - 1, 1 - slot, target, terms)
+            update_rows(i, slot, r, r + HALF)
+            if behind and r == 0:
+                probe(i - 1, 1 - slot)
 
     body(0, 0, behind=False)
 
@@ -323,8 +326,9 @@
 
     lax.fori_loop(0, tiles // 2 - 1, pair, 0)
     body(tiles - 1, 1, ahead=False)
-    probe(tiles - 1, 1, along, firsts)
-    probe(tiles - 1, 1, across, seconds)
+    probe(tiles - 1, 1)
+    along[...] = probes[0:width, :].T
+    across[...] = probes[width:, :].T
 
     height = count // n
     places = owners(n)
@@ -352,7 +356,6 @@
     far = pl.BlockSpec(memory_space=pl.ANY)
     vmem = pl.BlockSpec(memory_space=pltpu.VMEM)
     like = lambda x: pltpu.VMEM(x.shape, x.dtype)
-    block = lambda dtype: pltpu.VMEM((TILE, width), dtype)
     return pl.pallas_call(
         functools.partial(replay_kernel, n, half),
         in_specs=[far] * (half + 1) + [vmem] * 8,
@@ -370,12 +373,11 @@
         scratch_shapes=[
             pltpu.VMEM((count, width), jnp.bfloat16),
             pltpu.VMEM((count, width), jnp.float32),
-            block(jnp.float32),
-            block(jnp.float32),
-            block(jnp.bfloat16),
-            block(jnp.bfloat16),
-            block(jnp.bfloat16),
-            block(jnp.bfloat16),
+            pltpu.VMEM((TILE, width), jnp.float32),
+            pltpu.VMEM((TILE, width), jnp.float32),
+            pltpu.VMEM((TILE, 2 * width), jnp.bfloat16),
+            pltpu.VMEM((TILE, 2 * width), jnp.bfloat16),
+            pltpu.VMEM((2 * width, count), jnp.float32),
             pltpu.VMEM((2, 8, min(COLUMNS, width)), jnp.float32),
             pltpu.VMEM((count, 128), jnp.float32),
             pltpu.SemaphoreType.DMA((half,)),
@@ -409,12 +411,12 @@
     bent = (bend[...] * (lead_here * along[...] + rest_here * across[...])).astype(jnp.bfloat16)
 
     def copy(i):
-        at = pl.ds(i * TILE, TILE)
+        at = pl.ds(i * SAMPLE, SAMPLE)
         return pltpu.make_async_copy(ready.at[at, :], theta.at[at, :], sent.at[i])
 
-    tiles = theta.shape[0] // TILE
+    tiles = theta.shape[0] // SAMPLE
     for i in range(tiles):
-        at = pl.ds(i * TILE, TILE)
+        at = pl.ds(i * SAMPLE, SAMPLE)
         ready[at, :] = 0.999 * adjoint[at, :] + f32dot(turned[at, :], bent)
         copy(i).start()
     for i in range(tiles):
@@ -433,7 +435,7 @@
             jax.ShapeDtypeStruct((depth, width), jnp.float32),
             jax.ShapeDtypeStruct((1, count // n), jnp.float32),
         ],
-        scratch_shapes=[pltpu.VMEM((depth, width), jnp.float32), pltpu.SemaphoreType.DMA((depth // TILE,))],
+        scratch_shapes=[pltpu.VMEM((depth, width), jnp.float32), pltpu.SemaphoreType.DMA((depth // SAMPLE,))],
         compiler_params=pltpu.CompilerParams(vmem_limit_bytes=VMEM_BYTES),
         name="theta",
     )(*sums, own, along, across, bend, turned, adjoint)

time: 53.9 us -> 54.3 us (level)
  no operation moved by 1% of the time
where the time goes in v11:
time: 54.3 us; the launch traced here: 54.1 us
  Pallas kernels  28.3 us (52%)
  starting transfers between devices  20 us (37%)
  waiting for transfers between devices  5.01 us (9%)
  between operations  0.78 us (1%)
    pallas_call x1, Pallas kernels, replay_call(): pl.pallas_call(functools.partial(replay_kernel, n, half), in_specs=[far]...  13.6 us
    ppermute x8, starting transfers between devices, onward(): return lax.ppermute(value, 'dp', pairs)  12.9 us
    ppermute x13, starting transfers between devices, swapped(): return lax.ppermute(value, 'dp', [(d ^ mask, d) for d in range(n)])  7.12 us
    ppermute x13, waiting for transfers between devices, swapped(): return lax.ppermute(value, 'dp', [(d ^ mask, d) for d in range(n)])  4.77 us
    pallas_call x2, Pallas kernels, fetch_wide(): pl.pallas_call(functools.partial(widen_kernel, factor), in_specs=[pl.Bloc...  4.57 us
    pallas_call x1, Pallas kernels, theta_call(): pl.pallas_call(functools.partial(theta_kernel, n, entries), in_specs=[vme...  4.27 us
    pallas_call x1, Pallas kernels, early_call(): pl.pallas_call(functools.partial(early_kernel, half), in_specs=[pl.BlockS...  3.35 us
    pallas_call x1, Pallas kernels, fetch(): pl.pallas_call(functools.partial(fetch_kernel, n), in_specs=[pl.BlockSpec...  2.52 us
  transfers between devices with their start and end apart: 21, of which 6 were waited for; matrix products, arithmetic and copies ran while one was open for 0% of the time, Pallas kernels for 19%

profile of v11, /device:TPU:0, one launch (start us, length us, event | category | flops | bytes accessed | tf_op | source)
XLA Modules:
  0.0 54.1 jit_solution(15849841545500932907)
XLA Ops:
  0.6 0.5 collective-permute-start.3
  1.1 2.6 %collective-permute-start = (bf16[16,4096]{1,0:T(8,128)(2,1)}, bf16[16,4096]{1,0:T(8,128)(2,1)S(1)}, u32[]{:S(2)}, u32[]{:S(2)}) collective-permute-start(bf16[16,4096]{1,0:T(8,128)(2,1)} %refs_0_.1), channel_id=1, source_target_pairs={{2,0},{5,1},{0,4},{9,5},{4,8},{13,9},{8,12},{15,13},{12,14},{11,15... | collective-permute-start | bytes 393224 | tf_op jit(solution)/shard_map/ppermute | solution.py:40
  3.8 0.0 collective-permute-done.3.refs_1_
  3.8 1.6 %collective-permute-start.4 = (bf16[16,4096]{1,0:T(8,128)(2,1)S(1)}, bf16[16,4096]{1,0:T(8,128)(2,1)S(1)}, u32[]{:S(2)}, u32[]{:S(2)}) collective-permute-start(bf16[16,4096]{1,0:T(8,128)(2,1)S(1)} %collective-permute-done.3.refs_1_), channel_id=1, source_target_pairs={{2,0},{5,1},{0,4},{9,5},{4,8},{13,9},{8,12},{15,13},{12,14},{11,15... | collective-permute-start | bytes 393224 | tf_op jit(solution)/shard_map/ppermute | solution.py:40
  5.4 2.5 %fetch.1 = (bf16[4096,512]{1,0:T(8,128)(2,1)S(1)}, bf16[256,512]{1,0:T(8,128)(2,1)S(1)}, f32[256,128]{1,0:T(8,128)S(1)}) custom-call(bf16[4096,512]{1,0:T(8,128)(2,1)} %far.3, bf16[256,512]{1,0:T(8,128)(2,1)} %far_cot.1, f32[1,256]{1,0:T(1,128)} %bitcast.2, bf16[16,4096]{1,0:T(8,128)(2,1)} %refs_0_.1), custom_call_target="tpu_custom_call" | custom-call | flops 4294967296 | bytes 8388608 | tf_op jit(solution)/shard_map/fetch/pallas_call | solution.py:165
  7.9 0.0 collective-permute-done.after.refs_2_
  7.9 0.1 collective-permute-start.13
  8.0 1.6 %collective-permute-start.1 = (bf16[16,4096]{1,0:T(8,128)(2,1)S(1)}, bf16[16,4096]{1,0:T(8,128)(2,1)S(1)}, u32[]{:S(2)}, u32[]{:S(2)}) collective-permute-start(bf16[16,4096]{1,0:T(8,128)(2,1)S(1)} %collective-permute-done.after.refs_2_), channel_id=1, source_target_pairs={{2,0},{5,1},{0,4},{9,5},{4,8},{13,9},{8,12},{15,13},{12,14},{11,15... | collective-permute-start | bytes 393224 | tf_op jit(solution)/shard_map/ppermute | solution.py:40
  9.6 0.0 collective-permute-done.4.refs_3_
  9.6 1.5 %collective-permute-start.5 = (bf16[16,4096]{1,0:T(8,128)(2,1)S(1)}, bf16[16,4096]{1,0:T(8,128)(2,1)S(1)}, u32[]{:S(2)}, u32[]{:S(2)}) collective-permute-start(bf16[16,4096]{1,0:T(8,128)(2,1)S(1)} %collective-permute-done.4.refs_3_), channel_id=1, source_target_pairs={{2,0},{5,1},{0,4},{9,5},{4,8},{13,9},{8,12},{15,13},{12,14},{11,15... | collective-permute-start | bytes 393224 | tf_op jit(solution)/shard_map/ppermute | solution.py:40
  11.1 2.3 %widen.2.refs_12_ = f32[4096,512]{1,0:T(8,128)S(1)} custom-call(bf16[4096,512]{1,0:T(8,128)(2,1)} %far.4, bf16[16,4096]{1,0:T(8,128)(2,1)S(1)} %collective-permute-done.after.refs_2_), custom_call_target="tpu_custom_call" | custom-call | flops 4294967296 | bytes 8388608 | tf_op jit(solution)/shard_map/widen/pallas_call | solution.py:127
  13.4 0.0 copy-start
  13.4 0.1 collective-permute-start.14
  13.5 0.0 collective-permute-done.1.after.refs_6_
  13.5 1.5 %collective-permute-start.7 = (bf16[16,4096]{1,0:T(8,128)(2,1)S(1)}, bf16[16,4096]{1,0:T(8,128)(2,1)S(1)}, u32[]{:S(2)}, u32[]{:S(2)}) collective-permute-start(bf16[16,4096]{1,0:T(8,128)(2,1)S(1)} %collective-permute-done.1.after.refs_6_), channel_id=1, source_target_pairs={{2,0},{5,1},{0,4},{9,5},{4,8},{13,9},{8,12},{15,13},{12,14},{11,15... | collective-permute-start | bytes 393224 | tf_op jit(solution)/shard_map/ppermute | solution.py:40
  15.1 0.0 collective-permute-start.2
  15.1 0.0 collective-permute-done.5.refs_7_
  15.1 1.0 %collective-permute-start.8 = (bf16[16,4096]{1,0:T(8,128)(2,1)S(1)}, bf16[16,4096]{1,0:T(8,128)(2,1)S(1)}, u32[]{:S(2)}, u32[]{:S(2)}) collective-permute-start(bf16[16,4096]{1,0:T(8,128)(2,1)S(1)} %collective-permute-done.5.refs_7_), channel_id=1, source_target_pairs={{2,0},{5,1},{0,4},{9,5},{4,8},{13,9},{8,12},{15,13},{12,14},{11,15... | collective-permute-start | bytes 393224 | tf_op jit(solution)/shard_map/ppermute | solution.py:40
  16.1 2.3 %widen.3.refs_13_ = f32[4096,512]{1,0:T(8,128)S(1)} custom-call(bf16[4096,512]{1,0:T(8,128)(2,1)} %far.5, bf16[16,4096]{1,0:T(8,128)(2,1)S(1)} %collective-permute-done.1.after.refs_6_), custom_call_target="tpu_custom_call" | custom-call | flops 4294967296 | bytes 8388608 | tf_op jit(solution)/shard_map/widen/pallas_call | solution.py:127
  18.4 0.0 collective-permute-done.13.refs_4_
  18.4 0.1 collective-permute-start.6
  18.5 0.1 collective-permute-done.7.refs_2_
  18.6 1.5 %collective-permute-start.11 = (bf16[16,4096]{1,0:T(8,128)(2,1)S(1)}, bf16[16,4096]{1,0:T(8,128)(2,1)S(1)}, u32[]{:S(2)}, u32[]{:S(2)}) collective-permute-start(bf16[16,4096]{1,0:T(8,128)(2,1)S(1)} %collective-permute-done.7.refs_2_), channel_id=1, source_target_pairs={{2,0},{5,1},{0,4},{9,5},{4,8},{13,9},{8,12},{15,13},{12,14},{11,15... | collective-permute-start | bytes 393224 | tf_op jit(solution)/shard_map/ppermute | solution.py:40
  20.0 0.0 collective-permute-done.14.refs_5_
  20.0 0.0 collective-permute-start.9
  20.1 0.0 collective-permute-done.8.refs_3_
  20.1 1.4 %collective-permute-start.12 = (bf16[16,4096]{1,0:T(8,128)(2,1)S(1)}, bf16[16,4096]{1,0:T(8,128)(2,1)S(1)}, u32[]{:S(2)}, u32[]{:S(2)}) collective-permute-start(bf16[16,4096]{1,0:T(8,128)(2,1)S(1)} %collective-permute-done.8.refs_3_), channel_id=1, source_target_pairs={{2,0},{5,1},{0,4},{9,5},{4,8},{13,9},{8,12},{15,13},{12,14},{11,15... | collective-permute-start | bytes 393224 | tf_op jit(solution)/shard_map/ppermute | solution.py:40
  21.5 0.0 collective-permute-done.2.refs_0_
  21.5 0.0 collective-permute-start.10
  21.5 3.4 %early.1 = (bf16[256,4096]{1,0:T(8,128)(2,1)S(1)}, bf16[4096,256]{1,0:T(8,128)(2,1)S(1)}, f32[256,512]{1,0:T(8,128)S(1)}) custom-call(bf16[16,4096]{1,0:T(8,128)(2,1)S(1)} %copy-done, bf16[16,4096]{1,0:T(8,128)(2,1)S(1)} %collective-permute-done.3.refs_1_, bf16[16,4096]{1,0:T(8,128)(2,1)S(1)} %collective-permute-done.after.refs_2_, ...), custom_call_target="tpu_custom_call" | custom-call | flops 4294967296 | bytes 12582912 | tf_op jit(solution)/shard_map/early/pallas_call | solution.py:222
  24.9 0.0 collective-permute-done.6.refs_1_
  24.9 0.0 collective-permute-done.11.refs_6_
  24.9 0.0 collective-permute-done.9.refs_4_
  24.9 0.2 collective-permute-done.12.refs_7_
  25.1 0.0 collective-permute-done.10.refs_5_
  25.1 13.6 %replay.1 = (bf16[256,4096]{1,0:T(8,128)(2,1)S(1)}, bf16[4096,256]{1,0:T(8,128)(2,1)S(1)}, f32[256,512]{1,0:T(8,128)S(1)}, f32[4096,512]{1,0:T(8,128)S(1)}, f32[...) custom-call(bf16[16,4096]{1,0:T(8,128)(2,1)S(1)} %collective-permute, ...), custom_call_target="tpu_custom_call", output_to_operand_aliasing={{0}: (14, {}), {1}: (15, {}), {2}: (16, {})} | custom-call | tf_op jit(solution)/shard_map/replay/pallas_call | solution.py:359
  38.6 2.8 %collective-permute-start.17 = (f32[8,256]{1,0:T(8,128)S(1)}, f32[8,256]{1,0:T(8,128)S(1)}, u32[]{:S(2)}, u32[]{:S(2)}) collective-permute-start(f32[8,256]{1,0:T(8,128)S(1)} %get-tuple-element.22.own), channel_id=1, source_target_pairs={{12,0},{13,1},{14,2},{15,3},{8,4},{9,5},{10,6},{11,7},{4,8},{5,9},... | collective-permute-start | bytes 24584 | tf_op jit(solution)/shard_map/ppermute | solution.py:26
  41.4 0.1 collective-permute-start.16
  41.6 1.5 %collective-permute-start.15 = (f32[8,256]{1,0:T(8,128)S(1)}, f32[8,256]{1,0:T(8,128)S(1)}, u32[]{:S(2)}, u32[]{:S(2)}) collective-permute-start(f32[8,256]{1,0:T(8,128)S(1)} %get-tuple-element.22.own), channel_id=1, source_target_pairs={{4,0},{5,1},{6,2},{7,3},{0,4},{1,5},{2,6},{3,7},{12,8},{13,9},{14,... | collective-permute-start | bytes 24584 | tf_op jit(solution)/shard_map/ppermute | solution.py:26
  43.1 1.1 %collective-permute-done.17 = f32[8,256]{1,0:T(8,128)S(1)} collective-permute-done((f32[8,256]{1,0:T(8,128)S(1)}, f32[8,256]{1,0:T(8,128)S(1)}, u32[]{:S(2)}, u32[]{:S(2)}) %collective-permute-start.17) | collective-permute-done | bytes 8224 | tf_op jit(solution)/shard_map/ppermute | solution.py:26
  44.2 1.8 %collective-permute-done.16 = f32[8,256]{1,0:T(8,128)S(1)} collective-permute-done((f32[8,256]{1,0:T(8,128)S(1)}, f32[8,256]{1,0:T(8,128)S(1)}, u32[]{:S(2)}, u32[]{:S(2)}) %collective-permute-start.16) | collective-permute-done | bytes 8224 | tf_op jit(solution)/shard_map/ppermute | solution.py:26
  46.0 0.1 collective-permute-start.20
  46.1 1.1 %collective-permute-start.19 = (f32[8,256]{1,0:T(8,128)S(1)}, f32[8,256]{1,0:T(8,128)S(1)}, u32[]{:S(2)}, u32[]{:S(2)}) collective-permute-start(f32[8,256]{1,0:T(8,128)S(1)} %add_add_fusion.s0), channel_id=1, source_target_pairs={{2,0},{3,1},{0,2},{1,3},{6,4},{7,5},{4,6},{5,7},{10,8},{11,9},{8,1... | collective-permute-start | bytes 24584 | tf_op jit(solution)/shard_map/ppermute | solution.py:26
  47.2 0.8 %collective-permute-start.18 = (f32[8,256]{1,0:T(8,128)S(1)}, f32[8,256]{1,0:T(8,128)S(1)}, u32[]{:S(2)}, u32[]{:S(2)}) collective-permute-start(f32[8,256]{1,0:T(8,128)S(1)} %add_add_fusion.s0), channel_id=1, source_target_pairs={{1,0},{0,1},{3,2},{2,3},{5,4},{4,5},{7,6},{6,7},{9,8},{8,9},{11,10... | collective-permute-start | bytes 24584 | tf_op jit(solution)/shard_map/ppermute | solution.py:26
  47.9 1.2 %collective-permute-done.20.s3 = f32[8,256]{1,0:T(8,128)S(1)} collective-permute-done((f32[8,256]{1,0:T(8,128)S(1)}, f32[8,256]{1,0:T(8,128)S(1)}, u32[]{:S(2)}, u32[]{:S(2)}) %collective-permute-start.20) | collective-permute-done | bytes 8224 | tf_op jit(solution)/shard_map/ppermute | solution.py:26
  49.1 0.7 %collective-permute-done.19.s2 = f32[8,256]{1,0:T(8,128)S(1)} collective-permute-done((f32[8,256]{1,0:T(8,128)S(1)}, f32[8,256]{1,0:T(8,128)S(1)}, u32[]{:S(2)}, u32[]{:S(2)}) %collective-permute-start.19) | collective-permute-done | bytes 8224 | tf_op jit(solution)/shard_map/ppermute | solution.py:26
  49.8 0.0 collective-permute-done.18.s1
  49.8 4.3 %theta.1 = (f32[4096,512]{1,0:T(8,128)}, f32[1,16]{1,0:T(1,128)}) custom-call(f32[8,256]{1,0:T(8,128)S(1)} %add_add_fusion.s0, f32[8,256]{1,0:T(8,128)S(1)} %collective-permute-done.18.s1, f32[8,256]{1,0:T(8,128)S(1)} %collective-permute-done.19.s2, f32[8,256]{1,0:T(8,128)S(1)} %collective-permute-done.20.s3, f32[8,256]{1,0:T(8,128)S(1)} %get-tuple-element.22.own, ...), custom_call_target="tpu_custom_call" | custom-call | tf_op jit(solution)/shard_map/theta/pallas_call | solution.py:430
  (3 shorter events, 0.0 us)
Async XLA Ops:
  0.6 3.2 %collective-permute-start.3 = (bf16[16,4096]{1,0:T(8,128)(2,1)}, bf16[16,4096]{1,0:T(8,128)(2,1)S(1)}, u32[]{:S(2)}, u32[]{:S(2)}) collective-permute-start(bf16[16,4096]{1,0:T(8,128)(2,1)} %refs_0_.1), channel_id=1, source_target_pairs={{1,0},{0,1},{3,2},{2,3},{5,4},{4,5},{7,6},{6,7},{9,8},{8,9},{11,10... | collective-permute-start | bytes 393224 | tf_op jit(solution)/shard_map/ppermute | solution.py:26
  1.1 6.8 %collective-permute-start = (bf16[16,4096]{1,0:T(8,128)(2,1)}, bf16[16,4096]{1,0:T(8,128)(2,1)S(1)}, u32[]{:S(2)}, u32[]{:S(2)}) collective-permute-start(bf16[16,4096]{1,0:T(8,128)(2,1)} %refs_0_.1), channel_id=1, source_target_pairs={{2,0},{5,1},{0,4},{9,5},{4,8},{13,9},{8,12},{15,13},{12,14},{11,15... | collective-permute-start | bytes 393224 | tf_op jit(solution)/shard_map/ppermute | solution.py:40
  3.8 5.8 %collective-permute-start.4 = (bf16[16,4096]{1,0:T(8,128)(2,1)S(1)}, bf16[16,4096]{1,0:T(8,128)(2,1)S(1)}, u32[]{:S(2)}, u32[]{:S(2)}) collective-permute-start(bf16[16,4096]{1,0:T(8,128)(2,1)S(1)} %collective-permute-done.3.refs_1_), channel_id=1, source_target_pairs={{2,0},{5,1},{0,4},{9,5},{4,8},{13,9},{8,12},{15,13},{12,14},{11,15... | collective-permute-start | bytes 393224 | tf_op jit(solution)/shard_map/ppermute | solution.py:40
  7.9 10.5 %collective-permute-start.13 = (bf16[16,4096]{1,0:T(8,128)(2,1)S(1)}, bf16[16,4096]{1,0:T(8,128)(2,1)S(1)}, u32[]{:S(2)}, u32[]{:S(2)}) collective-permute-start(bf16[16,4096]{1,0:T(8,128)(2,1)S(1)} %collective-permute-done.after.refs_2_), channel_id=1, source_target_pairs={{1,0},{0,1},{3,2},{2,3},{5,4},{4,5},{7,6},{6,7},{9,8},{8,9},{11,10... | collective-permute-start | bytes 393224 | tf_op jit(solution)/shard_map/ppermute | solution.py:26
  8.0 5.5 %collective-permute-start.1 = (bf16[16,4096]{1,0:T(8,128)(2,1)S(1)}, bf16[16,4096]{1,0:T(8,128)(2,1)S(1)}, u32[]{:S(2)}, u32[]{:S(2)}) collective-permute-start(bf16[16,4096]{1,0:T(8,128)(2,1)S(1)} %collective-permute-done.after.refs_2_), channel_id=1, source_target_pairs={{2,0},{5,1},{0,4},{9,5},{4,8},{13,9},{8,12},{15,13},{12,14},{11,15... | collective-permute-start | bytes 393224 | tf_op jit(solution)/shard_map/ppermute | solution.py:40
  9.6 5.5 %collective-permute-start.5 = (bf16[16,4096]{1,0:T(8,128)(2,1)S(1)}, bf16[16,4096]{1,0:T(8,128)(2,1)S(1)}, u32[]{:S(2)}, u32[]{:S(2)}) collective-permute-start(bf16[16,4096]{1,0:T(8,128)(2,1)S(1)} %collective-permute-done.4.refs_3_), channel_id=1, source_target_pairs={{2,0},{5,1},{0,4},{9,5},{4,8},{13,9},{8,12},{15,13},{12,14},{11,15... | collective-permute-start | bytes 393224 | tf_op jit(solution)/shard_map/ppermute | solution.py:40
  13.4 8.1 %copy-start = (bf16[16,4096]{1,0:T(8,128)(2,1)S(1)}, bf16[16,4096]{1,0:T(8,128)(2,1)}, u32[]{:S(2)}) copy-start(bf16[16,4096]{1,0:T(8,128)(2,1)} %refs_0_.1) | copy-start | bytes 393220
  13.4 6.6 %collective-permute-start.14 = (bf16[16,4096]{1,0:T(8,128)(2,1)S(1)}, bf16[16,4096]{1,0:T(8,128)(2,1)S(1)}, u32[]{:S(2)}, u32[]{:S(2)}) collective-permute-start(bf16[16,4096]{1,0:T(8,128)(2,1)S(1)} %collective-permute-done.4.refs_3_), channel_id=1, source_target_pairs={{1,0},{0,1},{3,2},{2,3},{5,4},{4,5},{7,6},{6,7},{9,8},{8,9},{11,10... | collective-permute-start | bytes 393224 | tf_op jit(solution)/shard_map/ppermute | solution.py:26
  13.5 5.0 %collective-permute-start.7 = (bf16[16,4096]{1,0:T(8,128)(2,1)S(1)}, bf16[16,4096]{1,0:T(8,128)(2,1)S(1)}, u32[]{:S(2)}, u32[]{:S(2)}) collective-permute-start(bf16[16,4096]{1,0:T(8,128)(2,1)S(1)} %collective-permute-done.1.after.refs_6_), channel_id=1, source_target_pairs={{2,0},{5,1},{0,4},{9,5},{4,8},{13,9},{8,12},{15,13},{12,14},{11,15... | collective-permute-start | bytes 393224 | tf_op jit(solution)/shard_map/ppermute | solution.py:40
  15.1 6.4 %collective-permute-start.2 = (bf16[16,4096]{1,0:T(8,128)(2,1)S(1)}, bf16[16,4096]{1,0:T(8,128)(2,1)S(1)}, u32[]{:S(2)}, u32[]{:S(2)}) collective-permute-start(bf16[16,4096]{1,0:T(8,128)(2,1)S(1)} %collective-permute-done.1.after.refs_6_), channel_id=1, source_target_pairs={{1,0},{0,1},{3,2},{2,3},{5,4},{4,5},{7,6},{6,7},{9,8},{8,9},{11,10... | collective-permute-start | bytes 393224 | tf_op jit(solution)/shard_map/ppermute | solution.py:26
  15.1 5.0 %collective-permute-start.8 = (bf16[16,4096]{1,0:T(8,128)(2,1)S(1)}, bf16[16,4096]{1,0:T(8,128)(2,1)S(1)}, u32[]{:S(2)}, u32[]{:S(2)}) collective-permute-start(bf16[16,4096]{1,0:T(8,128)(2,1)S(1)} %collective-permute-done.5.refs_7_), channel_id=1, source_target_pairs={{2,0},{5,1},{0,4},{9,5},{4,8},{13,9},{8,12},{15,13},{12,14},{11,15... | collective-permute-start | bytes 393224 | tf_op jit(solution)/shard_map/ppermute | solution.py:40
  18.4 6.5 %collective-permute-start.6 = (bf16[16,4096]{1,0:T(8,128)(2,1)S(1)}, bf16[16,4096]{1,0:T(8,128)(2,1)S(1)}, u32[]{:S(2)}, u32[]{:S(2)}) collective-permute-start(bf16[16,4096]{1,0:T(8,128)(2,1)S(1)} %collective-permute-done.5.refs_7_), channel_id=1, source_target_pairs={{1,0},{0,1},{3,2},{2,3},{5,4},{4,5},{7,6},{6,7},{9,8},{8,9},{11,10... | collective-permute-start | bytes 393224 | tf_op jit(solution)/shard_map/ppermute | solution.py:26
  18.6 6.3 %collective-permute-start.11 = (bf16[16,4096]{1,0:T(8,128)(2,1)S(1)}, bf16[16,4096]{1,0:T(8,128)(2,1)S(1)}, u32[]{:S(2)}, u32[]{:S(2)}) collective-permute-start(bf16[16,4096]{1,0:T(8,128)(2,1)S(1)} %collective-permute-done.7.refs_2_), channel_id=1, source_target_pairs={{2,0},{5,1},{0,4},{9,5},{4,8},{13,9},{8,12},{15,13},{12,14},{11,15... | collective-permute-start | bytes 393224 | tf_op jit(solution)/shard_map/ppermute | solution.py:40
  20.0 4.9 %collective-permute-start.9 = (bf16[16,4096]{1,0:T(8,128)(2,1)S(1)}, bf16[16,4096]{1,0:T(8,128)(2,1)S(1)}, u32[]{:S(2)}, u32[]{:S(2)}) collective-permute-start(bf16[16,4096]{1,0:T(8,128)(2,1)S(1)} %collective-permute-done.7.refs_2_), channel_id=1, source_target_pairs={{1,0},{0,1},{3,2},{2,3},{5,4},{4,5},{7,6},{6,7},{9,8},{8,9},{11,10... | collective-permute-start | bytes 393224 | tf_op jit(solution)/shard_map/ppermute | solution.py:26
  20.1 5.0 %collective-permute-start.12 = (bf16[16,4096]{1,0:T(8,128)(2,1)S(1)}, bf16[16,4096]{1,0:T(8,128)(2,1)S(1)}, u32[]{:S(2)}, u32[]{:S(2)}) collective-permute-start(bf16[16,4096]{1,0:T(8,128)(2,1)S(1)} %collective-permute-done.8.refs_3_), channel_id=1, source_target_pairs={{2,0},{5,1},{0,4},{9,5},{4,8},{13,9},{8,12},{15,13},{12,14},{11,15... | collective-permute-start | bytes 393224 | tf_op jit(solution)/shard_map/ppermute | solution.py:40
  21.5 3.6 %collective-permute-start.10 = (bf16[16,4096]{1,0:T(8,128)(2,1)S(1)}, bf16[16,4096]{1,0:T(8,128)(2,1)S(1)}, u32[]{:S(2)}, u32[]{:S(2)}) collective-permute-start(bf16[16,4096]{1,0:T(8,128)(2,1)S(1)} %collective-permute-done.8.refs_3_), channel_id=1, source_target_pairs={{1,0},{0,1},{3,2},{2,3},{5,4},{4,5},{7,6},{6,7},{9,8},{8,9},{11,10... | collective-permute-start | bytes 393224 | tf_op jit(solution)/shard_map/ppermute | solution.py:26
  38.6 5.5 %collective-permute-start.17 = (f32[8,256]{1,0:T(8,128)S(1)}, f32[8,256]{1,0:T(8,128)S(1)}, u32[]{:S(2)}, u32[]{:S(2)}) collective-permute-start(f32[8,256]{1,0:T(8,128)S(1)} %get-tuple-element.22.own), channel_id=1, source_target_pairs={{12,0},{13,1},{14,2},{15,3},{8,4},{9,5},{10,6},{11,7},{4,8},{5,9},... | collective-permute-start | bytes 24584 | tf_op jit(solution)/shard_map/ppermute | solution.py:26
  41.4 4.5 %collective-permute-start.16 = (f32[8,256]{1,0:T(8,128)S(1)}, f32[8,256]{1,0:T(8,128)S(1)}, u32[]{:S(2)}, u32[]{:S(2)}) collective-permute-start(f32[8,256]{1,0:T(8,128)S(1)} %get-tuple-element.22.own), channel_id=1, source_target_pairs={{8,0},{9,1},{10,2},{11,3},{12,4},{13,5},{14,6},{15,7},{0,8},{1,9},... | collective-permute-start | bytes 24584 | tf_op jit(solution)/shard_map/ppermute | solution.py:26
  41.6 4.4 %collective-permute-start.15 = (f32[8,256]{1,0:T(8,128)S(1)}, f32[8,256]{1,0:T(8,128)S(1)}, u32[]{:S(2)}, u32[]{:S(2)}) collective-permute-start(f32[8,256]{1,0:T(8,128)S(1)} %get-tuple-element.22.own), channel_id=1, source_target_pairs={{4,0},{5,1},{6,2},{7,3},{0,4},{1,5},{2,6},{3,7},{12,8},{13,9},{14,... | collective-permute-start | bytes 24584 | tf_op jit(solution)/shard_map/ppermute | solution.py:26
  46.0 3.1 %collective-permute-start.20 = (f32[8,256]{1,0:T(8,128)S(1)}, f32[8,256]{1,0:T(8,128)S(1)}, u32[]{:S(2)}, u32[]{:S(2)}) collective-permute-start(f32[8,256]{1,0:T(8,128)S(1)} %add_add_fusion.s0), channel_id=1, source_target_pairs={{3,0},{2,1},{1,2},{0,3},{7,4},{6,5},{5,6},{4,7},{11,8},{10,9},{9,1... | collective-permute-start | bytes 24584 | tf_op jit(solution)/shard_map/ppermute | solution.py:26
  46.1 3.7 %collective-permute-start.19 = (f32[8,256]{1,0:T(8,128)S(1)}, f32[8,256]{1,0:T(8,128)S(1)}, u32[]{:S(2)}, u32[]{:S(2)}) collective-permute-start(f32[8,256]{1,0:T(8,128)S(1)} %add_add_fusion.s0), channel_id=1, source_target_pairs={{2,0},{3,1},{0,2},{1,3},{6,4},{7,5},{4,6},{5,7},{10,8},{11,9},{8,1... | collective-permute-start | bytes 24584 | tf_op jit(solution)/shard_map/ppermute | solution.py:26
  47.2 2.6 %collective-permute-start.18 = (f32[8,256]{1,0:T(8,128)S(1)}, f32[8,256]{1,0:T(8,128)S(1)}, u32[]{:S(2)}, u32[]{:S(2)}) collective-permute-start(f32[8,256]{1,0:T(8,128)S(1)} %add_add_fusion.s0), channel_id=1, source_target_pairs={{1,0},{0,1},{3,2},{2,3},{5,4},{4,5},{7,6},{6,7},{9,8},{8,9},{11,10... | collective-permute-start | bytes 24584 | tf_op jit(solution)/shard_map/ppermute | solution.py:26

commit v12 on v9

--- a/solution.py
+++ b/solution.py
@@ -94,7 +94,8 @@
     first = one + grad
     second = two + grad * grad
     over = lax.rsqrt(second)
-    inv = pltpu.reciprocal(second * over + 1e-08 / 0.05**0.5, approx=True)
+    den = second * over + 1e-08 / 0.05**0.5
+    inv = over * (2.0 - den * over)
     return over, inv, first * inv
 
 

time: 53.9 us -> 54.5 us (1.011)
  Pallas kernels: 27.8 us -> 28.4 us
    pallas_call x1, Pallas kernels: 13.1 us -> 13.7 us  [replay_call(): pl.pallas_call(functools.partial(replay_kernel, n, half), in_specs=[far]...]
where the time goes in v12:
time: 54.5 us; the launch traced here: 54.2 us
  Pallas kernels  28.4 us (52%)
  starting transfers between devices  20 us (37%)
  waiting for transfers between devices  5.01 us (9%)
  between operations  0.78 us (1%)
    pallas_call x1, Pallas kernels, replay_call(): pl.pallas_call(functools.partial(replay_kernel, n, half), in_specs=[far]...  13.7 us
    ppermute x8, starting transfers between devices, onward(): return lax.ppermute(value, 'dp', pairs)  12.9 us
    ppermute x13, starting transfers between devices, swapped(): return lax.ppermute(value, 'dp', [(d ^ mask, d) for d in range(n)])  7.12 us
    ppermute x13, waiting for transfers between devices, swapped(): return lax.ppermute(value, 'dp', [(d ^ mask, d) for d in range(n)])  4.77 us
    pallas_call x2, Pallas kernels, fetch_wide(): pl.pallas_call(functools.partial(widen_kernel, factor), in_specs=[pl.Bloc...  4.57 us
    pallas_call x1, Pallas kernels, theta_call(): pl.pallas_call(functools.partial(theta_kernel, n, entries), in_specs=[vme...  4.29 us
    pallas_call x1, Pallas kernels, early_call(): pl.pallas_call(functools.partial(early_kernel, half), in_specs=[pl.BlockS...  3.35 us
    pallas_call x1, Pallas kernels, fetch(): pl.pallas_call(functools.partial(fetch_kernel, n), in_specs=[pl.BlockSpec...  2.52 us
  transfers between devices with their start and end apart: 21, of which 6 were waited for; matrix products, arithmetic and copies ran while one was open for 0% of the time, Pallas kernels for 19%

profile of v12, /device:TPU:0, one launch (start us, length us, event | category | flops | bytes accessed | tf_op | source)
XLA Modules:
  0.0 54.2 jit_solution(6984791009775365305)
XLA Ops:
  0.6 0.5 collective-permute-start.3
  1.1 2.6 %collective-permute-start = (bf16[16,4096]{1,0:T(8,128)(2,1)}, bf16[16,4096]{1,0:T(8,128)(2,1)S(1)}, u32[]{:S(2)}, u32[]{:S(2)}) collective-permute-start(bf16[16,4096]{1,0:T(8,128)(2,1)} %refs_0_.1), channel_id=1, source_target_pairs={{2,0},{5,1},{0,4},{9,5},{4,8},{13,9},{8,12},{15,13},{12,14},{11,15... | collective-permute-start | bytes 393224 | tf_op jit(solution)/shard_map/ppermute | solution.py:39
  3.8 0.0 collective-permute-done.3.refs_1_
  3.8 1.6 %collective-permute-start.4 = (bf16[16,4096]{1,0:T(8,128)(2,1)S(1)}, bf16[16,4096]{1,0:T(8,128)(2,1)S(1)}, u32[]{:S(2)}, u32[]{:S(2)}) collective-permute-start(bf16[16,4096]{1,0:T(8,128)(2,1)S(1)} %collective-permute-done.3.refs_1_), channel_id=1, source_target_pairs={{2,0},{5,1},{0,4},{9,5},{4,8},{13,9},{8,12},{15,13},{12,14},{11,15... | collective-permute-start | bytes 393224 | tf_op jit(solution)/shard_map/ppermute | solution.py:39
  5.4 2.5 %fetch.1 = (bf16[4096,512]{1,0:T(8,128)(2,1)S(1)}, bf16[256,512]{1,0:T(8,128)(2,1)S(1)}, f32[256,128]{1,0:T(8,128)S(1)}) custom-call(bf16[4096,512]{1,0:T(8,128)(2,1)} %far.3, bf16[256,512]{1,0:T(8,128)(2,1)} %far_cot.1, f32[1,256]{1,0:T(1,128)} %bitcast.2, bf16[16,4096]{1,0:T(8,128)(2,1)} %refs_0_.1), custom_call_target="tpu_custom_call" | custom-call | flops 4294967296 | bytes 8388608 | tf_op jit(solution)/shard_map/fetch/pallas_call | solution.py:165
  7.9 0.0 collective-permute-done.after.refs_2_
  7.9 0.1 collective-permute-start.13
  8.0 1.6 %collective-permute-start.1 = (bf16[16,4096]{1,0:T(8,128)(2,1)S(1)}, bf16[16,4096]{1,0:T(8,128)(2,1)S(1)}, u32[]{:S(2)}, u32[]{:S(2)}) collective-permute-start(bf16[16,4096]{1,0:T(8,128)(2,1)S(1)} %collective-permute-done.after.refs_2_), channel_id=1, source_target_pairs={{2,0},{5,1},{0,4},{9,5},{4,8},{13,9},{8,12},{15,13},{12,14},{11,15... | collective-permute-start | bytes 393224 | tf_op jit(solution)/shard_map/ppermute | solution.py:39
  9.6 0.0 collective-permute-done.4.refs_3_
  9.6 1.5 %collective-permute-start.5 = (bf16[16,4096]{1,0:T(8,128)(2,1)S(1)}, bf16[16,4096]{1,0:T(8,128)(2,1)S(1)}, u32[]{:S(2)}, u32[]{:S(2)}) collective-permute-start(bf16[16,4096]{1,0:T(8,128)(2,1)S(1)} %collective-permute-done.4.refs_3_), channel_id=1, source_target_pairs={{2,0},{5,1},{0,4},{9,5},{4,8},{13,9},{8,12},{15,13},{12,14},{11,15... | collective-permute-start | bytes 393224 | tf_op jit(solution)/shard_map/ppermute | solution.py:39
  11.1 2.3 %widen.2.refs_12_ = f32[4096,512]{1,0:T(8,128)S(1)} custom-call(bf16[4096,512]{1,0:T(8,128)(2,1)} %far.4, bf16[16,4096]{1,0:T(8,128)(2,1)S(1)} %collective-permute-done.after.refs_2_), custom_call_target="tpu_custom_call" | custom-call | flops 4294967296 | bytes 8388608 | tf_op jit(solution)/shard_map/widen/pallas_call | solution.py:127
  13.4 0.0 copy-start
  13.4 0.1 collective-permute-start.14
  13.5 0.0 collective-permute-done.1.after.refs_6_
  13.5 1.5 %collective-permute-start.7 = (bf16[16,4096]{1,0:T(8,128)(2,1)S(1)}, bf16[16,4096]{1,0:T(8,128)(2,1)S(1)}, u32[]{:S(2)}, u32[]{:S(2)}) collective-permute-start(bf16[16,4096]{1,0:T(8,128)(2,1)S(1)} %collective-permute-done.1.after.refs_6_), channel_id=1, source_target_pairs={{2,0},{5,1},{0,4},{9,5},{4,8},{13,9},{8,12},{15,13},{12,14},{11,15... | collective-permute-start | bytes 393224 | tf_op jit(solution)/shard_map/ppermute | solution.py:39
  15.1 0.0 collective-permute-start.2
  15.1 0.0 collective-permute-done.5.refs_7_
  15.1 1.0 %collective-permute-start.8 = (bf16[16,4096]{1,0:T(8,128)(2,1)S(1)}, bf16[16,4096]{1,0:T(8,128)(2,1)S(1)}, u32[]{:S(2)}, u32[]{:S(2)}) collective-permute-start(bf16[16,4096]{1,0:T(8,128)(2,1)S(1)} %collective-permute-done.5.refs_7_), channel_id=1, source_target_pairs={{2,0},{5,1},{0,4},{9,5},{4,8},{13,9},{8,12},{15,13},{12,14},{11,15... | collective-permute-start | bytes 393224 | tf_op jit(solution)/shard_map/ppermute | solution.py:39
  16.1 2.3 %widen.3.refs_13_ = f32[4096,512]{1,0:T(8,128)S(1)} custom-call(bf16[4096,512]{1,0:T(8,128)(2,1)} %far.5, bf16[16,4096]{1,0:T(8,128)(2,1)S(1)} %collective-permute-done.1.after.refs_6_), custom_call_target="tpu_custom_call" | custom-call | flops 4294967296 | bytes 8388608 | tf_op jit(solution)/shard_map/widen/pallas_call | solution.py:127
  18.4 0.0 collective-permute-done.13.refs_4_
  18.4 0.1 collective-permute-start.6
  18.5 0.1 collective-permute-done.7.refs_2_
  18.6 1.5 %collective-permute-start.11 = (bf16[16,4096]{1,0:T(8,128)(2,1)S(1)}, bf16[16,4096]{1,0:T(8,128)(2,1)S(1)}, u32[]{:S(2)}, u32[]{:S(2)}) collective-permute-start(bf16[16,4096]{1,0:T(8,128)(2,1)S(1)} %collective-permute-done.7.refs_2_), channel_id=1, source_target_pairs={{2,0},{5,1},{0,4},{9,5},{4,8},{13,9},{8,12},{15,13},{12,14},{11,15... | collective-permute-start | bytes 393224 | tf_op jit(solution)/shard_map/ppermute | solution.py:39
  20.0 0.0 collective-permute-done.14.refs_5_
  20.0 0.0 collective-permute-start.9
  20.1 0.0 collective-permute-done.8.refs_3_
  20.1 1.4 %collective-permute-start.12 = (bf16[16,4096]{1,0:T(8,128)(2,1)S(1)}, bf16[16,4096]{1,0:T(8,128)(2,1)S(1)}, u32[]{:S(2)}, u32[]{:S(2)}) collective-permute-start(bf16[16,4096]{1,0:T(8,128)(2,1)S(1)} %collective-permute-done.8.refs_3_), channel_id=1, source_target_pairs={{2,0},{5,1},{0,4},{9,5},{4,8},{13,9},{8,12},{15,13},{12,14},{11,15... | collective-permute-start | bytes 393224 | tf_op jit(solution)/shard_map/ppermute | solution.py:39
  21.5 0.0 collective-permute-done.2.refs_0_
  21.5 0.0 collective-permute-start.10
  21.5 3.4 %early.1 = (bf16[256,4096]{1,0:T(8,128)(2,1)S(1)}, bf16[4096,256]{1,0:T(8,128)(2,1)S(1)}, f32[256,512]{1,0:T(8,128)S(1)}) custom-call(bf16[16,4096]{1,0:T(8,128)(2,1)S(1)} %copy-done, bf16[16,4096]{1,0:T(8,128)(2,1)S(1)} %collective-permute-done.3.refs_1_, bf16[16,4096]{1,0:T(8,128)(2,1)S(1)} %collective-permute-done.after.refs_2_, ...), custom_call_target="tpu_custom_call" | custom-call | flops 4294967296 | bytes 12582912 | tf_op jit(solution)/shard_map/early/pallas_call | solution.py:222
  24.9 0.0 collective-permute-done.6.refs_1_
  24.9 0.0 collective-permute-done.11.refs_6_
  24.9 0.0 collective-permute-done.9.refs_4_
  24.9 0.2 collective-permute-done.12.refs_7_
  25.1 13.7 %replay.1 = (bf16[256,4096]{1,0:T(8,128)(2,1)S(1)}, bf16[4096,256]{1,0:T(8,128)(2,1)S(1)}, f32[256,512]{1,0:T(8,128)S(1)}, f32[4096,512]{1,0:T(8,128)S(1)}, f32[...) custom-call(bf16[16,4096]{1,0:T(8,128)(2,1)S(1)} %collective-permute, ...), custom_call_target="tpu_custom_call", output_to_operand_aliasing={{0}: (14, {}), {1}: (15, {}), {2}: (16, {})} | custom-call | tf_op jit(solution)/shard_map/replay/pallas_call | solution.py:357
  38.8 2.8 %collective-permute-start.17 = (f32[8,256]{1,0:T(8,128)S(1)}, f32[8,256]{1,0:T(8,128)S(1)}, u32[]{:S(2)}, u32[]{:S(2)}) collective-permute-start(f32[8,256]{1,0:T(8,128)S(1)} %get-tuple-element.22.own), channel_id=1, source_target_pairs={{12,0},{13,1},{14,2},{15,3},{8,4},{9,5},{10,6},{11,7},{4,8},{5,9},... | collective-permute-start | bytes 24584 | tf_op jit(solution)/shard_map/ppermute | solution.py:25
  41.6 0.1 collective-permute-start.16
  41.7 1.5 %collective-permute-start.15 = (f32[8,256]{1,0:T(8,128)S(1)}, f32[8,256]{1,0:T(8,128)S(1)}, u32[]{:S(2)}, u32[]{:S(2)}) collective-permute-start(f32[8,256]{1,0:T(8,128)S(1)} %get-tuple-element.22.own), channel_id=1, source_target_pairs={{4,0},{5,1},{6,2},{7,3},{0,4},{1,5},{2,6},{3,7},{12,8},{13,9},{14,... | collective-permute-start | bytes 24584 | tf_op jit(solution)/shard_map/ppermute | solution.py:25
  43.2 1.1 %collective-permute-done.17 = f32[8,256]{1,0:T(8,128)S(1)} collective-permute-done((f32[8,256]{1,0:T(8,128)S(1)}, f32[8,256]{1,0:T(8,128)S(1)}, u32[]{:S(2)}, u32[]{:S(2)}) %collective-permute-start.17) | collective-permute-done | bytes 8224 | tf_op jit(solution)/shard_map/ppermute | solution.py:25
  44.3 1.8 %collective-permute-done.16 = f32[8,256]{1,0:T(8,128)S(1)} collective-permute-done((f32[8,256]{1,0:T(8,128)S(1)}, f32[8,256]{1,0:T(8,128)S(1)}, u32[]{:S(2)}, u32[]{:S(2)}) %collective-permute-start.16) | collective-permute-done | bytes 8224 | tf_op jit(solution)/shard_map/ppermute | solution.py:25
  46.1 0.0 collective-permute-done.15
  46.1 0.1 collective-permute-start.20
  46.2 1.1 %collective-permute-start.19 = (f32[8,256]{1,0:T(8,128)S(1)}, f32[8,256]{1,0:T(8,128)S(1)}, u32[]{:S(2)}, u32[]{:S(2)}) collective-permute-start(f32[8,256]{1,0:T(8,128)S(1)} %add_add_fusion.s0), channel_id=1, source_target_pairs={{2,0},{3,1},{0,2},{1,3},{6,4},{7,5},{4,6},{5,7},{10,8},{11,9},{8,1... | collective-permute-start | bytes 24584 | tf_op jit(solution)/shard_map/ppermute | solution.py:25
  47.3 0.8 %collective-permute-start.18 = (f32[8,256]{1,0:T(8,128)S(1)}, f32[8,256]{1,0:T(8,128)S(1)}, u32[]{:S(2)}, u32[]{:S(2)}) collective-permute-start(f32[8,256]{1,0:T(8,128)S(1)} %add_add_fusion.s0), channel_id=1, source_target_pairs={{1,0},{0,1},{3,2},{2,3},{5,4},{4,5},{7,6},{6,7},{9,8},{8,9},{11,10... | collective-permute-start | bytes 24584 | tf_op jit(solution)/shard_map/ppermute | solution.py:25
  48.1 1.2 %collective-permute-done.20.s3 = f32[8,256]{1,0:T(8,128)S(1)} collective-permute-done((f32[8,256]{1,0:T(8,128)S(1)}, f32[8,256]{1,0:T(8,128)S(1)}, u32[]{:S(2)}, u32[]{:S(2)}) %collective-permute-start.20) | collective-permute-done | bytes 8224 | tf_op jit(solution)/shard_map/ppermute | solution.py:25
  49.3 0.7 %collective-permute-done.19.s2 = f32[8,256]{1,0:T(8,128)S(1)} collective-permute-done((f32[8,256]{1,0:T(8,128)S(1)}, f32[8,256]{1,0:T(8,128)S(1)}, u32[]{:S(2)}, u32[]{:S(2)}) %collective-permute-start.19) | collective-permute-done | bytes 8224 | tf_op jit(solution)/shard_map/ppermute | solution.py:25
  49.9 0.0 collective-permute-done.18.s1
  49.9 4.3 %theta.1 = (f32[4096,512]{1,0:T(8,128)}, f32[1,16]{1,0:T(1,128)}) custom-call(f32[8,256]{1,0:T(8,128)S(1)} %add_add_fusion.s0, f32[8,256]{1,0:T(8,128)S(1)} %collective-permute-done.18.s1, f32[8,256]{1,0:T(8,128)S(1)} %collective-permute-done.19.s2, f32[8,256]{1,0:T(8,128)S(1)} %collective-permute-done.20.s3, f32[8,256]{1,0:T(8,128)S(1)} %get-tuple-element.22.own, ...), custom_call_target="tpu_custom_call" | custom-call | tf_op jit(solution)/shard_map/theta/pallas_call | solution.py:429
  (3 shorter events, 0.0 us)
Async XLA Ops:
  0.6 3.2 %collective-permute-start.3 = (bf16[16,4096]{1,0:T(8,128)(2,1)}, bf16[16,4096]{1,0:T(8,128)(2,1)S(1)}, u32[]{:S(2)}, u32[]{:S(2)}) collective-permute-start(bf16[16,4096]{1,0:T(8,128)(2,1)} %refs_0_.1), channel_id=1, source_target_pairs={{1,0},{0,1},{3,2},{2,3},{5,4},{4,5},{7,6},{6,7},{9,8},{8,9},{11,10... | collective-permute-start | bytes 393224 | tf_op jit(solution)/shard_map/ppermute | solution.py:25
  1.1 6.8 %collective-permute-start = (bf16[16,4096]{1,0:T(8,128)(2,1)}, bf16[16,4096]{1,0:T(8,128)(2,1)S(1)}, u32[]{:S(2)}, u32[]{:S(2)}) collective-permute-start(bf16[16,4096]{1,0:T(8,128)(2,1)} %refs_0_.1), channel_id=1, source_target_pairs={{2,0},{5,1},{0,4},{9,5},{4,8},{13,9},{8,12},{15,13},{12,14},{11,15... | collective-permute-start | bytes 393224 | tf_op jit(solution)/shard_map/ppermute | solution.py:39
  3.8 5.8 %collective-permute-start.4 = (bf16[16,4096]{1,0:T(8,128)(2,1)S(1)}, bf16[16,4096]{1,0:T(8,128)(2,1)S(1)}, u32[]{:S(2)}, u32[]{:S(2)}) collective-permute-start(bf16[16,4096]{1,0:T(8,128)(2,1)S(1)} %collective-permute-done.3.refs_1_), channel_id=1, source_target_pairs={{2,0},{5,1},{0,4},{9,5},{4,8},{13,9},{8,12},{15,13},{12,14},{11,15... | collective-permute-start | bytes 393224 | tf_op jit(solution)/shard_map/ppermute | solution.py:39
  7.9 10.5 %collective-permute-start.13 = (bf16[16,4096]{1,0:T(8,128)(2,1)S(1)}, bf16[16,4096]{1,0:T(8,128)(2,1)S(1)}, u32[]{:S(2)}, u32[]{:S(2)}) collective-permute-start(bf16[16,4096]{1,0:T(8,128)(2,1)S(1)} %collective-permute-done.after.refs_2_), channel_id=1, source_target_pairs={{1,0},{0,1},{3,2},{2,3},{5,4},{4,5},{7,6},{6,7},{9,8},{8,9},{11,10... | collective-permute-start | bytes 393224 | tf_op jit(solution)/shard_map/ppermute | solution.py:25
  8.0 5.5 %collective-permute-start.1 = (bf16[16,4096]{1,0:T(8,128)(2,1)S(1)}, bf16[16,4096]{1,0:T(8,128)(2,1)S(1)}, u32[]{:S(2)}, u32[]{:S(2)}) collective-permute-start(bf16[16,4096]{1,0:T(8,128)(2,1)S(1)} %collective-permute-done.after.refs_2_), channel_id=1, source_target_pairs={{2,0},{5,1},{0,4},{9,5},{4,8},{13,9},{8,12},{15,13},{12,14},{11,15... | collective-permute-start | bytes 393224 | tf_op jit(solution)/shard_map/ppermute | solution.py:39
  9.6 5.5 %collective-permute-start.5 = (bf16[16,4096]{1,0:T(8,128)(2,1)S(1)}, bf16[16,4096]{1,0:T(8,128)(2,1)S(1)}, u32[]{:S(2)}, u32[]{:S(2)}) collective-permute-start(bf16[16,4096]{1,0:T(8,128)(2,1)S(1)} %collective-permute-done.4.refs_3_), channel_id=1, source_target_pairs={{2,0},{5,1},{0,4},{9,5},{4,8},{13,9},{8,12},{15,13},{12,14},{11,15... | collective-permute-start | bytes 393224 | tf_op jit(solution)/shard_map/ppermute | solution.py:39
  13.4 8.1 %copy-start = (bf16[16,4096]{1,0:T(8,128)(2,1)S(1)}, bf16[16,4096]{1,0:T(8,128)(2,1)}, u32[]{:S(2)}) copy-start(bf16[16,4096]{1,0:T(8,128)(2,1)} %refs_0_.1) | copy-start | bytes 393220
  13.4 6.6 %collective-permute-start.14 = (bf16[16,4096]{1,0:T(8,128)(2,1)S(1)}, bf16[16,4096]{1,0:T(8,128)(2,1)S(1)}, u32[]{:S(2)}, u32[]{:S(2)}) collective-permute-start(bf16[16,4096]{1,0:T(8,128)(2,1)S(1)} %collective-permute-done.4.refs_3_), channel_id=1, source_target_pairs={{1,0},{0,1},{3,2},{2,3},{5,4},{4,5},{7,6},{6,7},{9,8},{8,9},{11,10... | collective-permute-start | bytes 393224 | tf_op jit(solution)/shard_map/ppermute | solution.py:25
  13.5 5.0 %collective-permute-start.7 = (bf16[16,4096]{1,0:T(8,128)(2,1)S(1)}, bf16[16,4096]{1,0:T(8,128)(2,1)S(1)}, u32[]{:S(2)}, u32[]{:S(2)}) collective-permute-start(bf16[16,4096]{1,0:T(8,128)(2,1)S(1)} %collective-permute-done.1.after.refs_6_), channel_id=1, source_target_pairs={{2,0},{5,1},{0,4},{9,5},{4,8},{13,9},{8,12},{15,13},{12,14},{11,15... | collective-permute-start | bytes 393224 | tf_op jit(solution)/shard_map/ppermute | solution.py:39
  15.1 6.4 %collective-permute-start.2 = (bf16[16,4096]{1,0:T(8,128)(2,1)S(1)}, bf16[16,4096]{1,0:T(8,128)(2,1)S(1)}, u32[]{:S(2)}, u32[]{:S(2)}) collective-permute-start(bf16[16,4096]{1,0:T(8,128)(2,1)S(1)} %collective-permute-done.1.after.refs_6_), channel_id=1, source_target_pairs={{1,0},{0,1},{3,2},{2,3},{5,4},{4,5},{7,6},{6,7},{9,8},{8,9},{11,10... | collective-permute-start | bytes 393224 | tf_op jit(solution)/shard_map/ppermute | solution.py:25
  15.1 5.0 %collective-permute-start.8 = (bf16[16,4096]{1,0:T(8,128)(2,1)S(1)}, bf16[16,4096]{1,0:T(8,128)(2,1)S(1)}, u32[]{:S(2)}, u32[]{:S(2)}) collective-permute-start(bf16[16,4096]{1,0:T(8,128)(2,1)S(1)} %collective-permute-done.5.refs_7_), channel_id=1, source_target_pairs={{2,0},{5,1},{0,4},{9,5},{4,8},{13,9},{8,12},{15,13},{12,14},{11,15... | collective-permute-start | bytes 393224 | tf_op jit(solution)/shard_map/ppermute | solution.py:39
  18.4 6.5 %collective-permute-start.6 = (bf16[16,4096]{1,0:T(8,128)(2,1)S(1)}, bf16[16,4096]{1,0:T(8,128)(2,1)S(1)}, u32[]{:S(2)}, u32[]{:S(2)}) collective-permute-start(bf16[16,4096]{1,0:T(8,128)(2,1)S(1)} %collective-permute-done.5.refs_7_), channel_id=1, source_target_pairs={{1,0},{0,1},{3,2},{2,3},{5,4},{4,5},{7,6},{6,7},{9,8},{8,9},{11,10... | collective-permute-start | bytes 393224 | tf_op jit(solution)/shard_map/ppermute | solution.py:25
  18.6 6.3 %collective-permute-start.11 = (bf16[16,4096]{1,0:T(8,128)(2,1)S(1)}, bf16[16,4096]{1,0:T(8,128)(2,1)S(1)}, u32[]{:S(2)}, u32[]{:S(2)}) collective-permute-start(bf16[16,4096]{1,0:T(8,128)(2,1)S(1)} %collective-permute-done.7.refs_2_), channel_id=1, source_target_pairs={{2,0},{5,1},{0,4},{9,5},{4,8},{13,9},{8,12},{15,13},{12,14},{11,15... | collective-permute-start | bytes 393224 | tf_op jit(solution)/shard_map/ppermute | solution.py:39
  20.0 4.9 %collective-permute-start.9 = (bf16[16,4096]{1,0:T(8,128)(2,1)S(1)}, bf16[16,4096]{1,0:T(8,128)(2,1)S(1)}, u32[]{:S(2)}, u32[]{:S(2)}) collective-permute-start(bf16[16,4096]{1,0:T(8,128)(2,1)S(1)} %collective-permute-done.7.refs_2_), channel_id=1, source_target_pairs={{1,0},{0,1},{3,2},{2,3},{5,4},{4,5},{7,6},{6,7},{9,8},{8,9},{11,10... | collective-permute-start | bytes 393224 | tf_op jit(solution)/shard_map/ppermute | solution.py:25
  20.1 5.0 %collective-permute-start.12 = (bf16[16,4096]{1,0:T(8,128)(2,1)S(1)}, bf16[16,4096]{1,0:T(8,128)(2,1)S(1)}, u32[]{:S(2)}, u32[]{:S(2)}) collective-permute-start(bf16[16,4096]{1,0:T(8,128)(2,1)S(1)} %collective-permute-done.8.refs_3_), channel_id=1, source_target_pairs={{2,0},{5,1},{0,4},{9,5},{4,8},{13,9},{8,12},{15,13},{12,14},{11,15... | collective-permute-start | bytes 393224 | tf_op jit(solution)/shard_map/ppermute | solution.py:39
  21.5 3.6 %collective-permute-start.10 = (bf16[16,4096]{1,0:T(8,128)(2,1)S(1)}, bf16[16,4096]{1,0:T(8,128)(2,1)S(1)}, u32[]{:S(2)}, u32[]{:S(2)}) collective-permute-start(bf16[16,4096]{1,0:T(8,128)(2,1)S(1)} %collective-permute-done.8.refs_3_), channel_id=1, source_target_pairs={{1,0},{0,1},{3,2},{2,3},{5,4},{4,5},{7,6},{6,7},{9,8},{8,9},{11,10... | collective-permute-start | bytes 393224 | tf_op jit(solution)/shard_map/ppermute | solution.py:25
  38.8 5.5 %collective-permute-start.17 = (f32[8,256]{1,0:T(8,128)S(1)}, f32[8,256]{1,0:T(8,128)S(1)}, u32[]{:S(2)}, u32[]{:S(2)}) collective-permute-start(f32[8,256]{1,0:T(8,128)S(1)} %get-tuple-element.22.own), channel_id=1, source_target_pairs={{12,0},{13,1},{14,2},{15,3},{8,4},{9,5},{10,6},{11,7},{4,8},{5,9},... | collective-permute-start | bytes 24584 | tf_op jit(solution)/shard_map/ppermute | solution.py:25
  41.6 4.5 %collective-permute-start.16 = (f32[8,256]{1,0:T(8,128)S(1)}, f32[8,256]{1,0:T(8,128)S(1)}, u32[]{:S(2)}, u32[]{:S(2)}) collective-permute-start(f32[8,256]{1,0:T(8,128)S(1)} %get-tuple-element.22.own), channel_id=1, source_target_pairs={{8,0},{9,1},{10,2},{11,3},{12,4},{13,5},{14,6},{15,7},{0,8},{1,9},... | collective-permute-start | bytes 24584 | tf_op jit(solution)/shard_map/ppermute | solution.py:25
  41.7 4.4 %collective-permute-start.15 = (f32[8,256]{1,0:T(8,128)S(1)}, f32[8,256]{1,0:T(8,128)S(1)}, u32[]{:S(2)}, u32[]{:S(2)}) collective-permute-start(f32[8,256]{1,0:T(8,128)S(1)} %get-tuple-element.22.own), channel_id=1, source_target_pairs={{4,0},{5,1},{6,2},{7,3},{0,4},{1,5},{2,6},{3,7},{12,8},{13,9},{14,... | collective-permute-start | bytes 24584 | tf_op jit(solution)/shard_map/ppermute | solution.py:25
  46.1 3.1 %collective-permute-start.20 = (f32[8,256]{1,0:T(8,128)S(1)}, f32[8,256]{1,0:T(8,128)S(1)}, u32[]{:S(2)}, u32[]{:S(2)}) collective-permute-start(f32[8,256]{1,0:T(8,128)S(1)} %add_add_fusion.s0), channel_id=1, source_target_pairs={{3,0},{2,1},{1,2},{0,3},{7,4},{6,5},{5,6},{4,7},{11,8},{10,9},{9,1... | collective-permute-start | bytes 24584 | tf_op jit(solution)/shard_map/ppermute | solution.py:25
  46.2 3.7 %collective-permute-start.19 = (f32[8,256]{1,0:T(8,128)S(1)}, f32[8,256]{1,0:T(8,128)S(1)}, u32[]{:S(2)}, u32[]{:S(2)}) collective-permute-start(f32[8,256]{1,0:T(8,128)S(1)} %add_add_fusion.s0), channel_id=1, source_target_pairs={{2,0},{3,1},{0,2},{1,3},{6,4},{7,5},{4,6},{5,7},{10,8},{11,9},{8,1... | collective-permute-start | bytes 24584 | tf_op jit(solution)/shard_map/ppermute | solution.py:25
  47.3 2.6 %collective-permute-start.18 = (f32[8,256]{1,0:T(8,128)S(1)}, f32[8,256]{1,0:T(8,128)S(1)}, u32[]{:S(2)}, u32[]{:S(2)}) collective-permute-start(f32[8,256]{1,0:T(8,128)S(1)} %add_add_fusion.s0), channel_id=1, source_target_pairs={{1,0},{0,1},{3,2},{2,3},{5,4},{4,5},{7,6},{6,7},{9,8},{8,9},{11,10... | collective-permute-start | bytes 24584 | tf_op jit(solution)/shard_map/ppermute | solution.py:25

commit v13 on v9

--- a/solution.py
+++ b/solution.py
@@ -1,4 +1,5 @@
 import functools
+import itertools
 
 import jax
 import jax.numpy as jnp
@@ -8,7 +9,7 @@
 from jax.sharding import PartitionSpec as P
 
 TILE = 512
-HALF = 256
+QUARTER = 128
 ROWS = 16
 COLUMNS = 256
 COST = 4 << 30
@@ -263,11 +264,31 @@
     across[...] = jnp.zeros_like(across)
 
     def grad_rows(i, slot, r):
-        at = pl.ds(pl.multiple_of(i * TILE + r, HALF), HALF)
-        grads[slot][r : r + HALF, :] = f32dot(turned[at, :], scaled[...])
-
-    def probe(i, slot, target, terms):
-        target[...] += f32dot(tokens[:, span(i)], terms[slot][...])
+        at = pl.ds(pl.multiple_of(i * TILE + r, QUARTER), QUARTER)
+        product = f32dot(turned[at, :], scaled[...])
+
+        def store():
+            grads[slot][r : r + QUARTER, :] = product
+
+        return store
+
+    def probe(i, slot, target, terms, cols):
+        product = f32dot(tokens[:, span(i)], terms[slot][:, cols])
+
+        def store():
+            target[:, cols] += product
+
+        return store
+
+    def units(i, slot, ahead, behind):
+        grad_units = [functools.partial(grad_rows, i + 1, 1 - slot, r) for r in range(0, TILE, QUARTER)]
+        probe_units = [
+            functools.partial(probe, i - 1, 1 - slot, target, terms, slice(c, min(c + COLUMNS, width)))
+            for target, terms in ((along, firsts), (across, seconds))
+            for c in range(0, width, COLUMNS)
+        ]
+        both = [unit for two in itertools.zip_longest(grad_units, probe_units) for unit in zip(two, (ahead, behind))]
+        return [unit for unit, wanted in both if unit and wanted]
 
     def pieces(i, slot, first, last):
         for r in range(first, last, ROWS):
@@ -278,8 +299,8 @@
 
     for i in range(2):
         tile_copy(i).wait()
-    grad_rows(0, 0, 0)
-    grad_rows(0, 0, HALF)
+    for r in range(0, TILE, QUARTER):
+        grad_rows(0, 0, r)()
     sq, cross = {}, {}
     for r, cols, g, m1, m2, adj in pieces(0, 0, 0, SAMPLE):
         _, _, upd = update(g, m1, m2)
@@ -292,9 +313,9 @@
 
     sums[...] = jnp.zeros_like(sums)
 
-    def update_rows(i, slot, first):
+    def update_rows(i, slot, first, last):
         sq, cross = {}, {}
-        for r, cols, g, m1, m2, adj in pieces(i, slot, first, first + HALF):
+        for r, cols, g, m1, m2, adj in pieces(i, slot, first, last):
             over, inv, upd = update(g, m1, m2)
             sq[cols.start] = sq.get(cols.start, 0.0) + fold(upd * upd)
             cross[cols.start] = cross.get(cols.start, 0.0) + fold(adj * upd)
@@ -305,12 +326,12 @@
         sums[1] += sum(cross.values())
 
     def body(i, slot, ahead=True, behind=True):
-        for r, target, terms in ((0, along, firsts), (HALF, across, seconds)):
-            if ahead:
-                grad_rows(i + 1, 1 - slot, r)
-            update_rows(i, slot, r)
-            if behind:
-                probe(i - 1, 1 - slot, target, terms)
+        work = units(i, slot, ahead, behind)
+        bounds = [TILE // ROWS * k // len(work) * ROWS for k in range(len(work) + 1)]
+        for unit, first, last in zip(work, bounds, bounds[1:]):
+            store = unit()
+            update_rows(i, slot, first, last)
+            store()
 
     body(0, 0, behind=False)
 
@@ -323,8 +344,8 @@
 
     lax.fori_loop(0, tiles // 2 - 1, pair, 0)
     body(tiles - 1, 1, ahead=False)
-    probe(tiles - 1, 1, along, firsts)
-    probe(tiles - 1, 1, across, seconds)
+    for unit in units(tiles, 0, False, True):
+        unit()()
 
     height = count // n
     places = owners(n)

time: 53.9 us -> 54.1 us (level)
  no operation moved by 1% of the time
where the time goes in v13:
time: 54.1 us; the launch traced here: 53.9 us
  Pallas kernels  28.1 us (52%)
  starting transfers between devices  20 us (37%)
  waiting for transfers between devices  5.03 us (9%)
  between operations  0.78 us (1%)
    pallas_call x1, Pallas kernels, replay_call(): pl.pallas_call(functools.partial(replay_kernel, n, half), in_specs=[far]...  13.3 us
    ppermute x8, starting transfers between devices, onward(): return lax.ppermute(value, 'dp', pairs)  12.9 us
    ppermute x13, starting transfers between devices, swapped(): return lax.ppermute(value, 'dp', [(d ^ mask, d) for d in range(n)])  7.11 us
    ppermute x13, waiting for transfers between devices, swapped(): return lax.ppermute(value, 'dp', [(d ^ mask, d) for d in range(n)])  4.79 us
    pallas_call x2, Pallas kernels, fetch_wide(): pl.pallas_call(functools.partial(widen_kernel, factor), in_specs=[pl.Bloc...  4.57 us
    pallas_call x1, Pallas kernels, theta_call(): pl.pallas_call(functools.partial(theta_kernel, n, entries), in_specs=[vme...  4.29 us
    pallas_call x1, Pallas kernels, early_call(): pl.pallas_call(functools.partial(early_kernel, half), in_specs=[pl.BlockS...  3.35 us
    pallas_call x1, Pallas kernels, fetch(): pl.pallas_call(functools.partial(fetch_kernel, n), in_specs=[pl.BlockSpec...  2.52 us
  transfers between devices with their start and end apart: 21, of which 6 were waited for; matrix products, arithmetic and copies ran while one was open for 0% of the time, Pallas kernels for 19%

profile of v13, /device:TPU:0, one launch (start us, length us, event | category | flops | bytes accessed | tf_op | source)
XLA Modules:
  0.0 53.9 jit_solution(1420846252405250206)
XLA Ops:
  0.6 0.5 collective-permute-start.3
  1.1 2.6 %collective-permute-start = (bf16[16,4096]{1,0:T(8,128)(2,1)}, bf16[16,4096]{1,0:T(8,128)(2,1)S(1)}, u32[]{:S(2)}, u32[]{:S(2)}) collective-permute-start(bf16[16,4096]{1,0:T(8,128)(2,1)} %refs_0_.1), channel_id=1, source_target_pairs={{2,0},{5,1},{0,4},{9,5},{4,8},{13,9},{8,12},{15,13},{12,14},{11,15... | collective-permute-start | bytes 393224 | tf_op jit(solution)/shard_map/ppermute | solution.py:40
  3.8 0.0 collective-permute-done.3.refs_1_
  3.8 1.6 %collective-permute-start.4 = (bf16[16,4096]{1,0:T(8,128)(2,1)S(1)}, bf16[16,4096]{1,0:T(8,128)(2,1)S(1)}, u32[]{:S(2)}, u32[]{:S(2)}) collective-permute-start(bf16[16,4096]{1,0:T(8,128)(2,1)S(1)} %collective-permute-done.3.refs_1_), channel_id=1, source_target_pairs={{2,0},{5,1},{0,4},{9,5},{4,8},{13,9},{8,12},{15,13},{12,14},{11,15... | collective-permute-start | bytes 393224 | tf_op jit(solution)/shard_map/ppermute | solution.py:40
  5.4 2.5 %fetch.1 = (bf16[4096,512]{1,0:T(8,128)(2,1)S(1)}, bf16[256,512]{1,0:T(8,128)(2,1)S(1)}, f32[256,128]{1,0:T(8,128)S(1)}) custom-call(bf16[4096,512]{1,0:T(8,128)(2,1)} %far.3, bf16[256,512]{1,0:T(8,128)(2,1)} %far_cot.1, f32[1,256]{1,0:T(1,128)} %bitcast.2, bf16[16,4096]{1,0:T(8,128)(2,1)} %refs_0_.1), custom_call_target="tpu_custom_call" | custom-call | flops 4294967296 | bytes 8388608 | tf_op jit(solution)/shard_map/fetch/pallas_call | solution.py:165
  7.9 0.0 collective-permute-done.after.refs_2_
  7.9 0.1 collective-permute-start.13
  8.0 1.6 %collective-permute-start.1 = (bf16[16,4096]{1,0:T(8,128)(2,1)S(1)}, bf16[16,4096]{1,0:T(8,128)(2,1)S(1)}, u32[]{:S(2)}, u32[]{:S(2)}) collective-permute-start(bf16[16,4096]{1,0:T(8,128)(2,1)S(1)} %collective-permute-done.after.refs_2_), channel_id=1, source_target_pairs={{2,0},{5,1},{0,4},{9,5},{4,8},{13,9},{8,12},{15,13},{12,14},{11,15... | collective-permute-start | bytes 393224 | tf_op jit(solution)/shard_map/ppermute | solution.py:40
  9.6 0.0 collective-permute-done.4.refs_3_
  9.6 1.5 %collective-permute-start.5 = (bf16[16,4096]{1,0:T(8,128)(2,1)S(1)}, bf16[16,4096]{1,0:T(8,128)(2,1)S(1)}, u32[]{:S(2)}, u32[]{:S(2)}) collective-permute-start(bf16[16,4096]{1,0:T(8,128)(2,1)S(1)} %collective-permute-done.4.refs_3_), channel_id=1, source_target_pairs={{2,0},{5,1},{0,4},{9,5},{4,8},{13,9},{8,12},{15,13},{12,14},{11,15... | collective-permute-start | bytes 393224 | tf_op jit(solution)/shard_map/ppermute | solution.py:40
  11.1 2.3 %widen.2.refs_12_ = f32[4096,512]{1,0:T(8,128)S(1)} custom-call(bf16[4096,512]{1,0:T(8,128)(2,1)} %far.4, bf16[16,4096]{1,0:T(8,128)(2,1)S(1)} %collective-permute-done.after.refs_2_), custom_call_target="tpu_custom_call" | custom-call | flops 4294967296 | bytes 8388608 | tf_op jit(solution)/shard_map/widen/pallas_call | solution.py:127
  13.4 0.0 copy-start
  13.4 0.1 collective-permute-start.14
  13.5 0.0 collective-permute-done.1.after.refs_6_
  13.5 1.5 %collective-permute-start.7 = (bf16[16,4096]{1,0:T(8,128)(2,1)S(1)}, bf16[16,4096]{1,0:T(8,128)(2,1)S(1)}, u32[]{:S(2)}, u32[]{:S(2)}) collective-permute-start(bf16[16,4096]{1,0:T(8,128)(2,1)S(1)} %collective-permute-done.1.after.refs_6_), channel_id=1, source_target_pairs={{2,0},{5,1},{0,4},{9,5},{4,8},{13,9},{8,12},{15,13},{12,14},{11,15... | collective-permute-start | bytes 393224 | tf_op jit(solution)/shard_map/ppermute | solution.py:40
  15.1 0.0 collective-permute-start.2
  15.1 0.0 collective-permute-done.5.refs_7_
  15.1 1.0 %collective-permute-start.8 = (bf16[16,4096]{1,0:T(8,128)(2,1)S(1)}, bf16[16,4096]{1,0:T(8,128)(2,1)S(1)}, u32[]{:S(2)}, u32[]{:S(2)}) collective-permute-start(bf16[16,4096]{1,0:T(8,128)(2,1)S(1)} %collective-permute-done.5.refs_7_), channel_id=1, source_target_pairs={{2,0},{5,1},{0,4},{9,5},{4,8},{13,9},{8,12},{15,13},{12,14},{11,15... | collective-permute-start | bytes 393224 | tf_op jit(solution)/shard_map/ppermute | solution.py:40
  16.1 2.3 %widen.3.refs_13_ = f32[4096,512]{1,0:T(8,128)S(1)} custom-call(bf16[4096,512]{1,0:T(8,128)(2,1)} %far.5, bf16[16,4096]{1,0:T(8,128)(2,1)S(1)} %collective-permute-done.1.after.refs_6_), custom_call_target="tpu_custom_call" | custom-call | flops 4294967296 | bytes 8388608 | tf_op jit(solution)/shard_map/widen/pallas_call | solution.py:127
  18.4 0.0 collective-permute-done.13.refs_4_
  18.4 0.1 collective-permute-start.6
  18.5 0.1 collective-permute-done.7.refs_2_
  18.6 1.5 %collective-permute-start.11 = (bf16[16,4096]{1,0:T(8,128)(2,1)S(1)}, bf16[16,4096]{1,0:T(8,128)(2,1)S(1)}, u32[]{:S(2)}, u32[]{:S(2)}) collective-permute-start(bf16[16,4096]{1,0:T(8,128)(2,1)S(1)} %collective-permute-done.7.refs_2_), channel_id=1, source_target_pairs={{2,0},{5,1},{0,4},{9,5},{4,8},{13,9},{8,12},{15,13},{12,14},{11,15... | collective-permute-start | bytes 393224 | tf_op jit(solution)/shard_map/ppermute | solution.py:40
  20.0 0.0 collective-permute-done.14.refs_5_
  20.0 0.0 collective-permute-start.9
  20.1 0.0 collective-permute-done.8.refs_3_
  20.1 1.4 %collective-permute-start.12 = (bf16[16,4096]{1,0:T(8,128)(2,1)S(1)}, bf16[16,4096]{1,0:T(8,128)(2,1)S(1)}, u32[]{:S(2)}, u32[]{:S(2)}) collective-permute-start(bf16[16,4096]{1,0:T(8,128)(2,1)S(1)} %collective-permute-done.8.refs_3_), channel_id=1, source_target_pairs={{2,0},{5,1},{0,4},{9,5},{4,8},{13,9},{8,12},{15,13},{12,14},{11,15... | collective-permute-start | bytes 393224 | tf_op jit(solution)/shard_map/ppermute | solution.py:40
  21.5 0.0 collective-permute-done.2.refs_0_
  21.5 0.0 collective-permute-start.10
  21.5 3.4 %early.1 = (bf16[256,4096]{1,0:T(8,128)(2,1)S(1)}, bf16[4096,256]{1,0:T(8,128)(2,1)S(1)}, f32[256,512]{1,0:T(8,128)S(1)}) custom-call(bf16[16,4096]{1,0:T(8,128)(2,1)S(1)} %copy-done, bf16[16,4096]{1,0:T(8,128)(2,1)S(1)} %collective-permute-done.3.refs_1_, bf16[16,4096]{1,0:T(8,128)(2,1)S(1)} %collective-permute-done.after.refs_2_, ...), custom_call_target="tpu_custom_call" | custom-call | flops 4294967296 | bytes 12582912 | tf_op jit(solution)/shard_map/early/pallas_call | solution.py:222
  24.9 0.0 collective-permute-done.6.refs_1_
  24.9 0.0 collective-permute-done.11.refs_6_
  24.9 0.0 collective-permute-done.9.refs_4_
  24.9 0.2 collective-permute-done.12.refs_7_
  25.1 13.3 %replay.1 = (bf16[256,4096]{1,0:T(8,128)(2,1)S(1)}, bf16[4096,256]{1,0:T(8,128)(2,1)S(1)}, f32[256,512]{1,0:T(8,128)S(1)}, f32[4096,512]{1,0:T(8,128)S(1)}, f32[...) custom-call(bf16[16,4096]{1,0:T(8,128)(2,1)S(1)} %collective-permute, ...), custom_call_target="tpu_custom_call", output_to_operand_aliasing={{0}: (14, {}), {1}: (15, {}), {2}: (16, {})} | custom-call | tf_op jit(solution)/shard_map/replay/pallas_call | solution.py:377
  38.4 2.8 %collective-permute-start.17 = (f32[8,256]{1,0:T(8,128)S(1)}, f32[8,256]{1,0:T(8,128)S(1)}, u32[]{:S(2)}, u32[]{:S(2)}) collective-permute-start(f32[8,256]{1,0:T(8,128)S(1)} %get-tuple-element.22.own), channel_id=1, source_target_pairs={{12,0},{13,1},{14,2},{15,3},{8,4},{9,5},{10,6},{11,7},{4,8},{5,9},... | collective-permute-start | bytes 24584 | tf_op jit(solution)/shard_map/ppermute | solution.py:26
  41.2 0.1 collective-permute-start.16
  41.4 1.5 %collective-permute-start.15 = (f32[8,256]{1,0:T(8,128)S(1)}, f32[8,256]{1,0:T(8,128)S(1)}, u32[]{:S(2)}, u32[]{:S(2)}) collective-permute-start(f32[8,256]{1,0:T(8,128)S(1)} %get-tuple-element.22.own), channel_id=1, source_target_pairs={{4,0},{5,1},{6,2},{7,3},{0,4},{1,5},{2,6},{3,7},{12,8},{13,9},{14,... | collective-permute-start | bytes 24584 | tf_op jit(solution)/shard_map/ppermute | solution.py:26
  42.9 1.1 %collective-permute-done.17 = f32[8,256]{1,0:T(8,128)S(1)} collective-permute-done((f32[8,256]{1,0:T(8,128)S(1)}, f32[8,256]{1,0:T(8,128)S(1)}, u32[]{:S(2)}, u32[]{:S(2)}) %collective-permute-start.17) | collective-permute-done | bytes 8224 | tf_op jit(solution)/shard_map/ppermute | solution.py:26
  43.9 1.8 %collective-permute-done.16 = f32[8,256]{1,0:T(8,128)S(1)} collective-permute-done((f32[8,256]{1,0:T(8,128)S(1)}, f32[8,256]{1,0:T(8,128)S(1)}, u32[]{:S(2)}, u32[]{:S(2)}) %collective-permute-start.16) | collective-permute-done | bytes 8224 | tf_op jit(solution)/shard_map/ppermute | solution.py:26
  45.8 0.0 collective-permute-done.15
  45.8 0.1 collective-permute-start.20
  45.9 1.1 %collective-permute-start.19 = (f32[8,256]{1,0:T(8,128)S(1)}, f32[8,256]{1,0:T(8,128)S(1)}, u32[]{:S(2)}, u32[]{:S(2)}) collective-permute-start(f32[8,256]{1,0:T(8,128)S(1)} %add_add_fusion.s0), channel_id=1, source_target_pairs={{2,0},{3,1},{0,2},{1,3},{6,4},{7,5},{4,6},{5,7},{10,8},{11,9},{8,1... | collective-permute-start | bytes 24584 | tf_op jit(solution)/shard_map/ppermute | solution.py:26
  46.9 0.8 %collective-permute-start.18 = (f32[8,256]{1,0:T(8,128)S(1)}, f32[8,256]{1,0:T(8,128)S(1)}, u32[]{:S(2)}, u32[]{:S(2)}) collective-permute-start(f32[8,256]{1,0:T(8,128)S(1)} %add_add_fusion.s0), channel_id=1, source_target_pairs={{1,0},{0,1},{3,2},{2,3},{5,4},{4,5},{7,6},{6,7},{9,8},{8,9},{11,10... | collective-permute-start | bytes 24584 | tf_op jit(solution)/shard_map/ppermute | solution.py:26
  47.7 1.2 %collective-permute-done.20.s3 = f32[8,256]{1,0:T(8,128)S(1)} collective-permute-done((f32[8,256]{1,0:T(8,128)S(1)}, f32[8,256]{1,0:T(8,128)S(1)}, u32[]{:S(2)}, u32[]{:S(2)}) %collective-permute-start.20) | collective-permute-done | bytes 8224 | tf_op jit(solution)/shard_map/ppermute | solution.py:26
  48.9 0.7 %collective-permute-done.19.s2 = f32[8,256]{1,0:T(8,128)S(1)} collective-permute-done((f32[8,256]{1,0:T(8,128)S(1)}, f32[8,256]{1,0:T(8,128)S(1)}, u32[]{:S(2)}, u32[]{:S(2)}) %collective-permute-start.19) | collective-permute-done | bytes 8224 | tf_op jit(solution)/shard_map/ppermute | solution.py:26
  49.6 0.0 collective-permute-done.18.s1
  49.6 4.3 %theta.1 = (f32[4096,512]{1,0:T(8,128)}, f32[1,16]{1,0:T(1,128)}) custom-call(f32[8,256]{1,0:T(8,128)S(1)} %add_add_fusion.s0, f32[8,256]{1,0:T(8,128)S(1)} %collective-permute-done.18.s1, f32[8,256]{1,0:T(8,128)S(1)} %collective-permute-done.19.s2, f32[8,256]{1,0:T(8,128)S(1)} %collective-permute-done.20.s3, f32[8,256]{1,0:T(8,128)S(1)} %get-tuple-element.22.own, ...), custom_call_target="tpu_custom_call" | custom-call | tf_op jit(solution)/shard_map/theta/pallas_call | solution.py:449
  (3 shorter events, 0.0 us)
Async XLA Ops:
  0.6 3.2 %collective-permute-start.3 = (bf16[16,4096]{1,0:T(8,128)(2,1)}, bf16[16,4096]{1,0:T(8,128)(2,1)S(1)}, u32[]{:S(2)}, u32[]{:S(2)}) collective-permute-start(bf16[16,4096]{1,0:T(8,128)(2,1)} %refs_0_.1), channel_id=1, source_target_pairs={{1,0},{0,1},{3,2},{2,3},{5,4},{4,5},{7,6},{6,7},{9,8},{8,9},{11,10... | collective-permute-start | bytes 393224 | tf_op jit(solution)/shard_map/ppermute | solution.py:26
  1.1 6.8 %collective-permute-start = (bf16[16,4096]{1,0:T(8,128)(2,1)}, bf16[16,4096]{1,0:T(8,128)(2,1)S(1)}, u32[]{:S(2)}, u32[]{:S(2)}) collective-permute-start(bf16[16,4096]{1,0:T(8,128)(2,1)} %refs_0_.1), channel_id=1, source_target_pairs={{2,0},{5,1},{0,4},{9,5},{4,8},{13,9},{8,12},{15,13},{12,14},{11,15... | collective-permute-start | bytes 393224 | tf_op jit(solution)/shard_map/ppermute | solution.py:40
  3.8 5.8 %collective-permute-start.4 = (bf16[16,4096]{1,0:T(8,128)(2,1)S(1)}, bf16[16,4096]{1,0:T(8,128)(2,1)S(1)}, u32[]{:S(2)}, u32[]{:S(2)}) collective-permute-start(bf16[16,4096]{1,0:T(8,128)(2,1)S(1)} %collective-permute-done.3.refs_1_), channel_id=1, source_target_pairs={{2,0},{5,1},{0,4},{9,5},{4,8},{13,9},{8,12},{15,13},{12,14},{11,15... | collective-permute-start | bytes 393224 | tf_op jit(solution)/shard_map/ppermute | solution.py:40
  7.9 10.5 %collective-permute-start.13 = (bf16[16,4096]{1,0:T(8,128)(2,1)S(1)}, bf16[16,4096]{1,0:T(8,128)(2,1)S(1)}, u32[]{:S(2)}, u32[]{:S(2)}) collective-permute-start(bf16[16,4096]{1,0:T(8,128)(2,1)S(1)} %collective-permute-done.after.refs_2_), channel_id=1, source_target_pairs={{1,0},{0,1},{3,2},{2,3},{5,4},{4,5},{7,6},{6,7},{9,8},{8,9},{11,10... | collective-permute-start | bytes 393224 | tf_op jit(solution)/shard_map/ppermute | solution.py:26
  8.0 5.5 %collective-permute-start.1 = (bf16[16,4096]{1,0:T(8,128)(2,1)S(1)}, bf16[16,4096]{1,0:T(8,128)(2,1)S(1)}, u32[]{:S(2)}, u32[]{:S(2)}) collective-permute-start(bf16[16,4096]{1,0:T(8,128)(2,1)S(1)} %collective-permute-done.after.refs_2_), channel_id=1, source_target_pairs={{2,0},{5,1},{0,4},{9,5},{4,8},{13,9},{8,12},{15,13},{12,14},{11,15... | collective-permute-start | bytes 393224 | tf_op jit(solution)/shard_map/ppermute | solution.py:40
  9.6 5.5 %collective-permute-start.5 = (bf16[16,4096]{1,0:T(8,128)(2,1)S(1)}, bf16[16,4096]{1,0:T(8,128)(2,1)S(1)}, u32[]{:S(2)}, u32[]{:S(2)}) collective-permute-start(bf16[16,4096]{1,0:T(8,128)(2,1)S(1)} %collective-permute-done.4.refs_3_), channel_id=1, source_target_pairs={{2,0},{5,1},{0,4},{9,5},{4,8},{13,9},{8,12},{15,13},{12,14},{11,15... | collective-permute-start | bytes 393224 | tf_op jit(solution)/shard_map/ppermute | solution.py:40
  13.4 8.1 %copy-start = (bf16[16,4096]{1,0:T(8,128)(2,1)S(1)}, bf16[16,4096]{1,0:T(8,128)(2,1)}, u32[]{:S(2)}) copy-start(bf16[16,4096]{1,0:T(8,128)(2,1)} %refs_0_.1) | copy-start | bytes 393220
  13.4 6.6 %collective-permute-start.14 = (bf16[16,4096]{1,0:T(8,128)(2,1)S(1)}, bf16[16,4096]{1,0:T(8,128)(2,1)S(1)}, u32[]{:S(2)}, u32[]{:S(2)}) collective-permute-start(bf16[16,4096]{1,0:T(8,128)(2,1)S(1)} %collective-permute-done.4.refs_3_), channel_id=1, source_target_pairs={{1,0},{0,1},{3,2},{2,3},{5,4},{4,5},{7,6},{6,7},{9,8},{8,9},{11,10... | collective-permute-start | bytes 393224 | tf_op jit(solution)/shard_map/ppermute | solution.py:26
  13.5 5.0 %collective-permute-start.7 = (bf16[16,4096]{1,0:T(8,128)(2,1)S(1)}, bf16[16,4096]{1,0:T(8,128)(2,1)S(1)}, u32[]{:S(2)}, u32[]{:S(2)}) collective-permute-start(bf16[16,4096]{1,0:T(8,128)(2,1)S(1)} %collective-permute-done.1.after.refs_6_), channel_id=1, source_target_pairs={{2,0},{5,1},{0,4},{9,5},{4,8},{13,9},{8,12},{15,13},{12,14},{11,15... | collective-permute-start | bytes 393224 | tf_op jit(solution)/shard_map/ppermute | solution.py:40
  15.1 6.4 %collective-permute-start.2 = (bf16[16,4096]{1,0:T(8,128)(2,1)S(1)}, bf16[16,4096]{1,0:T(8,128)(2,1)S(1)}, u32[]{:S(2)}, u32[]{:S(2)}) collective-permute-start(bf16[16,4096]{1,0:T(8,128)(2,1)S(1)} %collective-permute-done.1.after.refs_6_), channel_id=1, source_target_pairs={{1,0},{0,1},{3,2},{2,3},{5,4},{4,5},{7,6},{6,7},{9,8},{8,9},{11,10... | collective-permute-start | bytes 393224 | tf_op jit(solution)/shard_map/ppermute | solution.py:26
  15.1 5.0 %collective-permute-start.8 = (bf16[16,4096]{1,0:T(8,128)(2,1)S(1)}, bf16[16,4096]{1,0:T(8,128)(2,1)S(1)}, u32[]{:S(2)}, u32[]{:S(2)}) collective-permute-start(bf16[16,4096]{1,0:T(8,128)(2,1)S(1)} %collective-permute-done.5.refs_7_), channel_id=1, source_target_pairs={{2,0},{5,1},{0,4},{9,5},{4,8},{13,9},{8,12},{15,13},{12,14},{11,15... | collective-permute-start | bytes 393224 | tf_op jit(solution)/shard_map/ppermute | solution.py:40
  18.4 6.5 %collective-permute-start.6 = (bf16[16,4096]{1,0:T(8,128)(2,1)S(1)}, bf16[16,4096]{1,0:T(8,128)(2,1)S(1)}, u32[]{:S(2)}, u32[]{:S(2)}) collective-permute-start(bf16[16,4096]{1,0:T(8,128)(2,1)S(1)} %collective-permute-done.5.refs_7_), channel_id=1, source_target_pairs={{1,0},{0,1},{3,2},{2,3},{5,4},{4,5},{7,6},{6,7},{9,8},{8,9},{11,10... | collective-permute-start | bytes 393224 | tf_op jit(solution)/shard_map/ppermute | solution.py:26
  18.6 6.3 %collective-permute-start.11 = (bf16[16,4096]{1,0:T(8,128)(2,1)S(1)}, bf16[16,4096]{1,0:T(8,128)(2,1)S(1)}, u32[]{:S(2)}, u32[]{:S(2)}) collective-permute-start(bf16[16,4096]{1,0:T(8,128)(2,1)S(1)} %collective-permute-done.7.refs_2_), channel_id=1, source_target_pairs={{2,0},{5,1},{0,4},{9,5},{4,8},{13,9},{8,12},{15,13},{12,14},{11,15... | collective-permute-start | bytes 393224 | tf_op jit(solution)/shard_map/ppermute | solution.py:40
  20.0 4.9 %collective-permute-start.9 = (bf16[16,4096]{1,0:T(8,128)(2,1)S(1)}, bf16[16,4096]{1,0:T(8,128)(2,1)S(1)}, u32[]{:S(2)}, u32[]{:S(2)}) collective-permute-start(bf16[16,4096]{1,0:T(8,128)(2,1)S(1)} %collective-permute-done.7.refs_2_), channel_id=1, source_target_pairs={{1,0},{0,1},{3,2},{2,3},{5,4},{4,5},{7,6},{6,7},{9,8},{8,9},{11,10... | collective-permute-start | bytes 393224 | tf_op jit(solution)/shard_map/ppermute | solution.py:26
  20.1 5.0 %collective-permute-start.12 = (bf16[16,4096]{1,0:T(8,128)(2,1)S(1)}, bf16[16,4096]{1,0:T(8,128)(2,1)S(1)}, u32[]{:S(2)}, u32[]{:S(2)}) collective-permute-start(bf16[16,4096]{1,0:T(8,128)(2,1)S(1)} %collective-permute-done.8.refs_3_), channel_id=1, source_target_pairs={{2,0},{5,1},{0,4},{9,5},{4,8},{13,9},{8,12},{15,13},{12,14},{11,15... | collective-permute-start | bytes 393224 | tf_op jit(solution)/shard_map/ppermute | solution.py:40
  21.5 3.6 %collective-permute-start.10 = (bf16[16,4096]{1,0:T(8,128)(2,1)S(1)}, bf16[16,4096]{1,0:T(8,128)(2,1)S(1)}, u32[]{:S(2)}, u32[]{:S(2)}) collective-permute-start(bf16[16,4096]{1,0:T(8,128)(2,1)S(1)} %collective-permute-done.8.refs_3_), channel_id=1, source_target_pairs={{1,0},{0,1},{3,2},{2,3},{5,4},{4,5},{7,6},{6,7},{9,8},{8,9},{11,10... | collective-permute-start | bytes 393224 | tf_op jit(solution)/shard_map/ppermute | solution.py:26
  38.4 5.5 %collective-permute-start.17 = (f32[8,256]{1,0:T(8,128)S(1)}, f32[8,256]{1,0:T(8,128)S(1)}, u32[]{:S(2)}, u32[]{:S(2)}) collective-permute-start(f32[8,256]{1,0:T(8,128)S(1)} %get-tuple-element.22.own), channel_id=1, source_target_pairs={{12,0},{13,1},{14,2},{15,3},{8,4},{9,5},{10,6},{11,7},{4,8},{5,9},... | collective-permute-start | bytes 24584 | tf_op jit(solution)/shard_map/ppermute | solution.py:26
  41.2 4.5 %collective-permute-start.16 = (f32[8,256]{1,0:T(8,128)S(1)}, f32[8,256]{1,0:T(8,128)S(1)}, u32[]{:S(2)}, u32[]{:S(2)}) collective-permute-start(f32[8,256]{1,0:T(8,128)S(1)} %get-tuple-element.22.own), channel_id=1, source_target_pairs={{8,0},{9,1},{10,2},{11,3},{12,4},{13,5},{14,6},{15,7},{0,8},{1,9},... | collective-permute-start | bytes 24584 | tf_op jit(solution)/shard_map/ppermute | solution.py:26
  41.4 4.4 %collective-permute-start.15 = (f32[8,256]{1,0:T(8,128)S(1)}, f32[8,256]{1,0:T(8,128)S(1)}, u32[]{:S(2)}, u32[]{:S(2)}) collective-permute-start(f32[8,256]{1,0:T(8,128)S(1)} %get-tuple-element.22.own), channel_id=1, source_target_pairs={{4,0},{5,1},{6,2},{7,3},{0,4},{1,5},{2,6},{3,7},{12,8},{13,9},{14,... | collective-permute-start | bytes 24584 | tf_op jit(solution)/shard_map/ppermute | solution.py:26
  45.8 3.1 %collective-permute-start.20 = (f32[8,256]{1,0:T(8,128)S(1)}, f32[8,256]{1,0:T(8,128)S(1)}, u32[]{:S(2)}, u32[]{:S(2)}) collective-permute-start(f32[8,256]{1,0:T(8,128)S(1)} %add_add_fusion.s0), channel_id=1, source_target_pairs={{3,0},{2,1},{1,2},{0,3},{7,4},{6,5},{5,6},{4,7},{11,8},{10,9},{9,1... | collective-permute-start | bytes 24584 | tf_op jit(solution)/shard_map/ppermute | solution.py:26
  45.9 3.7 %collective-permute-start.19 = (f32[8,256]{1,0:T(8,128)S(1)}, f32[8,256]{1,0:T(8,128)S(1)}, u32[]{:S(2)}, u32[]{:S(2)}) collective-permute-start(f32[8,256]{1,0:T(8,128)S(1)} %add_add_fusion.s0), channel_id=1, source_target_pairs={{2,0},{3,1},{0,2},{1,3},{6,4},{7,5},{4,6},{5,7},{10,8},{11,9},{8,1... | collective-permute-start | bytes 24584 | tf_op jit(solution)/shard_map/ppermute | solution.py:26
  46.9 2.7 %collective-permute-start.18 = (f32[8,256]{1,0:T(8,128)S(1)}, f32[8,256]{1,0:T(8,128)S(1)}, u32[]{:S(2)}, u32[]{:S(2)}) collective-permute-start(f32[8,256]{1,0:T(8,128)S(1)} %add_add_fusion.s0), channel_id=1, source_target_pairs={{1,0},{0,1},{3,2},{2,3},{5,4},{4,5},{7,6},{6,7},{9,8},{8,9},{11,10... | collective-permute-start | bytes 24584 | tf_op jit(solution)/shard_map/ppermute | solution.py:26

commit v14 on v9

--- a/solution.py
+++ b/solution.py
@@ -75,11 +75,8 @@
     return places
 
 
-def all_sum(value, n):
-    total = value
-    for mask in range(4, n, 4):
-        total = total + swapped(value, n, mask)
-    return [total] + [swapped(total, n, mask) for mask in (1, 2, 3)]
+def to_all(copies):
+    return lax.all_to_all(copies, "dp", split_axis=0, concat_axis=0, tiled=True)
 
 
 def over_columns(row):
@@ -236,8 +233,8 @@
 
 def replay_kernel(n, half, *refs):
     blocks, (far, weight, cot, weights, one, two) = refs[:half], refs[half : half + 6]
-    (tokens, turned, gate, adjoint, along, across, bend, stats) = refs[half + 9 : half + 17]
-    (scaled, score, g0, g1, a0, a1, b0, b1, sums, upright, sems, tile_sems) = refs[half + 17 :]
+    (tokens, turned, gate, adjoint, along, across, bend, stats, copies) = refs[half + 9 : half + 18]
+    (scaled, score, g0, g1, a0, a1, b0, b1, sums, upright, sems, tile_sems) = refs[half + 18 :]
     grads, firsts, seconds = (g0, g1), (a0, a1), (b0, b1)
     depth = one.shape[0]
     count, width = scaled.shape
@@ -343,6 +340,8 @@
     stats[2:3, :] = RATIO**2 * whole(sums[0])
     stats[3:4, :] = RATIO * whole(sums[1])
     stats[4:8, :] = jnp.broadcast_to(guess, (4, count))
+    for k in range(n):
+        copies[8 * k : 8 * (k + 1), :] = stats[...]
 
 
 def replay_call(n, blocks, adjoint, weight, cot, weights, one, two, tokens, turned, gate):
@@ -356,7 +355,7 @@
     return pl.pallas_call(
         functools.partial(replay_kernel, n, half),
         in_specs=[far] * (half + 1) + [vmem] * 8,
-        out_specs=[vmem] * 8,
+        out_specs=[vmem] * 9,
         out_shape=[
             like(tokens),
             like(turned),
@@ -366,6 +365,7 @@
             pltpu.VMEM((count, width), jnp.float32),
             pltpu.VMEM((count, width), jnp.float32),
             pltpu.VMEM((8, count), jnp.float32),
+            jax.ShapeDtypeStruct((8 * n, count), jnp.float32),
         ],
         scratch_shapes=[
             pltpu.VMEM((count, width), jnp.bfloat16),
@@ -391,8 +391,8 @@
     return pltpu.with_memory_space_constraint(x, pltpu.HBM)
 
 
-def theta_kernel(n, entries, s0, s1, s2, s3, own, along, across, bend, turned, adjoint, theta, scores, ready, sent):
-    total = s0[...] + s1[...] + (s2[...] + s3[...])
+def theta_kernel(n, entries, everyone, own, along, across, bend, turned, adjoint, theta, scores, ready, sent):
+    total = sum(everyone[8 * k : 8 * (k + 1), :] for k in range(n))
     sq, cross = total[2:3, 0:1], total[3:4, 0:1]
     rms = jnp.sqrt(sq / entries)
     scale = 1.0 / jnp.maximum(1.0, rms)
@@ -421,13 +421,13 @@
         copy(i).wait()
 
 
-def theta_call(n, entries, sums, own, along, across, bend, turned, adjoint):
+def theta_call(n, entries, everyone, own, along, across, bend, turned, adjoint):
     depth, width = adjoint.shape
     count = turned.shape[1]
     vmem = pl.BlockSpec(memory_space=pltpu.VMEM)
     return pl.pallas_call(
         functools.partial(theta_kernel, n, entries),
-        in_specs=[vmem] * 10,
+        in_specs=[vmem] * 7,
         out_specs=[pl.BlockSpec(memory_space=pl.ANY), vmem],
         out_shape=[
             jax.ShapeDtypeStruct((depth, width), jnp.float32),
@@ -436,7 +436,7 @@
         scratch_shapes=[pltpu.VMEM((depth, width), jnp.float32), pltpu.SemaphoreType.DMA((depth // TILE,))],
         compiler_params=pltpu.CompilerParams(vmem_limit_bytes=VMEM_BYTES),
         name="theta",
-    )(*sums, own, along, across, bend, turned, adjoint)
+    )(everyone, own, along, across, bend, turned, adjoint)
 
 
 def shards(n, tokens, cotangent, token_weight, weight, moment_one, moment_two, adjoint):
@@ -449,11 +449,11 @@
     blocks, ((weight_near, cot, weights), one, two) = gather(tokens, n, errands)
     half = len(blocks) // 2
     rows, turned, gate = early_call(blocks[:half], weight_near, cot.shape[0])
-    _, turned, _, adjoint_near, along, across, bend, stats = replay_call(
+    _, turned, _, adjoint_near, along, across, bend, stats, copies = replay_call(
         n, blocks[half:], adjoint, weight_near, cot, weights, one, two, rows, turned, gate
     )
-    sums = all_sum(stats, n)
-    theta_bar, scores = theta_call(n, entries, sums, stats, along, across, bend, turned, adjoint_near)
+    everyone = to_all(copies)
+    theta_bar, scores = theta_call(n, entries, everyone, stats, along, across, bend, turned, adjoint_near)
     return (theta_bar, scores.reshape(-1))
 
 

time: 53.9 us -> 55.1 us (1.022)
  blocking collectives: 0 us -> 12.3 us
  starting transfers between devices: 20 us -> 13.6 us
  waiting for transfers between devices: 5.01 us -> 0.26 us
    all_to_all x0 -> x1, blocking collectives: none -> 12.3 us  [to_all(): return lax.all_to_all(copies, 'dp', split_axis=0, concat_axis=0, tiled=True)]
    ppermute x13 -> x7, starting transfers between devices: 7.12 us -> 0.74 us  [swapped(): return lax.ppermute(value, 'dp', [(d ^ mask, d) for d in range(n)])]
    ppermute x13 -> x7, waiting for transfers between devices: 4.77 us -> 0.02 us  [swapped(): return lax.ppermute(value, 'dp', [(d ^ mask, d) for d in range(n)])]
  transfers between devices with their start and end apart: 21 -> 15, of which waited for: 6 -> 2; matrix products, arithmetic and copies ran while one was open for 0% -> 0% of each run, Pallas kernels for 19% -> 19%
where the time goes in v14:
time: 55.1 us; the launch traced here: 54.8 us
  Pallas kernels  27.8 us (50%)
  starting transfers between devices  13.6 us (25%)
  blocking collectives  12.3 us (22%)
  between operations  0.77 us (1%)
    pallas_call x1, Pallas kernels, replay_call(): pl.pallas_call(functools.partial(replay_kernel, n, half), in_specs=[far]...  13.1 us
    ppermute x8, starting transfers between devices, onward(): return lax.ppermute(value, 'dp', pairs)  12.9 us
    all_to_all x1, blocking collectives, to_all(): return lax.all_to_all(copies, 'dp', split_axis=0, concat_axis=0, tiled=True)  12.3 us
    pallas_call x2, Pallas kernels, fetch_wide(): pl.pallas_call(functools.partial(widen_kernel, factor), in_specs=[pl.Bloc...  4.57 us
    pallas_call x1, Pallas kernels, theta_call(): pl.pallas_call(functools.partial(theta_kernel, n, entries), in_specs=[vme...  4.3 us
    pallas_call x1, Pallas kernels, early_call(): pl.pallas_call(functools.partial(early_kernel, half), in_specs=[pl.BlockS...  3.35 us
    pallas_call x1, Pallas kernels, fetch(): pl.pallas_call(functools.partial(fetch_kernel, n), in_specs=[pl.BlockSpec...  2.52 us
  transfers between devices with their start and end apart: 15, of which 2 were waited for; matrix products, arithmetic and copies ran while one was open for 0% of the time, Pallas kernels for 19%

profile of v14, /device:TPU:0, one launch (start us, length us, event | category | flops | bytes accessed | tf_op | source)
XLA Modules:
  0.0 54.8 jit_solution(15732184675986507339)
XLA Ops:
  0.6 0.5 collective-permute-start.3
  1.1 2.6 %collective-permute-start = (bf16[16,4096]{1,0:T(8,128)(2,1)}, bf16[16,4096]{1,0:T(8,128)(2,1)S(1)}, u32[]{:S(2)}, u32[]{:S(2)}) collective-permute-start(bf16[16,4096]{1,0:T(8,128)(2,1)} %refs_0_.1), channel_id=1, source_target_pairs={{2,0},{5,1},{0,4},{9,5},{4,8},{13,9},{8,12},{15,13},{12,14},{11,15... | collective-permute-start | bytes 393224 | tf_op jit(solution)/shard_map/ppermute | solution.py:39
  3.8 0.0 collective-permute-done.3.refs_1_
  3.8 1.6 %collective-permute-start.4 = (bf16[16,4096]{1,0:T(8,128)(2,1)S(1)}, bf16[16,4096]{1,0:T(8,128)(2,1)S(1)}, u32[]{:S(2)}, u32[]{:S(2)}) collective-permute-start(bf16[16,4096]{1,0:T(8,128)(2,1)S(1)} %collective-permute-done.3.refs_1_), channel_id=1, source_target_pairs={{2,0},{5,1},{0,4},{9,5},{4,8},{13,9},{8,12},{15,13},{12,14},{11,15... | collective-permute-start | bytes 393224 | tf_op jit(solution)/shard_map/ppermute | solution.py:39
  5.4 2.5 %fetch.1 = (bf16[4096,512]{1,0:T(8,128)(2,1)S(1)}, bf16[256,512]{1,0:T(8,128)(2,1)S(1)}, f32[256,128]{1,0:T(8,128)S(1)}) custom-call(bf16[4096,512]{1,0:T(8,128)(2,1)} %far.3, bf16[256,512]{1,0:T(8,128)(2,1)} %far_cot.1, f32[1,256]{1,0:T(1,128)} %bitcast.6, bf16[16,4096]{1,0:T(8,128)(2,1)} %refs_0_.1), custom_call_target="tpu_custom_call" | custom-call | flops 4294967296 | bytes 8388608 | tf_op jit(solution)/shard_map/fetch/pallas_call | solution.py:161
  7.9 0.0 collective-permute-done.after.refs_2_
  7.9 0.1 collective-permute-start.13
  8.0 1.6 %collective-permute-start.1 = (bf16[16,4096]{1,0:T(8,128)(2,1)S(1)}, bf16[16,4096]{1,0:T(8,128)(2,1)S(1)}, u32[]{:S(2)}, u32[]{:S(2)}) collective-permute-start(bf16[16,4096]{1,0:T(8,128)(2,1)S(1)} %collective-permute-done.after.refs_2_), channel_id=1, source_target_pairs={{2,0},{5,1},{0,4},{9,5},{4,8},{13,9},{8,12},{15,13},{12,14},{11,15... | collective-permute-start | bytes 393224 | tf_op jit(solution)/shard_map/ppermute | solution.py:39
  9.6 0.0 collective-permute-done.4.refs_3_
  9.6 1.5 %collective-permute-start.5 = (bf16[16,4096]{1,0:T(8,128)(2,1)S(1)}, bf16[16,4096]{1,0:T(8,128)(2,1)S(1)}, u32[]{:S(2)}, u32[]{:S(2)}) collective-permute-start(bf16[16,4096]{1,0:T(8,128)(2,1)S(1)} %collective-permute-done.4.refs_3_), channel_id=1, source_target_pairs={{2,0},{5,1},{0,4},{9,5},{4,8},{13,9},{8,12},{15,13},{12,14},{11,15... | collective-permute-start | bytes 393224 | tf_op jit(solution)/shard_map/ppermute | solution.py:39
  11.1 2.3 %widen.2.refs_12_ = f32[4096,512]{1,0:T(8,128)S(1)} custom-call(bf16[4096,512]{1,0:T(8,128)(2,1)} %far.4, bf16[16,4096]{1,0:T(8,128)(2,1)S(1)} %collective-permute-done.after.refs_2_), custom_call_target="tpu_custom_call" | custom-call | flops 4294967296 | bytes 8388608 | tf_op jit(solution)/shard_map/widen/pallas_call | solution.py:123
  13.4 0.0 copy-start
  13.4 0.1 collective-permute-start.14
  13.5 0.0 collective-permute-done.1.after.refs_6_
  13.5 1.5 %collective-permute-start.7 = (bf16[16,4096]{1,0:T(8,128)(2,1)S(1)}, bf16[16,4096]{1,0:T(8,128)(2,1)S(1)}, u32[]{:S(2)}, u32[]{:S(2)}) collective-permute-start(bf16[16,4096]{1,0:T(8,128)(2,1)S(1)} %collective-permute-done.1.after.refs_6_), channel_id=1, source_target_pairs={{2,0},{5,1},{0,4},{9,5},{4,8},{13,9},{8,12},{15,13},{12,14},{11,15... | collective-permute-start | bytes 393224 | tf_op jit(solution)/shard_map/ppermute | solution.py:39
  15.1 0.0 collective-permute-start.2
  15.1 0.0 collective-permute-done.5.refs_7_
  15.1 1.0 %collective-permute-start.8 = (bf16[16,4096]{1,0:T(8,128)(2,1)S(1)}, bf16[16,4096]{1,0:T(8,128)(2,1)S(1)}, u32[]{:S(2)}, u32[]{:S(2)}) collective-permute-start(bf16[16,4096]{1,0:T(8,128)(2,1)S(1)} %collective-permute-done.5.refs_7_), channel_id=1, source_target_pairs={{2,0},{5,1},{0,4},{9,5},{4,8},{13,9},{8,12},{15,13},{12,14},{11,15... | collective-permute-start | bytes 393224 | tf_op jit(solution)/shard_map/ppermute | solution.py:39
  16.1 2.3 %widen.3.refs_13_ = f32[4096,512]{1,0:T(8,128)S(1)} custom-call(bf16[4096,512]{1,0:T(8,128)(2,1)} %far.5, bf16[16,4096]{1,0:T(8,128)(2,1)S(1)} %collective-permute-done.1.after.refs_6_), custom_call_target="tpu_custom_call" | custom-call | flops 4294967296 | bytes 8388608 | tf_op jit(solution)/shard_map/widen/pallas_call | solution.py:123
  18.4 0.0 collective-permute-done.13.refs_4_
  18.4 0.1 collective-permute-start.6
  18.5 0.1 collective-permute-done.7.refs_2_
  18.6 1.5 %collective-permute-start.11 = (bf16[16,4096]{1,0:T(8,128)(2,1)S(1)}, bf16[16,4096]{1,0:T(8,128)(2,1)S(1)}, u32[]{:S(2)}, u32[]{:S(2)}) collective-permute-start(bf16[16,4096]{1,0:T(8,128)(2,1)S(1)} %collective-permute-done.7.refs_2_), channel_id=1, source_target_pairs={{2,0},{5,1},{0,4},{9,5},{4,8},{13,9},{8,12},{15,13},{12,14},{11,15... | collective-permute-start | bytes 393224 | tf_op jit(solution)/shard_map/ppermute | solution.py:39
  20.0 0.0 collective-permute-done.14.refs_5_
  20.0 0.0 collective-permute-start.9
  20.1 0.0 collective-permute-done.8.refs_3_
  20.1 1.4 %collective-permute-start.12 = (bf16[16,4096]{1,0:T(8,128)(2,1)S(1)}, bf16[16,4096]{1,0:T(8,128)(2,1)S(1)}, u32[]{:S(2)}, u32[]{:S(2)}) collective-permute-start(bf16[16,4096]{1,0:T(8,128)(2,1)S(1)} %collective-permute-done.8.refs_3_), channel_id=1, source_target_pairs={{2,0},{5,1},{0,4},{9,5},{4,8},{13,9},{8,12},{15,13},{12,14},{11,15... | collective-permute-start | bytes 393224 | tf_op jit(solution)/shard_map/ppermute | solution.py:39
  21.5 0.0 collective-permute-done.2.refs_0_
  21.5 0.0 collective-permute-start.10
  21.5 0.0 copy-done
  21.5 3.4 %early.1 = (bf16[256,4096]{1,0:T(8,128)(2,1)S(1)}, bf16[4096,256]{1,0:T(8,128)(2,1)S(1)}, f32[256,512]{1,0:T(8,128)S(1)}) custom-call(bf16[16,4096]{1,0:T(8,128)(2,1)S(1)} %copy-done, bf16[16,4096]{1,0:T(8,128)(2,1)S(1)} %collective-permute-done.3.refs_1_, bf16[16,4096]{1,0:T(8,128)(2,1)S(1)} %collective-permute-done.after.refs_2_, ...), custom_call_target="tpu_custom_call" | custom-call | flops 4294967296 | bytes 12582912 | tf_op jit(solution)/shard_map/early/pallas_call | solution.py:218
  24.9 0.0 collective-permute-done.6.refs_1_
  24.9 0.0 collective-permute-done.11.refs_6_
  24.9 0.0 collective-permute-done.9.refs_4_
  24.9 0.2 collective-permute-done.12.refs_7_
  25.1 0.0 collective-permute-done.10.refs_5_
  25.1 13.1 %replay.1 = (bf16[256,4096]{1,0:T(8,128)(2,1)S(1)}, bf16[4096,256]{1,0:T(8,128)(2,1)S(1)}, f32[256,512]{1,0:T(8,128)S(1)}, f32[4096,512]{1,0:T(8,128)S(1)}, f32[...) custom-call(bf16[16,4096]{1,0:T(8,128)(2,1)S(1)} %collective-permute, ...), custom_call_target="tpu_custom_call", output_to_operand_aliasing={{0}: (14, {}), {1}: (15, {}), {2}: (16, {})} | custom-call | tf_op jit(solution)/shard_map/replay/pallas_call | solution.py:355
  38.2 12.3 %all_to_all.11 = f32[16,8,256]{2,1,0:T(8,128)S(1)} all-to-all(f32[16,8,256]{2,1,0:T(8,128)S(1)} %bitcast.5), channel_id=1, replica_groups=mesh['group'=2,'dp'=16] {'dp'}, dimensions={0} | all-to-all | bytes 262144 | tf_op jit(solution)/shard_map/all_to_all | solution.py:79
  50.5 4.3 %theta.1 = (f32[4096,512]{1,0:T(8,128)}, f32[1,16]{1,0:T(1,128)}) custom-call(f32[128,256]{1,0:T(8,128)S(1)} %bitcast.4, f32[8,256]{1,0:T(8,128)S(1)} %get-tuple-element.24.own, f32[256,512]{1,0:T(8,128)S(1)} %get-tuple-element.25.along, f32[256,512]{1,0:T(8,128)S(1)} %get-tuple-element.26.across, f32[256,512]{1,0:T(8,128)S(1)} %get-tuple-element.27.bend, ...), custom_call_target="tpu_custom_call" | custom-call | tf_op jit(solution)/shard_map/theta/pallas_call | solution.py:428
Async XLA Ops:
  0.6 3.2 %collective-permute-start.3 = (bf16[16,4096]{1,0:T(8,128)(2,1)}, bf16[16,4096]{1,0:T(8,128)(2,1)S(1)}, u32[]{:S(2)}, u32[]{:S(2)}) collective-permute-start(bf16[16,4096]{1,0:T(8,128)(2,1)} %refs_0_.1), channel_id=1, source_target_pairs={{1,0},{0,1},{3,2},{2,3},{5,4},{4,5},{7,6},{6,7},{9,8},{8,9},{11,10... | collective-permute-start | bytes 393224 | tf_op jit(solution)/shard_map/ppermute | solution.py:25
  1.1 6.8 %collective-permute-start = (bf16[16,4096]{1,0:T(8,128)(2,1)}, bf16[16,4096]{1,0:T(8,128)(2,1)S(1)}, u32[]{:S(2)}, u32[]{:S(2)}) collective-permute-start(bf16[16,4096]{1,0:T(8,128)(2,1)} %refs_0_.1), channel_id=1, source_target_pairs={{2,0},{5,1},{0,4},{9,5},{4,8},{13,9},{8,12},{15,13},{12,14},{11,15... | collective-permute-start | bytes 393224 | tf_op jit(solution)/shard_map/ppermute | solution.py:39
  3.8 5.8 %collective-permute-start.4 = (bf16[16,4096]{1,0:T(8,128)(2,1)S(1)}, bf16[16,4096]{1,0:T(8,128)(2,1)S(1)}, u32[]{:S(2)}, u32[]{:S(2)}) collective-permute-start(bf16[16,4096]{1,0:T(8,128)(2,1)S(1)} %collective-permute-done.3.refs_1_), channel_id=1, source_target_pairs={{2,0},{5,1},{0,4},{9,5},{4,8},{13,9},{8,12},{15,13},{12,14},{11,15... | collective-permute-start | bytes 393224 | tf_op jit(solution)/shard_map/ppermute | solution.py:39
  7.9 10.5 %collective-permute-start.13 = (bf16[16,4096]{1,0:T(8,128)(2,1)S(1)}, bf16[16,4096]{1,0:T(8,128)(2,1)S(1)}, u32[]{:S(2)}, u32[]{:S(2)}) collective-permute-start(bf16[16,4096]{1,0:T(8,128)(2,1)S(1)} %collective-permute-done.after.refs_2_), channel_id=1, source_target_pairs={{1,0},{0,1},{3,2},{2,3},{5,4},{4,5},{7,6},{6,7},{9,8},{8,9},{11,10... | collective-permute-start | bytes 393224 | tf_op jit(solution)/shard_map/ppermute | solution.py:25
  8.0 5.5 %collective-permute-start.1 = (bf16[16,4096]{1,0:T(8,128)(2,1)S(1)}, bf16[16,4096]{1,0:T(8,128)(2,1)S(1)}, u32[]{:S(2)}, u32[]{:S(2)}) collective-permute-start(bf16[16,4096]{1,0:T(8,128)(2,1)S(1)} %collective-permute-done.after.refs_2_), channel_id=1, source_target_pairs={{2,0},{5,1},{0,4},{9,5},{4,8},{13,9},{8,12},{15,13},{12,14},{11,15... | collective-permute-start | bytes 393224 | tf_op jit(solution)/shard_map/ppermute | solution.py:39
  9.6 5.5 %collective-permute-start.5 = (bf16[16,4096]{1,0:T(8,128)(2,1)S(1)}, bf16[16,4096]{1,0:T(8,128)(2,1)S(1)}, u32[]{:S(2)}, u32[]{:S(2)}) collective-permute-start(bf16[16,4096]{1,0:T(8,128)(2,1)S(1)} %collective-permute-done.4.refs_3_), channel_id=1, source_target_pairs={{2,0},{5,1},{0,4},{9,5},{4,8},{13,9},{8,12},{15,13},{12,14},{11,15... | collective-permute-start | bytes 393224 | tf_op jit(solution)/shard_map/ppermute | solution.py:39
  13.4 8.1 %copy-start = (bf16[16,4096]{1,0:T(8,128)(2,1)S(1)}, bf16[16,4096]{1,0:T(8,128)(2,1)}, u32[]{:S(2)}) copy-start(bf16[16,4096]{1,0:T(8,128)(2,1)} %refs_0_.1) | copy-start | bytes 393220
  13.4 6.6 %collective-permute-start.14 = (bf16[16,4096]{1,0:T(8,128)(2,1)S(1)}, bf16[16,4096]{1,0:T(8,128)(2,1)S(1)}, u32[]{:S(2)}, u32[]{:S(2)}) collective-permute-start(bf16[16,4096]{1,0:T(8,128)(2,1)S(1)} %collective-permute-done.4.refs_3_), channel_id=1, source_target_pairs={{1,0},{0,1},{3,2},{2,3},{5,4},{4,5},{7,6},{6,7},{9,8},{8,9},{11,10... | collective-permute-start | bytes 393224 | tf_op jit(solution)/shard_map/ppermute | solution.py:25
  13.5 5.0 %collective-permute-start.7 = (bf16[16,4096]{1,0:T(8,128)(2,1)S(1)}, bf16[16,4096]{1,0:T(8,128)(2,1)S(1)}, u32[]{:S(2)}, u32[]{:S(2)}) collective-permute-start(bf16[16,4096]{1,0:T(8,128)(2,1)S(1)} %collective-permute-done.1.after.refs_6_), channel_id=1, source_target_pairs={{2,0},{5,1},{0,4},{9,5},{4,8},{13,9},{8,12},{15,13},{12,14},{11,15... | collective-permute-start | bytes 393224 | tf_op jit(solution)/shard_map/ppermute | solution.py:39
  15.1 6.4 %collective-permute-start.2 = (bf16[16,4096]{1,0:T(8,128)(2,1)S(1)}, bf16[16,4096]{1,0:T(8,128)(2,1)S(1)}, u32[]{:S(2)}, u32[]{:S(2)}) collective-permute-start(bf16[16,4096]{1,0:T(8,128)(2,1)S(1)} %collective-permute-done.1.after.refs_6_), channel_id=1, source_target_pairs={{1,0},{0,1},{3,2},{2,3},{5,4},{4,5},{7,6},{6,7},{9,8},{8,9},{11,10... | collective-permute-start | bytes 393224 | tf_op jit(solution)/shard_map/ppermute | solution.py:25
  15.1 5.0 %collective-permute-start.8 = (bf16[16,4096]{1,0:T(8,128)(2,1)S(1)}, bf16[16,4096]{1,0:T(8,128)(2,1)S(1)}, u32[]{:S(2)}, u32[]{:S(2)}) collective-permute-start(bf16[16,4096]{1,0:T(8,128)(2,1)S(1)} %collective-permute-done.5.refs_7_), channel_id=1, source_target_pairs={{2,0},{5,1},{0,4},{9,5},{4,8},{13,9},{8,12},{15,13},{12,14},{11,15... | collective-permute-start | bytes 393224 | tf_op jit(solution)/shard_map/ppermute | solution.py:39
  18.4 6.5 %collective-permute-start.6 = (bf16[16,4096]{1,0:T(8,128)(2,1)S(1)}, bf16[16,4096]{1,0:T(8,128)(2,1)S(1)}, u32[]{:S(2)}, u32[]{:S(2)}) collective-permute-start(bf16[16,4096]{1,0:T(8,128)(2,1)S(1)} %collective-permute-done.5.refs_7_), channel_id=1, source_target_pairs={{1,0},{0,1},{3,2},{2,3},{5,4},{4,5},{7,6},{6,7},{9,8},{8,9},{11,10... | collective-permute-start | bytes 393224 | tf_op jit(solution)/shard_map/ppermute | solution.py:25
  18.6 6.3 %collective-permute-start.11 = (bf16[16,4096]{1,0:T(8,128)(2,1)S(1)}, bf16[16,4096]{1,0:T(8,128)(2,1)S(1)}, u32[]{:S(2)}, u32[]{:S(2)}) collective-permute-start(bf16[16,4096]{1,0:T(8,128)(2,1)S(1)} %collective-permute-done.7.refs_2_), channel_id=1, source_target_pairs={{2,0},{5,1},{0,4},{9,5},{4,8},{13,9},{8,12},{15,13},{12,14},{11,15... | collective-permute-start | bytes 393224 | tf_op jit(solution)/shard_map/ppermute | solution.py:39
  20.0 4.9 %collective-permute-start.9 = (bf16[16,4096]{1,0:T(8,128)(2,1)S(1)}, bf16[16,4096]{1,0:T(8,128)(2,1)S(1)}, u32[]{:S(2)}, u32[]{:S(2)}) collective-permute-start(bf16[16,4096]{1,0:T(8,128)(2,1)S(1)} %collective-permute-done.7.refs_2_), channel_id=1, source_target_pairs={{1,0},{0,1},{3,2},{2,3},{5,4},{4,5},{7,6},{6,7},{9,8},{8,9},{11,10... | collective-permute-start | bytes 393224 | tf_op jit(solution)/shard_map/ppermute | solution.py:25
  20.1 5.0 %collective-permute-start.12 = (bf16[16,4096]{1,0:T(8,128)(2,1)S(1)}, bf16[16,4096]{1,0:T(8,128)(2,1)S(1)}, u32[]{:S(2)}, u32[]{:S(2)}) collective-permute-start(bf16[16,4096]{1,0:T(8,128)(2,1)S(1)} %collective-permute-done.8.refs_3_), channel_id=1, source_target_pairs={{2,0},{5,1},{0,4},{9,5},{4,8},{13,9},{8,12},{15,13},{12,14},{11,15... | collective-permute-start | bytes 393224 | tf_op jit(solution)/shard_map/ppermute | solution.py:39
  21.5 3.6 %collective-permute-start.10 = (bf16[16,4096]{1,0:T(8,128)(2,1)S(1)}, bf16[16,4096]{1,0:T(8,128)(2,1)S(1)}, u32[]{:S(2)}, u32[]{:S(2)}) collective-permute-start(bf16[16,4096]{1,0:T(8,128)(2,1)S(1)} %collective-permute-done.8.refs_3_), channel_id=1, source_target_pairs={{1,0},{0,1},{3,2},{2,3},{5,4},{4,5},{7,6},{6,7},{9,8},{8,9},{11,10... | collective-permute-start | bytes 393224 | tf_op jit(solution)/shard_map/ppermute | solution.py:25

commit v15 on v14

--- a/solution.py
+++ b/solution.py
@@ -12,7 +12,7 @@
 ROWS = 16
 COLUMNS = 256
 COST = 4 << 30
-SAMPLE = 256
+SAMPLE = 64
 VMEM_BYTES = 12 << 20
 RATIO = 0.1 / 0.05**0.5
 
@@ -75,8 +75,8 @@
     return places
 
 
-def to_all(copies):
-    return lax.all_to_all(copies, "dp", split_axis=0, concat_axis=0, tiled=True)
+def to_all(rows):
+    return lax.all_to_all(rows, "dp", split_axis=0, concat_axis=0, tiled=True)
 
 
 def over_columns(row):
@@ -233,7 +233,7 @@
 
 def replay_kernel(n, half, *refs):
     blocks, (far, weight, cot, weights, one, two) = refs[:half], refs[half : half + 6]
-    (tokens, turned, gate, adjoint, along, across, bend, stats, copies) = refs[half + 9 : half + 18]
+    (tokens, turned, gate, adjoint, along, across, bend, own, deal) = refs[half + 9 : half + 18]
     (scaled, score, g0, g1, a0, a1, b0, b1, sums, upright, sems, tile_sems) = refs[half + 18 :]
     grads, firsts, seconds = (g0, g1), (a0, a1), (b0, b1)
     depth = one.shape[0]
@@ -335,13 +335,15 @@
     b = score[...] * across[...]
     a = score[...] * along[...] + guess * b
     whole = lambda x: jnp.broadcast_to(jnp.sum(x, keepdims=True), (1, count))
-    stats[0:1, :] = RATIO * spread(a)
-    stats[1:2, :] = RATIO**2 * spread(b)
-    stats[2:3, :] = RATIO**2 * whole(sums[0])
-    stats[3:4, :] = RATIO * whole(sums[1])
-    stats[4:8, :] = jnp.broadcast_to(guess, (4, count))
-    for k in range(n):
-        copies[8 * k : 8 * (k + 1), :] = stats[...]
+    own[...] = jnp.broadcast_to(guess, own.shape)
+
+    total = lambda x: jnp.broadcast_to(jnp.sum(x, keepdims=True), (n, 1))
+    deal[...] = jnp.zeros_like(deal)
+    for part, row in enumerate((RATIO * spread(a), RATIO**2 * spread(b))):
+        for k in range(n):
+            deal[k : k + 1, part * height : (part + 1) * height] = row[:, k * height : (k + 1) * height]
+    deal[:, 2 * height : 2 * height + 1] = RATIO**2 * total(sums[0])
+    deal[:, 2 * height + 1 : 2 * height + 2] = RATIO * total(sums[1])
 
 
 def replay_call(n, blocks, adjoint, weight, cot, weights, one, two, tokens, turned, gate):
@@ -364,8 +366,8 @@
             pltpu.VMEM((count, width), jnp.float32),
             pltpu.VMEM((count, width), jnp.float32),
             pltpu.VMEM((count, width), jnp.float32),
-            pltpu.VMEM((8, count), jnp.float32),
-            jax.ShapeDtypeStruct((8 * n, count), jnp.float32),
+            pltpu.VMEM((8, 128), jnp.float32),
+            jax.ShapeDtypeStruct((n, 128), jnp.float32),
         ],
         scratch_shapes=[
             pltpu.VMEM((count, width), jnp.bfloat16),
@@ -391,21 +393,18 @@
     return pltpu.with_memory_space_constraint(x, pltpu.HBM)
 
 
-def theta_kernel(n, entries, everyone, own, along, across, bend, turned, adjoint, theta, scores, ready, sent):
-    total = sum(everyone[8 * k : 8 * (k + 1), :] for k in range(n))
-    sq, cross = total[2:3, 0:1], total[3:4, 0:1]
+def theta_kernel(entries, everyone, own, along, across, bend, turned, adjoint, theta, scores, ready, sent):
+    height = scores.shape[1]
+    total = jnp.sum(everyone[...], axis=0, keepdims=True)
+    sq, cross = total[:, 2 * height : 2 * height + 1], total[:, 2 * height + 1 : 2 * height + 2]
     rms = jnp.sqrt(sq / entries)
     scale = 1.0 / jnp.maximum(1.0, rms)
     bind = jnp.where(rms > 1.0, 1.0 / (rms * rms * rms), 0.0)
     lead = -0.01 * scale
     rest = 0.01 * cross * bind / entries
-    mine = lead * total[0:8, :] + rest * pltpu.roll(total, 7, 0)
-    count = total.shape[1]
-    height = count // n
-    mine = pltpu.roll(mine, lax.rem(count - lax.axis_index("dp") * height, count), 1)
-    scores[...] = mine[0:1, 0:height]
+    scores[...] = lead * total[:, 0:height] + rest * total[:, height : 2 * height]
     lead_here = RATIO * lead
-    rest_here = RATIO**2 * rest + lead_here * own[4:5, 0:1]
+    rest_here = RATIO**2 * rest + lead_here * own[0:1, 0:1]
     bent = (bend[...] * (lead_here * along[...] + rest_here * across[...])).astype(jnp.bfloat16)
 
     def copy(i):
@@ -426,7 +425,7 @@
     count = turned.shape[1]
     vmem = pl.BlockSpec(memory_space=pltpu.VMEM)
     return pl.pallas_call(
-        functools.partial(theta_kernel, n, entries),
+        functools.partial(theta_kernel, entries),
         in_specs=[vmem] * 7,
         out_specs=[pl.BlockSpec(memory_space=pl.ANY), vmem],
         out_shape=[
@@ -449,11 +448,11 @@
     blocks, ((weight_near, cot, weights), one, two) = gather(tokens, n, errands)
     half = len(blocks) // 2
     rows, turned, gate = early_call(blocks[:half], weight_near, cot.shape[0])
-    _, turned, _, adjoint_near, along, across, bend, stats, copies = replay_call(
+    _, turned, _, adjoint_near, along, across, bend, own, deal = replay_call(
         n, blocks[half:], adjoint, weight_near, cot, weights, one, two, rows, turned, gate
     )
-    everyone = to_all(copies)
-    theta_bar, scores = theta_call(n, entries, everyone, stats, along, across, bend, turned, adjoint_near)
+    everyone = to_all(deal)
+    theta_bar, scores = theta_call(n, entries, everyone, own, along, across, bend, turned, adjoint_near)
     return (theta_bar, scores.reshape(-1))
 
 

time: 55.1 us -> 53.7 us (0.975)
  blocking collectives: 12.3 us -> 10.8 us
    all_to_all x1, blocking collectives: 12.3 us -> 10.8 us  [to_all(): return lax.all_to_all(rows, 'dp', split_axis=0, concat_axis=0, tiled=True)]
  transfers between devices with their start and end apart: 15 -> 15, of which waited for: 2 -> 2; matrix products, arithmetic and copies ran while one was open for 0% -> 0% of each run, Pallas kernels for 19% -> 20%
where the time goes in v15:
time: 53.7 us; the launch traced here: 53.4 us
  Pallas kernels  28.1 us (52%)
  starting transfers between devices  13.6 us (25%)
  blocking collectives  10.8 us (20%)
  between operations  0.77 us (1%)
    pallas_call x1, Pallas kernels, replay_call(): pl.pallas_call(functools.partial(replay_kernel, n, half), in_specs=[far]...  13.1 us
    ppermute x8, starting transfers between devices, onward(): return lax.ppermute(value, 'dp', pairs)  12.9 us
    all_to_all x1, blocking collectives, to_all(): return lax.all_to_all(rows, 'dp', split_axis=0, concat_axis=0, tiled=True)  10.8 us
    pallas_call x2, Pallas kernels, fetch_wide(): pl.pallas_call(functools.partial(widen_kernel, factor), in_specs=[pl.Bloc...  4.57 us
    pallas_call x1, Pallas kernels, theta_call(): pl.pallas_call(functools.partial(theta_kernel, entries), in_specs=[vmem]...  4.45 us
    pallas_call x1, Pallas kernels, early_call(): pl.pallas_call(functools.partial(early_kernel, half), in_specs=[pl.BlockS...  3.45 us
    pallas_call x1, Pallas kernels, fetch(): pl.pallas_call(functools.partial(fetch_kernel, n), in_specs=[pl.BlockSpec...  2.52 us
  transfers between devices with their start and end apart: 15, of which 2 were waited for; matrix products, arithmetic and copies ran while one was open for 0% of the time, Pallas kernels for 20%

profile of v15, /device:TPU:0, one launch (start us, length us, event | category | flops | bytes accessed | tf_op | source)
XLA Modules:
  0.0 53.4 jit_solution(12995724164691263797)
XLA Ops:
  0.6 0.5 collective-permute-start.3
  1.1 2.6 %collective-permute-start = (bf16[16,4096]{1,0:T(8,128)(2,1)}, bf16[16,4096]{1,0:T(8,128)(2,1)S(1)}, u32[]{:S(2)}, u32[]{:S(2)}) collective-permute-start(bf16[16,4096]{1,0:T(8,128)(2,1)} %refs_0_.1), channel_id=1, source_target_pairs={{2,0},{5,1},{0,4},{9,5},{4,8},{13,9},{8,12},{15,13},{12,14},{11,15... | collective-permute-start | bytes 393224 | tf_op jit(solution)/shard_map/ppermute | solution.py:39
  3.8 0.0 collective-permute-done.3.refs_1_
  3.8 1.6 %collective-permute-start.4 = (bf16[16,4096]{1,0:T(8,128)(2,1)S(1)}, bf16[16,4096]{1,0:T(8,128)(2,1)S(1)}, u32[]{:S(2)}, u32[]{:S(2)}) collective-permute-start(bf16[16,4096]{1,0:T(8,128)(2,1)S(1)} %collective-permute-done.3.refs_1_), channel_id=1, source_target_pairs={{2,0},{5,1},{0,4},{9,5},{4,8},{13,9},{8,12},{15,13},{12,14},{11,15... | collective-permute-start | bytes 393224 | tf_op jit(solution)/shard_map/ppermute | solution.py:39
  5.4 2.5 %fetch.1 = (bf16[4096,512]{1,0:T(8,128)(2,1)S(1)}, bf16[256,512]{1,0:T(8,128)(2,1)S(1)}, f32[256,128]{1,0:T(8,128)S(1)}) custom-call(bf16[4096,512]{1,0:T(8,128)(2,1)} %far.3, bf16[256,512]{1,0:T(8,128)(2,1)} %far_cot.1, f32[1,256]{1,0:T(1,128)} %bitcast.8, bf16[16,4096]{1,0:T(8,128)(2,1)} %refs_0_.1), custom_call_target="tpu_custom_call" | custom-call | flops 4294967296 | bytes 8388608 | tf_op jit(solution)/shard_map/fetch/pallas_call | solution.py:161
  7.9 0.0 collective-permute-done.after.refs_2_
  7.9 0.1 collective-permute-start.13
  8.0 1.6 %collective-permute-start.1 = (bf16[16,4096]{1,0:T(8,128)(2,1)S(1)}, bf16[16,4096]{1,0:T(8,128)(2,1)S(1)}, u32[]{:S(2)}, u32[]{:S(2)}) collective-permute-start(bf16[16,4096]{1,0:T(8,128)(2,1)S(1)} %collective-permute-done.after.refs_2_), channel_id=1, source_target_pairs={{2,0},{5,1},{0,4},{9,5},{4,8},{13,9},{8,12},{15,13},{12,14},{11,15... | collective-permute-start | bytes 393224 | tf_op jit(solution)/shard_map/ppermute | solution.py:39
  9.6 0.0 collective-permute-done.4.refs_3_
  9.6 1.5 %collective-permute-start.5 = (bf16[16,4096]{1,0:T(8,128)(2,1)S(1)}, bf16[16,4096]{1,0:T(8,128)(2,1)S(1)}, u32[]{:S(2)}, u32[]{:S(2)}) collective-permute-start(bf16[16,4096]{1,0:T(8,128)(2,1)S(1)} %collective-permute-done.4.refs_3_), channel_id=1, source_target_pairs={{2,0},{5,1},{0,4},{9,5},{4,8},{13,9},{8,12},{15,13},{12,14},{11,15... | collective-permute-start | bytes 393224 | tf_op jit(solution)/shard_map/ppermute | solution.py:39
  11.1 2.3 %widen.2.refs_12_ = f32[4096,512]{1,0:T(8,128)S(1)} custom-call(bf16[4096,512]{1,0:T(8,128)(2,1)} %far.4, bf16[16,4096]{1,0:T(8,128)(2,1)S(1)} %collective-permute-done.after.refs_2_), custom_call_target="tpu_custom_call" | custom-call | flops 4294967296 | bytes 8388608 | tf_op jit(solution)/shard_map/widen/pallas_call | solution.py:123
  13.4 0.0 copy-start
  13.4 0.1 collective-permute-start.14
  13.5 0.0 collective-permute-done.1.after.refs_6_
  13.5 1.5 %collective-permute-start.7 = (bf16[16,4096]{1,0:T(8,128)(2,1)S(1)}, bf16[16,4096]{1,0:T(8,128)(2,1)S(1)}, u32[]{:S(2)}, u32[]{:S(2)}) collective-permute-start(bf16[16,4096]{1,0:T(8,128)(2,1)S(1)} %collective-permute-done.1.after.refs_6_), channel_id=1, source_target_pairs={{2,0},{5,1},{0,4},{9,5},{4,8},{13,9},{8,12},{15,13},{12,14},{11,15... | collective-permute-start | bytes 393224 | tf_op jit(solution)/shard_map/ppermute | solution.py:39
  15.1 0.0 collective-permute-start.2
  15.1 0.0 collective-permute-done.5.refs_7_
  15.1 1.0 %collective-permute-start.8 = (bf16[16,4096]{1,0:T(8,128)(2,1)S(1)}, bf16[16,4096]{1,0:T(8,128)(2,1)S(1)}, u32[]{:S(2)}, u32[]{:S(2)}) collective-permute-start(bf16[16,4096]{1,0:T(8,128)(2,1)S(1)} %collective-permute-done.5.refs_7_), channel_id=1, source_target_pairs={{2,0},{5,1},{0,4},{9,5},{4,8},{13,9},{8,12},{15,13},{12,14},{11,15... | collective-permute-start | bytes 393224 | tf_op jit(solution)/shard_map/ppermute | solution.py:39
  16.1 2.3 %widen.3.refs_13_ = f32[4096,512]{1,0:T(8,128)S(1)} custom-call(bf16[4096,512]{1,0:T(8,128)(2,1)} %far.5, bf16[16,4096]{1,0:T(8,128)(2,1)S(1)} %collective-permute-done.1.after.refs_6_), custom_call_target="tpu_custom_call" | custom-call | flops 4294967296 | bytes 8388608 | tf_op jit(solution)/shard_map/widen/pallas_call | solution.py:123
  18.4 0.0 collective-permute-done.13.refs_4_
  18.4 0.1 collective-permute-start.6
  18.5 0.1 collective-permute-done.7.refs_2_
  18.6 1.5 %collective-permute-start.11 = (bf16[16,4096]{1,0:T(8,128)(2,1)S(1)}, bf16[16,4096]{1,0:T(8,128)(2,1)S(1)}, u32[]{:S(2)}, u32[]{:S(2)}) collective-permute-start(bf16[16,4096]{1,0:T(8,128)(2,1)S(1)} %collective-permute-done.7.refs_2_), channel_id=1, source_target_pairs={{2,0},{5,1},{0,4},{9,5},{4,8},{13,9},{8,12},{15,13},{12,14},{11,15... | collective-permute-start | bytes 393224 | tf_op jit(solution)/shard_map/ppermute | solution.py:39
  20.0 0.0 collective-permute-done.14.refs_5_
  20.0 0.0 collective-permute-start.9
  20.1 0.0 collective-permute-done.8.refs_3_
  20.1 1.4 %collective-permute-start.12 = (bf16[16,4096]{1,0:T(8,128)(2,1)S(1)}, bf16[16,4096]{1,0:T(8,128)(2,1)S(1)}, u32[]{:S(2)}, u32[]{:S(2)}) collective-permute-start(bf16[16,4096]{1,0:T(8,128)(2,1)S(1)} %collective-permute-done.8.refs_3_), channel_id=1, source_target_pairs={{2,0},{5,1},{0,4},{9,5},{4,8},{13,9},{8,12},{15,13},{12,14},{11,15... | collective-permute-start | bytes 393224 | tf_op jit(solution)/shard_map/ppermute | solution.py:39
  21.5 0.0 collective-permute-done.2.refs_0_
  21.5 0.0 collective-permute-start.10
  21.5 0.0 copy-done
  21.5 3.4 %early.1 = (bf16[256,4096]{1,0:T(8,128)(2,1)S(1)}, bf16[4096,256]{1,0:T(8,128)(2,1)S(1)}, f32[256,512]{1,0:T(8,128)S(1)}) custom-call(bf16[16,4096]{1,0:T(8,128)(2,1)S(1)} %copy-done, bf16[16,4096]{1,0:T(8,128)(2,1)S(1)} %collective-permute-done.3.refs_1_, bf16[16,4096]{1,0:T(8,128)(2,1)S(1)} %collective-permute-done.after.refs_2_, ...), custom_call_target="tpu_custom_call" | custom-call | flops 4294967296 | bytes 12582912 | tf_op jit(solution)/shard_map/early/pallas_call | solution.py:218
  25.0 0.0 collective-permute-done.6.refs_1_
  25.0 0.0 collective-permute-done.11.refs_6_
  25.0 0.0 collective-permute-done.9.refs_4_
  25.0 0.1 collective-permute-done.12.refs_7_
  25.1 0.0 collective-permute-done.10.refs_5_
  25.1 13.1 %replay.1 = (bf16[256,4096]{1,0:T(8,128)(2,1)S(1)}, bf16[4096,256]{1,0:T(8,128)(2,1)S(1)}, f32[256,512]{1,0:T(8,128)S(1)}, f32[4096,512]{1,0:T(8,128)S(1)}, f32[...) custom-call(bf16[16,4096]{1,0:T(8,128)(2,1)S(1)} %collective-permute, ...), custom_call_target="tpu_custom_call", output_to_operand_aliasing={{0}: (14, {}), {1}: (15, {}), {2}: (16, {})} | custom-call | tf_op jit(solution)/shard_map/replay/pallas_call | solution.py:357
  38.2 10.8 %all_to_all.11 = f32[16,1,128]{2,1,0:T(1,128)S(1)} all-to-all(f32[16,1,128]{2,1,0:T(1,128)S(1)} %bitcast.7), channel_id=1, replica_groups=mesh['group'=2,'dp'=16] {'dp'}, dimensions={0} | all-to-all | bytes 16384 | tf_op jit(solution)/shard_map/all_to_all | solution.py:79
  49.0 4.4 %theta.1 = (f32[4096,512]{1,0:T(8,128)}, f32[1,16]{1,0:T(1,128)}) custom-call(f32[16,128]{1,0:T(8,128)S(1)} %bitcast.6, f32[8,128]{1,0:T(8,128)S(1)} %get-tuple-element.24.own, f32[256,512]{1,0:T(8,128)S(1)} %get-tuple-element.25.along, f32[256,512]{1,0:T(8,128)S(1)} %get-tuple-element.26.across, f32[256,512]{1,0:T(8,128)S(1)} %get-tuple-element.27.bend, ...), custom_call_target="tpu_custom_call" | custom-call | tf_op jit(solution)/shard_map/theta/pallas_call | solution.py:427
Async XLA Ops:
  0.6 3.2 %collective-permute-start.3 = (bf16[16,4096]{1,0:T(8,128)(2,1)}, bf16[16,4096]{1,0:T(8,128)(2,1)S(1)}, u32[]{:S(2)}, u32[]{:S(2)}) collective-permute-start(bf16[16,4096]{1,0:T(8,128)(2,1)} %refs_0_.1), channel_id=1, source_target_pairs={{1,0},{0,1},{3,2},{2,3},{5,4},{4,5},{7,6},{6,7},{9,8},{8,9},{11,10... | collective-permute-start | bytes 393224 | tf_op jit(solution)/shard_map/ppermute | solution.py:25
  1.1 6.8 %collective-permute-start = (bf16[16,4096]{1,0:T(8,128)(2,1)}, bf16[16,4096]{1,0:T(8,128)(2,1)S(1)}, u32[]{:S(2)}, u32[]{:S(2)}) collective-permute-start(bf16[16,4096]{1,0:T(8,128)(2,1)} %refs_0_.1), channel_id=1, source_target_pairs={{2,0},{5,1},{0,4},{9,5},{4,8},{13,9},{8,12},{15,13},{12,14},{11,15... | collective-permute-start | bytes 393224 | tf_op jit(solution)/shard_map/ppermute | solution.py:39
  3.8 5.8 %collective-permute-start.4 = (bf16[16,4096]{1,0:T(8,128)(2,1)S(1)}, bf16[16,4096]{1,0:T(8,128)(2,1)S(1)}, u32[]{:S(2)}, u32[]{:S(2)}) collective-permute-start(bf16[16,4096]{1,0:T(8,128)(2,1)S(1)} %collective-permute-done.3.refs_1_), channel_id=1, source_target_pairs={{2,0},{5,1},{0,4},{9,5},{4,8},{13,9},{8,12},{15,13},{12,14},{11,15... | collective-permute-start | bytes 393224 | tf_op jit(solution)/shard_map/ppermute | solution.py:39
  7.9 10.5 %collective-permute-start.13 = (bf16[16,4096]{1,0:T(8,128)(2,1)S(1)}, bf16[16,4096]{1,0:T(8,128)(2,1)S(1)}, u32[]{:S(2)}, u32[]{:S(2)}) collective-permute-start(bf16[16,4096]{1,0:T(8,128)(2,1)S(1)} %collective-permute-done.after.refs_2_), channel_id=1, source_target_pairs={{1,0},{0,1},{3,2},{2,3},{5,4},{4,5},{7,6},{6,7},{9,8},{8,9},{11,10... | collective-permute-start | bytes 393224 | tf_op jit(solution)/shard_map/ppermute | solution.py:25
  8.0 5.5 %collective-permute-start.1 = (bf16[16,4096]{1,0:T(8,128)(2,1)S(1)}, bf16[16,4096]{1,0:T(8,128)(2,1)S(1)}, u32[]{:S(2)}, u32[]{:S(2)}) collective-permute-start(bf16[16,4096]{1,0:T(8,128)(2,1)S(1)} %collective-permute-done.after.refs_2_), channel_id=1, source_target_pairs={{2,0},{5,1},{0,4},{9,5},{4,8},{13,9},{8,12},{15,13},{12,14},{11,15... | collective-permute-start | bytes 393224 | tf_op jit(solution)/shard_map/ppermute | solution.py:39
  9.6 5.5 %collective-permute-start.5 = (bf16[16,4096]{1,0:T(8,128)(2,1)S(1)}, bf16[16,4096]{1,0:T(8,128)(2,1)S(1)}, u32[]{:S(2)}, u32[]{:S(2)}) collective-permute-start(bf16[16,4096]{1,0:T(8,128)(2,1)S(1)} %collective-permute-done.4.refs_3_), channel_id=1, source_target_pairs={{2,0},{5,1},{0,4},{9,5},{4,8},{13,9},{8,12},{15,13},{12,14},{11,15... | collective-permute-start | bytes 393224 | tf_op jit(solution)/shard_map/ppermute | solution.py:39
  13.4 8.1 %copy-start = (bf16[16,4096]{1,0:T(8,128)(2,1)S(1)}, bf16[16,4096]{1,0:T(8,128)(2,1)}, u32[]{:S(2)}) copy-start(bf16[16,4096]{1,0:T(8,128)(2,1)} %refs_0_.1) | copy-start | bytes 393220
  13.4 6.6 %collective-permute-start.14 = (bf16[16,4096]{1,0:T(8,128)(2,1)S(1)}, bf16[16,4096]{1,0:T(8,128)(2,1)S(1)}, u32[]{:S(2)}, u32[]{:S(2)}) collective-permute-start(bf16[16,4096]{1,0:T(8,128)(2,1)S(1)} %collective-permute-done.4.refs_3_), channel_id=1, source_target_pairs={{1,0},{0,1},{3,2},{2,3},{5,4},{4,5},{7,6},{6,7},{9,8},{8,9},{11,10... | collective-permute-start | bytes 393224 | tf_op jit(solution)/shard_map/ppermute | solution.py:25
  13.5 5.0 %collective-permute-start.7 = (bf16[16,4096]{1,0:T(8,128)(2,1)S(1)}, bf16[16,4096]{1,0:T(8,128)(2,1)S(1)}, u32[]{:S(2)}, u32[]{:S(2)}) collective-permute-start(bf16[16,4096]{1,0:T(8,128)(2,1)S(1)} %collective-permute-done.1.after.refs_6_), channel_id=1, source_target_pairs={{2,0},{5,1},{0,4},{9,5},{4,8},{13,9},{8,12},{15,13},{12,14},{11,15... | collective-permute-start | bytes 393224 | tf_op jit(solution)/shard_map/ppermute | solution.py:39
  15.1 6.4 %collective-permute-start.2 = (bf16[16,4096]{1,0:T(8,128)(2,1)S(1)}, bf16[16,4096]{1,0:T(8,128)(2,1)S(1)}, u32[]{:S(2)}, u32[]{:S(2)}) collective-permute-start(bf16[16,4096]{1,0:T(8,128)(2,1)S(1)} %collective-permute-done.1.after.refs_6_), channel_id=1, source_target_pairs={{1,0},{0,1},{3,2},{2,3},{5,4},{4,5},{7,6},{6,7},{9,8},{8,9},{11,10... | collective-permute-start | bytes 393224 | tf_op jit(solution)/shard_map/ppermute | solution.py:25
  15.1 5.0 %collective-permute-start.8 = (bf16[16,4096]{1,0:T(8,128)(2,1)S(1)}, bf16[16,4096]{1,0:T(8,128)(2,1)S(1)}, u32[]{:S(2)}, u32[]{:S(2)}) collective-permute-start(bf16[16,4096]{1,0:T(8,128)(2,1)S(1)} %collective-permute-done.5.refs_7_), channel_id=1, source_target_pairs={{2,0},{5,1},{0,4},{9,5},{4,8},{13,9},{8,12},{15,13},{12,14},{11,15... | collective-permute-start | bytes 393224 | tf_op jit(solution)/shard_map/ppermute | solution.py:39
  18.4 6.6 %collective-permute-start.6 = (bf16[16,4096]{1,0:T(8,128)(2,1)S(1)}, bf16[16,4096]{1,0:T(8,128)(2,1)S(1)}, u32[]{:S(2)}, u32[]{:S(2)}) collective-permute-start(bf16[16,4096]{1,0:T(8,128)(2,1)S(1)} %collective-permute-done.5.refs_7_), channel_id=1, source_target_pairs={{1,0},{0,1},{3,2},{2,3},{5,4},{4,5},{7,6},{6,7},{9,8},{8,9},{11,10... | collective-permute-start | bytes 393224 | tf_op jit(solution)/shard_map/ppermute | solution.py:25
  18.6 6.4 %collective-permute-start.11 = (bf16[16,4096]{1,0:T(8,128)(2,1)S(1)}, bf16[16,4096]{1,0:T(8,128)(2,1)S(1)}, u32[]{:S(2)}, u32[]{:S(2)}) collective-permute-start(bf16[16,4096]{1,0:T(8,128)(2,1)S(1)} %collective-permute-done.7.refs_2_), channel_id=1, source_target_pairs={{2,0},{5,1},{0,4},{9,5},{4,8},{13,9},{8,12},{15,13},{12,14},{11,15... | collective-permute-start | bytes 393224 | tf_op jit(solution)/shard_map/ppermute | solution.py:39
  20.0 4.9 %collective-permute-start.9 = (bf16[16,4096]{1,0:T(8,128)(2,1)S(1)}, bf16[16,4096]{1,0:T(8,128)(2,1)S(1)}, u32[]{:S(2)}, u32[]{:S(2)}) collective-permute-start(bf16[16,4096]{1,0:T(8,128)(2,1)S(1)} %collective-permute-done.7.refs_2_), channel_id=1, source_target_pairs={{1,0},{0,1},{3,2},{2,3},{5,4},{4,5},{7,6},{6,7},{9,8},{8,9},{11,10... | collective-permute-start | bytes 393224 | tf_op jit(solution)/shard_map/ppermute | solution.py:25
  20.1 5.0 %collective-permute-start.12 = (bf16[16,4096]{1,0:T(8,128)(2,1)S(1)}, bf16[16,4096]{1,0:T(8,128)(2,1)S(1)}, u32[]{:S(2)}, u32[]{:S(2)}) collective-permute-start(bf16[16,4096]{1,0:T(8,128)(2,1)S(1)} %collective-permute-done.8.refs_3_), channel_id=1, source_target_pairs={{2,0},{5,1},{0,4},{9,5},{4,8},{13,9},{8,12},{15,13},{12,14},{11,15... | collective-permute-start | bytes 393224 | tf_op jit(solution)/shard_map/ppermute | solution.py:39
  21.5 3.6 %collective-permute-start.10 = (bf16[16,4096]{1,0:T(8,128)(2,1)S(1)}, bf16[16,4096]{1,0:T(8,128)(2,1)S(1)}, u32[]{:S(2)}, u32[]{:S(2)}) collective-permute-start(bf16[16,4096]{1,0:T(8,128)(2,1)S(1)} %collective-permute-done.8.refs_3_), channel_id=1, source_target_pairs={{1,0},{0,1},{3,2},{2,3},{5,4},{4,5},{7,6},{6,7},{9,8},{8,9},{11,10... | collective-permute-start | bytes 393224 | tf_op jit(solution)/shard_map/ppermute | solution.py:25

commit v16 on v15

--- a/solution.py
+++ b/solution.py
@@ -41,18 +41,17 @@
 
 def gather(tokens, n, errands):
     hops = n // 4
-    done = []
     here = [tokens, swapped(tokens, n, 1)]
     parts = list(here)
     for hop in range(1, hops + 1):
         after = in_hbm(tokens) if hop == 1 else here[0]
         here = [onward(x, n) for x in here]
-        if errands[len(done) :]:
-            done.append(errands[len(done)](after))
+        for errand in errands[hop - 1 : hop]:
+            errand(after)
         parts += here
         if hop < hops:
             parts += [swapped(x, n, 1) for x in here]
-    return parts, done
+    return parts
 
 
 def owners(n):
@@ -95,6 +94,12 @@
     return over, inv, first * inv
 
 
+def quarter_copy(k, far, near, sem):
+    rows = far.shape[0] // 4
+    at = pl.ds(k * rows, rows)
+    return pltpu.make_async_copy(far.at[at, :], near.at[at, :], sem)
+
+
 def fetch_params():
     return {
         "compiler_params": pltpu.CompilerParams(vmem_limit_bytes=6 << 20),
@@ -102,7 +107,7 @@
     }
 
 
-def widen_kernel(factor, far, after, near, raw, sems):
+def widen_kernel(factor, k, far, far_adjoint, _, after, near, adjoint, raw, sems, adjoint_sem):
     tiles = far.shape[0] // TILE
 
     def copy(i):
@@ -110,6 +115,8 @@
 
     for i in range(tiles):
         copy(i).start()
+    adjoint_copy = quarter_copy(k, far_adjoint, adjoint, adjoint_sem.at[0])
+    adjoint_copy.start()
 
     def step(i, _):
         copy(i).wait()
@@ -117,22 +124,32 @@
         return 0
 
     lax.fori_loop(0, tiles, step, 0)
-
-
-def fetch_wide(x, factor, after):
+    adjoint_copy.wait()
+
+
+def fetch_wide(x, factor, k, far_adjoint, adjoint, after):
+    far, vmem = pl.BlockSpec(memory_space=pl.ANY), pl.BlockSpec(memory_space=pltpu.VMEM)
     return pl.pallas_call(
-        functools.partial(widen_kernel, factor),
-        in_specs=[pl.BlockSpec(memory_space=pl.ANY)] * 2,
-        out_specs=pl.BlockSpec(memory_space=pltpu.VMEM),
-        out_shape=pltpu.VMEM(x.shape, jnp.float32),
-        scratch_shapes=[pltpu.VMEM(x.shape, x.dtype), pltpu.SemaphoreType.DMA((x.shape[0] // TILE,))],
+        functools.partial(widen_kernel, factor, k),
+        in_specs=[far, far, vmem, far],
+        out_specs=[vmem] * 2,
+        out_shape=[pltpu.VMEM(x.shape, jnp.float32), pltpu.VMEM(adjoint.shape, adjoint.dtype)],
+        scratch_shapes=[
+            pltpu.VMEM(x.shape, x.dtype),
+            pltpu.SemaphoreType.DMA((x.shape[0] // TILE,)),
+            pltpu.SemaphoreType.DMA((1,)),
+        ],
+        input_output_aliases={2: 1},
         name="widen",
         **fetch_params(),
-    )(in_hbm(x), after)
-
-
-def fetch_kernel(n, far, far_cot, far_weight, after, near, cot, weights, token_weight, upright, sems, cot_sems):
+    )(in_hbm(x), in_hbm(far_adjoint), adjoint, after)
+
+
+def fetch_kernel(n, *refs):
+    (far, far_cot, far_weight, far_adjoint, after, near, cot, weights, adjoint) = refs[:9]
+    (token_weight, upright, sems, cot_sems) = refs[9:]
     height = cot.shape[0] // n
+    adjoint_copy = quarter_copy(0, far_adjoint, adjoint, sems.at[2])
     copy = pltpu.make_async_copy(far, near, sems.at[0])
     weight_copy = pltpu.make_async_copy(far_weight, token_weight, sems.at[1])
     weight_copy.start()
@@ -146,6 +163,7 @@
     ]
     for cot_copy in cot_copies:
         cot_copy.start()
+    adjoint_copy.start()
     weight_copy.wait()
     upright[...] = jnp.broadcast_to(over_columns(token_weight[...]), upright.shape)
     for k, place in enumerate(places):
@@ -153,36 +171,38 @@
     for cot_copy in cot_copies:
         cot_copy.wait()
     copy.wait()
-
-
-def fetch(n, weight, cot, token_weight, after):
+    adjoint_copy.wait()
+
+
+def fetch(n, weight, cot, token_weight, adjoint, after):
     count = cot.shape[0]
     vmem = pl.BlockSpec(memory_space=pltpu.VMEM)
     return pl.pallas_call(
         functools.partial(fetch_kernel, n),
-        in_specs=[pl.BlockSpec(memory_space=pl.ANY)] * 4,
-        out_specs=[vmem] * 3,
+        in_specs=[pl.BlockSpec(memory_space=pl.ANY)] * 5,
+        out_specs=[vmem] * 4,
         out_shape=[
             pltpu.VMEM(weight.shape, weight.dtype),
             pltpu.VMEM(cot.shape, cot.dtype),
             pltpu.VMEM((count, 128), jnp.float32),
+            pltpu.VMEM(adjoint.shape, adjoint.dtype),
         ],
         scratch_shapes=[
             pltpu.VMEM((1, count), jnp.float32),
             pltpu.VMEM((count, 128), jnp.float32),
-            pltpu.SemaphoreType.DMA((2,)),
+            pltpu.SemaphoreType.DMA((3,)),
             pltpu.SemaphoreType.DMA((n,)),
         ],
         name="fetch",
         **fetch_params(),
-    )(in_hbm(weight), in_hbm(cot), in_hbm(token_weight), after)
+    )(in_hbm(weight), in_hbm(cot), in_hbm(token_weight), in_hbm(adjoint), after)
 
 
 def span(i):
     return pl.ds(pl.multiple_of(i * TILE, TILE), TILE)
 
 
-def gate_rows(blocks, first, sems, weight, tokens, turned, gate, beside):
+def gate_rows(blocks, first, sems, weight, tokens, turned, gate):
     height, depth = blocks[0].shape
     count = len(blocks) * height
     rows = slice(first, first + count)
@@ -197,7 +217,6 @@
         copy.wait()
 
     def step(i, _):
-        beside(i)
         here = tokens[rows, span(i)]
         gate[rows, :] += f32dot(here, weight[span(i), :])
         turned[span(i), rows] = here.T
@@ -207,43 +226,46 @@
 
 
 def early_kernel(half, *refs):
-    blocks, weight, (tokens, turned, gate, sems) = refs[:half], refs[half], refs[half + 1 :]
-    gate_rows(blocks, 0, sems, weight, tokens, turned, gate, lambda i: None)
-
-
-def early_call(blocks, weight, count):
+    blocks, (weight, far_adjoint) = refs[:half], refs[half : half + 2]
+    (tokens, turned, gate, adjoint, sems, adjoint_sem) = refs[half + 3 :]
+    adjoint_copy = quarter_copy(3, far_adjoint, adjoint, adjoint_sem.at[0])
+    adjoint_copy.start()
+    gate_rows(blocks, 0, sems, weight, tokens, turned, gate)
+    adjoint_copy.wait()
+
+
+def early_call(blocks, weight, count, far_adjoint, adjoint):
     half = len(blocks)
     depth, width = weight.shape
-    vmem = pl.BlockSpec(memory_space=pltpu.VMEM)
+    far, vmem = pl.BlockSpec(memory_space=pl.ANY), pl.BlockSpec(memory_space=pltpu.VMEM)
     return pl.pallas_call(
         functools.partial(early_kernel, half),
-        in_specs=[pl.BlockSpec(memory_space=pl.ANY)] * half + [vmem],
-        out_specs=[vmem] * 3,
+        in_specs=[far] * half + [vmem, far, vmem],
+        out_specs=[vmem] * 4,
         out_shape=[
             pltpu.VMEM((count, depth), jnp.bfloat16),
             pltpu.VMEM((depth, count), jnp.bfloat16),
             pltpu.VMEM((count, width), jnp.float32),
-        ],
-        scratch_shapes=[pltpu.SemaphoreType.DMA((half,))],
+            pltpu.VMEM(adjoint.shape, adjoint.dtype),
+        ],
+        scratch_shapes=[pltpu.SemaphoreType.DMA((half,)), pltpu.SemaphoreType.DMA((1,))],
+        input_output_aliases={half + 2: 3},
         compiler_params=pltpu.CompilerParams(vmem_limit_bytes=4 << 20),
         cost_estimate=pl.CostEstimate(flops=COST, bytes_accessed=12 << 20, transcendentals=0),
         name="early",
-    )(*blocks, weight)
+    )(*blocks, weight, in_hbm(far_adjoint), adjoint)
 
 
 def replay_kernel(n, half, *refs):
-    blocks, (far, weight, cot, weights, one, two) = refs[:half], refs[half : half + 6]
-    (tokens, turned, gate, adjoint, along, across, bend, own, deal) = refs[half + 9 : half + 18]
-    (scaled, score, g0, g1, a0, a1, b0, b1, sums, upright, sems, tile_sems) = refs[half + 18 :]
+    blocks, (adjoint, weight, cot, weights, one, two) = refs[:half], refs[half : half + 6]
+    (tokens, turned, gate, along, across, bend, own, deal) = refs[half + 9 : half + 17]
+    (scaled, score, g0, g1, a0, a1, b0, b1, sums, upright, sems) = refs[half + 17 :]
     grads, firsts, seconds = (g0, g1), (a0, a1), (b0, b1)
     depth = one.shape[0]
     count, width = scaled.shape
     tiles = depth // TILE
 
-    def tile_copy(i):
-        return pltpu.make_async_copy(far.at[span(i), :], adjoint.at[span(i), :], tile_sems.at[i])
-
-    gate_rows(blocks, count // 2, sems, weight, tokens, turned, gate, lambda i: tile_copy(i).start())
+    gate_rows(blocks, count // 2, sems, weight, tokens, turned, gate)
     for r in range(0, count, 64):
         at = slice(r, r + 64)
         x = gate[at, :]
@@ -273,8 +295,6 @@
                 cols = slice(c, min(c + COLUMNS, width))
                 yield r, cols, grads[slot][r : r + ROWS, cols], one[at, cols], two[at, cols], adjoint[at, cols]
 
-    for i in range(2):
-        tile_copy(i).wait()
     grad_rows(0, 0, 0)
     grad_rows(0, 0, HALF)
     sq, cross = {}, {}
@@ -312,8 +332,6 @@
     body(0, 0, behind=False)
 
     def pair(k, _):
-        tile_copy(2 * k + 2).wait()
-        tile_copy(2 * k + 3).wait()
         body(2 * k + 1, 1)
         body(2 * k + 2, 0)
         return 0
@@ -356,13 +374,12 @@
     block = lambda dtype: pltpu.VMEM((TILE, width), dtype)
     return pl.pallas_call(
         functools.partial(replay_kernel, n, half),
-        in_specs=[far] * (half + 1) + [vmem] * 8,
-        out_specs=[vmem] * 9,
+        in_specs=[far] * half + [vmem] * 9,
+        out_specs=[vmem] * 8,
         out_shape=[
             like(tokens),
             like(turned),
             like(gate),
-            pltpu.VMEM((depth, width), jnp.float32),
             pltpu.VMEM((count, width), jnp.float32),
             pltpu.VMEM((count, width), jnp.float32),
             pltpu.VMEM((count, width), jnp.float32),
@@ -381,12 +398,11 @@
             pltpu.VMEM((2, 8, min(COLUMNS, width)), jnp.float32),
             pltpu.VMEM((count, 128), jnp.float32),
             pltpu.SemaphoreType.DMA((half,)),
-            pltpu.SemaphoreType.DMA((depth // TILE,)),
         ],
         input_output_aliases={half + 6: 0, half + 7: 1, half + 8: 2},
         compiler_params=pltpu.CompilerParams(vmem_limit_bytes=VMEM_BYTES),
         name="replay",
-    )(*blocks, in_hbm(adjoint), weight, cot, weights, one, two, tokens, turned, gate)
+    )(*blocks, adjoint, weight, cot, weights, one, two, tokens, turned, gate)
 
 
 def in_hbm(x):
@@ -440,16 +456,26 @@
 
 def shards(n, tokens, cotangent, token_weight, weight, moment_one, moment_two, adjoint):
     entries = float(adjoint.shape[0] * adjoint.shape[1] * n)
-    errands = [
-        lambda after: fetch(n, weight, cotangent, token_weight.reshape(1, -1), after),
-        lambda after: fetch_wide(moment_one, 9.0, after),
-        lambda after: fetch_wide(moment_two, 19.0, after),
-    ]
-    blocks, ((weight_near, cot, weights), one, two) = gather(tokens, n, errands)
+    near = {}
+
+    def first(after):
+        near["weight"], near["cot"], near["weights"], near["adjoint"] = fetch(
+            n, weight, cotangent, token_weight.reshape(1, -1), adjoint, after
+        )
+
+    def second(after):
+        near["one"], near["adjoint"] = fetch_wide(moment_one, 9.0, 1, adjoint, near["adjoint"], after)
+
+    def third(after):
+        near["two"], near["adjoint"] = fetch_wide(moment_two, 19.0, 2, adjoint, near["adjoint"], after)
+
+    blocks = gather(tokens, n, [first, second, third])
     half = len(blocks) // 2
-    rows, turned, gate = early_call(blocks[:half], weight_near, cot.shape[0])
-    _, turned, _, adjoint_near, along, across, bend, own, deal = replay_call(
-        n, blocks[half:], adjoint, weight_near, cot, weights, one, two, rows, turned, gate
+    rows, turned, gate, adjoint_near = early_call(
+        blocks[:half], near["weight"], cotangent.shape[0], adjoint, near["adjoint"]
+    )
+    _, turned, _, along, across, bend, own, deal = replay_call(
+        n, blocks[half:], adjoint_near, near["weight"], near["cot"], near["weights"], near["one"], near["two"], rows, turned, gate
     )
     everyone = to_all(deal)
     theta_bar, scores = theta_call(n, entries, everyone, own, along, across, bend, turned, adjoint_near)

time: 53.7 us -> 55.1 us (1.026)
  Pallas kernels: 28.1 us -> 30.4 us
  blocking collectives: 10.8 us -> 9.83 us
    pallas_call x3, Pallas kernels: 8.01 us -> 9.37 us  [the longest x2 5.94 us: fetch_wide(): pl.pallas_call(functools.partial(widen_kernel, factor, k), in_specs=[far,...]
    all_to_all x1, blocking collectives: 10.8 us -> 9.83 us  [to_all(): return lax.all_to_all(rows, 'dp', split_axis=0, concat_axis=0, tiled=True)]
    pallas_call x1, Pallas kernels: 2.52 us -> 3.2 us  [fetch(): pl.pallas_call(functools.partial(fetch_kernel, n), in_specs=[pl.BlockSpec...]
    ppermute x8, starting transfers between devices: 12.9 us -> 12.2 us  [onward(): return lax.ppermute(value, 'dp', pairs)]
  transfers between devices with their start and end apart: 15 -> 15, of which waited for: 2 -> 1; matrix products, arithmetic and copies ran while one was open for 0% -> 0% of each run, Pallas kernels for 20% -> 23%
where the time goes in v16:
time: 55.1 us; the launch traced here: 54.8 us
  Pallas kernels  30.4 us (55%)
  starting transfers between devices  13.4 us (24%)
  blocking collectives  9.83 us (18%)
  between operations  0.75 us (1%)
    pallas_call x1, Pallas kernels, replay_call(): pl.pallas_call(functools.partial(replay_kernel, n, half), in_specs=[far]...  13.4 us
    ppermute x8, starting transfers between devices, onward(): return lax.ppermute(value, 'dp', pairs)  12.2 us
    all_to_all x1, blocking collectives, to_all(): return lax.all_to_all(rows, 'dp', split_axis=0, concat_axis=0, tiled=True)  9.83 us
    pallas_call x2, Pallas kernels, fetch_wide(): pl.pallas_call(functools.partial(widen_kernel, factor, k), in_specs=[far,...  5.94 us
    pallas_call x1, Pallas kernels, theta_call(): pl.pallas_call(functools.partial(theta_kernel, entries), in_specs=[vmem]...  4.46 us
    pallas_call x1, Pallas kernels, early_call(): pl.pallas_call(functools.partial(early_kernel, half), in_specs=[far] * ha...  3.43 us
    pallas_call x1, Pallas kernels, fetch(): pl.pallas_call(functools.partial(fetch_kernel, n), in_specs=[pl.BlockSpec...  3.2 us
    ppermute x7, starting transfers between devices, swapped(): return lax.ppermute(value, 'dp', [(d ^ mask, d) for d in range(n)])  1.17 us
  transfers between devices with their start and end apart: 15, of which 1 were waited for; matrix products, arithmetic and copies ran while one was open for 0% of the time, Pallas kernels for 23%

profile of v16, /device:TPU:0, one launch (start us, length us, event | category | flops | bytes accessed | tf_op | source)
XLA Modules:
  0.0 54.8 jit_solution(7556015281486206113)
XLA Ops:
  0.6 0.5 collective-permute-start.3
  1.1 2.6 %collective-permute-start = (bf16[16,4096]{1,0:T(8,128)(2,1)}, bf16[16,4096]{1,0:T(8,128)(2,1)S(1)}, u32[]{:S(2)}, u32[]{:S(2)}) collective-permute-start(bf16[16,4096]{1,0:T(8,128)(2,1)} %refs_0_.3), channel_id=1, source_target_pairs={{2,0},{5,1},{0,4},{9,5},{4,8},{13,9},{8,12},{15,13},{12,14},{11,15... | collective-permute-start | bytes 393224 | tf_op jit(solution)/shard_map/ppermute | solution.py:39
  3.8 0.0 collective-permute-done.3.refs_1_
  3.8 1.6 %collective-permute-start.4 = (bf16[16,4096]{1,0:T(8,128)(2,1)S(1)}, bf16[16,4096]{1,0:T(8,128)(2,1)S(1)}, u32[]{:S(2)}, u32[]{:S(2)}) collective-permute-start(bf16[16,4096]{1,0:T(8,128)(2,1)S(1)} %collective-permute-done.3.refs_1_), channel_id=1, source_target_pairs={{2,0},{5,1},{0,4},{9,5},{4,8},{13,9},{8,12},{15,13},{12,14},{11,15... | collective-permute-start | bytes 393224 | tf_op jit(solution)/shard_map/ppermute | solution.py:39
  5.4 3.2 %fetch.1 = (bf16[4096,512]{1,0:T(8,128)(2,1)S(1)}, bf16[256,512]{1,0:T(8,128)(2,1)S(1)}, f32[256,128]{1,0:T(8,128)S(1)}, f32[4096,512]{1,0:T(8,128)S(1)}) custom-call(bf16[4096,512]{1,0:T(8,128)(2,1)} %refs_0_.2, bf16[256,512]{1,0:T(8,128)(2,1)} %refs_1_.1, f32[1,256]{1,0:T(1,128)} %bitcast.8, f32[4096,512]{1,0:T(8,128)} %refs_9_.1, bf16[16,4096]{1,0:T(8,128)(2,1)} %refs_0_.3), custom_call_target="tpu_custom_call" | custom-call | flops 4294967296 | bytes 8388608 | tf_op jit(solution)/shard_map/fetch/pallas_call | solution.py:180
  8.6 0.0 collective-permute-done.after.refs_2_
  8.6 1.6 %collective-permute-start.1 = (bf16[16,4096]{1,0:T(8,128)(2,1)S(1)}, bf16[16,4096]{1,0:T(8,128)(2,1)S(1)}, u32[]{:S(2)}, u32[]{:S(2)}) collective-permute-start(bf16[16,4096]{1,0:T(8,128)(2,1)S(1)} %collective-permute-done.after.refs_2_), channel_id=1, source_target_pairs={{2,0},{5,1},{0,4},{9,5},{4,8},{13,9},{8,12},{15,13},{12,14},{11,15... | collective-permute-start | bytes 393224 | tf_op jit(solution)/shard_map/ppermute | solution.py:39
  10.2 0.0 collective-permute-start.13
  10.2 0.0 collective-permute-done.4.refs_3_
  10.2 1.5 %collective-permute-start.5 = (bf16[16,4096]{1,0:T(8,128)(2,1)S(1)}, bf16[16,4096]{1,0:T(8,128)(2,1)S(1)}, u32[]{:S(2)}, u32[]{:S(2)}) collective-permute-start(bf16[16,4096]{1,0:T(8,128)(2,1)S(1)} %collective-permute-done.4.refs_3_), channel_id=1, source_target_pairs={{2,0},{5,1},{0,4},{9,5},{4,8},{13,9},{8,12},{15,13},{12,14},{11,15... | collective-permute-start | bytes 393224 | tf_op jit(solution)/shard_map/ppermute | solution.py:39
  11.7 3.0 %widen.2 = (f32[4096,512]{1,0:T(8,128)S(1)}, f32[4096,512]{1,0:T(8,128)S(1)}) custom-call(bf16[4096,512]{1,0:T(8,128)(2,1)} %far.2, f32[4096,512]{1,0:T(8,128)} %refs_9_.1, f32[4096,512]{1,0:T(8,128)S(1)} %get-tuple-element.23._, bf16[16,4096]{1,0:T(8,128)(2,1)S(1)} %collective-permute-done.after.refs_2_), custom_call_target="tpu_custom_call", output_to_operand_aliasing={{1}: (2, {})} | custom-call | flops 4294967296 | bytes 8388608 | tf_op jit(solution)/shard_map/widen/pallas_call | solution.py:132
  14.7 0.1 collective-permute-start.14
  14.8 0.0 collective-permute-done.1.after.refs_6_
  14.8 1.5 %collective-permute-start.7 = (bf16[16,4096]{1,0:T(8,128)(2,1)S(1)}, bf16[16,4096]{1,0:T(8,128)(2,1)S(1)}, u32[]{:S(2)}, u32[]{:S(2)}) collective-permute-start(bf16[16,4096]{1,0:T(8,128)(2,1)S(1)} %collective-permute-done.1.after.refs_6_), channel_id=1, source_target_pairs={{2,0},{5,1},{0,4},{9,5},{4,8},{13,9},{8,12},{15,13},{12,14},{11,15... | collective-permute-start | bytes 393224 | tf_op jit(solution)/shard_map/ppermute | solution.py:39
  16.3 0.0 collective-permute-start.2
  16.3 0.0 collective-permute-done.5.refs_7_
  16.3 0.7 %collective-permute-start.8 = (bf16[16,4096]{1,0:T(8,128)(2,1)S(1)}, bf16[16,4096]{1,0:T(8,128)(2,1)S(1)}, u32[]{:S(2)}, u32[]{:S(2)}) collective-permute-start(bf16[16,4096]{1,0:T(8,128)(2,1)S(1)} %collective-permute-done.5.refs_7_), channel_id=1, source_target_pairs={{2,0},{5,1},{0,4},{9,5},{4,8},{13,9},{8,12},{15,13},{12,14},{11,15... | collective-permute-start | bytes 393224 | tf_op jit(solution)/shard_map/ppermute | solution.py:39
  17.0 0.0 copy-start
  17.0 3.0 %widen.3 = (f32[4096,512]{1,0:T(8,128)S(1)}, f32[4096,512]{1,0:T(8,128)S(1)}) custom-call(bf16[4096,512]{1,0:T(8,128)(2,1)} %far.3, f32[4096,512]{1,0:T(8,128)} %refs_9_.1, f32[4096,512]{1,0:T(8,128)S(1)} %get-tuple-element.24._, bf16[16,4096]{1,0:T(8,128)(2,1)S(1)} %collective-permute-done.1.after.refs_6_), custom_call_target="tpu_custom_call", output_to_operand_aliasing={{1}: (2, {})} | custom-call | flops 4294967296 | bytes 8388608 | tf_op jit(solution)/shard_map/widen/pallas_call | solution.py:132
  20.0 0.0 collective-permute-done.7.refs_2_
  20.0 1.5 %collective-permute-start.11 = (bf16[16,4096]{1,0:T(8,128)(2,1)S(1)}, bf16[16,4096]{1,0:T(8,128)(2,1)S(1)}, u32[]{:S(2)}, u32[]{:S(2)}) collective-permute-start(bf16[16,4096]{1,0:T(8,128)(2,1)S(1)} %collective-permute-done.7.refs_2_), channel_id=1, source_target_pairs={{2,0},{5,1},{0,4},{9,5},{4,8},{13,9},{8,12},{15,13},{12,14},{11,15... | collective-permute-start | bytes 393224 | tf_op jit(solution)/shard_map/ppermute | solution.py:39
  21.6 0.0 collective-permute-done.13.refs_4_
  21.6 0.0 collective-permute-start.9
  21.6 0.0 collective-permute-done.14.refs_5_
  21.6 0.5 collective-permute-start.6
  22.1 0.0 collective-permute-done.8.refs_3_
  22.1 0.1 collective-permute-start.10
  22.2 0.0 collective-permute-done.2.refs_0_
  22.2 1.1 %collective-permute-start.12 = (bf16[16,4096]{1,0:T(8,128)(2,1)S(1)}, bf16[16,4096]{1,0:T(8,128)(2,1)S(1)}, u32[]{:S(2)}, u32[]{:S(2)}) collective-permute-start(bf16[16,4096]{1,0:T(8,128)(2,1)S(1)} %collective-permute-done.8.refs_3_), channel_id=1, source_target_pairs={{2,0},{5,1},{0,4},{9,5},{4,8},{13,9},{8,12},{15,13},{12,14},{11,15... | collective-permute-start | bytes 393224 | tf_op jit(solution)/shard_map/ppermute | solution.py:39
  23.2 0.0 copy-done
  23.2 3.4 %early.1 = (bf16[256,4096]{1,0:T(8,128)(2,1)S(1)}, bf16[4096,256]{1,0:T(8,128)(2,1)S(1)}, f32[256,512]{1,0:T(8,128)S(1)}, f32[4096,512]{1,0:T(8,128)S(1)}) custom-call(bf16[16,4096]{1,0:T(8,128)(2,1)S(1)} %copy-done, bf16[16,4096]{1,0:T(8,128)(2,1)S(1)} %collective-permute-done.3.refs_1_, ...), custom_call_target="tpu_custom_call", output_to_operand_aliasing={{3}: (10, {})} | custom-call | flops 4294967296 | bytes 12582912 | tf_op jit(solution)/shard_map/early/pallas_call | solution.py:241
  26.7 0.0 collective-permute-done.11.refs_6_
  26.7 0.0 collective-permute-done.9.refs_4_
  26.7 0.0 collective-permute-done.6.refs_1_
  26.7 0.0 collective-permute-done.10.refs_5_
  26.7 0.4 collective-permute-done.12.refs_7_
  27.1 13.4 %replay.1 = (bf16[256,4096]{1,0:T(8,128)(2,1)S(1)}, bf16[4096,256]{1,0:T(8,128)(2,1)S(1)}, f32[256,512]{1,0:T(8,128)S(1)}, f32[256,512]{1,0:T(8,128)S(1)}, f32[2...) custom-call(bf16[16,4096]{1,0:T(8,128)(2,1)S(1)} %collective-permute, ...), custom_call_target="tpu_custom_call", output_to_operand_aliasing={{0}: (14, {}), {1}: (15, {}), {2}: (16, {})} | custom-call | tf_op jit(solution)/shard_map/replay/pallas_call | solution.py:375
  40.6 9.8 %all_to_all.11 = f32[16,1,128]{2,1,0:T(1,128)S(1)} all-to-all(f32[16,1,128]{2,1,0:T(1,128)S(1)} %bitcast.7), channel_id=1, replica_groups=mesh['group'=2,'dp'=16] {'dp'}, dimensions={0} | all-to-all | bytes 16384 | tf_op jit(solution)/shard_map/all_to_all | solution.py:78
  50.4 4.5 %theta.1 = (f32[4096,512]{1,0:T(8,128)}, f32[1,16]{1,0:T(1,128)}) custom-call(f32[16,128]{1,0:T(8,128)S(1)} %bitcast.6, f32[8,128]{1,0:T(8,128)S(1)} %get-tuple-element.35.own, f32[256,512]{1,0:T(8,128)S(1)} %get-tuple-element.36.along, f32[256,512]{1,0:T(8,128)S(1)} %get-tuple-element.37.across, f32[256,512]{1,0:T(8,128)S(1)} %get-tuple-element.38.bend, ...), custom_call_target="tpu_custom_call" | custom-call | tf_op jit(solution)/shard_map/theta/pallas_call | solution.py:443
Async XLA Ops:
  0.6 3.2 %collective-permute-start.3 = (bf16[16,4096]{1,0:T(8,128)(2,1)}, bf16[16,4096]{1,0:T(8,128)(2,1)S(1)}, u32[]{:S(2)}, u32[]{:S(2)}) collective-permute-start(bf16[16,4096]{1,0:T(8,128)(2,1)} %refs_0_.3), channel_id=1, source_target_pairs={{1,0},{0,1},{3,2},{2,3},{5,4},{4,5},{7,6},{6,7},{9,8},{8,9},{11,10... | collective-permute-start | bytes 393224 | tf_op jit(solution)/shard_map/ppermute | solution.py:25
  1.1 7.4 %collective-permute-start = (bf16[16,4096]{1,0:T(8,128)(2,1)}, bf16[16,4096]{1,0:T(8,128)(2,1)S(1)}, u32[]{:S(2)}, u32[]{:S(2)}) collective-permute-start(bf16[16,4096]{1,0:T(8,128)(2,1)} %refs_0_.3), channel_id=1, source_target_pairs={{2,0},{5,1},{0,4},{9,5},{4,8},{13,9},{8,12},{15,13},{12,14},{11,15... | collective-permute-start | bytes 393224 | tf_op jit(solution)/shard_map/ppermute | solution.py:39
  3.8 6.4 %collective-permute-start.4 = (bf16[16,4096]{1,0:T(8,128)(2,1)S(1)}, bf16[16,4096]{1,0:T(8,128)(2,1)S(1)}, u32[]{:S(2)}, u32[]{:S(2)}) collective-permute-start(bf16[16,4096]{1,0:T(8,128)(2,1)S(1)} %collective-permute-done.3.refs_1_), channel_id=1, source_target_pairs={{2,0},{5,1},{0,4},{9,5},{4,8},{13,9},{8,12},{15,13},{12,14},{11,15... | collective-permute-start | bytes 393224 | tf_op jit(solution)/shard_map/ppermute | solution.py:39
  8.6 6.2 %collective-permute-start.1 = (bf16[16,4096]{1,0:T(8,128)(2,1)S(1)}, bf16[16,4096]{1,0:T(8,128)(2,1)S(1)}, u32[]{:S(2)}, u32[]{:S(2)}) collective-permute-start(bf16[16,4096]{1,0:T(8,128)(2,1)S(1)} %collective-permute-done.after.refs_2_), channel_id=1, source_target_pairs={{2,0},{5,1},{0,4},{9,5},{4,8},{13,9},{8,12},{15,13},{12,14},{11,15... | collective-permute-start | bytes 393224 | tf_op jit(solution)/shard_map/ppermute | solution.py:39
  10.2 11.4 %collective-permute-start.13 = (bf16[16,4096]{1,0:T(8,128)(2,1)S(1)}, bf16[16,4096]{1,0:T(8,128)(2,1)S(1)}, u32[]{:S(2)}, u32[]{:S(2)}) collective-permute-start(bf16[16,4096]{1,0:T(8,128)(2,1)S(1)} %collective-permute-done.after.refs_2_), channel_id=1, source_target_pairs={{1,0},{0,1},{3,2},{2,3},{5,4},{4,5},{7,6},{6,7},{9,8},{8,9},{11,10... | collective-permute-start | bytes 393224 | tf_op jit(solution)/shard_map/ppermute | solution.py:25
  10.2 6.1 %collective-permute-start.5 = (bf16[16,4096]{1,0:T(8,128)(2,1)S(1)}, bf16[16,4096]{1,0:T(8,128)(2,1)S(1)}, u32[]{:S(2)}, u32[]{:S(2)}) collective-permute-start(bf16[16,4096]{1,0:T(8,128)(2,1)S(1)} %collective-permute-done.4.refs_3_), channel_id=1, source_target_pairs={{2,0},{5,1},{0,4},{9,5},{4,8},{13,9},{8,12},{15,13},{12,14},{11,15... | collective-permute-start | bytes 393224 | tf_op jit(solution)/shard_map/ppermute | solution.py:39
  14.7 6.9 %collective-permute-start.14 = (bf16[16,4096]{1,0:T(8,128)(2,1)S(1)}, bf16[16,4096]{1,0:T(8,128)(2,1)S(1)}, u32[]{:S(2)}, u32[]{:S(2)}) collective-permute-start(bf16[16,4096]{1,0:T(8,128)(2,1)S(1)} %collective-permute-done.4.refs_3_), channel_id=1, source_target_pairs={{1,0},{0,1},{3,2},{2,3},{5,4},{4,5},{7,6},{6,7},{9,8},{8,9},{11,10... | collective-permute-start | bytes 393224 | tf_op jit(solution)/shard_map/ppermute | solution.py:25
  14.8 5.2 %collective-permute-start.7 = (bf16[16,4096]{1,0:T(8,128)(2,1)S(1)}, bf16[16,4096]{1,0:T(8,128)(2,1)S(1)}, u32[]{:S(2)}, u32[]{:S(2)}) collective-permute-start(bf16[16,4096]{1,0:T(8,128)(2,1)S(1)} %collective-permute-done.1.after.refs_6_), channel_id=1, source_target_pairs={{2,0},{5,1},{0,4},{9,5},{4,8},{13,9},{8,12},{15,13},{12,14},{11,15... | collective-permute-start | bytes 393224 | tf_op jit(solution)/shard_map/ppermute | solution.py:39
  16.3 5.8 %collective-permute-start.2 = (bf16[16,4096]{1,0:T(8,128)(2,1)S(1)}, bf16[16,4096]{1,0:T(8,128)(2,1)S(1)}, u32[]{:S(2)}, u32[]{:S(2)}) collective-permute-start(bf16[16,4096]{1,0:T(8,128)(2,1)S(1)} %collective-permute-done.1.after.refs_6_), channel_id=1, source_target_pairs={{1,0},{0,1},{3,2},{2,3},{5,4},{4,5},{7,6},{6,7},{9,8},{8,9},{11,10... | collective-permute-start | bytes 393224 | tf_op jit(solution)/shard_map/ppermute | solution.py:25
  16.3 5.8 %collective-permute-start.8 = (bf16[16,4096]{1,0:T(8,128)(2,1)S(1)}, bf16[16,4096]{1,0:T(8,128)(2,1)S(1)}, u32[]{:S(2)}, u32[]{:S(2)}) collective-permute-start(bf16[16,4096]{1,0:T(8,128)(2,1)S(1)} %collective-permute-done.5.refs_7_), channel_id=1, source_target_pairs={{2,0},{5,1},{0,4},{9,5},{4,8},{13,9},{8,12},{15,13},{12,14},{11,15... | collective-permute-start | bytes 393224 | tf_op jit(solution)/shard_map/ppermute | solution.py:39
  17.0 6.2 %copy-start = (bf16[16,4096]{1,0:T(8,128)(2,1)S(1)}, bf16[16,4096]{1,0:T(8,128)(2,1)}, u32[]{:S(2)}) copy-start(bf16[16,4096]{1,0:T(8,128)(2,1)} %refs_0_.3) | copy-start | bytes 393220
  20.0 6.7 %collective-permute-start.11 = (bf16[16,4096]{1,0:T(8,128)(2,1)S(1)}, bf16[16,4096]{1,0:T(8,128)(2,1)S(1)}, u32[]{:S(2)}, u32[]{:S(2)}) collective-permute-start(bf16[16,4096]{1,0:T(8,128)(2,1)S(1)} %collective-permute-done.7.refs_2_), channel_id=1, source_target_pairs={{2,0},{5,1},{0,4},{9,5},{4,8},{13,9},{8,12},{15,13},{12,14},{11,15... | collective-permute-start | bytes 393224 | tf_op jit(solution)/shard_map/ppermute | solution.py:39
  21.6 5.1 %collective-permute-start.9 = (bf16[16,4096]{1,0:T(8,128)(2,1)S(1)}, bf16[16,4096]{1,0:T(8,128)(2,1)S(1)}, u32[]{:S(2)}, u32[]{:S(2)}) collective-permute-start(bf16[16,4096]{1,0:T(8,128)(2,1)S(1)} %collective-permute-done.7.refs_2_), channel_id=1, source_target_pairs={{1,0},{0,1},{3,2},{2,3},{5,4},{4,5},{7,6},{6,7},{9,8},{8,9},{11,10... | collective-permute-start | bytes 393224 | tf_op jit(solution)/shard_map/ppermute | solution.py:25
  21.6 5.1 %collective-permute-start.6 = (bf16[16,4096]{1,0:T(8,128)(2,1)S(1)}, bf16[16,4096]{1,0:T(8,128)(2,1)S(1)}, u32[]{:S(2)}, u32[]{:S(2)}) collective-permute-start(bf16[16,4096]{1,0:T(8,128)(2,1)S(1)} %collective-permute-done.5.refs_7_), channel_id=1, source_target_pairs={{1,0},{0,1},{3,2},{2,3},{5,4},{4,5},{7,6},{6,7},{9,8},{8,9},{11,10... | collective-permute-start | bytes 393224 | tf_op jit(solution)/shard_map/ppermute | solution.py:25
  22.1 4.6 %collective-permute-start.10 = (bf16[16,4096]{1,0:T(8,128)(2,1)S(1)}, bf16[16,4096]{1,0:T(8,128)(2,1)S(1)}, u32[]{:S(2)}, u32[]{:S(2)}) collective-permute-start(bf16[16,4096]{1,0:T(8,128)(2,1)S(1)} %collective-permute-done.8.refs_3_), channel_id=1, source_target_pairs={{1,0},{0,1},{3,2},{2,3},{5,4},{4,5},{7,6},{6,7},{9,8},{8,9},{11,10... | collective-permute-start | bytes 393224 | tf_op jit(solution)/shard_map/ppermute | solution.py:25
  22.2 5.0 %collective-permute-start.12 = (bf16[16,4096]{1,0:T(8,128)(2,1)S(1)}, bf16[16,4096]{1,0:T(8,128)(2,1)S(1)}, u32[]{:S(2)}, u32[]{:S(2)}) collective-permute-start(bf16[16,4096]{1,0:T(8,128)(2,1)S(1)} %collective-permute-done.8.refs_3_), channel_id=1, source_target_pairs={{2,0},{5,1},{0,4},{9,5},{4,8},{13,9},{8,12},{15,13},{12,14},{11,15... | collective-permute-start | bytes 393224 | tf_op jit(solution)/shard_map/ppermute | solution.py:39

commit v17 on v15

--- a/solution.py
+++ b/solution.py
@@ -182,19 +182,19 @@
     return pl.ds(pl.multiple_of(i * TILE, TILE), TILE)
 
 
-def gate_rows(blocks, first, sems, weight, tokens, turned, gate, beside):
-    height, depth = blocks[0].shape
-    count = len(blocks) * height
-    rows = slice(first, first + count)
+def bring(blocks, first, sems, tokens):
+    height = blocks[0].shape[0]
     copies = [
         pltpu.make_async_copy(ref, tokens.at[pl.ds(first + k * height, height), :], sems.at[k])
         for k, ref in enumerate(blocks)
     ]
     for copy in copies:
         copy.start()
-    gate[rows, :] = jnp.zeros((count, gate.shape[1]), jnp.float32)
-    for copy in copies:
-        copy.wait()
+    return copies
+
+
+def gate_rows(rows, weight, tokens, turned, gate, beside):
+    gate[rows, :] = jnp.zeros((rows.stop - rows.start, gate.shape[1]), jnp.float32)
 
     def step(i, _):
         beside(i)
@@ -203,48 +203,11 @@
         turned[span(i), rows] = here.T
         return 0
 
-    lax.fori_loop(0, depth // TILE, step, 0)
-
-
-def early_kernel(half, *refs):
-    blocks, weight, (tokens, turned, gate, sems) = refs[:half], refs[half], refs[half + 1 :]
-    gate_rows(blocks, 0, sems, weight, tokens, turned, gate, lambda i: None)
-
-
-def early_call(blocks, weight, count):
-    half = len(blocks)
-    depth, width = weight.shape
-    vmem = pl.BlockSpec(memory_space=pltpu.VMEM)
-    return pl.pallas_call(
-        functools.partial(early_kernel, half),
-        in_specs=[pl.BlockSpec(memory_space=pl.ANY)] * half + [vmem],
-        out_specs=[vmem] * 3,
-        out_shape=[
-            pltpu.VMEM((count, depth), jnp.bfloat16),
-            pltpu.VMEM((depth, count), jnp.bfloat16),
-            pltpu.VMEM((count, width), jnp.float32),
-        ],
-        scratch_shapes=[pltpu.SemaphoreType.DMA((half,))],
-        compiler_params=pltpu.CompilerParams(vmem_limit_bytes=4 << 20),
-        cost_estimate=pl.CostEstimate(flops=COST, bytes_accessed=12 << 20, transcendentals=0),
-        name="early",
-    )(*blocks, weight)
-
-
-def replay_kernel(n, half, *refs):
-    blocks, (far, weight, cot, weights, one, two) = refs[:half], refs[half : half + 6]
-    (tokens, turned, gate, adjoint, along, across, bend, own, deal) = refs[half + 9 : half + 18]
-    (scaled, score, g0, g1, a0, a1, b0, b1, sums, upright, sems, tile_sems) = refs[half + 18 :]
-    grads, firsts, seconds = (g0, g1), (a0, a1), (b0, b1)
-    depth = one.shape[0]
-    count, width = scaled.shape
-    tiles = depth // TILE
-
-    def tile_copy(i):
-        return pltpu.make_async_copy(far.at[span(i), :], adjoint.at[span(i), :], tile_sems.at[i])
-
-    gate_rows(blocks, count // 2, sems, weight, tokens, turned, gate, lambda i: tile_copy(i).start())
-    for r in range(0, count, 64):
+    lax.fori_loop(0, weight.shape[0] // TILE, step, 0)
+
+
+def slope_rows(rows, gate, cot, weights, scaled, bend, score):
+    for r in range(rows.start, rows.stop, 64):
         at = slice(r, r + 64)
         x = gate[at, :]
         token_weight = weights[at, 0:1]
@@ -255,6 +218,60 @@
         scaled[at, :] = (token_weight * cot_f * slope).astype(jnp.bfloat16)
         bend[at, :] = token_weight * cot_f * curve
         score[at, :] = cot_f * slope
+
+
+def early_kernel(parts, *refs):
+    blocks, (weight, cot, weights) = refs[:parts], refs[parts : parts + 3]
+    (tokens, turned, gate, scaled, bend, score, sems) = refs[parts + 3 :]
+    rows = slice(0, gate.shape[0] // 2)
+    for copy in bring(blocks, 0, sems, tokens):
+        copy.wait()
+    gate_rows(rows, weight, tokens, turned, gate, lambda i: None)
+    slope_rows(rows, gate, cot, weights, scaled, bend, score)
+
+
+def early_call(blocks, weight, cot, weights):
+    parts = len(blocks)
+    depth, width = weight.shape
+    count = cot.shape[0]
+    vmem = pl.BlockSpec(memory_space=pltpu.VMEM)
+    return pl.pallas_call(
+        functools.partial(early_kernel, parts),
+        in_specs=[pl.BlockSpec(memory_space=pl.ANY)] * parts + [vmem] * 3,
+        out_specs=[vmem] * 6,
+        out_shape=[
+            pltpu.VMEM((count, depth), jnp.bfloat16),
+            pltpu.VMEM((depth, count), jnp.bfloat16),
+            pltpu.VMEM((count, width), jnp.float32),
+            pltpu.VMEM((count, width), jnp.bfloat16),
+            pltpu.VMEM((count, width), jnp.float32),
+            pltpu.VMEM((count, width), jnp.float32),
+        ],
+        scratch_shapes=[pltpu.SemaphoreType.DMA((parts,))],
+        compiler_params=pltpu.CompilerParams(vmem_limit_bytes=4 << 20),
+        cost_estimate=pl.CostEstimate(flops=COST, bytes_accessed=12 << 20, transcendentals=0),
+        name="early",
+    )(*blocks, weight, cot, weights)
+
+
+def replay_kernel(n, half, *refs):
+    blocks, (far, weight, cot, weights, one, two) = refs[:half], refs[half : half + 6]
+    (tokens, turned, gate, scaled, bend, score) = refs[half + 12 : half + 18]
+    (adjoint, along, across, own, deal) = refs[half + 18 : half + 23]
+    (g0, g1, a0, a1, b0, b1, sums, upright, sems, tile_sems) = refs[half + 23 :]
+    grads, firsts, seconds = (g0, g1), (a0, a1), (b0, b1)
+    depth = one.shape[0]
+    count, width = scaled.shape
+    tiles = depth // TILE
+
+    def tile_copy(i):
+        return pltpu.make_async_copy(far.at[span(i), :], adjoint.at[span(i), :], tile_sems.at[i])
+
+    rows = slice(count // 2, count)
+    for copy in bring(blocks, count - half * blocks[0].shape[0], sems, tokens):
+        copy.wait()
+    gate_rows(rows, weight, tokens, turned, gate, lambda i: tile_copy(i).start())
+    slope_rows(rows, gate, cot, weights, scaled, bend, score)
 
     along[...] = jnp.zeros_like(along)
     across[...] = jnp.zeros_like(across)
@@ -346,7 +363,7 @@
     deal[:, 2 * height + 1 : 2 * height + 2] = RATIO * total(sums[1])
 
 
-def replay_call(n, blocks, adjoint, weight, cot, weights, one, two, tokens, turned, gate):
+def replay_call(n, blocks, adjoint, weight, cot, weights, one, two, *rows):
     half = len(blocks)
     depth = one.shape[0]
     count, width = cot.shape
@@ -356,22 +373,17 @@
     block = lambda dtype: pltpu.VMEM((TILE, width), dtype)
     return pl.pallas_call(
         functools.partial(replay_kernel, n, half),
-        in_specs=[far] * (half + 1) + [vmem] * 8,
-        out_specs=[vmem] * 9,
+        in_specs=[far] * (half + 1) + [vmem] * 11,
+        out_specs=[vmem] * 11,
         out_shape=[
-            like(tokens),
-            like(turned),
-            like(gate),
+            *[like(x) for x in rows],
             pltpu.VMEM((depth, width), jnp.float32),
-            pltpu.VMEM((count, width), jnp.float32),
             pltpu.VMEM((count, width), jnp.float32),
             pltpu.VMEM((count, width), jnp.float32),
             pltpu.VMEM((8, 128), jnp.float32),
             jax.ShapeDtypeStruct((n, 128), jnp.float32),
         ],
         scratch_shapes=[
-            pltpu.VMEM((count, width), jnp.bfloat16),
-            pltpu.VMEM((count, width), jnp.float32),
             block(jnp.float32),
             block(jnp.float32),
             block(jnp.bfloat16),
@@ -383,10 +395,10 @@
             pltpu.SemaphoreType.DMA((half,)),
             pltpu.SemaphoreType.DMA((depth // TILE,)),
         ],
-        input_output_aliases={half + 6: 0, half + 7: 1, half + 8: 2},
+        input_output_aliases={half + 6 + k: k for k in range(6)},
         compiler_params=pltpu.CompilerParams(vmem_limit_bytes=VMEM_BYTES),
         name="replay",
-    )(*blocks, in_hbm(adjoint), weight, cot, weights, one, two, tokens, turned, gate)
+    )(*blocks, in_hbm(adjoint), weight, cot, weights, one, two, *rows)
 
 
 def in_hbm(x):
@@ -446,10 +458,10 @@
         lambda after: fetch_wide(moment_two, 19.0, after),
     ]
     blocks, ((weight_near, cot, weights), one, two) = gather(tokens, n, errands)
-    half = len(blocks) // 2
-    rows, turned, gate = early_call(blocks[:half], weight_near, cot.shape[0])
-    _, turned, _, adjoint_near, along, across, bend, own, deal = replay_call(
-        n, blocks[half:], adjoint, weight_near, cot, weights, one, two, rows, turned, gate
+    soon = len(blocks) // 2
+    rows = early_call(blocks[:soon], weight_near, cot, weights)
+    _, turned, _, _, bend, _, adjoint_near, along, across, own, deal = replay_call(
+        n, blocks[soon:], adjoint, weight_near, cot, weights, one, two, *rows
     )
     everyone = to_all(deal)
     theta_bar, scores = theta_call(n, entries, everyone, own, along, across, bend, turned, adjoint_near)

time: 53.7 us -> 53.3 us (level)
  transfers between devices with their start and end apart: 15 -> 15, of which waited for: 2 -> 1; matrix products, arithmetic and copies ran while one was open for 0% -> 0% of each run, Pallas kernels for 20% -> 20%
where the time goes in v17:
time: 53.3 us; the launch traced here: 53 us
  Pallas kernels  27.9 us (52%)
  starting transfers between devices  13.6 us (26%)
  blocking collectives  10.5 us (20%)
  between operations  0.78 us (1%)
    ppermute x8, starting transfers between devices, onward(): return lax.ppermute(value, 'dp', pairs)  12.9 us
    pallas_call x1, Pallas kernels, replay_call(): pl.pallas_call(functools.partial(replay_kernel, n, half), in_specs=[far]...  12.7 us
    all_to_all x1, blocking collectives, to_all(): return lax.all_to_all(rows, 'dp', split_axis=0, concat_axis=0, tiled=True)  10.5 us
    pallas_call x2, Pallas kernels, fetch_wide(): pl.pallas_call(functools.partial(widen_kernel, factor), in_specs=[pl.Bloc...  4.57 us
    pallas_call x1, Pallas kernels, theta_call(): pl.pallas_call(functools.partial(theta_kernel, entries), in_specs=[vmem]...  4.45 us
    pallas_call x1, Pallas kernels, early_call(): pl.pallas_call(functools.partial(early_kernel, parts), in_specs=[pl.Block...  3.68 us
    pallas_call x1, Pallas kernels, fetch(): pl.pallas_call(functools.partial(fetch_kernel, n), in_specs=[pl.BlockSpec...  2.52 us
  transfers between devices with their start and end apart: 15, of which 1 were waited for; matrix products, arithmetic and copies ran while one was open for 0% of the time, Pallas kernels for 20%

profile of v17, /device:TPU:0, one launch (start us, length us, event | category | flops | bytes accessed | tf_op | source)
XLA Modules:
  0.0 53.0 jit_solution(5687762524444367879)
XLA Ops:
  0.6 0.5 collective-permute-start.3
  1.1 2.6 %collective-permute-start = (bf16[16,4096]{1,0:T(8,128)(2,1)}, bf16[16,4096]{1,0:T(8,128)(2,1)S(1)}, u32[]{:S(2)}, u32[]{:S(2)}) collective-permute-start(bf16[16,4096]{1,0:T(8,128)(2,1)} %refs_0_.1), channel_id=1, source_target_pairs={{2,0},{5,1},{0,4},{9,5},{4,8},{13,9},{8,12},{15,13},{12,14},{11,15... | collective-permute-start | bytes 393224 | tf_op jit(solution)/shard_map/ppermute | solution.py:39
  3.8 0.0 collective-permute-done.3.refs_1_
  3.8 1.6 %collective-permute-start.4 = (bf16[16,4096]{1,0:T(8,128)(2,1)S(1)}, bf16[16,4096]{1,0:T(8,128)(2,1)S(1)}, u32[]{:S(2)}, u32[]{:S(2)}) collective-permute-start(bf16[16,4096]{1,0:T(8,128)(2,1)S(1)} %collective-permute-done.3.refs_1_), channel_id=1, source_target_pairs={{2,0},{5,1},{0,4},{9,5},{4,8},{13,9},{8,12},{15,13},{12,14},{11,15... | collective-permute-start | bytes 393224 | tf_op jit(solution)/shard_map/ppermute | solution.py:39
  5.4 2.5 %fetch.1 = (bf16[4096,512]{1,0:T(8,128)(2,1)S(1)}, bf16[256,512]{1,0:T(8,128)(2,1)S(1)}, f32[256,128]{1,0:T(8,128)S(1)}) custom-call(bf16[4096,512]{1,0:T(8,128)(2,1)} %far.3, bf16[256,512]{1,0:T(8,128)(2,1)} %far_cot.1, f32[1,256]{1,0:T(1,128)} %bitcast.8, bf16[16,4096]{1,0:T(8,128)(2,1)} %refs_0_.1), custom_call_target="tpu_custom_call" | custom-call | flops 4294967296 | bytes 8388608 | tf_op jit(solution)/shard_map/fetch/pallas_call | solution.py:161
  7.9 0.0 collective-permute-done.after.refs_2_
  7.9 0.1 collective-permute-start.13
  8.0 1.6 %collective-permute-start.1 = (bf16[16,4096]{1,0:T(8,128)(2,1)S(1)}, bf16[16,4096]{1,0:T(8,128)(2,1)S(1)}, u32[]{:S(2)}, u32[]{:S(2)}) collective-permute-start(bf16[16,4096]{1,0:T(8,128)(2,1)S(1)} %collective-permute-done.after.refs_2_), channel_id=1, source_target_pairs={{2,0},{5,1},{0,4},{9,5},{4,8},{13,9},{8,12},{15,13},{12,14},{11,15... | collective-permute-start | bytes 393224 | tf_op jit(solution)/shard_map/ppermute | solution.py:39
  9.6 0.0 collective-permute-done.4.refs_3_
  9.6 1.5 %collective-permute-start.5 = (bf16[16,4096]{1,0:T(8,128)(2,1)S(1)}, bf16[16,4096]{1,0:T(8,128)(2,1)S(1)}, u32[]{:S(2)}, u32[]{:S(2)}) collective-permute-start(bf16[16,4096]{1,0:T(8,128)(2,1)S(1)} %collective-permute-done.4.refs_3_), channel_id=1, source_target_pairs={{2,0},{5,1},{0,4},{9,5},{4,8},{13,9},{8,12},{15,13},{12,14},{11,15... | collective-permute-start | bytes 393224 | tf_op jit(solution)/shard_map/ppermute | solution.py:39
  11.1 2.3 %widen.2.refs_12_ = f32[4096,512]{1,0:T(8,128)S(1)} custom-call(bf16[4096,512]{1,0:T(8,128)(2,1)} %far.4, bf16[16,4096]{1,0:T(8,128)(2,1)S(1)} %collective-permute-done.after.refs_2_), custom_call_target="tpu_custom_call" | custom-call | flops 4294967296 | bytes 8388608 | tf_op jit(solution)/shard_map/widen/pallas_call | solution.py:123
  13.4 0.0 copy-start
  13.4 0.1 collective-permute-start.14
  13.5 0.0 collective-permute-done.1.after.refs_6_
  13.5 1.5 %collective-permute-start.7 = (bf16[16,4096]{1,0:T(8,128)(2,1)S(1)}, bf16[16,4096]{1,0:T(8,128)(2,1)S(1)}, u32[]{:S(2)}, u32[]{:S(2)}) collective-permute-start(bf16[16,4096]{1,0:T(8,128)(2,1)S(1)} %collective-permute-done.1.after.refs_6_), channel_id=1, source_target_pairs={{2,0},{5,1},{0,4},{9,5},{4,8},{13,9},{8,12},{15,13},{12,14},{11,15... | collective-permute-start | bytes 393224 | tf_op jit(solution)/shard_map/ppermute | solution.py:39
  15.1 0.0 collective-permute-start.2
  15.1 0.0 collective-permute-done.5.refs_7_
  15.1 1.0 %collective-permute-start.8 = (bf16[16,4096]{1,0:T(8,128)(2,1)S(1)}, bf16[16,4096]{1,0:T(8,128)(2,1)S(1)}, u32[]{:S(2)}, u32[]{:S(2)}) collective-permute-start(bf16[16,4096]{1,0:T(8,128)(2,1)S(1)} %collective-permute-done.5.refs_7_), channel_id=1, source_target_pairs={{2,0},{5,1},{0,4},{9,5},{4,8},{13,9},{8,12},{15,13},{12,14},{11,15... | collective-permute-start | bytes 393224 | tf_op jit(solution)/shard_map/ppermute | solution.py:39
  16.1 2.3 %widen.3.refs_13_ = f32[4096,512]{1,0:T(8,128)S(1)} custom-call(bf16[4096,512]{1,0:T(8,128)(2,1)} %far.5, bf16[16,4096]{1,0:T(8,128)(2,1)S(1)} %collective-permute-done.1.after.refs_6_), custom_call_target="tpu_custom_call" | custom-call | flops 4294967296 | bytes 8388608 | tf_op jit(solution)/shard_map/widen/pallas_call | solution.py:123
  18.4 0.0 collective-permute-done.13.refs_4_
  18.4 0.1 collective-permute-start.6
  18.5 0.1 collective-permute-done.7.refs_2_
  18.6 1.5 %collective-permute-start.11 = (bf16[16,4096]{1,0:T(8,128)(2,1)S(1)}, bf16[16,4096]{1,0:T(8,128)(2,1)S(1)}, u32[]{:S(2)}, u32[]{:S(2)}) collective-permute-start(bf16[16,4096]{1,0:T(8,128)(2,1)S(1)} %collective-permute-done.7.refs_2_), channel_id=1, source_target_pairs={{2,0},{5,1},{0,4},{9,5},{4,8},{13,9},{8,12},{15,13},{12,14},{11,15... | collective-permute-start | bytes 393224 | tf_op jit(solution)/shard_map/ppermute | solution.py:39
  20.0 0.0 collective-permute-done.14.refs_5_
  20.0 0.0 collective-permute-start.9
  20.1 0.0 collective-permute-done.8.refs_3_
  20.1 1.4 %collective-permute-start.12 = (bf16[16,4096]{1,0:T(8,128)(2,1)S(1)}, bf16[16,4096]{1,0:T(8,128)(2,1)S(1)}, u32[]{:S(2)}, u32[]{:S(2)}) collective-permute-start(bf16[16,4096]{1,0:T(8,128)(2,1)S(1)} %collective-permute-done.8.refs_3_), channel_id=1, source_target_pairs={{2,0},{5,1},{0,4},{9,5},{4,8},{13,9},{8,12},{15,13},{12,14},{11,15... | collective-permute-start | bytes 393224 | tf_op jit(solution)/shard_map/ppermute | solution.py:39
  21.5 0.0 collective-permute-done.2.refs_0_
  21.5 0.0 collective-permute-start.10
  21.5 0.0 copy-done
  21.5 3.7 %early.1 = (bf16[256,4096]{1,0:T(8,128)(2,1)S(1)}, bf16[4096,256]{1,0:T(8,128)(2,1)S(1)}, f32[256,512]{1,0:T(8,128)S(1)}, bf16[256,512]{1,0:T(8,128)(2,1)S(1)}, ...) custom-call(bf16[16,4096]{1,0:T(8,128)(2,1)S(1)} %copy-done, bf16[16,4096]{1,0:T(8,128)(2,1)S(1)} %collective-permute-done.3.refs_1_, ...), custom_call_target="tpu_custom_call" | custom-call | flops 4294967296 | bytes 12582912 | tf_op jit(solution)/shard_map/early/pallas_call | solution.py:238
  25.2 0.0 collective-permute-done.6.refs_1_
  25.2 0.0 collective-permute-done.11.refs_6_
  25.2 0.0 collective-permute-done.9.refs_4_
  25.2 0.0 collective-permute-done.12.refs_7_
  25.2 0.0 collective-permute-done.10.refs_5_
  25.3 12.7 %replay.1 = (bf16[256,4096]{1,0:T(8,128)(2,1)S(1)}, bf16[4096,256]{1,0:T(8,128)(2,1)S(1)}, f32[256,512]{1,0:T(8,128)S(1)}, bf16[256,512]{1,0:T(8,128)(2,1)S(1)},...) custom-call(bf16[16,4096]{1,0:T(8,128)(2,1)S(1)} %collective-permute, ...), custom_call_target="tpu_custom_call", output_to_operand_aliasing={{0}: (14, {}), {1}: (15, {}), {2}: (16, {}), {3}: (17, {}),... | custom-call | tf_op jit(solution)/shard_map/replay/pallas_call | solution.py:374
  38.0 10.5 %all_to_all.11 = f32[16,1,128]{2,1,0:T(1,128)S(1)} all-to-all(f32[16,1,128]{2,1,0:T(1,128)S(1)} %bitcast.7), channel_id=1, replica_groups=mesh['group'=2,'dp'=16] {'dp'}, dimensions={0} | all-to-all | bytes 16384 | tf_op jit(solution)/shard_map/all_to_all | solution.py:79
  48.5 4.5 %theta.1 = (f32[4096,512]{1,0:T(8,128)}, f32[1,16]{1,0:T(1,128)}) custom-call(f32[16,128]{1,0:T(8,128)S(1)} %bitcast.6, f32[8,128]{1,0:T(8,128)S(1)} %get-tuple-element.30.own, f32[256,512]{1,0:T(8,128)S(1)} %get-tuple-element.31.along, f32[256,512]{1,0:T(8,128)S(1)} %get-tuple-element.32.across, f32[256,512]{1,0:T(8,128)S(1)} %get-tuple-element.33.bend, ...), custom_call_target="tpu_custom_call" | custom-call | tf_op jit(solution)/shard_map/theta/pallas_call | solution.py:439
Async XLA Ops:
  0.6 3.2 %collective-permute-start.3 = (bf16[16,4096]{1,0:T(8,128)(2,1)}, bf16[16,4096]{1,0:T(8,128)(2,1)S(1)}, u32[]{:S(2)}, u32[]{:S(2)}) collective-permute-start(bf16[16,4096]{1,0:T(8,128)(2,1)} %refs_0_.1), channel_id=1, source_target_pairs={{1,0},{0,1},{3,2},{2,3},{5,4},{4,5},{7,6},{6,7},{9,8},{8,9},{11,10... | collective-permute-start | bytes 393224 | tf_op jit(solution)/shard_map/ppermute | solution.py:25
  1.1 6.8 %collective-permute-start = (bf16[16,4096]{1,0:T(8,128)(2,1)}, bf16[16,4096]{1,0:T(8,128)(2,1)S(1)}, u32[]{:S(2)}, u32[]{:S(2)}) collective-permute-start(bf16[16,4096]{1,0:T(8,128)(2,1)} %refs_0_.1), channel_id=1, source_target_pairs={{2,0},{5,1},{0,4},{9,5},{4,8},{13,9},{8,12},{15,13},{12,14},{11,15... | collective-permute-start | bytes 393224 | tf_op jit(solution)/shard_map/ppermute | solution.py:39
  3.8 5.8 %collective-permute-start.4 = (bf16[16,4096]{1,0:T(8,128)(2,1)S(1)}, bf16[16,4096]{1,0:T(8,128)(2,1)S(1)}, u32[]{:S(2)}, u32[]{:S(2)}) collective-permute-start(bf16[16,4096]{1,0:T(8,128)(2,1)S(1)} %collective-permute-done.3.refs_1_), channel_id=1, source_target_pairs={{2,0},{5,1},{0,4},{9,5},{4,8},{13,9},{8,12},{15,13},{12,14},{11,15... | collective-permute-start | bytes 393224 | tf_op jit(solution)/shard_map/ppermute | solution.py:39
  7.9 10.5 %collective-permute-start.13 = (bf16[16,4096]{1,0:T(8,128)(2,1)S(1)}, bf16[16,4096]{1,0:T(8,128)(2,1)S(1)}, u32[]{:S(2)}, u32[]{:S(2)}) collective-permute-start(bf16[16,4096]{1,0:T(8,128)(2,1)S(1)} %collective-permute-done.after.refs_2_), channel_id=1, source_target_pairs={{1,0},{0,1},{3,2},{2,3},{5,4},{4,5},{7,6},{6,7},{9,8},{8,9},{11,10... | collective-permute-start | bytes 393224 | tf_op jit(solution)/shard_map/ppermute | solution.py:25
  8.0 5.5 %collective-permute-start.1 = (bf16[16,4096]{1,0:T(8,128)(2,1)S(1)}, bf16[16,4096]{1,0:T(8,128)(2,1)S(1)}, u32[]{:S(2)}, u32[]{:S(2)}) collective-permute-start(bf16[16,4096]{1,0:T(8,128)(2,1)S(1)} %collective-permute-done.after.refs_2_), channel_id=1, source_target_pairs={{2,0},{5,1},{0,4},{9,5},{4,8},{13,9},{8,12},{15,13},{12,14},{11,15... | collective-permute-start | bytes 393224 | tf_op jit(solution)/shard_map/ppermute | solution.py:39
  9.6 5.5 %collective-permute-start.5 = (bf16[16,4096]{1,0:T(8,128)(2,1)S(1)}, bf16[16,4096]{1,0:T(8,128)(2,1)S(1)}, u32[]{:S(2)}, u32[]{:S(2)}) collective-permute-start(bf16[16,4096]{1,0:T(8,128)(2,1)S(1)} %collective-permute-done.4.refs_3_), channel_id=1, source_target_pairs={{2,0},{5,1},{0,4},{9,5},{4,8},{13,9},{8,12},{15,13},{12,14},{11,15... | collective-permute-start | bytes 393224 | tf_op jit(solution)/shard_map/ppermute | solution.py:39
  13.4 8.1 %copy-start = (bf16[16,4096]{1,0:T(8,128)(2,1)S(1)}, bf16[16,4096]{1,0:T(8,128)(2,1)}, u32[]{:S(2)}) copy-start(bf16[16,4096]{1,0:T(8,128)(2,1)} %refs_0_.1) | copy-start | bytes 393220
  13.4 6.6 %collective-permute-start.14 = (bf16[16,4096]{1,0:T(8,128)(2,1)S(1)}, bf16[16,4096]{1,0:T(8,128)(2,1)S(1)}, u32[]{:S(2)}, u32[]{:S(2)}) collective-permute-start(bf16[16,4096]{1,0:T(8,128)(2,1)S(1)} %collective-permute-done.4.refs_3_), channel_id=1, source_target_pairs={{1,0},{0,1},{3,2},{2,3},{5,4},{4,5},{7,6},{6,7},{9,8},{8,9},{11,10... | collective-permute-start | bytes 393224 | tf_op jit(solution)/shard_map/ppermute | solution.py:25
  13.5 5.0 %collective-permute-start.7 = (bf16[16,4096]{1,0:T(8,128)(2,1)S(1)}, bf16[16,4096]{1,0:T(8,128)(2,1)S(1)}, u32[]{:S(2)}, u32[]{:S(2)}) collective-permute-start(bf16[16,4096]{1,0:T(8,128)(2,1)S(1)} %collective-permute-done.1.after.refs_6_), channel_id=1, source_target_pairs={{2,0},{5,1},{0,4},{9,5},{4,8},{13,9},{8,12},{15,13},{12,14},{11,15... | collective-permute-start | bytes 393224 | tf_op jit(solution)/shard_map/ppermute | solution.py:39
  15.1 6.4 %collective-permute-start.2 = (bf16[16,4096]{1,0:T(8,128)(2,1)S(1)}, bf16[16,4096]{1,0:T(8,128)(2,1)S(1)}, u32[]{:S(2)}, u32[]{:S(2)}) collective-permute-start(bf16[16,4096]{1,0:T(8,128)(2,1)S(1)} %collective-permute-done.1.after.refs_6_), channel_id=1, source_target_pairs={{1,0},{0,1},{3,2},{2,3},{5,4},{4,5},{7,6},{6,7},{9,8},{8,9},{11,10... | collective-permute-start | bytes 393224 | tf_op jit(solution)/shard_map/ppermute | solution.py:25
  15.1 5.0 %collective-permute-start.8 = (bf16[16,4096]{1,0:T(8,128)(2,1)S(1)}, bf16[16,4096]{1,0:T(8,128)(2,1)S(1)}, u32[]{:S(2)}, u32[]{:S(2)}) collective-permute-start(bf16[16,4096]{1,0:T(8,128)(2,1)S(1)} %collective-permute-done.5.refs_7_), channel_id=1, source_target_pairs={{2,0},{5,1},{0,4},{9,5},{4,8},{13,9},{8,12},{15,13},{12,14},{11,15... | collective-permute-start | bytes 393224 | tf_op jit(solution)/shard_map/ppermute | solution.py:39
  18.4 6.8 %collective-permute-start.6 = (bf16[16,4096]{1,0:T(8,128)(2,1)S(1)}, bf16[16,4096]{1,0:T(8,128)(2,1)S(1)}, u32[]{:S(2)}, u32[]{:S(2)}) collective-permute-start(bf16[16,4096]{1,0:T(8,128)(2,1)S(1)} %collective-permute-done.5.refs_7_), channel_id=1, source_target_pairs={{1,0},{0,1},{3,2},{2,3},{5,4},{4,5},{7,6},{6,7},{9,8},{8,9},{11,10... | collective-permute-start | bytes 393224 | tf_op jit(solution)/shard_map/ppermute | solution.py:25
  18.6 6.7 %collective-permute-start.11 = (bf16[16,4096]{1,0:T(8,128)(2,1)S(1)}, bf16[16,4096]{1,0:T(8,128)(2,1)S(1)}, u32[]{:S(2)}, u32[]{:S(2)}) collective-permute-start(bf16[16,4096]{1,0:T(8,128)(2,1)S(1)} %collective-permute-done.7.refs_2_), channel_id=1, source_target_pairs={{2,0},{5,1},{0,4},{9,5},{4,8},{13,9},{8,12},{15,13},{12,14},{11,15... | collective-permute-start | bytes 393224 | tf_op jit(solution)/shard_map/ppermute | solution.py:39
  20.0 5.2 %collective-permute-start.9 = (bf16[16,4096]{1,0:T(8,128)(2,1)S(1)}, bf16[16,4096]{1,0:T(8,128)(2,1)S(1)}, u32[]{:S(2)}, u32[]{:S(2)}) collective-permute-start(bf16[16,4096]{1,0:T(8,128)(2,1)S(1)} %collective-permute-done.7.refs_2_), channel_id=1, source_target_pairs={{1,0},{0,1},{3,2},{2,3},{5,4},{4,5},{7,6},{6,7},{9,8},{8,9},{11,10... | collective-permute-start | bytes 393224 | tf_op jit(solution)/shard_map/ppermute | solution.py:25
  20.1 5.2 %collective-permute-start.12 = (bf16[16,4096]{1,0:T(8,128)(2,1)S(1)}, bf16[16,4096]{1,0:T(8,128)(2,1)S(1)}, u32[]{:S(2)}, u32[]{:S(2)}) collective-permute-start(bf16[16,4096]{1,0:T(8,128)(2,1)S(1)} %collective-permute-done.8.refs_3_), channel_id=1, source_target_pairs={{2,0},{5,1},{0,4},{9,5},{4,8},{13,9},{8,12},{15,13},{12,14},{11,15... | collective-permute-start | bytes 393224 | tf_op jit(solution)/shard_map/ppermute | solution.py:39
  21.5 3.7 %collective-permute-start.10 = (bf16[16,4096]{1,0:T(8,128)(2,1)S(1)}, bf16[16,4096]{1,0:T(8,128)(2,1)S(1)}, u32[]{:S(2)}, u32[]{:S(2)}) collective-permute-start(bf16[16,4096]{1,0:T(8,128)(2,1)S(1)} %collective-permute-done.8.refs_3_), channel_id=1, source_target_pairs={{1,0},{0,1},{3,2},{2,3},{5,4},{4,5},{7,6},{6,7},{9,8},{8,9},{11,10... | collective-permute-start | bytes 393224 | tf_op jit(solution)/shard_map/ppermute | solution.py:25

commit v18 on v17

--- a/solution.py
+++ b/solution.py
@@ -43,16 +43,16 @@
     hops = n // 4
     done = []
     here = [tokens, swapped(tokens, n, 1)]
-    parts = list(here)
+    parts, others = list(here), []
     for hop in range(1, hops + 1):
         after = in_hbm(tokens) if hop == 1 else here[0]
         here = [onward(x, n) for x in here]
         if errands[len(done) :]:
             done.append(errands[len(done)](after))
-        parts += here
         if hop < hops:
-            parts += [swapped(x, n, 1) for x in here]
-    return parts, done
+            parts += here
+            others += [swapped(x, n, 1) for x in here]
+    return parts + others + here, done
 
 
 def owners(n):
@@ -61,11 +61,9 @@
     chip, core = me >> 1, me & 1
     at = jnp.where(chip & 1 == 0, chip >> 1, chips - 1 - (chip >> 1))
     way = 2 * core - 1
-    blocks = [(0, core)]
-    for hop in range(1, chips // 2 + 1):
-        blocks.append((way * hop, core))
-        if 2 * hop < chips:
-            blocks.append((-way * hop, 1 - core))
+    hops = range(1, chips // 2)
+    blocks = [(0, core), *[(way * hop, core) for hop in hops], *[(-way * hop, 1 - core) for hop in hops]]
+    blocks.append((way * (chips // 2), core))
     places = []
     for step, first in blocks:
         there = at + step

time: 53.3 us -> 53.3 us (level)
  transfers between devices with their start and end apart: 15 -> 15, of which waited for: 1 -> 0; matrix products, arithmetic and copies ran while one was open for 0% -> 0% of each run, Pallas kernels for 20% -> 20%
where the time goes in v18:
time: 53.3 us; the launch traced here: 53 us
  Pallas kernels  27.9 us (52%)
  starting transfers between devices  13.6 us (26%)
  blocking collectives  10.6 us (20%)
  between operations  0.78 us (1%)
    ppermute x8, starting transfers between devices, onward(): return lax.ppermute(value, 'dp', pairs)  12.9 us
    pallas_call x1, Pallas kernels, replay_call(): pl.pallas_call(functools.partial(replay_kernel, n, half), in_specs=[far]...  12.7 us
    all_to_all x1, blocking collectives, to_all(): return lax.all_to_all(rows, 'dp', split_axis=0, concat_axis=0, tiled=True)  10.6 us
    pallas_call x2, Pallas kernels, fetch_wide(): pl.pallas_call(functools.partial(widen_kernel, factor), in_specs=[pl.Bloc...  4.57 us
    pallas_call x1, Pallas kernels, theta_call(): pl.pallas_call(functools.partial(theta_kernel, entries), in_specs=[vmem]...  4.45 us
    pallas_call x1, Pallas kernels, early_call(): pl.pallas_call(functools.partial(early_kernel, parts), in_specs=[pl.Block...  3.68 us
    pallas_call x1, Pallas kernels, fetch(): pl.pallas_call(functools.partial(fetch_kernel, n), in_specs=[pl.BlockSpec...  2.52 us
  transfers between devices with their start and end apart: 15, of which 0 were waited for; matrix products, arithmetic and copies ran while one was open for 0% of the time, Pallas kernels for 20%

profile of v18, /device:TPU:0, one launch (start us, length us, event | category | flops | bytes accessed | tf_op | source)
XLA Modules:
  0.0 53.0 jit_solution(2974219882108363863)
XLA Ops:
  0.6 0.5 collective-permute-start.2
  1.1 2.6 %collective-permute-start = (bf16[16,4096]{1,0:T(8,128)(2,1)}, bf16[16,4096]{1,0:T(8,128)(2,1)S(1)}, u32[]{:S(2)}, u32[]{:S(2)}) collective-permute-start(bf16[16,4096]{1,0:T(8,128)(2,1)} %refs_0_.1), channel_id=1, source_target_pairs={{2,0},{5,1},{0,4},{9,5},{4,8},{13,9},{8,12},{15,13},{12,14},{11,15... | collective-permute-start | bytes 393224 | tf_op jit(solution)/shard_map/ppermute | solution.py:39
  3.8 0.0 collective-permute-done.2.refs_1_
  3.8 1.6 %collective-permute-start.3 = (bf16[16,4096]{1,0:T(8,128)(2,1)S(1)}, bf16[16,4096]{1,0:T(8,128)(2,1)S(1)}, u32[]{:S(2)}, u32[]{:S(2)}) collective-permute-start(bf16[16,4096]{1,0:T(8,128)(2,1)S(1)} %collective-permute-done.2.refs_1_), channel_id=1, source_target_pairs={{2,0},{5,1},{0,4},{9,5},{4,8},{13,9},{8,12},{15,13},{12,14},{11,15... | collective-permute-start | bytes 393224 | tf_op jit(solution)/shard_map/ppermute | solution.py:39
  5.4 2.5 %fetch.1 = (bf16[4096,512]{1,0:T(8,128)(2,1)S(1)}, bf16[256,512]{1,0:T(8,128)(2,1)S(1)}, f32[256,128]{1,0:T(8,128)S(1)}) custom-call(bf16[4096,512]{1,0:T(8,128)(2,1)} %far.3, bf16[256,512]{1,0:T(8,128)(2,1)} %far_cot.1, f32[1,256]{1,0:T(1,128)} %bitcast.8, bf16[16,4096]{1,0:T(8,128)(2,1)} %refs_0_.1), custom_call_target="tpu_custom_call" | custom-call | flops 4294967296 | bytes 8388608 | tf_op jit(solution)/shard_map/fetch/pallas_call | solution.py:159
  7.9 0.0 collective-permute-done.after.refs_2_
  7.9 1.6 %collective-permute-start.5 = (bf16[16,4096]{1,0:T(8,128)(2,1)S(1)}, bf16[16,4096]{1,0:T(8,128)(2,1)S(1)}, u32[]{:S(2)}, u32[]{:S(2)}) collective-permute-start(bf16[16,4096]{1,0:T(8,128)(2,1)S(1)} %collective-permute-done.after.refs_2_), channel_id=1, source_target_pairs={{2,0},{5,1},{0,4},{9,5},{4,8},{13,9},{8,12},{15,13},{12,14},{11,15... | collective-permute-start | bytes 393224 | tf_op jit(solution)/shard_map/ppermute | solution.py:39
  9.5 0.0 collective-permute-start.1
  9.5 0.0 collective-permute-done.3.refs_3_
  9.5 1.5 %collective-permute-start.7 = (bf16[16,4096]{1,0:T(8,128)(2,1)S(1)}, bf16[16,4096]{1,0:T(8,128)(2,1)S(1)}, u32[]{:S(2)}, u32[]{:S(2)}) collective-permute-start(bf16[16,4096]{1,0:T(8,128)(2,1)S(1)} %collective-permute-done.3.refs_3_), channel_id=1, source_target_pairs={{2,0},{5,1},{0,4},{9,5},{4,8},{13,9},{8,12},{15,13},{12,14},{11,15... | collective-permute-start | bytes 393224 | tf_op jit(solution)/shard_map/ppermute | solution.py:39
  11.1 2.3 %widen.2.refs_12_ = f32[4096,512]{1,0:T(8,128)S(1)} custom-call(bf16[4096,512]{1,0:T(8,128)(2,1)} %far.4, bf16[16,4096]{1,0:T(8,128)(2,1)S(1)} %collective-permute-done.after.refs_2_), custom_call_target="tpu_custom_call" | custom-call | flops 4294967296 | bytes 8388608 | tf_op jit(solution)/shard_map/widen/pallas_call | solution.py:121
  13.4 0.0 copy-start
  13.4 0.1 collective-permute-start.4
  13.4 0.0 collective-permute-done.5.after.refs_4_
  13.5 1.5 %collective-permute-start.9 = (bf16[16,4096]{1,0:T(8,128)(2,1)S(1)}, bf16[16,4096]{1,0:T(8,128)(2,1)S(1)}, u32[]{:S(2)}, u32[]{:S(2)}) collective-permute-start(bf16[16,4096]{1,0:T(8,128)(2,1)S(1)} %collective-permute-done.5.after.refs_4_), channel_id=1, source_target_pairs={{2,0},{5,1},{0,4},{9,5},{4,8},{13,9},{8,12},{15,13},{12,14},{11,15... | collective-permute-start | bytes 393224 | tf_op jit(solution)/shard_map/ppermute | solution.py:39
  15.0 0.0 collective-permute-start.6
  15.0 0.0 collective-permute-done.7.refs_5_
  15.0 1.1 %collective-permute-start.11 = (bf16[16,4096]{1,0:T(8,128)(2,1)S(1)}, bf16[16,4096]{1,0:T(8,128)(2,1)S(1)}, u32[]{:S(2)}, u32[]{:S(2)}) collective-permute-start(bf16[16,4096]{1,0:T(8,128)(2,1)S(1)} %collective-permute-done.7.refs_5_), channel_id=1, source_target_pairs={{2,0},{5,1},{0,4},{9,5},{4,8},{13,9},{8,12},{15,13},{12,14},{11,15... | collective-permute-start | bytes 393224 | tf_op jit(solution)/shard_map/ppermute | solution.py:39
  16.1 2.3 %widen.3.refs_13_ = f32[4096,512]{1,0:T(8,128)S(1)} custom-call(bf16[4096,512]{1,0:T(8,128)(2,1)} %far.5, bf16[16,4096]{1,0:T(8,128)(2,1)S(1)} %collective-permute-done.5.after.refs_4_), custom_call_target="tpu_custom_call" | custom-call | flops 4294967296 | bytes 8388608 | tf_op jit(solution)/shard_map/widen/pallas_call | solution.py:121
  18.4 0.0 collective-permute-done.1.refs_0_
  18.4 0.1 collective-permute-start.8
  18.5 0.0 collective-permute-done.9.refs_6_
  18.5 1.5 %collective-permute-start.13 = (bf16[16,4096]{1,0:T(8,128)(2,1)S(1)}, bf16[16,4096]{1,0:T(8,128)(2,1)S(1)}, u32[]{:S(2)}, u32[]{:S(2)}) collective-permute-start(bf16[16,4096]{1,0:T(8,128)(2,1)S(1)} %collective-permute-done.9.refs_6_), channel_id=1, source_target_pairs={{2,0},{5,1},{0,4},{9,5},{4,8},{13,9},{8,12},{15,13},{12,14},{11,15... | collective-permute-start | bytes 393224 | tf_op jit(solution)/shard_map/ppermute | solution.py:39
  20.0 0.0 collective-permute-done.4.refs_1_
  20.0 0.0 collective-permute-start.10
  20.0 0.0 collective-permute-done.11.refs_7_
  20.0 1.4 %collective-permute-start.14 = (bf16[16,4096]{1,0:T(8,128)(2,1)S(1)}, bf16[16,4096]{1,0:T(8,128)(2,1)S(1)}, u32[]{:S(2)}, u32[]{:S(2)}) collective-permute-start(bf16[16,4096]{1,0:T(8,128)(2,1)S(1)} %collective-permute-done.11.refs_7_), channel_id=1, source_target_pairs={{2,0},{5,1},{0,4},{9,5},{4,8},{13,9},{8,12},{15,13},{12,14},{11,15... | collective-permute-start | bytes 393224 | tf_op jit(solution)/shard_map/ppermute | solution.py:39
  21.4 0.0 collective-permute-done.6.refs_2_
  21.4 0.0 collective-permute-start.12
  21.4 0.0 copy-done
  21.4 3.7 %early.1 = (bf16[256,4096]{1,0:T(8,128)(2,1)S(1)}, bf16[4096,256]{1,0:T(8,128)(2,1)S(1)}, f32[256,512]{1,0:T(8,128)S(1)}, bf16[256,512]{1,0:T(8,128)(2,1)S(1)}, ...) custom-call(bf16[16,4096]{1,0:T(8,128)(2,1)S(1)} %copy-done, bf16[16,4096]{1,0:T(8,128)(2,1)S(1)} %collective-permute-done.2.refs_1_, ...), custom_call_target="tpu_custom_call" | custom-call | flops 4294967296 | bytes 12582912 | tf_op jit(solution)/shard_map/early/pallas_call | solution.py:236
  25.1 0.0 collective-permute-done.8.refs_3_
  25.1 0.0 collective-permute-done.13.refs_6_
  25.1 0.0 collective-permute-done.10.refs_4_
  25.2 0.0 collective-permute-done.14.refs_7_
  25.2 0.0 collective-permute-done.12.refs_5_
  25.2 12.7 %replay.1 = (bf16[256,4096]{1,0:T(8,128)(2,1)S(1)}, bf16[4096,256]{1,0:T(8,128)(2,1)S(1)}, f32[256,512]{1,0:T(8,128)S(1)}, bf16[256,512]{1,0:T(8,128)(2,1)S(1)},...) custom-call(bf16[16,4096]{1,0:T(8,128)(2,1)S(1)} %collective-permute, ...), custom_call_target="tpu_custom_call", output_to_operand_aliasing={{0}: (14, {}), {1}: (15, {}), {2}: (16, {}), {3}: (17, {}),... | custom-call | tf_op jit(solution)/shard_map/replay/pallas_call | solution.py:372
  37.9 10.6 %all_to_all.11 = f32[16,1,128]{2,1,0:T(1,128)S(1)} all-to-all(f32[16,1,128]{2,1,0:T(1,128)S(1)} %bitcast.7), channel_id=1, replica_groups=mesh['group'=2,'dp'=16] {'dp'}, dimensions={0} | all-to-all | bytes 16384 | tf_op jit(solution)/shard_map/all_to_all | solution.py:77
  48.5 4.5 %theta.1 = (f32[4096,512]{1,0:T(8,128)}, f32[1,16]{1,0:T(1,128)}) custom-call(f32[16,128]{1,0:T(8,128)S(1)} %bitcast.6, f32[8,128]{1,0:T(8,128)S(1)} %get-tuple-element.30.own, f32[256,512]{1,0:T(8,128)S(1)} %get-tuple-element.31.along, f32[256,512]{1,0:T(8,128)S(1)} %get-tuple-element.32.across, f32[256,512]{1,0:T(8,128)S(1)} %get-tuple-element.33.bend, ...), custom_call_target="tpu_custom_call" | custom-call | tf_op jit(solution)/shard_map/theta/pallas_call | solution.py:437
Async XLA Ops:
  0.6 3.2 %collective-permute-start.2 = (bf16[16,4096]{1,0:T(8,128)(2,1)}, bf16[16,4096]{1,0:T(8,128)(2,1)S(1)}, u32[]{:S(2)}, u32[]{:S(2)}) collective-permute-start(bf16[16,4096]{1,0:T(8,128)(2,1)} %refs_0_.1), channel_id=1, source_target_pairs={{1,0},{0,1},{3,2},{2,3},{5,4},{4,5},{7,6},{6,7},{9,8},{8,9},{11,10... | collective-permute-start | bytes 393224 | tf_op jit(solution)/shard_map/ppermute | solution.py:25
  1.1 6.8 %collective-permute-start = (bf16[16,4096]{1,0:T(8,128)(2,1)}, bf16[16,4096]{1,0:T(8,128)(2,1)S(1)}, u32[]{:S(2)}, u32[]{:S(2)}) collective-permute-start(bf16[16,4096]{1,0:T(8,128)(2,1)} %refs_0_.1), channel_id=1, source_target_pairs={{2,0},{5,1},{0,4},{9,5},{4,8},{13,9},{8,12},{15,13},{12,14},{11,15... | collective-permute-start | bytes 393224 | tf_op jit(solution)/shard_map/ppermute | solution.py:39
  3.8 5.8 %collective-permute-start.3 = (bf16[16,4096]{1,0:T(8,128)(2,1)S(1)}, bf16[16,4096]{1,0:T(8,128)(2,1)S(1)}, u32[]{:S(2)}, u32[]{:S(2)}) collective-permute-start(bf16[16,4096]{1,0:T(8,128)(2,1)S(1)} %collective-permute-done.2.refs_1_), channel_id=1, source_target_pairs={{2,0},{5,1},{0,4},{9,5},{4,8},{13,9},{8,12},{15,13},{12,14},{11,15... | collective-permute-start | bytes 393224 | tf_op jit(solution)/shard_map/ppermute | solution.py:39
  7.9 5.5 %collective-permute-start.5 = (bf16[16,4096]{1,0:T(8,128)(2,1)S(1)}, bf16[16,4096]{1,0:T(8,128)(2,1)S(1)}, u32[]{:S(2)}, u32[]{:S(2)}) collective-permute-start(bf16[16,4096]{1,0:T(8,128)(2,1)S(1)} %collective-permute-done.after.refs_2_), channel_id=1, source_target_pairs={{2,0},{5,1},{0,4},{9,5},{4,8},{13,9},{8,12},{15,13},{12,14},{11,15... | collective-permute-start | bytes 393224 | tf_op jit(solution)/shard_map/ppermute | solution.py:39
  9.5 8.9 %collective-permute-start.1 = (bf16[16,4096]{1,0:T(8,128)(2,1)S(1)}, bf16[16,4096]{1,0:T(8,128)(2,1)S(1)}, u32[]{:S(2)}, u32[]{:S(2)}) collective-permute-start(bf16[16,4096]{1,0:T(8,128)(2,1)S(1)} %collective-permute-done.after.refs_2_), channel_id=1, source_target_pairs={{1,0},{0,1},{3,2},{2,3},{5,4},{4,5},{7,6},{6,7},{9,8},{8,9},{11,10... | collective-permute-start | bytes 393224 | tf_op jit(solution)/shard_map/ppermute | solution.py:25
  9.5 5.5 %collective-permute-start.7 = (bf16[16,4096]{1,0:T(8,128)(2,1)S(1)}, bf16[16,4096]{1,0:T(8,128)(2,1)S(1)}, u32[]{:S(2)}, u32[]{:S(2)}) collective-permute-start(bf16[16,4096]{1,0:T(8,128)(2,1)S(1)} %collective-permute-done.3.refs_3_), channel_id=1, source_target_pairs={{2,0},{5,1},{0,4},{9,5},{4,8},{13,9},{8,12},{15,13},{12,14},{11,15... | collective-permute-start | bytes 393224 | tf_op jit(solution)/shard_map/ppermute | solution.py:39
  13.4 8.1 %copy-start = (bf16[16,4096]{1,0:T(8,128)(2,1)S(1)}, bf16[16,4096]{1,0:T(8,128)(2,1)}, u32[]{:S(2)}) copy-start(bf16[16,4096]{1,0:T(8,128)(2,1)} %refs_0_.1) | copy-start | bytes 393220
  13.4 6.6 %collective-permute-start.4 = (bf16[16,4096]{1,0:T(8,128)(2,1)S(1)}, bf16[16,4096]{1,0:T(8,128)(2,1)S(1)}, u32[]{:S(2)}, u32[]{:S(2)}) collective-permute-start(bf16[16,4096]{1,0:T(8,128)(2,1)S(1)} %collective-permute-done.3.refs_3_), channel_id=1, source_target_pairs={{1,0},{0,1},{3,2},{2,3},{5,4},{4,5},{7,6},{6,7},{9,8},{8,9},{11,10... | collective-permute-start | bytes 393224 | tf_op jit(solution)/shard_map/ppermute | solution.py:25
  13.5 5.0 %collective-permute-start.9 = (bf16[16,4096]{1,0:T(8,128)(2,1)S(1)}, bf16[16,4096]{1,0:T(8,128)(2,1)S(1)}, u32[]{:S(2)}, u32[]{:S(2)}) collective-permute-start(bf16[16,4096]{1,0:T(8,128)(2,1)S(1)} %collective-permute-done.5.after.refs_4_), channel_id=1, source_target_pairs={{2,0},{5,1},{0,4},{9,5},{4,8},{13,9},{8,12},{15,13},{12,14},{11,15... | collective-permute-start | bytes 393224 | tf_op jit(solution)/shard_map/ppermute | solution.py:39
  15.0 6.4 %collective-permute-start.6 = (bf16[16,4096]{1,0:T(8,128)(2,1)S(1)}, bf16[16,4096]{1,0:T(8,128)(2,1)S(1)}, u32[]{:S(2)}, u32[]{:S(2)}) collective-permute-start(bf16[16,4096]{1,0:T(8,128)(2,1)S(1)} %collective-permute-done.5.after.refs_4_), channel_id=1, source_target_pairs={{1,0},{0,1},{3,2},{2,3},{5,4},{4,5},{7,6},{6,7},{9,8},{8,9},{11,10... | collective-permute-start | bytes 393224 | tf_op jit(solution)/shard_map/ppermute | solution.py:25
  15.0 5.0 %collective-permute-start.11 = (bf16[16,4096]{1,0:T(8,128)(2,1)S(1)}, bf16[16,4096]{1,0:T(8,128)(2,1)S(1)}, u32[]{:S(2)}, u32[]{:S(2)}) collective-permute-start(bf16[16,4096]{1,0:T(8,128)(2,1)S(1)} %collective-permute-done.7.refs_5_), channel_id=1, source_target_pairs={{2,0},{5,1},{0,4},{9,5},{4,8},{13,9},{8,12},{15,13},{12,14},{11,15... | collective-permute-start | bytes 393224 | tf_op jit(solution)/shard_map/ppermute | solution.py:39
  18.4 6.7 %collective-permute-start.8 = (bf16[16,4096]{1,0:T(8,128)(2,1)S(1)}, bf16[16,4096]{1,0:T(8,128)(2,1)S(1)}, u32[]{:S(2)}, u32[]{:S(2)}) collective-permute-start(bf16[16,4096]{1,0:T(8,128)(2,1)S(1)} %collective-permute-done.7.refs_5_), channel_id=1, source_target_pairs={{1,0},{0,1},{3,2},{2,3},{5,4},{4,5},{7,6},{6,7},{9,8},{8,9},{11,10... | collective-permute-start | bytes 393224 | tf_op jit(solution)/shard_map/ppermute | solution.py:25
  18.5 6.6 %collective-permute-start.13 = (bf16[16,4096]{1,0:T(8,128)(2,1)S(1)}, bf16[16,4096]{1,0:T(8,128)(2,1)S(1)}, u32[]{:S(2)}, u32[]{:S(2)}) collective-permute-start(bf16[16,4096]{1,0:T(8,128)(2,1)S(1)} %collective-permute-done.9.refs_6_), channel_id=1, source_target_pairs={{2,0},{5,1},{0,4},{9,5},{4,8},{13,9},{8,12},{15,13},{12,14},{11,15... | collective-permute-start | bytes 393224 | tf_op jit(solution)/shard_map/ppermute | solution.py:39
  20.0 5.2 %collective-permute-start.10 = (bf16[16,4096]{1,0:T(8,128)(2,1)S(1)}, bf16[16,4096]{1,0:T(8,128)(2,1)S(1)}, u32[]{:S(2)}, u32[]{:S(2)}) collective-permute-start(bf16[16,4096]{1,0:T(8,128)(2,1)S(1)} %collective-permute-done.9.refs_6_), channel_id=1, source_target_pairs={{1,0},{0,1},{3,2},{2,3},{5,4},{4,5},{7,6},{6,7},{9,8},{8,9},{11,10... | collective-permute-start | bytes 393224 | tf_op jit(solution)/shard_map/ppermute | solution.py:25
  20.0 5.2 %collective-permute-start.14 = (bf16[16,4096]{1,0:T(8,128)(2,1)S(1)}, bf16[16,4096]{1,0:T(8,128)(2,1)S(1)}, u32[]{:S(2)}, u32[]{:S(2)}) collective-permute-start(bf16[16,4096]{1,0:T(8,128)(2,1)S(1)} %collective-permute-done.11.refs_7_), channel_id=1, source_target_pairs={{2,0},{5,1},{0,4},{9,5},{4,8},{13,9},{8,12},{15,13},{12,14},{11,15... | collective-permute-start | bytes 393224 | tf_op jit(solution)/shard_map/ppermute | solution.py:39
  21.4 3.7 %collective-permute-start.12 = (bf16[16,4096]{1,0:T(8,128)(2,1)S(1)}, bf16[16,4096]{1,0:T(8,128)(2,1)S(1)}, u32[]{:S(2)}, u32[]{:S(2)}) collective-permute-start(bf16[16,4096]{1,0:T(8,128)(2,1)S(1)} %collective-permute-done.11.refs_7_), channel_id=1, source_target_pairs={{1,0},{0,1},{3,2},{2,3},{5,4},{4,5},{7,6},{6,7},{9,8},{8,9},{11,10... | collective-permute-start | bytes 393224 | tf_op jit(solution)/shard_map/ppermute | solution.py:25

commit v19 on v18

--- a/solution.py
+++ b/solution.py
@@ -10,7 +10,7 @@
 TILE = 512
 HALF = 256
 ROWS = 16
-COLUMNS = 256
+COLUMNS = 128
 COST = 4 << 30
 SAMPLE = 64
 VMEM_BYTES = 12 << 20

time: 53.3 us -> 53.9 us (1.011)
  Pallas kernels: 27.9 us -> 28.6 us
    pallas_call x1, Pallas kernels: 12.7 us -> 13.4 us  [replay_call(): pl.pallas_call(functools.partial(replay_kernel, n, half), in_specs=[far]...]
where the time goes in v19:
time: 53.9 us; the launch traced here: 53.6 us
  Pallas kernels  28.6 us (53%)
  starting transfers between devices  13.6 us (25%)
  blocking collectives  10.6 us (20%)
  between operations  0.78 us (1%)
    pallas_call x1, Pallas kernels, replay_call(): pl.pallas_call(functools.partial(replay_kernel, n, half), in_specs=[far]...  13.4 us
    ppermute x8, starting transfers between devices, onward(): return lax.ppermute(value, 'dp', pairs)  12.9 us
    all_to_all x1, blocking collectives, to_all(): return lax.all_to_all(rows, 'dp', split_axis=0, concat_axis=0, tiled=True)  10.6 us
    pallas_call x2, Pallas kernels, fetch_wide(): pl.pallas_call(functools.partial(widen_kernel, factor), in_specs=[pl.Bloc...  4.57 us
    pallas_call x1, Pallas kernels, theta_call(): pl.pallas_call(functools.partial(theta_kernel, entries), in_specs=[vmem]...  4.45 us
    pallas_call x1, Pallas kernels, early_call(): pl.pallas_call(functools.partial(early_kernel, parts), in_specs=[pl.Block...  3.68 us
    pallas_call x1, Pallas kernels, fetch(): pl.pallas_call(functools.partial(fetch_kernel, n), in_specs=[pl.BlockSpec...  2.52 us
  transfers between devices with their start and end apart: 15, of which 0 were waited for; matrix products, arithmetic and copies ran while one was open for 0% of the time, Pallas kernels for 20%

profile of v19, /device:TPU:0, one launch (start us, length us, event | category | flops | bytes accessed | tf_op | source)
XLA Modules:
  0.0 53.6 jit_solution(7741957812646966457)
XLA Ops:
  0.6 0.5 collective-permute-start.2
  1.1 2.6 %collective-permute-start = (bf16[16,4096]{1,0:T(8,128)(2,1)}, bf16[16,4096]{1,0:T(8,128)(2,1)S(1)}, u32[]{:S(2)}, u32[]{:S(2)}) collective-permute-start(bf16[16,4096]{1,0:T(8,128)(2,1)} %refs_0_.1), channel_id=1, source_target_pairs={{2,0},{5,1},{0,4},{9,5},{4,8},{13,9},{8,12},{15,13},{12,14},{11,15... | collective-permute-start | bytes 393224 | tf_op jit(solution)/shard_map/ppermute | solution.py:39
  3.8 0.0 collective-permute-done.2.refs_1_
  3.8 1.6 %collective-permute-start.3 = (bf16[16,4096]{1,0:T(8,128)(2,1)S(1)}, bf16[16,4096]{1,0:T(8,128)(2,1)S(1)}, u32[]{:S(2)}, u32[]{:S(2)}) collective-permute-start(bf16[16,4096]{1,0:T(8,128)(2,1)S(1)} %collective-permute-done.2.refs_1_), channel_id=1, source_target_pairs={{2,0},{5,1},{0,4},{9,5},{4,8},{13,9},{8,12},{15,13},{12,14},{11,15... | collective-permute-start | bytes 393224 | tf_op jit(solution)/shard_map/ppermute | solution.py:39
  5.4 2.5 %fetch.1 = (bf16[4096,512]{1,0:T(8,128)(2,1)S(1)}, bf16[256,512]{1,0:T(8,128)(2,1)S(1)}, f32[256,128]{1,0:T(8,128)S(1)}) custom-call(bf16[4096,512]{1,0:T(8,128)(2,1)} %far.3, bf16[256,512]{1,0:T(8,128)(2,1)} %far_cot.1, f32[1,256]{1,0:T(1,128)} %bitcast.8, bf16[16,4096]{1,0:T(8,128)(2,1)} %refs_0_.1), custom_call_target="tpu_custom_call" | custom-call | flops 4294967296 | bytes 8388608 | tf_op jit(solution)/shard_map/fetch/pallas_call | solution.py:159
  7.9 0.0 collective-permute-done.after.refs_2_
  7.9 1.6 %collective-permute-start.5 = (bf16[16,4096]{1,0:T(8,128)(2,1)S(1)}, bf16[16,4096]{1,0:T(8,128)(2,1)S(1)}, u32[]{:S(2)}, u32[]{:S(2)}) collective-permute-start(bf16[16,4096]{1,0:T(8,128)(2,1)S(1)} %collective-permute-done.after.refs_2_), channel_id=1, source_target_pairs={{2,0},{5,1},{0,4},{9,5},{4,8},{13,9},{8,12},{15,13},{12,14},{11,15... | collective-permute-start | bytes 393224 | tf_op jit(solution)/shard_map/ppermute | solution.py:39
  9.5 0.0 collective-permute-start.1
  9.5 0.0 collective-permute-done.3.refs_3_
  9.5 1.5 %collective-permute-start.7 = (bf16[16,4096]{1,0:T(8,128)(2,1)S(1)}, bf16[16,4096]{1,0:T(8,128)(2,1)S(1)}, u32[]{:S(2)}, u32[]{:S(2)}) collective-permute-start(bf16[16,4096]{1,0:T(8,128)(2,1)S(1)} %collective-permute-done.3.refs_3_), channel_id=1, source_target_pairs={{2,0},{5,1},{0,4},{9,5},{4,8},{13,9},{8,12},{15,13},{12,14},{11,15... | collective-permute-start | bytes 393224 | tf_op jit(solution)/shard_map/ppermute | solution.py:39
  11.1 2.3 %widen.2.refs_12_ = f32[4096,512]{1,0:T(8,128)S(1)} custom-call(bf16[4096,512]{1,0:T(8,128)(2,1)} %far.4, bf16[16,4096]{1,0:T(8,128)(2,1)S(1)} %collective-permute-done.after.refs_2_), custom_call_target="tpu_custom_call" | custom-call | flops 4294967296 | bytes 8388608 | tf_op jit(solution)/shard_map/widen/pallas_call | solution.py:121
  13.4 0.0 copy-start
  13.4 0.1 collective-permute-start.4
  13.4 0.0 collective-permute-done.5.after.refs_4_
  13.5 1.5 %collective-permute-start.9 = (bf16[16,4096]{1,0:T(8,128)(2,1)S(1)}, bf16[16,4096]{1,0:T(8,128)(2,1)S(1)}, u32[]{:S(2)}, u32[]{:S(2)}) collective-permute-start(bf16[16,4096]{1,0:T(8,128)(2,1)S(1)} %collective-permute-done.5.after.refs_4_), channel_id=1, source_target_pairs={{2,0},{5,1},{0,4},{9,5},{4,8},{13,9},{8,12},{15,13},{12,14},{11,15... | collective-permute-start | bytes 393224 | tf_op jit(solution)/shard_map/ppermute | solution.py:39
  15.0 0.0 collective-permute-start.6
  15.0 0.0 collective-permute-done.7.refs_5_
  15.0 1.1 %collective-permute-start.11 = (bf16[16,4096]{1,0:T(8,128)(2,1)S(1)}, bf16[16,4096]{1,0:T(8,128)(2,1)S(1)}, u32[]{:S(2)}, u32[]{:S(2)}) collective-permute-start(bf16[16,4096]{1,0:T(8,128)(2,1)S(1)} %collective-permute-done.7.refs_5_), channel_id=1, source_target_pairs={{2,0},{5,1},{0,4},{9,5},{4,8},{13,9},{8,12},{15,13},{12,14},{11,15... | collective-permute-start | bytes 393224 | tf_op jit(solution)/shard_map/ppermute | solution.py:39
  16.1 2.3 %widen.3.refs_13_ = f32[4096,512]{1,0:T(8,128)S(1)} custom-call(bf16[4096,512]{1,0:T(8,128)(2,1)} %far.5, bf16[16,4096]{1,0:T(8,128)(2,1)S(1)} %collective-permute-done.5.after.refs_4_), custom_call_target="tpu_custom_call" | custom-call | flops 4294967296 | bytes 8388608 | tf_op jit(solution)/shard_map/widen/pallas_call | solution.py:121
  18.4 0.0 collective-permute-done.1.refs_0_
  18.4 0.1 collective-permute-start.8
  18.5 0.0 collective-permute-done.9.refs_6_
  18.5 1.5 %collective-permute-start.13 = (bf16[16,4096]{1,0:T(8,128)(2,1)S(1)}, bf16[16,4096]{1,0:T(8,128)(2,1)S(1)}, u32[]{:S(2)}, u32[]{:S(2)}) collective-permute-start(bf16[16,4096]{1,0:T(8,128)(2,1)S(1)} %collective-permute-done.9.refs_6_), channel_id=1, source_target_pairs={{2,0},{5,1},{0,4},{9,5},{4,8},{13,9},{8,12},{15,13},{12,14},{11,15... | collective-permute-start | bytes 393224 | tf_op jit(solution)/shard_map/ppermute | solution.py:39
  20.0 0.0 collective-permute-done.4.refs_1_
  20.0 0.0 collective-permute-start.10
  20.0 0.0 collective-permute-done.11.refs_7_
  20.0 1.4 %collective-permute-start.14 = (bf16[16,4096]{1,0:T(8,128)(2,1)S(1)}, bf16[16,4096]{1,0:T(8,128)(2,1)S(1)}, u32[]{:S(2)}, u32[]{:S(2)}) collective-permute-start(bf16[16,4096]{1,0:T(8,128)(2,1)S(1)} %collective-permute-done.11.refs_7_), channel_id=1, source_target_pairs={{2,0},{5,1},{0,4},{9,5},{4,8},{13,9},{8,12},{15,13},{12,14},{11,15... | collective-permute-start | bytes 393224 | tf_op jit(solution)/shard_map/ppermute | solution.py:39
  21.4 0.0 collective-permute-done.6.refs_2_
  21.4 0.0 collective-permute-start.12
  21.4 0.0 copy-done
  21.4 3.7 %early.1 = (bf16[256,4096]{1,0:T(8,128)(2,1)S(1)}, bf16[4096,256]{1,0:T(8,128)(2,1)S(1)}, f32[256,512]{1,0:T(8,128)S(1)}, bf16[256,512]{1,0:T(8,128)(2,1)S(1)}, ...) custom-call(bf16[16,4096]{1,0:T(8,128)(2,1)S(1)} %copy-done, bf16[16,4096]{1,0:T(8,128)(2,1)S(1)} %collective-permute-done.2.refs_1_, ...), custom_call_target="tpu_custom_call" | custom-call | flops 4294967296 | bytes 12582912 | tf_op jit(solution)/shard_map/early/pallas_call | solution.py:236
  25.1 0.0 collective-permute-done.8.refs_3_
  25.1 0.0 collective-permute-done.13.refs_6_
  25.1 0.0 collective-permute-done.10.refs_4_
  25.2 0.0 collective-permute-done.14.refs_7_
  25.2 0.0 collective-permute-done.12.refs_5_
  25.2 13.4 %replay.1 = (bf16[256,4096]{1,0:T(8,128)(2,1)S(1)}, bf16[4096,256]{1,0:T(8,128)(2,1)S(1)}, f32[256,512]{1,0:T(8,128)S(1)}, bf16[256,512]{1,0:T(8,128)(2,1)S(1)},...) custom-call(bf16[16,4096]{1,0:T(8,128)(2,1)S(1)} %collective-permute, ...), custom_call_target="tpu_custom_call", output_to_operand_aliasing={{0}: (14, {}), {1}: (15, {}), {2}: (16, {}), {3}: (17, {}),... | custom-call | tf_op jit(solution)/shard_map/replay/pallas_call | solution.py:372
  38.6 10.6 %all_to_all.11 = f32[16,1,128]{2,1,0:T(1,128)S(1)} all-to-all(f32[16,1,128]{2,1,0:T(1,128)S(1)} %bitcast.7), channel_id=1, replica_groups=mesh['group'=2,'dp'=16] {'dp'}, dimensions={0} | all-to-all | bytes 16384 | tf_op jit(solution)/shard_map/all_to_all | solution.py:77
  49.2 4.5 %theta.1 = (f32[4096,512]{1,0:T(8,128)}, f32[1,16]{1,0:T(1,128)}) custom-call(f32[16,128]{1,0:T(8,128)S(1)} %bitcast.6, f32[8,128]{1,0:T(8,128)S(1)} %get-tuple-element.30.own, f32[256,512]{1,0:T(8,128)S(1)} %get-tuple-element.31.along, f32[256,512]{1,0:T(8,128)S(1)} %get-tuple-element.32.across, f32[256,512]{1,0:T(8,128)S(1)} %get-tuple-element.33.bend, ...), custom_call_target="tpu_custom_call" | custom-call | tf_op jit(solution)/shard_map/theta/pallas_call | solution.py:437
Async XLA Ops:
  0.6 3.2 %collective-permute-start.2 = (bf16[16,4096]{1,0:T(8,128)(2,1)}, bf16[16,4096]{1,0:T(8,128)(2,1)S(1)}, u32[]{:S(2)}, u32[]{:S(2)}) collective-permute-start(bf16[16,4096]{1,0:T(8,128)(2,1)} %refs_0_.1), channel_id=1, source_target_pairs={{1,0},{0,1},{3,2},{2,3},{5,4},{4,5},{7,6},{6,7},{9,8},{8,9},{11,10... | collective-permute-start | bytes 393224 | tf_op jit(solution)/shard_map/ppermute | solution.py:25
  1.1 6.8 %collective-permute-start = (bf16[16,4096]{1,0:T(8,128)(2,1)}, bf16[16,4096]{1,0:T(8,128)(2,1)S(1)}, u32[]{:S(2)}, u32[]{:S(2)}) collective-permute-start(bf16[16,4096]{1,0:T(8,128)(2,1)} %refs_0_.1), channel_id=1, source_target_pairs={{2,0},{5,1},{0,4},{9,5},{4,8},{13,9},{8,12},{15,13},{12,14},{11,15... | collective-permute-start | bytes 393224 | tf_op jit(solution)/shard_map/ppermute | solution.py:39
  3.8 5.8 %collective-permute-start.3 = (bf16[16,4096]{1,0:T(8,128)(2,1)S(1)}, bf16[16,4096]{1,0:T(8,128)(2,1)S(1)}, u32[]{:S(2)}, u32[]{:S(2)}) collective-permute-start(bf16[16,4096]{1,0:T(8,128)(2,1)S(1)} %collective-permute-done.2.refs_1_), channel_id=1, source_target_pairs={{2,0},{5,1},{0,4},{9,5},{4,8},{13,9},{8,12},{15,13},{12,14},{11,15... | collective-permute-start | bytes 393224 | tf_op jit(solution)/shard_map/ppermute | solution.py:39
  7.9 5.5 %collective-permute-start.5 = (bf16[16,4096]{1,0:T(8,128)(2,1)S(1)}, bf16[16,4096]{1,0:T(8,128)(2,1)S(1)}, u32[]{:S(2)}, u32[]{:S(2)}) collective-permute-start(bf16[16,4096]{1,0:T(8,128)(2,1)S(1)} %collective-permute-done.after.refs_2_), channel_id=1, source_target_pairs={{2,0},{5,1},{0,4},{9,5},{4,8},{13,9},{8,12},{15,13},{12,14},{11,15... | collective-permute-start | bytes 393224 | tf_op jit(solution)/shard_map/ppermute | solution.py:39
  9.5 8.9 %collective-permute-start.1 = (bf16[16,4096]{1,0:T(8,128)(2,1)S(1)}, bf16[16,4096]{1,0:T(8,128)(2,1)S(1)}, u32[]{:S(2)}, u32[]{:S(2)}) collective-permute-start(bf16[16,4096]{1,0:T(8,128)(2,1)S(1)} %collective-permute-done.after.refs_2_), channel_id=1, source_target_pairs={{1,0},{0,1},{3,2},{2,3},{5,4},{4,5},{7,6},{6,7},{9,8},{8,9},{11,10... | collective-permute-start | bytes 393224 | tf_op jit(solution)/shard_map/ppermute | solution.py:25
  9.5 5.5 %collective-permute-start.7 = (bf16[16,4096]{1,0:T(8,128)(2,1)S(1)}, bf16[16,4096]{1,0:T(8,128)(2,1)S(1)}, u32[]{:S(2)}, u32[]{:S(2)}) collective-permute-start(bf16[16,4096]{1,0:T(8,128)(2,1)S(1)} %collective-permute-done.3.refs_3_), channel_id=1, source_target_pairs={{2,0},{5,1},{0,4},{9,5},{4,8},{13,9},{8,12},{15,13},{12,14},{11,15... | collective-permute-start | bytes 393224 | tf_op jit(solution)/shard_map/ppermute | solution.py:39
  13.4 8.1 %copy-start = (bf16[16,4096]{1,0:T(8,128)(2,1)S(1)}, bf16[16,4096]{1,0:T(8,128)(2,1)}, u32[]{:S(2)}) copy-start(bf16[16,4096]{1,0:T(8,128)(2,1)} %refs_0_.1) | copy-start | bytes 393220
  13.4 6.6 %collective-permute-start.4 = (bf16[16,4096]{1,0:T(8,128)(2,1)S(1)}, bf16[16,4096]{1,0:T(8,128)(2,1)S(1)}, u32[]{:S(2)}, u32[]{:S(2)}) collective-permute-start(bf16[16,4096]{1,0:T(8,128)(2,1)S(1)} %collective-permute-done.3.refs_3_), channel_id=1, source_target_pairs={{1,0},{0,1},{3,2},{2,3},{5,4},{4,5},{7,6},{6,7},{9,8},{8,9},{11,10... | collective-permute-start | bytes 393224 | tf_op jit(solution)/shard_map/ppermute | solution.py:25
  13.5 5.0 %collective-permute-start.9 = (bf16[16,4096]{1,0:T(8,128)(2,1)S(1)}, bf16[16,4096]{1,0:T(8,128)(2,1)S(1)}, u32[]{:S(2)}, u32[]{:S(2)}) collective-permute-start(bf16[16,4096]{1,0:T(8,128)(2,1)S(1)} %collective-permute-done.5.after.refs_4_), channel_id=1, source_target_pairs={{2,0},{5,1},{0,4},{9,5},{4,8},{13,9},{8,12},{15,13},{12,14},{11,15... | collective-permute-start | bytes 393224 | tf_op jit(solution)/shard_map/ppermute | solution.py:39
  15.0 6.4 %collective-permute-start.6 = (bf16[16,4096]{1,0:T(8,128)(2,1)S(1)}, bf16[16,4096]{1,0:T(8,128)(2,1)S(1)}, u32[]{:S(2)}, u32[]{:S(2)}) collective-permute-start(bf16[16,4096]{1,0:T(8,128)(2,1)S(1)} %collective-permute-done.5.after.refs_4_), channel_id=1, source_target_pairs={{1,0},{0,1},{3,2},{2,3},{5,4},{4,5},{7,6},{6,7},{9,8},{8,9},{11,10... | collective-permute-start | bytes 393224 | tf_op jit(solution)/shard_map/ppermute | solution.py:25
  15.0 5.0 %collective-permute-start.11 = (bf16[16,4096]{1,0:T(8,128)(2,1)S(1)}, bf16[16,4096]{1,0:T(8,128)(2,1)S(1)}, u32[]{:S(2)}, u32[]{:S(2)}) collective-permute-start(bf16[16,4096]{1,0:T(8,128)(2,1)S(1)} %collective-permute-done.7.refs_5_), channel_id=1, source_target_pairs={{2,0},{5,1},{0,4},{9,5},{4,8},{13,9},{8,12},{15,13},{12,14},{11,15... | collective-permute-start | bytes 393224 | tf_op jit(solution)/shard_map/ppermute | solution.py:39
  18.4 6.7 %collective-permute-start.8 = (bf16[16,4096]{1,0:T(8,128)(2,1)S(1)}, bf16[16,4096]{1,0:T(8,128)(2,1)S(1)}, u32[]{:S(2)}, u32[]{:S(2)}) collective-permute-start(bf16[16,4096]{1,0:T(8,128)(2,1)S(1)} %collective-permute-done.7.refs_5_), channel_id=1, source_target_pairs={{1,0},{0,1},{3,2},{2,3},{5,4},{4,5},{7,6},{6,7},{9,8},{8,9},{11,10... | collective-permute-start | bytes 393224 | tf_op jit(solution)/shard_map/ppermute | solution.py:25
  18.5 6.6 %collective-permute-start.13 = (bf16[16,4096]{1,0:T(8,128)(2,1)S(1)}, bf16[16,4096]{1,0:T(8,128)(2,1)S(1)}, u32[]{:S(2)}, u32[]{:S(2)}) collective-permute-start(bf16[16,4096]{1,0:T(8,128)(2,1)S(1)} %collective-permute-done.9.refs_6_), channel_id=1, source_target_pairs={{2,0},{5,1},{0,4},{9,5},{4,8},{13,9},{8,12},{15,13},{12,14},{11,15... | collective-permute-start | bytes 393224 | tf_op jit(solution)/shard_map/ppermute | solution.py:39
  20.0 5.2 %collective-permute-start.10 = (bf16[16,4096]{1,0:T(8,128)(2,1)S(1)}, bf16[16,4096]{1,0:T(8,128)(2,1)S(1)}, u32[]{:S(2)}, u32[]{:S(2)}) collective-permute-start(bf16[16,4096]{1,0:T(8,128)(2,1)S(1)} %collective-permute-done.9.refs_6_), channel_id=1, source_target_pairs={{1,0},{0,1},{3,2},{2,3},{5,4},{4,5},{7,6},{6,7},{9,8},{8,9},{11,10... | collective-permute-start | bytes 393224 | tf_op jit(solution)/shard_map/ppermute | solution.py:25
  20.0 5.2 %collective-permute-start.14 = (bf16[16,4096]{1,0:T(8,128)(2,1)S(1)}, bf16[16,4096]{1,0:T(8,128)(2,1)S(1)}, u32[]{:S(2)}, u32[]{:S(2)}) collective-permute-start(bf16[16,4096]{1,0:T(8,128)(2,1)S(1)} %collective-permute-done.11.refs_7_), channel_id=1, source_target_pairs={{2,0},{5,1},{0,4},{9,5},{4,8},{13,9},{8,12},{15,13},{12,14},{11,15... | collective-permute-start | bytes 393224 | tf_op jit(solution)/shard_map/ppermute | solution.py:39
  21.4 3.7 %collective-permute-start.12 = (bf16[16,4096]{1,0:T(8,128)(2,1)S(1)}, bf16[16,4096]{1,0:T(8,128)(2,1)S(1)}, u32[]{:S(2)}, u32[]{:S(2)}) collective-permute-start(bf16[16,4096]{1,0:T(8,128)(2,1)S(1)} %collective-permute-done.11.refs_7_), channel_id=1, source_target_pairs={{1,0},{0,1},{3,2},{2,3},{5,4},{4,5},{7,6},{6,7},{9,8},{8,9},{11,10... | collective-permute-start | bytes 393224 | tf_op jit(solution)/shard_map/ppermute | solution.py:25
